TPU v7x, 32 devices: a whole 2x2x4 slice. The times are simulated.
32 devices in a mesh: groups: 2 (over x), blk: 16 (over z, y, core).
Axes of the slice: x: 2, y: 2, z: 4, core: 2. Of those that a mesh axis runs over, the one named last changes fastest.
Arguments:
- features: float32 [64, 16384], P(None, ('groups', 'blk')), parts along dimension 1, may hold values from -6 to 6
- solves: float32 [16, 16384], P(None, ('groups', 'blk')), parts along dimension 1, may hold values from -6 to 6
- probes: float32 [16, 16384], P(None, ('groups', 'blk')), parts along dimension 1, may hold values from -6 to 6
Outputs:
- feature_grad: float32 [64, 16384], P(None, ('groups', 'blk')), parts along dimension 1
There are 2 independent parts, one for each index of `groups`. A program takes and returns all parts, laid end to end along the dimension named above; each array names one. Nothing has to cross between parts.
All inputs are finite; a program needn't handle non-finite values.
Results may differ from a plain program's by a relative error of at most 0.0003.
Values sent between devices are 32-bit elements; how exact they have to be, the bound alone decides.
No kernel may reach another device: no remote copies, remote signals or barrier semaphores. Data moves between devices by JAX's collectives and lax.ppermute only.
A program may use at most 64 MiB of HBM per device.

v0:
```python
import jax
import jax.numpy as jnp
from jax import lax
from jax.sharding import PartitionSpec as P


def passed_along(value, axis, steps):
    count = lax.axis_size(axis)
    pairs = [(source, (source + steps) % count) for source in range(count)]
    return lax.ppermute(value, axis, pairs)


def term_weights(vectors):
    position = jnp.arange(vectors)
    return jnp.where(position == 0, 0.5, -0.5 / (vectors - 1)).astype(jnp.float32)


def pair_terms(mine, theirs, width, vectors):
    highest = lax.Precision.HIGHEST
    feat_mine = mine[:width]
    solve_mine = mine[width : width + vectors]
    probe_mine = mine[width + vectors : width + 2 * vectors]
    feat_theirs = theirs[:width]
    solve_theirs = theirs[width : width + vectors]
    probe_theirs = theirs[width + vectors : width + 2 * vectors]
    norms_mine = jnp.sum(feat_mine * feat_mine, axis=0)
    norms_theirs = jnp.sum(feat_theirs * feat_theirs, axis=0)
    inner = lax.dot_general(feat_mine, feat_theirs, (((0,), (0,)), ((), ())), precision=highest)
    distance = norms_mine[:, None] + norms_theirs[None, :] - 2.0 * inner
    kernel = jnp.exp(-distance / (2.0 * width))
    weights = term_weights(vectors)[:, None]
    lefthand = jnp.concatenate([solve_mine, probe_mine], 0)
    righthand = jnp.concatenate([weights * probe_theirs, weights * solve_theirs], 0)
    coupling = (
        lax.dot_general(lefthand, righthand, (((0,), (0,)), ((), ())), precision=highest) * kernel
    )
    pulled_mine = lax.dot_general(
        feat_theirs, coupling, (((1,), (1,)), ((), ())), precision=highest
    )
    pulled_theirs = lax.dot_general(
        feat_mine, coupling, (((1,), (0,)), ((), ())), precision=highest
    )
    toward_mine = -(feat_mine * jnp.sum(coupling, axis=1)[None, :] - pulled_mine) / width
    toward_theirs = -(feat_theirs * jnp.sum(coupling, axis=0)[None, :] - pulled_theirs) / width
    return (toward_mine, toward_theirs)


def absorb_block(mine, moving, keep, width, vectors):
    depth = mine.shape[0]
    toward_mine, toward_theirs = pair_terms(mine, moving[:depth], width, vectors)
    partial_value = moving[depth:] + keep * toward_theirs
    return (jnp.concatenate([moving[:depth], partial_value], 0), toward_mine)


def local(features, solves, probes):
    width = features.shape[0]
    vectors = solves.shape[0]
    points = features.shape[1]
    mine = jnp.concatenate([features, solves, probes], 0)
    depth = mine.shape[0]
    half = lax.axis_size("blk") // 2
    own_terms, unused = pair_terms(mine, mine, width, vectors)
    carried = jnp.concatenate([mine, jnp.zeros((width, points), jnp.float32)], 0)

    def advance(stride, carry):
        moving, total = carry
        moving = passed_along(moving, "blk", 1)
        keep = jnp.where(stride < half, 1.0, 0.0).astype(jnp.float32)
        moving, toward_mine = absorb_block(mine, moving, keep, width, vectors)
        return (moving, total + toward_mine)

    moving, total = lax.fori_loop(1, half + 1, advance, (carried, own_terms))
    returned = passed_along(moving[depth:], "blk", -half)
    return total + returned


def solution(mesh):
    in_specs = (P(None, ("groups", "blk")), P(None, ("groups", "blk")), P(None, ("groups", "blk")))
    out_specs = P(None, ("groups", "blk"))
    return jax.shard_map(local, mesh=mesh, in_specs=in_specs, out_specs=out_specs, check_vma=False)
```

profile of v0, /device:TPU:0, one launch (start us, length us, event | category | flops | bytes accessed | tf_op | source)
XLA Modules:
  0.0 124.0 jit_solution(11252689744211331735)
XLA Ops:
  0.0 1.0 multiply_reduce_fusion.1
  1.0 1.2 fusion.14
  2.3 0.7 copy-done.1
  3.2 1.1 fusion.23
  4.3 0.8 fusion.17
  5.1 112.3 %while.17 = (s32[]{:T(128)}, f32[160,512]{1,0:T(8,128)S(1)}, f32[64,512]{1,0:T(8,128)S(1)}, f32[32,512]{1,0:T(8,128)S(1)}, f32[512]{0:T(512)S(1)}, /*index=5*/f3...) while((s32[]{:T(128)}, f32[160,512]{1,0:T(8,128)S(1)}, ...), condition=%wide.region_6.7_spmd, body=%wide.region_2.6_spmd.sunk | while | flops 707246592 | bytes 9320763 | solution.py:72
  5.6 9.8 %collective-permute-done = f32[160,512]{1,0:T(8,128)S(1)} collective-permute-done((f32[160,512]{1,0:T(8,128)S(1)}, f32[160,512]{1,0:T(8,128)S(1)}, u32[]{:S(2)}, u32[]{:S(2)}) %collective-permute-start) | collective-permute-done | bytes 327712 | tf_op jit(solution)/shard_map/while/body/eval_jaxpr/ppermute | solution.py:10
  15.4 1.0 convolution_multiply_fusion.4
  16.5 1.3 %fusion.50 = (f32[512]{0:T(512)S(1)}, f32[512]{0:T(512)S(1)}, f32[512,512]{0,1:T(8,128)S(1)}) fusion(f32[512,512]{0,1:T(8,128)S(1)} %convolution_multiply_fusion.4, f32[512]{0:T(512)S(1)} %multiply_reduce_fusion.3, f32[512]{0:T(512)S(1)} %get-tuple-element.257, f32[32,512]{1,0:T(8,128)S(1)} %get-tuple-element.256, ...), kind=kOutput, calls=%fused_computation.42.clone.1 | convolution fusion | flops 102513664 | bytes 2236416 | tf_op jit(solution)/shard_map/while/body/eval_jaxpr/dot_general | solution.py:35
  17.8 1.1 slice_add_fusion.2
  19.0 0.8 fusion.51
  19.9 9.2 %collective-permute-done = f32[160,512]{1,0:T(8,128)S(1)} collective-permute-done((f32[160,512]{1,0:T(8,128)S(1)}, f32[160,512]{1,0:T(8,128)S(1)}, u32[]{:S(2)}, u32[]{:S(2)}) %collective-permute-start) | collective-permute-done | bytes 327712 | tf_op jit(solution)/shard_map/while/body/eval_jaxpr/ppermute | solution.py:10
  29.1 1.0 convolution_multiply_fusion.4
  30.2 1.3 %fusion.50 = (f32[512]{0:T(512)S(1)}, f32[512]{0:T(512)S(1)}, f32[512,512]{0,1:T(8,128)S(1)}) fusion(f32[512,512]{0,1:T(8,128)S(1)} %convolution_multiply_fusion.4, f32[512]{0:T(512)S(1)} %multiply_reduce_fusion.3, f32[512]{0:T(512)S(1)} %get-tuple-element.257, f32[32,512]{1,0:T(8,128)S(1)} %get-tuple-element.256, ...), kind=kOutput, calls=%fused_computation.42.clone.1 | convolution fusion | flops 102513664 | bytes 2236416 | tf_op jit(solution)/shard_map/while/body/eval_jaxpr/dot_general | solution.py:35
  31.5 1.1 slice_add_fusion.2
  32.7 0.8 fusion.51
  33.6 9.2 %collective-permute-done = f32[160,512]{1,0:T(8,128)S(1)} collective-permute-done((f32[160,512]{1,0:T(8,128)S(1)}, f32[160,512]{1,0:T(8,128)S(1)}, u32[]{:S(2)}, u32[]{:S(2)}) %collective-permute-start) | collective-permute-done | bytes 327712 | tf_op jit(solution)/shard_map/while/body/eval_jaxpr/ppermute | solution.py:10
  42.8 1.0 convolution_multiply_fusion.4
  43.9 1.3 %fusion.50 = (f32[512]{0:T(512)S(1)}, f32[512]{0:T(512)S(1)}, f32[512,512]{0,1:T(8,128)S(1)}) fusion(f32[512,512]{0,1:T(8,128)S(1)} %convolution_multiply_fusion.4, f32[512]{0:T(512)S(1)} %multiply_reduce_fusion.3, f32[512]{0:T(512)S(1)} %get-tuple-element.257, f32[32,512]{1,0:T(8,128)S(1)} %get-tuple-element.256, ...), kind=kOutput, calls=%fused_computation.42.clone.1 | convolution fusion | flops 102513664 | bytes 2236416 | tf_op jit(solution)/shard_map/while/body/eval_jaxpr/dot_general | solution.py:35
  45.3 1.1 slice_add_fusion.2
  46.4 0.8 fusion.51
  47.4 9.2 %collective-permute-done = f32[160,512]{1,0:T(8,128)S(1)} collective-permute-done((f32[160,512]{1,0:T(8,128)S(1)}, f32[160,512]{1,0:T(8,128)S(1)}, u32[]{:S(2)}, u32[]{:S(2)}) %collective-permute-start) | collective-permute-done | bytes 327712 | tf_op jit(solution)/shard_map/while/body/eval_jaxpr/ppermute | solution.py:10
  56.6 1.0 convolution_multiply_fusion.4
  57.7 1.3 %fusion.50 = (f32[512]{0:T(512)S(1)}, f32[512]{0:T(512)S(1)}, f32[512,512]{0,1:T(8,128)S(1)}) fusion(f32[512,512]{0,1:T(8,128)S(1)} %convolution_multiply_fusion.4, f32[512]{0:T(512)S(1)} %multiply_reduce_fusion.3, f32[512]{0:T(512)S(1)} %get-tuple-element.257, f32[32,512]{1,0:T(8,128)S(1)} %get-tuple-element.256, ...), kind=kOutput, calls=%fused_computation.42.clone.1 | convolution fusion | flops 102513664 | bytes 2236416 | tf_op jit(solution)/shard_map/while/body/eval_jaxpr/dot_general | solution.py:35
  59.0 1.1 slice_add_fusion.2
  60.2 0.8 fusion.51
  61.1 9.2 %collective-permute-done = f32[160,512]{1,0:T(8,128)S(1)} collective-permute-done((f32[160,512]{1,0:T(8,128)S(1)}, f32[160,512]{1,0:T(8,128)S(1)}, u32[]{:S(2)}, u32[]{:S(2)}) %collective-permute-start) | collective-permute-done | bytes 327712 | tf_op jit(solution)/shard_map/while/body/eval_jaxpr/ppermute | solution.py:10
  70.3 1.0 convolution_multiply_fusion.4
  71.4 1.3 %fusion.50 = (f32[512]{0:T(512)S(1)}, f32[512]{0:T(512)S(1)}, f32[512,512]{0,1:T(8,128)S(1)}) fusion(f32[512,512]{0,1:T(8,128)S(1)} %convolution_multiply_fusion.4, f32[512]{0:T(512)S(1)} %multiply_reduce_fusion.3, f32[512]{0:T(512)S(1)} %get-tuple-element.257, f32[32,512]{1,0:T(8,128)S(1)} %get-tuple-element.256, ...), kind=kOutput, calls=%fused_computation.42.clone.1 | convolution fusion | flops 102513664 | bytes 2236416 | tf_op jit(solution)/shard_map/while/body/eval_jaxpr/dot_general | solution.py:35
  72.7 1.1 slice_add_fusion.2
  73.9 0.8 fusion.51
  74.8 9.2 %collective-permute-done = f32[160,512]{1,0:T(8,128)S(1)} collective-permute-done((f32[160,512]{1,0:T(8,128)S(1)}, f32[160,512]{1,0:T(8,128)S(1)}, u32[]{:S(2)}, u32[]{:S(2)}) %collective-permute-start) | collective-permute-done | bytes 327712 | tf_op jit(solution)/shard_map/while/body/eval_jaxpr/ppermute | solution.py:10
  84.0 1.0 convolution_multiply_fusion.4
  85.1 1.3 %fusion.50 = (f32[512]{0:T(512)S(1)}, f32[512]{0:T(512)S(1)}, f32[512,512]{0,1:T(8,128)S(1)}) fusion(f32[512,512]{0,1:T(8,128)S(1)} %convolution_multiply_fusion.4, f32[512]{0:T(512)S(1)} %multiply_reduce_fusion.3, f32[512]{0:T(512)S(1)} %get-tuple-element.257, f32[32,512]{1,0:T(8,128)S(1)} %get-tuple-element.256, ...), kind=kOutput, calls=%fused_computation.42.clone.1 | convolution fusion | flops 102513664 | bytes 2236416 | tf_op jit(solution)/shard_map/while/body/eval_jaxpr/dot_general | solution.py:35
  86.4 1.1 slice_add_fusion.2
  87.6 0.8 fusion.51
  88.5 9.2 %collective-permute-done = f32[160,512]{1,0:T(8,128)S(1)} collective-permute-done((f32[160,512]{1,0:T(8,128)S(1)}, f32[160,512]{1,0:T(8,128)S(1)}, u32[]{:S(2)}, u32[]{:S(2)}) %collective-permute-start) | collective-permute-done | bytes 327712 | tf_op jit(solution)/shard_map/while/body/eval_jaxpr/ppermute | solution.py:10
  97.7 1.0 convolution_multiply_fusion.4
  98.8 1.3 %fusion.50 = (f32[512]{0:T(512)S(1)}, f32[512]{0:T(512)S(1)}, f32[512,512]{0,1:T(8,128)S(1)}) fusion(f32[512,512]{0,1:T(8,128)S(1)} %convolution_multiply_fusion.4, f32[512]{0:T(512)S(1)} %multiply_reduce_fusion.3, f32[512]{0:T(512)S(1)} %get-tuple-element.257, f32[32,512]{1,0:T(8,128)S(1)} %get-tuple-element.256, ...), kind=kOutput, calls=%fused_computation.42.clone.1 | convolution fusion | flops 102513664 | bytes 2236416 | tf_op jit(solution)/shard_map/while/body/eval_jaxpr/dot_general | solution.py:35
  100.2 1.1 slice_add_fusion.2
  101.4 0.8 fusion.51
  102.3 10.7 %collective-permute-done = f32[160,512]{1,0:T(8,128)S(1)} collective-permute-done((f32[160,512]{1,0:T(8,128)S(1)}, f32[160,512]{1,0:T(8,128)S(1)}, u32[]{:S(2)}, u32[]{:S(2)}) %collective-permute-start) | collective-permute-done | bytes 327712 | tf_op jit(solution)/shard_map/while/body/eval_jaxpr/ppermute | solution.py:10
  113.0 1.0 convolution_multiply_fusion.4
  114.1 1.3 %fusion.50 = (f32[512]{0:T(512)S(1)}, f32[512]{0:T(512)S(1)}, f32[512,512]{0,1:T(8,128)S(1)}) fusion(f32[512,512]{0,1:T(8,128)S(1)} %convolution_multiply_fusion.4, f32[512]{0:T(512)S(1)} %multiply_reduce_fusion.3, f32[512]{0:T(512)S(1)} %get-tuple-element.257, f32[32,512]{1,0:T(8,128)S(1)} %get-tuple-element.256, ...), kind=kOutput, calls=%fused_computation.42.clone.1 | convolution fusion | flops 102513664 | bytes 2236416 | tf_op jit(solution)/shard_map/while/body/eval_jaxpr/dot_general | solution.py:35
  115.4 1.1 slice_add_fusion.2
  116.6 0.8 fusion.51
  117.5 5.9 %collective-permute-done.1 = f32[64,512]{1,0:T(8,128)S(1)} collective-permute-done((f32[64,512]{1,0:T(8,128)S(1)}, f32[64,512]{1,0:T(8,128)S(1)}, u32[]{:S(2)}, u32[]{:S(2)}) %collective-permute-start.1) | collective-permute-done | bytes 131104 | tf_op jit(solution)/shard_map/ppermute | solution.py:10
  123.4 0.7 add.95
  (61 shorter events, 2.5 us)
Async XLA Ops:
  0.0 1.0 copy-start
  1.0 1.2 copy-start.2
  2.2 0.8 copy-start.1
  5.1 10.3 %collective-permute-start = (f32[160,512]{1,0:T(8,128)S(1)}, f32[160,512]{1,0:T(8,128)S(1)}, u32[]{:S(2)}, u32[]{:S(2)}) collective-permute-start(f32[160,512]{1,0:T(8,128)S(1)} %get-tuple-element.243), channel_id=1, source_target_pairs={{0,1},{1,2},{2,3},{3,4},{4,5},{5,6},{6,7},{7,8},{8,9},{9,10},{10,1... | collective-permute-start | bytes 983048 | tf_op jit(solution)/shard_map/while/body/eval_jaxpr/ppermute | solution.py:10
  19.8 9.2 %collective-permute-start = (f32[160,512]{1,0:T(8,128)S(1)}, f32[160,512]{1,0:T(8,128)S(1)}, u32[]{:S(2)}, u32[]{:S(2)}) collective-permute-start(f32[160,512]{1,0:T(8,128)S(1)} %get-tuple-element.243), channel_id=1, source_target_pairs={{0,1},{1,2},{2,3},{3,4},{4,5},{5,6},{6,7},{7,8},{8,9},{9,10},{10,1... | collective-permute-start | bytes 983048 | tf_op jit(solution)/shard_map/while/body/eval_jaxpr/ppermute | solution.py:10
  33.6 9.2 %collective-permute-start = (f32[160,512]{1,0:T(8,128)S(1)}, f32[160,512]{1,0:T(8,128)S(1)}, u32[]{:S(2)}, u32[]{:S(2)}) collective-permute-start(f32[160,512]{1,0:T(8,128)S(1)} %get-tuple-element.243), channel_id=1, source_target_pairs={{0,1},{1,2},{2,3},{3,4},{4,5},{5,6},{6,7},{7,8},{8,9},{9,10},{10,1... | collective-permute-start | bytes 983048 | tf_op jit(solution)/shard_map/while/body/eval_jaxpr/ppermute | solution.py:10
  47.3 9.2 %collective-permute-start = (f32[160,512]{1,0:T(8,128)S(1)}, f32[160,512]{1,0:T(8,128)S(1)}, u32[]{:S(2)}, u32[]{:S(2)}) collective-permute-start(f32[160,512]{1,0:T(8,128)S(1)} %get-tuple-element.243), channel_id=1, source_target_pairs={{0,1},{1,2},{2,3},{3,4},{4,5},{5,6},{6,7},{7,8},{8,9},{9,10},{10,1... | collective-permute-start | bytes 983048 | tf_op jit(solution)/shard_map/while/body/eval_jaxpr/ppermute | solution.py:10
  61.0 9.2 %collective-permute-start = (f32[160,512]{1,0:T(8,128)S(1)}, f32[160,512]{1,0:T(8,128)S(1)}, u32[]{:S(2)}, u32[]{:S(2)}) collective-permute-start(f32[160,512]{1,0:T(8,128)S(1)} %get-tuple-element.243), channel_id=1, source_target_pairs={{0,1},{1,2},{2,3},{3,4},{4,5},{5,6},{6,7},{7,8},{8,9},{9,10},{10,1... | collective-permute-start | bytes 983048 | tf_op jit(solution)/shard_map/while/body/eval_jaxpr/ppermute | solution.py:10
  74.7 9.2 %collective-permute-start = (f32[160,512]{1,0:T(8,128)S(1)}, f32[160,512]{1,0:T(8,128)S(1)}, u32[]{:S(2)}, u32[]{:S(2)}) collective-permute-start(f32[160,512]{1,0:T(8,128)S(1)} %get-tuple-element.243), channel_id=1, source_target_pairs={{0,1},{1,2},{2,3},{3,4},{4,5},{5,6},{6,7},{7,8},{8,9},{9,10},{10,1... | collective-permute-start | bytes 983048 | tf_op jit(solution)/shard_map/while/body/eval_jaxpr/ppermute | solution.py:10
  88.5 9.2 %collective-permute-start = (f32[160,512]{1,0:T(8,128)S(1)}, f32[160,512]{1,0:T(8,128)S(1)}, u32[]{:S(2)}, u32[]{:S(2)}) collective-permute-start(f32[160,512]{1,0:T(8,128)S(1)} %get-tuple-element.243), channel_id=1, source_target_pairs={{0,1},{1,2},{2,3},{3,4},{4,5},{5,6},{6,7},{7,8},{8,9},{9,10},{10,1... | collective-permute-start | bytes 983048 | tf_op jit(solution)/shard_map/while/body/eval_jaxpr/ppermute | solution.py:10
  102.2 10.8 %collective-permute-start = (f32[160,512]{1,0:T(8,128)S(1)}, f32[160,512]{1,0:T(8,128)S(1)}, u32[]{:S(2)}, u32[]{:S(2)}) collective-permute-start(f32[160,512]{1,0:T(8,128)S(1)} %get-tuple-element.243), channel_id=1, source_target_pairs={{0,1},{1,2},{2,3},{3,4},{4,5},{5,6},{6,7},{7,8},{8,9},{9,10},{10,1... | collective-permute-start | bytes 983048 | tf_op jit(solution)/shard_map/while/body/eval_jaxpr/ppermute | solution.py:10
  117.4 5.9 %collective-permute-start.1 = (f32[64,512]{1,0:T(8,128)S(1)}, f32[64,512]{1,0:T(8,128)S(1)}, u32[]{:S(2)}, u32[]{:S(2)}) collective-permute-start(f32[64,512]{1,0:T(8,128)S(1)} %slice.52), channel_id=1, source_target_pairs={{0,8},{1,9},{2,10},{3,11},{4,12},{5,13},{6,14},{7,15},{8,0},{9,1},... | collective-permute-start | bytes 393224 | tf_op jit(solution)/shard_map/ppermute | solution.py:10
where the time goes:
time: 124 us
  waiting for transfers between devices  81.3 us (66%)
  matrix products  37.3 us (30%)
  other arithmetic  2.95 us (2%)
    ppermute x9, waiting for transfers between devices, passed_along(): return lax.ppermute(value, axis, pairs)  81.3 us
    dot_general x9, matrix products, pair_terms(): lax.dot_general(lefthand, righthand, (((0,), (0,)), ((), ())), precision=...  11.5 us
    dot_general x9, matrix products, pair_terms(): lax.dot_general(feat_mine, feat_theirs, (((0,), (0,)), ((), ())), precisi...  9.34 us
    dot_general x8, matrix products, pair_terms(): lax.dot_general(feat_mine, coupling, (((1,), (0,)), ((), ())), precision=...  9.17 us
    dot_general x9, matrix products, pair_terms(): lax.dot_general(feat_theirs, coupling, (((1,), (1,)), ((), ())), precisio...  7.32 us
  transfers between devices with their start and end apart: 9, of which 9 were waited for; matrix products, arithmetic and copies ran while one was open for 0% of the time, Pallas kernels for 0%

commit v1 on v0

v1 whole, which is shorter than its diff:
```python
import functools

import jax
import jax.numpy as jnp
from jax import lax
from jax.experimental import pallas as pl
from jax.experimental.pallas import tpu as pltpu
from jax.sharding import PartitionSpec as P

LOG2E = 1.4426950408889634
NORM_ROWS = 16


def split2(value):
    high = value.astype(jnp.bfloat16)
    low = (value - high.astype(jnp.float32)).astype(jnp.bfloat16)
    return high, low


def split3(value):
    high = value.astype(jnp.bfloat16).astype(jnp.float32)
    rest = value - high
    mid = rest.astype(jnp.bfloat16).astype(jnp.float32)
    return high, mid, rest - mid


def term_weights(vectors):
    position = lax.broadcasted_iota(jnp.int32, (2 * vectors, 1), 0)
    first = (position == 0) | (position == vectors)
    return jnp.where(first, 0.5, -0.5 / (vectors - 1)).astype(jnp.float32)


def norm_rows(norms, first):
    parts = split3(norms)
    points = norms.shape[1]
    row = lax.broadcasted_iota(jnp.int32, (NORM_ROWS, points), 0)
    at, ones = (0, 3) if first else (3, 0)
    rows = jnp.where((row >= ones) & (row < ones + 3), 1.0, 0.0)
    for place, part in enumerate(parts):
        rows = jnp.where(row == at + place, part, rows)
    return rows


def prepare_mine(mine, width, vectors, dist_ref, pair_ref):
    feat = mine[:width]
    scale = LOG2E / (2.0 * width)
    norms = jnp.sum(feat * feat, axis=0, keepdims=True) * -scale
    scaled = feat * (2.0 * scale)
    high = scaled.astype(jnp.bfloat16).astype(jnp.float32)
    low = scaled - high
    dist = jnp.concatenate([high, low, high, norm_rows(norms, True)], 0)
    dist_ref[...] = dist.T.astype(jnp.bfloat16)
    vecs = mine[width:] * term_weights(vectors)
    high = vecs.astype(jnp.bfloat16).astype(jnp.float32)
    low = vecs - high
    pair_ref[...] = jnp.concatenate([high, low, high], 0).T.astype(jnp.bfloat16)


def prepare_theirs(theirs, width, vectors):
    feat = theirs[:width]
    scale = LOG2E / (2.0 * width)
    points = feat.shape[1]
    norms = jnp.sum(feat * feat, axis=0, keepdims=True) * -scale
    high, low = split2(feat)
    norms = norm_rows(norms, False).astype(jnp.bfloat16)
    dist = jnp.concatenate([high, high, low, norms], 0)
    vecs = jnp.concatenate([theirs[width + vectors :], theirs[width : width + vectors]], 0)
    vec_high, vec_low = split2(vecs)
    pair = jnp.concatenate([vec_high, vec_high, vec_low], 0)
    pull = jnp.concatenate([high, low, jnp.ones((2 * width, points), jnp.bfloat16)], 0)
    return dist, pair, pull


def kernel(width, vectors, chunk, mine_ref, theirs_ref, out_ref, dist_ref, pair_ref, acc_ref):
    step = pl.program_id(0)

    @pl.when(step == 0)
    def _():
        prepare_mine(mine_ref[...], width, vectors, dist_ref, pair_ref)
        acc_ref[...] = jnp.zeros_like(acc_ref)

    dist, pair, pull = prepare_theirs(theirs_ref[0], width, vectors)
    points = mine_ref.shape[1]
    for start in range(0, points, chunk):
        rows = pl.ds(start, chunk)
        power = jnp.dot(dist_ref[rows], dist, preferred_element_type=jnp.float32)
        bilinear = jnp.dot(pair_ref[rows], pair, preferred_element_type=jnp.float32)
        coupling = jnp.exp2(power) * bilinear
        high, low = split2(coupling)
        across = (((1,), (1,)), ((), ()))
        acc_ref[rows] += lax.dot_general(
            high, pull, across, preferred_element_type=jnp.float32
        ) + lax.dot_general(low, pull, across, preferred_element_type=jnp.float32)

    @pl.when(step == pl.num_programs(0) - 1)
    def _():
        total = acc_ref[...].T
        pulled = total[:width] + total[width : 2 * width]
        sums = total[2 * width : 2 * width + 1]
        out_ref[...] = -(mine_ref[:width] * sums - pulled) / width


def pair_terms(mine, gathered, width, vectors):
    points = mine.shape[1]
    depth = mine.shape[0]
    blocks = gathered.shape[0]
    pairs = points * points * blocks
    return pl.pallas_call(
        functools.partial(kernel, width, vectors, min(256, points)),
        grid=(blocks,),
        in_specs=[
            pl.BlockSpec((depth, points), lambda b: (0, 0)),
            pl.BlockSpec((1, depth, points), lambda b: (b, 0, 0)),
        ],
        out_specs=pl.BlockSpec((width, points), lambda b: (0, 0)),
        out_shape=jax.ShapeDtypeStruct((width, points), jnp.float32),
        scratch_shapes=[
            pltpu.VMEM((points, 3 * width + NORM_ROWS), jnp.bfloat16),
            pltpu.VMEM((points, 6 * vectors), jnp.bfloat16),
            pltpu.VMEM((points, 4 * width), jnp.float32),
        ],
        compiler_params=pltpu.CompilerParams(vmem_limit_bytes=32 << 20),
        cost_estimate=pl.CostEstimate(
            flops=2 * pairs * 1024, bytes_accessed=4 * depth * points * blocks, transcendentals=pairs
        ),
    )(mine, gathered)


def local(features, solves, probes):
    width = features.shape[0]
    vectors = solves.shape[0]
    mine = jnp.concatenate([features, solves, probes], 0)
    gathered = lax.all_gather(mine, "blk")
    return pair_terms(mine, gathered, width, vectors)


def solution(mesh):
    in_specs = (P(None, ("groups", "blk")), P(None, ("groups", "blk")), P(None, ("groups", "blk")))
    out_specs = P(None, ("groups", "blk"))
    return jax.shard_map(local, mesh=mesh, in_specs=in_specs, out_specs=out_specs, check_vma=False)
```

time: 124 us -> 82.4 us (0.66)
  matrix products: 37.3 us -> 0 us
  waiting for transfers between devices: 81.3 us -> 48.1 us
  Pallas kernels: 0 us -> 14.7 us
  between operations: 0.08 us -> 13.4 us
  local copies, waits for them, and re-layouts: 0.9 us -> 5.92 us
  other arithmetic: 2.95 us -> 0 us
    ppermute x9 -> x0, waiting for transfers between devices: 81.3 us -> none  [passed_along(): return lax.ppermute(value, axis, pairs)]
    all_gather x0 -> x1, waiting for transfers between devices: none -> 48 us  [local(): gathered = lax.all_gather(mine, 'blk')]
    dot_general x35 -> x0, matrix products: 37.3 us -> none  [the longest x9 11.5 us: pair_terms(): lax.dot_general(lefthand, righthand, (((0,), (0,)), ((), ())), precision=...]
    pallas_call x0 -> x1, Pallas kernels: none -> 14.7 us  [pair_terms(): pl.pallas_call(functools.partial(kernel, width, vectors, min(256, points)...]
    unnamed x6 -> x8, local copies, waits for them, and re-layouts: 0.69 us -> 5.16 us
  transfers between devices with their start and end apart: 9 -> 1, of which waited for: 9 -> 1; matrix products, arithmetic and copies ran while one was open for 0% -> 0% of each run, Pallas kernels for 0% -> 0%
where the time goes in v1:
time: 82.4 us; the launch traced here: 82.1 us
  waiting for transfers between devices  48.1 us (58%)
  Pallas kernels  14.7 us (18%)
  between operations  13.4 us (16%)
  local copies, waits for them, and re-layouts  5.92 us (7%)
    all_gather x1, waiting for transfers between devices, local(): gathered = lax.all_gather(mine, 'blk')  48 us
    pallas_call x1, Pallas kernels, pair_terms(): pl.pallas_call(functools.partial(kernel, width, vectors, min(256, points)...  14.7 us
    unnamed x8, local copies, waits for them, and re-layouts  5.16 us
  transfers between devices with their start and end apart: 1, of which 1 were waited for; matrix products, arithmetic and copies ran while one was open for 0% of the time, Pallas kernels for 0%

profile of v1, /device:TPU:0, one launch (start us, length us, event | category | flops | bytes accessed | tf_op | source)
XLA Modules:
  0.0 82.1 jit_solution(17745627322101037686)
XLA Ops:
  6.5 0.0 all-gather.3.cloned.1.call-start
  6.5 0.9 %constant_dynamic-update-slice_fusion.2 = f32[96,512]{1,0:T(8,128)S(1)} fusion(f32[64,512]{1,0:T(8,128)} %param.3), kind=kLoop, calls=%fused_computation.2 | loop fusion | bytes 262144
  7.5 0.8 constant_dynamic-update-slice_fusion.1
  8.2 0.8 constant_dynamic-update-slice_fusion.mine_ref
  9.0 0.0 copy-start
  9.0 0.7 copy-done
  9.7 0.0 all-gather.3.cloned.1.call-update
  9.7 48.0 %all-gather.3.cloned.1.call-done = f32[1536,512]{1,0:T(8,128)} async-done(((f32[96,512]{1,0:T(8,128)}), f32[1536,512]{1,0:T(8,128)}) %all-gather.3.cloned.1.call-update) | async-done | bytes 3145744 | tf_op jit(solution)/shard_map/all_gather | solution.py:133
  57.7 0.0 copy-start.1
  57.7 0.9 %copy-done.1 = f32[96,512]{1,0:T(8,128)S(1)} copy-done((f32[96,512]{1,0:T(8,128)S(1)}, f32[96,512]{1,0:T(8,128)}, u32[]{:S(2)}) %copy-start.1) | copy-done | bytes 196632
  58.7 0.0 copy-start.2
  58.7 1.9 %copy-done.2 = f32[1536,512]{1,0:T(8,128)S(1)} copy-done((f32[1536,512]{1,0:T(8,128)S(1)}, f32[1536,512]{1,0:T(8,128)}, u32[]{:S(2)}) %copy-start.2) | copy-done | bytes 3145752
  60.5 14.7 %shard_map.37 = f32[64,512]{1,0:T(8,128)} custom-call(f32[96,512]{1,0:T(8,128)S(1)} %copy-done.1, f32[16,96,512]{2,1,0:T(8,128)S(1)} %bitcast.1), custom_call_target="tpu_custom_call" | custom-call | flops 8589934592 | bytes 3145728 | tf_op jit(solution)/shard_map/pallas_call | solution.py:108
Async XLA Ops:
  6.5 51.2 %all-gather.3.cloned.1.call-start = ((), (), s32[]{:S(2)}) async-start(), calls=%async_computation | async-start | bytes 3342336 | tf_op jit(solution)/shard_map/all_gather | solution.py:133
  9.0 0.7 copy-start
  57.7 0.9 %copy-start.1 = (f32[96,512]{1,0:T(8,128)S(1)}, f32[96,512]{1,0:T(8,128)}, u32[]{:S(2)}) copy-start(f32[96,512]{1,0:T(8,128)} %copy-done) | copy-start | bytes 589828
  58.7 1.9 %copy-start.2 = (f32[1536,512]{1,0:T(8,128)S(1)}, f32[1536,512]{1,0:T(8,128)}, u32[]{:S(2)}) copy-start(f32[1536,512]{1,0:T(8,128)} %all-gather.3.cloned.1.call-done) | copy-start | bytes 9437188
Sparse Core Ops, SparseCore 0:
  9.8 47.8 all-gather.2

commit v2 on v1

v2 whole, which is shorter than its diff:
```python
import functools

import jax
import jax.numpy as jnp
from jax import lax
from jax.experimental import pallas as pl
from jax.experimental.pallas import tpu as pltpu
from jax.sharding import PartitionSpec as P

LOG2E = 1.4426950408889634
NORM_ROWS = 16
VMEM_LIMIT = 40 << 20


def swapped(value, axis, bit):
    count = lax.axis_size(axis)
    return lax.ppermute(value, axis, [(source, source ^ bit) for source in range(count)])


def split2(value):
    high = value.astype(jnp.bfloat16)
    low = (value - high.astype(jnp.float32)).astype(jnp.bfloat16)
    return high, low


def term_weights(vectors):
    position = lax.broadcasted_iota(jnp.int32, (2 * vectors, 1), 0)
    first = (position == 0) | (position == vectors)
    return jnp.where(first, 0.5, -0.5 / (vectors - 1)).astype(jnp.float32)


def norm_rows(norms, first):
    high = norms.astype(jnp.bfloat16).astype(jnp.float32)
    rest = norms - high
    mid = rest.astype(jnp.bfloat16).astype(jnp.float32)
    row = lax.broadcasted_iota(jnp.int32, (NORM_ROWS, norms.shape[1]), 0)
    at, ones = (0, 3) if first else (3, 0)
    rows = jnp.where((row >= ones) & (row < ones + 3), 1.0, 0.0)
    for place, part in enumerate((high, mid, rest - mid)):
        rows = jnp.where(row == at + place, part, rows)
    return rows.astype(jnp.bfloat16)


def prepared_rows(block, width, vectors):
    feat = block[:width]
    scale = LOG2E / (2.0 * width)
    norms = jnp.sum(feat * feat, axis=0, keepdims=True) * -scale
    high, low = split2(feat * (2.0 * scale))
    dist = jnp.concatenate([high, low, high, norm_rows(norms, True)], 0)
    high, low = split2(block[width:] * term_weights(vectors))
    pair = jnp.concatenate([high, low, high], 0)
    return dist.T, pair.T


def prepared_columns(block, width, vectors):
    feat = block[:width]
    scale = LOG2E / (2.0 * width)
    norms = jnp.sum(feat * feat, axis=0, keepdims=True) * -scale
    high, low = split2(feat)
    dist = jnp.concatenate([high, high, low, norm_rows(norms, False)], 0)
    vecs = jnp.concatenate([block[width + vectors :], block[width : width + vectors]], 0)
    vec_high, vec_low = split2(vecs)
    pair = jnp.concatenate([vec_high, vec_high, vec_low], 0)
    ones = jnp.ones((2 * width, block.shape[1]), jnp.bfloat16)
    pull = jnp.concatenate([high, low, ones], 0)
    return dist, pair, pull


def block_terms(dist_rows, pair_rows, columns):
    across = (((1,), (1,)), ((), ()))
    total = None
    for dist, pair, pull in columns:
        power = jnp.dot(dist_rows, dist, preferred_element_type=jnp.float32)
        bilinear = jnp.dot(pair_rows, pair, preferred_element_type=jnp.float32)
        high, low = split2(jnp.exp2(power) * bilinear)
        for half in (high, low):
            term = lax.dot_general(half, pull, across, preferred_element_type=jnp.float32)
            total = term if total is None else total + term
    return total


def kernel(width, vectors, chunk, rows, columns, fresh, started, *refs):
    refs = list(refs)
    take = lambda count: [refs.pop(0) for _ in range(count)]
    row_refs = take(rows)
    column_refs = take(columns)
    ready = [] if fresh else take(2 * rows)
    before = take(rows) if started else []
    out = take(rows)
    made = take(2 * rows) if fresh else ready
    prepared = [prepared_columns(ref[...], width, vectors) for ref in column_refs]
    for place in range(rows):
        dist_ref, pair_ref = made[2 * place : 2 * place + 2]
        if fresh:
            dist_ref[...], pair_ref[...] = prepared_rows(row_refs[place][...], width, vectors)
        points = row_refs[place].shape[1]
        for start in range(0, points, chunk):
            span = pl.ds(start, chunk)
            total = block_terms(dist_ref[span], pair_ref[span], prepared).T
            pulled = total[:width] + total[width : 2 * width]
            sums = total[2 * width : 2 * width + 1]
            value = (pulled - row_refs[place][:width, span] * sums) / width
            if started:
                value += before[place][:, span]
            out[place][:, span] = value


def pair_terms(row_blocks, column_blocks, width, vectors, ready=None, before=None):
    points = row_blocks[0].shape[1]
    rows, columns = len(row_blocks), len(column_blocks)
    fresh, started = ready is None, before is not None
    shape = jax.ShapeDtypeStruct
    out_shape = [shape((width, points), jnp.float32)] * rows
    if fresh:
        out_shape += [
            shape((points, 3 * width + NORM_ROWS), jnp.bfloat16),
            shape((points, 6 * vectors), jnp.bfloat16),
        ] * rows
    operands = list(row_blocks) + list(column_blocks) + (ready or []) + (before or [])
    pairs = points * points * rows * columns
    results = pl.pallas_call(
        functools.partial(
            kernel, width, vectors, min(512, points), rows, columns, fresh, started
        ),
        out_shape=out_shape,
        in_specs=[pl.BlockSpec(memory_space=pltpu.VMEM)] * len(operands),
        out_specs=[pl.BlockSpec(memory_space=pltpu.VMEM)] * len(out_shape),
        compiler_params=pltpu.CompilerParams(vmem_limit_bytes=VMEM_LIMIT),
        cost_estimate=pl.CostEstimate(
            flops=2 * pairs * 1024,
            bytes_accessed=4 * points * 96 * (rows + columns),
            transcendentals=pairs,
        ),
    )(*operands)
    results = list(results)
    return results[:rows], results[rows:] if fresh else ready


def packed(features, solves, probes):
    width, points = features.shape
    vectors = solves.shape[0]

    def body(features_ref, solves_ref, probes_ref, out_ref):
        out_ref[:width] = features_ref[...]
        out_ref[width : width + vectors] = solves_ref[...]
        out_ref[width + vectors :] = probes_ref[...]

    return pl.pallas_call(
        body, out_shape=jax.ShapeDtypeStruct((width + 2 * vectors, points), jnp.float32)
    )(features, solves, probes)


def local(features, solves, probes):
    width = features.shape[0]
    vectors = solves.shape[0]
    count = lax.axis_size("blk")
    terms = functools.partial(pair_terms, width=width, vectors=vectors)
    swap = lambda value, bit: swapped(value, "blk", bit)

    mine = packed(features, solves, probes)
    sibling = swap(mine, 1)
    bits = [bit for bit in (1 << place for place in range(2, count.bit_length())) if bit < count]
    far = swap(mine, bits[-1])
    near = swap(mine, 2)
    direct = {bit: swap(mine, bit) for bit in bits[:-1]}

    here, ready_here = terms([mine, sibling], [mine])
    near, here = lax.optimization_barrier((near, here))
    near_sibling = swap(near, 1)
    there, ready_there = terms([near, near_sibling], [mine])
    far, there = lax.optimization_barrier((far, there))
    columns = [mine, far]
    for bit in reversed(bits[:-1]):
        columns += [direct[bit]] + [swap(block, bit) for block in columns[1:]]
    middle, last = columns[1:-1], columns[-1:]
    for start in range(0, len(middle), 2):
        both, _ = terms(
            [mine, sibling, near, near_sibling],
            middle[start : start + 2],
            ready=ready_here + ready_there,
            before=here + there,
        )
        here, there = both[:2], both[2:]
    there, _ = terms([near, near_sibling], last, ready=ready_there, before=there)
    here, _ = terms([mine, sibling], last, ready=ready_here, before=here)

    toward_near = there[0] + swap(there[1], 1)
    from_near = swap(toward_near, 2)
    return here[0] + swap(here[1], 1) + from_near


def solution(mesh):
    in_specs = (P(None, ("groups", "blk")), P(None, ("groups", "blk")), P(None, ("groups", "blk")))
    out_specs = P(None, ("groups", "blk"))
    return jax.shard_map(local, mesh=mesh, in_specs=in_specs, out_specs=out_specs, check_vma=False)
```

time: 82.4 us -> 40.9 us (0.50)
  waiting for transfers between devices: 48.1 us -> 13.3 us
  between operations: 13.4 us -> 0.06 us
  starting transfers between devices: 0.01 us -> 10.3 us
  local copies, waits for them, and re-layouts: 5.92 us -> 0 us
  Pallas kernels: 14.7 us -> 16.4 us
    all_gather x1 -> x0, waiting for transfers between devices: 48 us -> none  [local(): gathered = lax.all_gather(mine, 'blk')]
    ppermute x0 -> x9, waiting for transfers between devices: none -> 13.3 us  [swapped(): lax.ppermute(value, axis, [(source, source ^ bit) for source in range(cou...]
    ppermute x0 -> x9, starting transfers between devices: none -> 10.3 us  [swapped(): lax.ppermute(value, axis, [(source, source ^ bit) for source in range(cou...]
    unnamed x8 -> x0, local copies, waits for them, and re-layouts: 5.16 us -> none
    pallas_call x1 -> x6, Pallas kernels: 14.7 us -> 16.4 us  [the longest x5 14.8 us: pair_terms(): pl.pallas_call(functools.partial(kernel, width, vectors, min(512, points)...]
  transfers between devices with their start and end apart: 1 -> 9, of which waited for: 1 -> 4; matrix products, arithmetic and copies ran while one was open for 0% -> 0% of each run, Pallas kernels for 0% -> 33%
where the time goes in v2:
time: 40.9 us; the launch traced here: 40.7 us
  Pallas kernels  16.4 us (40%)
  waiting for transfers between devices  13.3 us (33%)
  starting transfers between devices  10.3 us (25%)
  other arithmetic  0.7 us (2%)
    pallas_call x5, Pallas kernels, pair_terms(): pl.pallas_call(functools.partial(kernel, width, vectors, min(512, points)...  14.8 us
    ppermute x9, waiting for transfers between devices, swapped(): lax.ppermute(value, axis, [(source, source ^ bit) for source in range(cou...  13.3 us
    ppermute x9, starting transfers between devices, swapped(): lax.ppermute(value, axis, [(source, source ^ bit) for source in range(cou...  10.3 us
    pallas_call x1, Pallas kernels, packed(): pl.pallas_call(body, out_shape=jax.ShapeDtypeStruct((width + 2 * vectors,...  1.62 us
  transfers between devices with their start and end apart: 9, of which 4 were waited for; matrix products, arithmetic and copies ran while one was open for 0% of the time, Pallas kernels for 33%

profile of v2, /device:TPU:0, one launch (start us, length us, event | category | flops | bytes accessed | tf_op | source)
XLA Modules:
  0.0 40.7 jit_solution(11992747568899240310)
XLA Ops:
  0.0 1.6 %shard_map.37.refs_0_.refs_2_ = f32[96,512]{1,0:T(8,128)} custom-call(f32[64,512]{1,0:T(8,128)} %features_ref.1, f32[16,512]{1,0:T(8,128)} %solves_ref.1, f32[16,512]{1,0:T(8,128)} %probes_ref.1), custom_call_target="tpu_custom_call" | custom-call | tf_op jit(solution)/shard_map/pallas_call | solution.py:148
  1.6 0.5 %collective-permute-start = (f32[96,512]{1,0:T(8,128)}, f32[96,512]{1,0:T(8,128)S(1)}, u32[]{:S(2)}, u32[]{:S(2)}) collective-permute-start(f32[96,512]{1,0:T(8,128)} %shard_map.37.refs_0_.refs_2_), channel_id=1, source_target_pairs={{0,1},{1,0},{2,3},{3,2},{4,5},{5,4},{6,7},{7,6},{8,9},{9,8},{10,11... | collective-permute-start | bytes 589832 | tf_op jit(solution)/shard_map/ppermute | solution.py:17
  2.1 2.5 %collective-permute-start.2 = (f32[96,512]{1,0:T(8,128)}, f32[96,512]{1,0:T(8,128)S(1)}, u32[]{:S(2)}, u32[]{:S(2)}) collective-permute-start(f32[96,512]{1,0:T(8,128)} %shard_map.37.refs_0_.refs_2_), channel_id=1, source_target_pairs={{0,2},{1,3},{2,0},{3,1},{4,6},{5,7},{6,4},{7,5},{8,10},{9,11},{10,... | collective-permute-start | bytes 589832 | tf_op jit(solution)/shard_map/ppermute | solution.py:17
  4.6 0.0 collective-permute-done.refs_1_
  4.6 2.6 %shard_map.38 = (f32[64,512]{1,0:T(8,128)S(1)}, f32[64,512]{1,0:T(8,128)S(1)}, bf16[512,208]{1,0:T(8,128)(2,1)S(1)}, bf16[512,96]{1,0:T(8,128)(2,1)S(1)}, bf16[5...) custom-call(f32[96,512]{1,0:T(8,128)} %shard_map.37.refs_0_.refs_2_, f32[96,512]{1,0:T(8,128)S(1)} %collective-permute-done.refs_1_, ...), custom_call_target="tpu_custom_call" | custom-call | flops 1073741824 | bytes 589824 | tf_op jit(solution)/shard_map/pallas_call | solution.py:121
  7.2 3.2 %collective-permute-done.2.refs_0_.refs_2_ = f32[96,512]{1,0:T(8,128)S(1)} collective-permute-done((f32[96,512]{1,0:T(8,128)}, f32[96,512]{1,0:T(8,128)S(1)}, u32[]{:S(2)}, u32[]{:S(2)}) %collective-permute-start.2) | collective-permute-done | bytes 196640 | tf_op jit(solution)/shard_map/ppermute | solution.py:17
  10.4 0.0 collective-permute-start.3
  10.4 2.8 %collective-permute-start.1 = (f32[96,512]{1,0:T(8,128)}, f32[96,512]{1,0:T(8,128)S(1)}, u32[]{:S(2)}, u32[]{:S(2)}) collective-permute-start(f32[96,512]{1,0:T(8,128)} %shard_map.37.refs_0_.refs_2_), channel_id=1, source_target_pairs={{0,8},{1,9},{2,10},{3,11},{4,12},{5,13},{6,14},{7,15},{8,0},{9,1},... | collective-permute-start | bytes 589832 | tf_op jit(solution)/shard_map/ppermute | solution.py:17
  13.2 1.6 %collective-permute-start.5 = (f32[96,512]{1,0:T(8,128)}, f32[96,512]{1,0:T(8,128)S(1)}, u32[]{:S(2)}, u32[]{:S(2)}) collective-permute-start(f32[96,512]{1,0:T(8,128)} %shard_map.37.refs_0_.refs_2_), channel_id=1, source_target_pairs={{0,4},{1,5},{2,6},{3,7},{4,0},{5,1},{6,2},{7,3},{8,12},{9,13},{10,... | collective-permute-start | bytes 589832 | tf_op jit(solution)/shard_map/ppermute | solution.py:17
  14.8 0.0 collective-permute-done.3.refs_1_.refs_3_
  14.8 2.5 %shard_map.39 = (f32[64,512]{1,0:T(8,128)S(1)}, f32[64,512]{1,0:T(8,128)S(1)}, bf16[512,208]{1,0:T(8,128)(2,1)S(1)}, bf16[512,96]{1,0:T(8,128)(2,1)S(1)}, bf16[5...) custom-call(f32[96,512]{1,0:T(8,128)S(1)} %collective-permute-done.2.refs_0_.refs_2_, ...), custom_call_target="tpu_custom_call" | custom-call | flops 1073741824 | bytes 589824 | tf_op jit(solution)/shard_map/pallas_call | solution.py:121
  17.3 6.0 %collective-permute-done.1.refs_4_ = f32[96,512]{1,0:T(8,128)S(1)} collective-permute-done((f32[96,512]{1,0:T(8,128)}, f32[96,512]{1,0:T(8,128)S(1)}, u32[]{:S(2)}, u32[]{:S(2)}) %collective-permute-start.1) | collective-permute-done | bytes 196640 | tf_op jit(solution)/shard_map/ppermute | solution.py:17
  23.3 0.7 %collective-permute-start.4 = (f32[96,512]{1,0:T(8,128)S(1)}, f32[96,512]{1,0:T(8,128)S(1)}, u32[]{:S(2)}, u32[]{:S(2)}) collective-permute-start(f32[96,512]{1,0:T(8,128)S(1)} %collective-permute-done.1.refs_4_), channel_id=1, source_target_pairs={{0,4},{1,5},{2,6},{3,7},{4,0},{5,1},{6,2},{7,3},{8,12},{9,13},{10,... | collective-permute-start | bytes 589832 | tf_op jit(solution)/shard_map/ppermute | solution.py:17
  24.0 0.0 collective-permute-done.5.refs_5_
  24.0 5.7 %shard_map.40 = (f32[64,512]{1,0:T(8,128)S(1)}, f32[64,512]{1,0:T(8,128)S(1)}, f32[64,512]{1,0:T(8,128)S(1)}, f32[64,512]{1,0:T(8,128)S(1)}) custom-call(f32[96,512]{1,0:T(8,128)} %shard_map.37.refs_0_.refs_2_, f32[96,512]{1,0:T(8,128)S(1)} %collective-permute-done.refs_1_, f32[96,512]{1,0:T(8,128)S(1)} %collective-permute-done.2.refs_0_.refs_2_, ...), custom_call_target="tpu_custom_call" | custom-call | flops 4294967296 | bytes 1179648 | tf_op jit(solution)/shard_map/pallas_call | solution.py:121
  29.7 0.1 collective-permute-done.4.refs_2_
  29.9 1.5 %shard_map.42 = (f32[64,512]{1,0:T(8,128)S(1)}, f32[64,512]{1,0:T(8,128)S(1)}) custom-call(f32[96,512]{1,0:T(8,128)S(1)} %collective-permute-done.2.refs_0_.refs_2_, f32[96,512]{1,0:T(8,128)S(1)} %collective-permute-done.3.refs_1_.refs_3_, f32[96,512]{1,0:T(8,128)S(1)} %collective-permute-done.4.refs_2_, ...), custom_call_target="tpu_custom_call" | custom-call | flops 1073741824 | bytes 589824 | tf_op jit(solution)/shard_map/pallas_call | solution.py:121
  31.4 0.1 collective-permute-start.7
  31.4 2.4 %shard_map.41 = (f32[64,512]{1,0:T(8,128)S(1)}, f32[64,512]{1,0:T(8,128)S(1)}) custom-call(f32[96,512]{1,0:T(8,128)} %shard_map.37.refs_0_.refs_2_, f32[96,512]{1,0:T(8,128)S(1)} %collective-permute-done.refs_1_, f32[96,512]{1,0:T(8,128)S(1)} %collective-permute-done.4.refs_2_, bf16[512,208]{1,0:T(8,128)(2,1)S(1)} %get-tuple-element.37.refs_6_.refs_3_, ...), custom_call_target="tpu_custom_call" | custom-call | flops 1073741824 | bytes 589824 | tf_op jit(solution)/shard_map/pallas_call | solution.py:121
  33.9 0.6 %collective-permute-start.6 = (f32[64,512]{1,0:T(8,128)S(1)}, f32[64,512]{1,0:T(8,128)S(1)}, u32[]{:S(2)}, u32[]{:S(2)}) collective-permute-start(f32[64,512]{1,0:T(8,128)S(1)} %get-tuple-element.52), channel_id=1, source_target_pairs={{0,1},{1,0},{2,3},{3,2},{4,5},{5,4},{6,7},{7,6},{8,9},{9,8},{10,11... | collective-permute-start | bytes 393224 | tf_op jit(solution)/shard_map/ppermute | solution.py:17
  34.5 0.0 collective-permute-done.7
  34.5 1.5 %collective-permute-start.8 = (f32[64,512]{1,0:T(8,128)S(1)}, f32[64,512]{1,0:T(8,128)S(1)}, u32[]{:S(2)}, u32[]{:S(2)}) collective-permute-start(f32[64,512]{1,0:T(8,128)S(1)} %add.10), channel_id=1, source_target_pairs={{0,2},{1,3},{2,0},{3,1},{4,6},{5,7},{6,4},{7,5},{8,10},{9,11},{10,... | collective-permute-start | bytes 393224 | tf_op jit(solution)/shard_map/ppermute | solution.py:17
  36.0 0.0 collective-permute-done.6
  36.0 3.9 %collective-permute-done.8 = f32[64,512]{1,0:T(8,128)S(1)} collective-permute-done((f32[64,512]{1,0:T(8,128)S(1)}, f32[64,512]{1,0:T(8,128)S(1)}, u32[]{:S(2)}, u32[]{:S(2)}) %collective-permute-start.8) | collective-permute-done | bytes 131104 | tf_op jit(solution)/shard_map/ppermute | solution.py:17
  40.0 0.7 %add_add_fusion = f32[64,512]{1,0:T(8,128)} fusion(f32[64,512]{1,0:T(8,128)S(1)} %collective-permute-done.8, f32[64,512]{1,0:T(8,128)S(1)} %get-tuple-element.51, f32[64,512]{1,0:T(8,128)S(1)} %collective-permute-done.6), kind=kLoop, calls=%fused_computation | loop fusion | flops 65536 | bytes 524288 | tf_op jit(solution)/shard_map/add | solution.py:189
  (1 shorter events, 0.0 us)
Async XLA Ops:
  1.6 3.0 %collective-permute-start = (f32[96,512]{1,0:T(8,128)}, f32[96,512]{1,0:T(8,128)S(1)}, u32[]{:S(2)}, u32[]{:S(2)}) collective-permute-start(f32[96,512]{1,0:T(8,128)} %shard_map.37.refs_0_.refs_2_), channel_id=1, source_target_pairs={{0,1},{1,0},{2,3},{3,2},{4,5},{5,4},{6,7},{7,6},{8,9},{9,8},{10,11... | collective-permute-start | bytes 589832 | tf_op jit(solution)/shard_map/ppermute | solution.py:17
  2.1 8.3 %collective-permute-start.2 = (f32[96,512]{1,0:T(8,128)}, f32[96,512]{1,0:T(8,128)S(1)}, u32[]{:S(2)}, u32[]{:S(2)}) collective-permute-start(f32[96,512]{1,0:T(8,128)} %shard_map.37.refs_0_.refs_2_), channel_id=1, source_target_pairs={{0,2},{1,3},{2,0},{3,1},{4,6},{5,7},{6,4},{7,5},{8,10},{9,11},{10,... | collective-permute-start | bytes 589832 | tf_op jit(solution)/shard_map/ppermute | solution.py:17
  10.4 4.4 %collective-permute-start.3 = (f32[96,512]{1,0:T(8,128)S(1)}, f32[96,512]{1,0:T(8,128)S(1)}, u32[]{:S(2)}, u32[]{:S(2)}) collective-permute-start(f32[96,512]{1,0:T(8,128)S(1)} %collective-permute-done.2.refs_0_.refs_2_), channel_id=1, source_target_pairs={{0,1},{1,0},{2,3},{3,2},{4,5},{5,4},{6,7},{7,6},{8,9},{9,8},{10,11... | collective-permute-start | bytes 589832 | tf_op jit(solution)/shard_map/ppermute | solution.py:17
  10.4 12.9 %collective-permute-start.1 = (f32[96,512]{1,0:T(8,128)}, f32[96,512]{1,0:T(8,128)S(1)}, u32[]{:S(2)}, u32[]{:S(2)}) collective-permute-start(f32[96,512]{1,0:T(8,128)} %shard_map.37.refs_0_.refs_2_), channel_id=1, source_target_pairs={{0,8},{1,9},{2,10},{3,11},{4,12},{5,13},{6,14},{7,15},{8,0},{9,1},... | collective-permute-start | bytes 589832 | tf_op jit(solution)/shard_map/ppermute | solution.py:17
  13.2 10.8 %collective-permute-start.5 = (f32[96,512]{1,0:T(8,128)}, f32[96,512]{1,0:T(8,128)S(1)}, u32[]{:S(2)}, u32[]{:S(2)}) collective-permute-start(f32[96,512]{1,0:T(8,128)} %shard_map.37.refs_0_.refs_2_), channel_id=1, source_target_pairs={{0,4},{1,5},{2,6},{3,7},{4,0},{5,1},{6,2},{7,3},{8,12},{9,13},{10,... | collective-permute-start | bytes 589832 | tf_op jit(solution)/shard_map/ppermute | solution.py:17
  23.3 6.6 %collective-permute-start.4 = (f32[96,512]{1,0:T(8,128)S(1)}, f32[96,512]{1,0:T(8,128)S(1)}, u32[]{:S(2)}, u32[]{:S(2)}) collective-permute-start(f32[96,512]{1,0:T(8,128)S(1)} %collective-permute-done.1.refs_4_), channel_id=1, source_target_pairs={{0,4},{1,5},{2,6},{3,7},{4,0},{5,1},{6,2},{7,3},{8,12},{9,13},{10,... | collective-permute-start | bytes 589832 | tf_op jit(solution)/shard_map/ppermute | solution.py:17
  31.4 3.1 %collective-permute-start.7 = (f32[64,512]{1,0:T(8,128)S(1)}, f32[64,512]{1,0:T(8,128)S(1)}, u32[]{:S(2)}, u32[]{:S(2)}) collective-permute-start(f32[64,512]{1,0:T(8,128)S(1)} %get-tuple-element.56), channel_id=1, source_target_pairs={{0,1},{1,0},{2,3},{3,2},{4,5},{5,4},{6,7},{7,6},{8,9},{9,8},{10,11... | collective-permute-start | bytes 393224 | tf_op jit(solution)/shard_map/ppermute | solution.py:17
  33.9 2.1 %collective-permute-start.6 = (f32[64,512]{1,0:T(8,128)S(1)}, f32[64,512]{1,0:T(8,128)S(1)}, u32[]{:S(2)}, u32[]{:S(2)}) collective-permute-start(f32[64,512]{1,0:T(8,128)S(1)} %get-tuple-element.52), channel_id=1, source_target_pairs={{0,1},{1,0},{2,3},{3,2},{4,5},{5,4},{6,7},{7,6},{8,9},{9,8},{10,11... | collective-permute-start | bytes 393224 | tf_op jit(solution)/shard_map/ppermute | solution.py:17
  34.5 5.5 %collective-permute-start.8 = (f32[64,512]{1,0:T(8,128)S(1)}, f32[64,512]{1,0:T(8,128)S(1)}, u32[]{:S(2)}, u32[]{:S(2)}) collective-permute-start(f32[64,512]{1,0:T(8,128)S(1)} %add.10), channel_id=1, source_target_pairs={{0,2},{1,3},{2,0},{3,1},{4,6},{5,7},{6,4},{7,5},{8,10},{9,11},{10,... | collective-permute-start | bytes 393224 | tf_op jit(solution)/shard_map/ppermute | solution.py:17

commit v3 on v2

--- a/solution.py
+++ b/solution.py
@@ -117,7 +117,6 @@
             shape((points, 6 * vectors), jnp.bfloat16),
         ] * rows
     operands = list(row_blocks) + list(column_blocks) + (ready or []) + (before or [])
-    pairs = points * points * rows * columns
     results = pl.pallas_call(
         functools.partial(
             kernel, width, vectors, min(512, points), rows, columns, fresh, started
@@ -126,11 +125,7 @@
         in_specs=[pl.BlockSpec(memory_space=pltpu.VMEM)] * len(operands),
         out_specs=[pl.BlockSpec(memory_space=pltpu.VMEM)] * len(out_shape),
         compiler_params=pltpu.CompilerParams(vmem_limit_bytes=VMEM_LIMIT),
-        cost_estimate=pl.CostEstimate(
-            flops=2 * pairs * 1024,
-            bytes_accessed=4 * points * 96 * (rows + columns),
-            transcendentals=pairs,
-        ),
+        cost_estimate=pl.CostEstimate(flops=1, bytes_accessed=1, transcendentals=1),
     )(*operands)
     results = list(results)
     return results[:rows], results[rows:] if fresh else ready
@@ -139,14 +134,20 @@
 def packed(features, solves, probes):
     width, points = features.shape
     vectors = solves.shape[0]
-
-    def body(features_ref, solves_ref, probes_ref, out_ref):
-        out_ref[:width] = features_ref[...]
-        out_ref[width : width + vectors] = solves_ref[...]
-        out_ref[width + vectors :] = probes_ref[...]
-
+    half = points // 2
+
+    def body(features_ref, solves_ref, probes_ref, out_ref, first_ref, second_ref):
+        rows = ((0, features_ref), (width, solves_ref), (width + vectors, probes_ref))
+        for start, ref in rows:
+            span = pl.ds(start, ref.shape[0])
+            out_ref[span] = ref[...]
+            first_ref[span] = ref[:, :half]
+            second_ref[span] = ref[:, half:]
+
+    depth = width + 2 * vectors
     return pl.pallas_call(
-        body, out_shape=jax.ShapeDtypeStruct((width + 2 * vectors, points), jnp.float32)
+        body,
+        out_shape=[jax.ShapeDtypeStruct((depth, n), jnp.float32) for n in (points, half, half)],
     )(features, solves, probes)
 
 
@@ -156,36 +157,44 @@
     count = lax.axis_size("blk")
     terms = functools.partial(pair_terms, width=width, vectors=vectors)
     swap = lambda value, bit: swapped(value, "blk", bit)
-
-    mine = packed(features, solves, probes)
+    tied = lax.optimization_barrier
+
+    top = count // 2
+    beside = [1 << place for place in range(1, count.bit_length() - 2) if place != 2]
+    mine, first, second = packed(features, solves, probes)
+    far_first = swap(first, top)
+    near = swap(mine, 4)
+    direct = [swap(mine, bit) for bit in beside]
     sibling = swap(mine, 1)
-    bits = [bit for bit in (1 << place for place in range(2, count.bit_length())) if bit < count]
-    far = swap(mine, bits[-1])
-    near = swap(mine, 2)
-    direct = {bit: swap(mine, bit) for bit in bits[:-1]}
+
+    def spread(block):
+        blocks = [block]
+        for bit in beside:
+            blocks += [swap(other, bit) for other in blocks]
+        return blocks
 
     here, ready_here = terms([mine, sibling], [mine])
-    near, here = lax.optimization_barrier((near, here))
+    far_first, here = tied((far_first, here))
+    early = direct + [far_first]
+    here, _ = terms([mine, sibling], early, ready=ready_here, before=here)
+    first_columns = spread(far_first)
+    far_second = swap(second, top)
+    near, here = tied((near, here))
     near_sibling = swap(near, 1)
-    there, ready_there = terms([near, near_sibling], [mine])
-    far, there = lax.optimization_barrier((far, there))
-    columns = [mine, far]
-    for bit in reversed(bits[:-1]):
-        columns += [direct[bit]] + [swap(block, bit) for block in columns[1:]]
-    middle, last = columns[1:-1], columns[-1:]
-    for start in range(0, len(middle), 2):
-        both, _ = terms(
-            [mine, sibling, near, near_sibling],
-            middle[start : start + 2],
-            ready=ready_here + ready_there,
-            before=here + there,
-        )
-        here, there = both[:2], both[2:]
+    there, ready_there = terms([near, near_sibling], [mine] + early)
+    all_rows = [mine, sibling, near, near_sibling]
+    ready = ready_here + ready_there
+    far_second, there = tied((far_second, there))
+    second_columns = spread(far_second)
+    middle = [*first_columns[1:], far_second]
+    both, _ = terms(all_rows, middle, ready=ready, before=here + there)
+    here, there = both[:2], both[2:]
+    last = second_columns[1:]
     there, _ = terms([near, near_sibling], last, ready=ready_there, before=there)
     here, _ = terms([mine, sibling], last, ready=ready_here, before=here)
 
     toward_near = there[0] + swap(there[1], 1)
-    from_near = swap(toward_near, 2)
+    from_near = swap(toward_near, 4)
     return here[0] + swap(here[1], 1) + from_near
 
 

time: 40.9 us -> 36.4 us (0.89)
  waiting for transfers between devices: 13.3 us -> 6.37 us
  starting transfers between devices: 10.3 us -> 15.6 us
  Pallas kernels: 16.4 us -> 12.4 us
  local copies, waits for them, and re-layouts: 0 us -> 1 us
    ppermute x9 -> x11, waiting for transfers between devices: 13.3 us -> 6.37 us  [swapped(): lax.ppermute(value, axis, [(source, source ^ bit) for source in range(cou...]
    ppermute x9 -> x11, starting transfers between devices: 10.3 us -> 15.6 us  [swapped(): lax.ppermute(value, axis, [(source, source ^ bit) for source in range(cou...]
    pallas_call x5 -> x6, Pallas kernels: 14.8 us -> 10.8 us  [pair_terms(): pl.pallas_call(functools.partial(kernel, width, vectors, min(512, points)...]
    unnamed x0 -> x6, local copies, waits for them, and re-layouts: none -> 1 us
  transfers between devices with their start and end apart: 9 -> 11, of which waited for: 4 -> 3; matrix products, arithmetic and copies ran while one was open for 0% -> 0% of each run, Pallas kernels for 33% -> 28%
where the time goes in v3:
time: 36.4 us; the launch traced here: 36.3 us
  starting transfers between devices  15.6 us (43%)
  Pallas kernels  12.4 us (34%)
  waiting for transfers between devices  6.37 us (18%)
  local copies, waits for them, and re-layouts  1 us (3%)
  other arithmetic  0.7 us (2%)
    ppermute x11, starting transfers between devices, swapped(): lax.ppermute(value, axis, [(source, source ^ bit) for source in range(cou...  15.6 us
    pallas_call x6, Pallas kernels, pair_terms(): pl.pallas_call(functools.partial(kernel, width, vectors, min(512, points)...  10.8 us
    ppermute x11, waiting for transfers between devices, swapped(): lax.ppermute(value, axis, [(source, source ^ bit) for source in range(cou...  6.37 us
    pallas_call x1, Pallas kernels, packed(): pl.pallas_call(body, out_shape=[jax.ShapeDtypeStruct((depth, n), jnp.floa...  1.67 us
    unnamed x6, local copies, waits for them, and re-layouts  1 us
  transfers between devices with their start and end apart: 11, of which 3 were waited for; matrix products, arithmetic and copies ran while one was open for 0% of the time, Pallas kernels for 28%

profile of v3, /device:TPU:0, one launch (start us, length us, event | category | flops | bytes accessed | tf_op | source)
XLA Modules:
  0.0 36.3 jit_solution(7879987895562392602)
XLA Ops:
  0.0 1.7 %shard_map.37 = (f32[96,512]{1,0:T(8,128)}, f32[96,256]{1,0:T(8,128)}, f32[96,256]{1,0:T(8,128)}) custom-call(f32[64,512]{1,0:T(8,128)} %features_ref.1, f32[16,512]{1,0:T(8,128)} %solves_ref.1, f32[16,512]{1,0:T(8,128)} %probes_ref.1), custom_call_target="tpu_custom_call" | custom-call | tf_op jit(solution)/shard_map/pallas_call | solution.py:148
  1.7 0.5 %collective-permute-start = (f32[96,512]{1,0:T(8,128)}, f32[96,512]{1,0:T(8,128)S(1)}, u32[]{:S(2)}, u32[]{:S(2)}) collective-permute-start(f32[96,512]{1,0:T(8,128)} %get-tuple-element.39.refs_0_.refs_2_), channel_id=1, source_target_pairs={{0,1},{1,0},{2,3},{3,2},{4,5},{5,4},{6,7},{7,6},{8,9},{9,8},{10,11... | collective-permute-start | bytes 589832 | tf_op jit(solution)/shard_map/ppermute | solution.py:17
  2.1 2.5 %collective-permute-start.3 = (f32[96,512]{1,0:T(8,128)}, f32[96,512]{1,0:T(8,128)S(1)}, u32[]{:S(2)}, u32[]{:S(2)}) collective-permute-start(f32[96,512]{1,0:T(8,128)} %get-tuple-element.39.refs_0_.refs_2_), channel_id=1, source_target_pairs={{0,2},{1,3},{2,0},{3,1},{4,6},{5,7},{6,4},{7,5},{8,10},{9,11},{10,... | collective-permute-start | bytes 589832 | tf_op jit(solution)/shard_map/ppermute | solution.py:17
  4.6 1.6 %collective-permute-start.2 = (f32[96,512]{1,0:T(8,128)}, f32[96,512]{1,0:T(8,128)S(1)}, u32[]{:S(2)}, u32[]{:S(2)}) collective-permute-start(f32[96,512]{1,0:T(8,128)} %get-tuple-element.39.refs_0_.refs_2_), channel_id=1, source_target_pairs={{0,4},{1,5},{2,6},{3,7},{4,0},{5,1},{6,2},{7,3},{8,12},{9,13},{10,... | collective-permute-start | bytes 589832 | tf_op jit(solution)/shard_map/ppermute | solution.py:17
  6.2 2.6 %collective-permute-start.4 = (f32[96,256]{1,0:T(8,128)}, f32[96,256]{1,0:T(8,128)S(1)}, u32[]{:S(2)}, u32[]{:S(2)}) collective-permute-start(f32[96,256]{1,0:T(8,128)} %get-tuple-element.41), channel_id=1, source_target_pairs={{0,8},{1,9},{2,10},{3,11},{4,12},{5,13},{6,14},{7,15},{8,0},{9,1},... | collective-permute-start | bytes 294920 | tf_op jit(solution)/shard_map/ppermute | solution.py:17
  8.8 0.0 collective-permute-done.refs_1_
  8.8 0.0 copy-start
  8.8 0.9 %copy-done = f32[96,512]{1,0:T(8,128)S(1)} copy-done((f32[96,512]{1,0:T(8,128)S(1)}, f32[96,512]{1,0:T(8,128)}, u32[]{:S(2)}) %copy-start) | copy-done | bytes 196632
  9.7 1.6 %shard_map.38 = (f32[64,512]{1,0:T(8,128)S(1)}, f32[64,512]{1,0:T(8,128)S(1)}, bf16[512,208]{1,0:T(8,128)(2,1)S(1)}, bf16[512,96]{1,0:T(8,128)(2,1)S(1)}, bf16[5...) custom-call(f32[96,512]{1,0:T(8,128)S(1)} %copy-done, f32[96,512]{1,0:T(8,128)S(1)} %collective-permute-done.refs_1_, ...), custom_call_target="tpu_custom_call" | custom-call | flops 1 | bytes 1 | tf_op jit(solution)/shard_map/pallas_call | solution.py:120
  11.3 1.9 %collective-permute-done.4.refs_3_.refs_4_ = f32[96,256]{1,0:T(8,128)S(1)} collective-permute-done((f32[96,256]{1,0:T(8,128)}, f32[96,256]{1,0:T(8,128)S(1)}, u32[]{:S(2)}, u32[]{:S(2)}) %collective-permute-start.4) | collective-permute-done | bytes 98336 | tf_op jit(solution)/shard_map/ppermute | solution.py:17
  13.2 0.0 collective-permute-done.3.refs_2_.refs_3_
  13.2 0.0 copy-start.2
  13.2 2.1 %shard_map.39 = (f32[64,512]{1,0:T(8,128)S(1)}, f32[64,512]{1,0:T(8,128)S(1)}) custom-call(f32[96,512]{1,0:T(8,128)S(1)} %copy-done, f32[96,512]{1,0:T(8,128)S(1)} %collective-permute-done.refs_1_, f32[96,512]{1,0:T(8,128)S(1)} %collective-permute-done.3.refs_2_.refs_3_, f32[96,256]{1,0:T(8,128)S(1)} %collective-permute-done.4.refs_3_.refs_4_, ...), custom_call_target="tpu_custom_call" | custom-call | flops 1 | bytes 1 | tf_op jit(solution)/shard_map/pallas_call | solution.py:120
  15.3 0.0 collective-permute-done.2.refs_0_.refs_2_
  15.3 0.1 collective-permute-start.5
  15.4 0.0 copy-done.2
  15.4 3.3 %collective-permute-start.1 = (f32[96,256]{1,0:T(8,128)S(1)}, f32[96,256]{1,0:T(8,128)S(1)}, u32[]{:S(2)}, u32[]{:S(2)}) collective-permute-start(f32[96,256]{1,0:T(8,128)S(1)} %copy-done.2), channel_id=1, source_target_pairs={{0,8},{1,9},{2,10},{3,11},{4,12},{5,13},{6,14},{7,15},{8,0},{9,1},... | collective-permute-start | bytes 294920 | tf_op jit(solution)/shard_map/ppermute | solution.py:17
  18.7 0.5 %collective-permute-start.7 = (f32[96,256]{1,0:T(8,128)S(1)}, f32[96,256]{1,0:T(8,128)S(1)}, u32[]{:S(2)}, u32[]{:S(2)}) collective-permute-start(f32[96,256]{1,0:T(8,128)S(1)} %collective-permute-done.4.refs_3_.refs_4_), channel_id=1, source_target_pairs={{0,2},{1,3},{2,0},{3,1},{4,6},{5,7},{6,4},{7,5},{8,10},{9,11},{10,... | collective-permute-start | bytes 294920 | tf_op jit(solution)/shard_map/ppermute | solution.py:17
  19.2 0.0 collective-permute-done.5.refs_1_.refs_3_
  19.2 3.2 %shard_map.40 = (f32[64,512]{1,0:T(8,128)S(1)}, f32[64,512]{1,0:T(8,128)S(1)}, bf16[512,208]{1,0:T(8,128)(2,1)S(1)}, bf16[512,96]{1,0:T(8,128)(2,1)S(1)}, bf16[5...) custom-call(f32[96,512]{1,0:T(8,128)S(1)} %collective-permute-done.2.refs_0_.refs_2_, ...), custom_call_target="tpu_custom_call" | custom-call | flops 1 | bytes 1 | tf_op jit(solution)/shard_map/pallas_call | solution.py:120
  22.4 0.0 collective-permute-done.1.refs_5_
  22.4 1.6 %collective-permute-start.6 = (f32[96,256]{1,0:T(8,128)S(1)}, f32[96,256]{1,0:T(8,128)S(1)}, u32[]{:S(2)}, u32[]{:S(2)}) collective-permute-start(f32[96,256]{1,0:T(8,128)S(1)} %collective-permute-done.1.refs_5_), channel_id=1, source_target_pairs={{0,2},{1,3},{2,0},{3,1},{4,6},{5,7},{6,4},{7,5},{8,10},{9,11},{10,... | collective-permute-start | bytes 294920 | tf_op jit(solution)/shard_map/ppermute | solution.py:17
  24.0 0.0 collective-permute-done.7.refs_4_
  24.0 2.4 %shard_map.41 = (f32[64,512]{1,0:T(8,128)S(1)}, f32[64,512]{1,0:T(8,128)S(1)}, f32[64,512]{1,0:T(8,128)S(1)}, f32[64,512]{1,0:T(8,128)S(1)}) custom-call(f32[96,512]{1,0:T(8,128)S(1)} %copy-done, f32[96,512]{1,0:T(8,128)S(1)} %collective-permute-done.refs_1_, f32[96,512]{1,0:T(8,128)S(1)} %collective-permute-done.2.refs_0_.refs_2_, ...), custom_call_target="tpu_custom_call" | custom-call | flops 1 | bytes 1 | tf_op jit(solution)/shard_map/pallas_call | solution.py:120
  26.4 0.7 %collective-permute-done.6.refs_2_ = f32[96,256]{1,0:T(8,128)S(1)} collective-permute-done((f32[96,256]{1,0:T(8,128)S(1)}, f32[96,256]{1,0:T(8,128)S(1)}, u32[]{:S(2)}, u32[]{:S(2)}) %collective-permute-start.6) | collective-permute-done | bytes 98336 | tf_op jit(solution)/shard_map/ppermute | solution.py:17
  27.1 0.0 copy-start.1
  27.1 0.8 %shard_map.43 = (f32[64,512]{1,0:T(8,128)S(1)}, f32[64,512]{1,0:T(8,128)S(1)}) custom-call(f32[96,512]{1,0:T(8,128)S(1)} %collective-permute-done.2.refs_0_.refs_2_, f32[96,512]{1,0:T(8,128)S(1)} %collective-permute-done.5.refs_1_.refs_3_, f32[96,256]{1,0:T(8,128)S(1)} %collective-permute-done.6.refs_2_, ...), custom_call_target="tpu_custom_call" | custom-call | flops 1 | bytes 1 | tf_op jit(solution)/shard_map/pallas_call | solution.py:120
  27.9 0.1 collective-permute-start.9
  28.0 0.1 copy-done.1
  28.0 0.8 %shard_map.42 = (f32[64,512]{1,0:T(8,128)S(1)}, f32[64,512]{1,0:T(8,128)S(1)}) custom-call(f32[96,512]{1,0:T(8,128)S(1)} %copy-done.1, f32[96,512]{1,0:T(8,128)S(1)} %collective-permute-done.refs_1_, f32[96,256]{1,0:T(8,128)S(1)} %collective-permute-done.6.refs_2_, bf16[512,208]{1,0:T(8,128)(2,1)S(1)} %get-tuple-element.45.refs_4_.refs_6_.refs_3_, ...), custom_call_target="tpu_custom_call" | custom-call | flops 1 | bytes 1 | tf_op jit(solution)/shard_map/pallas_call | solution.py:120
  28.8 0.5 %collective-permute-start.8 = (f32[64,512]{1,0:T(8,128)S(1)}, f32[64,512]{1,0:T(8,128)S(1)}, u32[]{:S(2)}, u32[]{:S(2)}) collective-permute-start(f32[64,512]{1,0:T(8,128)S(1)} %get-tuple-element.68), channel_id=1, source_target_pairs={{0,1},{1,0},{2,3},{3,2},{4,5},{5,4},{6,7},{7,6},{8,9},{9,8},{10,11... | collective-permute-start | bytes 393224 | tf_op jit(solution)/shard_map/ppermute | solution.py:17
  29.3 0.0 collective-permute-done.9
  29.3 2.4 %collective-permute-start.10 = (f32[64,512]{1,0:T(8,128)S(1)}, f32[64,512]{1,0:T(8,128)S(1)}, u32[]{:S(2)}, u32[]{:S(2)}) collective-permute-start(f32[64,512]{1,0:T(8,128)S(1)} %add.10), channel_id=1, source_target_pairs={{0,4},{1,5},{2,6},{3,7},{4,0},{5,1},{6,2},{7,3},{8,12},{9,13},{10,... | collective-permute-start | bytes 393224 | tf_op jit(solution)/shard_map/ppermute | solution.py:17
  31.8 0.0 collective-permute-done.8
  31.8 3.8 %collective-permute-done.10 = f32[64,512]{1,0:T(8,128)S(1)} collective-permute-done((f32[64,512]{1,0:T(8,128)S(1)}, f32[64,512]{1,0:T(8,128)S(1)}, u32[]{:S(2)}, u32[]{:S(2)}) %collective-permute-start.10) | collective-permute-done | bytes 131104 | tf_op jit(solution)/shard_map/ppermute | solution.py:17
  35.6 0.7 %add_add_fusion = f32[64,512]{1,0:T(8,128)} fusion(f32[64,512]{1,0:T(8,128)S(1)} %collective-permute-done.10, f32[64,512]{1,0:T(8,128)S(1)} %get-tuple-element.67, f32[64,512]{1,0:T(8,128)S(1)} %collective-permute-done.8), kind=kLoop, calls=%fused_computation | loop fusion | flops 65536 | bytes 524288 | tf_op jit(solution)/shard_map/add | solution.py:198
  (1 shorter events, 0.0 us)
Async XLA Ops:
  1.7 7.1 %collective-permute-start = (f32[96,512]{1,0:T(8,128)}, f32[96,512]{1,0:T(8,128)S(1)}, u32[]{:S(2)}, u32[]{:S(2)}) collective-permute-start(f32[96,512]{1,0:T(8,128)} %get-tuple-element.39.refs_0_.refs_2_), channel_id=1, source_target_pairs={{0,1},{1,0},{2,3},{3,2},{4,5},{5,4},{6,7},{7,6},{8,9},{9,8},{10,11... | collective-permute-start | bytes 589832 | tf_op jit(solution)/shard_map/ppermute | solution.py:17
  2.1 11.1 %collective-permute-start.3 = (f32[96,512]{1,0:T(8,128)}, f32[96,512]{1,0:T(8,128)S(1)}, u32[]{:S(2)}, u32[]{:S(2)}) collective-permute-start(f32[96,512]{1,0:T(8,128)} %get-tuple-element.39.refs_0_.refs_2_), channel_id=1, source_target_pairs={{0,2},{1,3},{2,0},{3,1},{4,6},{5,7},{6,4},{7,5},{8,10},{9,11},{10,... | collective-permute-start | bytes 589832 | tf_op jit(solution)/shard_map/ppermute | solution.py:17
  4.6 10.6 %collective-permute-start.2 = (f32[96,512]{1,0:T(8,128)}, f32[96,512]{1,0:T(8,128)S(1)}, u32[]{:S(2)}, u32[]{:S(2)}) collective-permute-start(f32[96,512]{1,0:T(8,128)} %get-tuple-element.39.refs_0_.refs_2_), channel_id=1, source_target_pairs={{0,4},{1,5},{2,6},{3,7},{4,0},{5,1},{6,2},{7,3},{8,12},{9,13},{10,... | collective-permute-start | bytes 589832 | tf_op jit(solution)/shard_map/ppermute | solution.py:17
  6.2 7.0 %collective-permute-start.4 = (f32[96,256]{1,0:T(8,128)}, f32[96,256]{1,0:T(8,128)S(1)}, u32[]{:S(2)}, u32[]{:S(2)}) collective-permute-start(f32[96,256]{1,0:T(8,128)} %get-tuple-element.41), channel_id=1, source_target_pairs={{0,8},{1,9},{2,10},{3,11},{4,12},{5,13},{6,14},{7,15},{8,0},{9,1},... | collective-permute-start | bytes 294920 | tf_op jit(solution)/shard_map/ppermute | solution.py:17
  8.8 0.9 %copy-start = (f32[96,512]{1,0:T(8,128)S(1)}, f32[96,512]{1,0:T(8,128)}, u32[]{:S(2)}) copy-start(f32[96,512]{1,0:T(8,128)} %get-tuple-element.39.refs_0_.refs_2_) | copy-start | bytes 589828
  13.2 2.2 %copy-start.2 = (f32[96,256]{1,0:T(8,128)S(1)}, f32[96,256]{1,0:T(8,128)}, u32[]{:S(2)}) copy-start(f32[96,256]{1,0:T(8,128)} %get-tuple-element.40) | copy-start | bytes 294916
  15.3 3.9 %collective-permute-start.5 = (f32[96,512]{1,0:T(8,128)S(1)}, f32[96,512]{1,0:T(8,128)S(1)}, u32[]{:S(2)}, u32[]{:S(2)}) collective-permute-start(f32[96,512]{1,0:T(8,128)S(1)} %collective-permute-done.2.refs_0_.refs_2_), channel_id=1, source_target_pairs={{0,1},{1,0},{2,3},{3,2},{4,5},{5,4},{6,7},{7,6},{8,9},{9,8},{10,11... | collective-permute-start | bytes 589832 | tf_op jit(solution)/shard_map/ppermute | solution.py:17
  15.4 7.0 %collective-permute-start.1 = (f32[96,256]{1,0:T(8,128)S(1)}, f32[96,256]{1,0:T(8,128)S(1)}, u32[]{:S(2)}, u32[]{:S(2)}) collective-permute-start(f32[96,256]{1,0:T(8,128)S(1)} %copy-done.2), channel_id=1, source_target_pairs={{0,8},{1,9},{2,10},{3,11},{4,12},{5,13},{6,14},{7,15},{8,0},{9,1},... | collective-permute-start | bytes 294920 | tf_op jit(solution)/shard_map/ppermute | solution.py:17
  18.7 5.3 %collective-permute-start.7 = (f32[96,256]{1,0:T(8,128)S(1)}, f32[96,256]{1,0:T(8,128)S(1)}, u32[]{:S(2)}, u32[]{:S(2)}) collective-permute-start(f32[96,256]{1,0:T(8,128)S(1)} %collective-permute-done.4.refs_3_.refs_4_), channel_id=1, source_target_pairs={{0,2},{1,3},{2,0},{3,1},{4,6},{5,7},{6,4},{7,5},{8,10},{9,11},{10,... | collective-permute-start | bytes 294920 | tf_op jit(solution)/shard_map/ppermute | solution.py:17
  22.4 4.7 %collective-permute-start.6 = (f32[96,256]{1,0:T(8,128)S(1)}, f32[96,256]{1,0:T(8,128)S(1)}, u32[]{:S(2)}, u32[]{:S(2)}) collective-permute-start(f32[96,256]{1,0:T(8,128)S(1)} %collective-permute-done.1.refs_5_), channel_id=1, source_target_pairs={{0,2},{1,3},{2,0},{3,1},{4,6},{5,7},{6,4},{7,5},{8,10},{9,11},{10,... | collective-permute-start | bytes 294920 | tf_op jit(solution)/shard_map/ppermute | solution.py:17
  27.1 0.9 %copy-start.1 = (f32[96,512]{1,0:T(8,128)S(1)}, f32[96,512]{1,0:T(8,128)}, u32[]{:S(2)}) copy-start(f32[96,512]{1,0:T(8,128)} %get-tuple-element.39.refs_0_.refs_2_) | copy-start | bytes 589828
  27.9 1.4 %collective-permute-start.9 = (f32[64,512]{1,0:T(8,128)S(1)}, f32[64,512]{1,0:T(8,128)S(1)}, u32[]{:S(2)}, u32[]{:S(2)}) collective-permute-start(f32[64,512]{1,0:T(8,128)S(1)} %get-tuple-element.72), channel_id=1, source_target_pairs={{0,1},{1,0},{2,3},{3,2},{4,5},{5,4},{6,7},{7,6},{8,9},{9,8},{10,11... | collective-permute-start | bytes 393224 | tf_op jit(solution)/shard_map/ppermute | solution.py:17
  28.8 3.0 %collective-permute-start.8 = (f32[64,512]{1,0:T(8,128)S(1)}, f32[64,512]{1,0:T(8,128)S(1)}, u32[]{:S(2)}, u32[]{:S(2)}) collective-permute-start(f32[64,512]{1,0:T(8,128)S(1)} %get-tuple-element.68), channel_id=1, source_target_pairs={{0,1},{1,0},{2,3},{3,2},{4,5},{5,4},{6,7},{7,6},{8,9},{9,8},{10,11... | collective-permute-start | bytes 393224 | tf_op jit(solution)/shard_map/ppermute | solution.py:17
  29.3 6.2 %collective-permute-start.10 = (f32[64,512]{1,0:T(8,128)S(1)}, f32[64,512]{1,0:T(8,128)S(1)}, u32[]{:S(2)}, u32[]{:S(2)}) collective-permute-start(f32[64,512]{1,0:T(8,128)S(1)} %add.10), channel_id=1, source_target_pairs={{0,4},{1,5},{2,6},{3,7},{4,0},{5,1},{6,2},{7,3},{8,12},{9,13},{10,... | collective-permute-start | bytes 393224 | tf_op jit(solution)/shard_map/ppermute | solution.py:17

commit v4 on v3

--- a/solution.py
+++ b/solution.py
@@ -9,7 +9,7 @@
 
 LOG2E = 1.4426950408889634
 NORM_ROWS = 16
-VMEM_LIMIT = 40 << 20
+VMEM_LIMIT = 24 << 20
 
 
 def swapped(value, axis, bit):
@@ -134,20 +134,16 @@
 def packed(features, solves, probes):
     width, points = features.shape
     vectors = solves.shape[0]
-    half = points // 2
 
-    def body(features_ref, solves_ref, probes_ref, out_ref, first_ref, second_ref):
-        rows = ((0, features_ref), (width, solves_ref), (width + vectors, probes_ref))
-        for start, ref in rows:
-            span = pl.ds(start, ref.shape[0])
-            out_ref[span] = ref[...]
-            first_ref[span] = ref[:, :half]
-            second_ref[span] = ref[:, half:]
+    def body(features_ref, solves_ref, probes_ref, out_ref):
+        out_ref[:width] = features_ref[...]
+        out_ref[width : width + vectors] = solves_ref[...]
+        out_ref[width + vectors :] = probes_ref[...]
 
-    depth = width + 2 * vectors
     return pl.pallas_call(
         body,
-        out_shape=[jax.ShapeDtypeStruct((depth, n), jnp.float32) for n in (points, half, half)],
+        out_shape=jax.ShapeDtypeStruct((width + 2 * vectors, points), jnp.float32),
+        compiler_params=pltpu.CompilerParams(vmem_limit_bytes=4 << 20),
     )(features, solves, probes)
 
 
@@ -161,8 +157,8 @@
 
     top = count // 2
     beside = [1 << place for place in range(1, count.bit_length() - 2) if place != 2]
-    mine, first, second = packed(features, solves, probes)
-    far_first = swap(first, top)
+    mine = packed(features, solves, probes)
+    far = swap(mine, top)
     near = swap(mine, 4)
     direct = [swap(mine, bit) for bit in beside]
     sibling = swap(mine, 1)
@@ -173,23 +169,16 @@
             blocks += [swap(other, bit) for other in blocks]
         return blocks
 
-    here, ready_here = terms([mine, sibling], [mine])
-    far_first, here = tied((far_first, here))
-    early = direct + [far_first]
-    here, _ = terms([mine, sibling], early, ready=ready_here, before=here)
-    first_columns = spread(far_first)
-    far_second = swap(second, top)
-    near, here = tied((near, here))
+    early = [mine] + direct
+    here, ready_here = terms([mine, sibling], early)
+    far, near, here = tied((far, near, here))
     near_sibling = swap(near, 1)
-    there, ready_there = terms([near, near_sibling], [mine] + early)
-    all_rows = [mine, sibling, near, near_sibling]
-    ready = ready_here + ready_there
-    far_second, there = tied((far_second, there))
-    second_columns = spread(far_second)
-    middle = [*first_columns[1:], far_second]
-    both, _ = terms(all_rows, middle, ready=ready, before=here + there)
-    here, there = both[:2], both[2:]
-    last = second_columns[1:]
+    far_columns = spread(far)
+    here, _ = terms([mine, sibling], [far], ready=ready_here, before=here)
+    near_sibling, here = tied((near_sibling, here))
+    there, ready_there = terms([near, near_sibling], early + [far])
+    last = far_columns[1:]
+    last[0], there = tied((last[0], there))
     there, _ = terms([near, near_sibling], last, ready=ready_there, before=there)
     here, _ = terms([mine, sibling], last, ready=ready_here, before=here)
 

time: 36.4 us -> 35.4 us (0.973)
  starting transfers between devices: 15.6 us -> 9.87 us
  waiting for transfers between devices: 6.37 us -> 11.1 us
  Pallas kernels: 12.4 us -> 10.9 us
  local copies, waits for them, and re-layouts: 1 us -> 2.42 us
    ppermute x11 -> x9, starting transfers between devices: 15.6 us -> 9.87 us  [swapped(): lax.ppermute(value, axis, [(source, source ^ bit) for source in range(cou...]
    ppermute x11 -> x9, waiting for transfers between devices: 6.37 us -> 11.1 us  [swapped(): lax.ppermute(value, axis, [(source, source ^ bit) for source in range(cou...]
    pallas_call x1, Pallas kernels: 1.67 us -> 0.01 us  [packed(): pl.pallas_call(body, out_shape=jax.ShapeDtypeStruct((width + 2 * vectors,...]
    unnamed x6, local copies, waits for them, and re-layouts: 1 us -> 2.42 us
    pallas_call x6 -> x5, Pallas kernels: 10.8 us -> 10.9 us  [pair_terms(): pl.pallas_call(functools.partial(kernel, width, vectors, min(512, points)...]
  transfers between devices with their start and end apart: 11 -> 9, of which waited for: 3 -> 5; matrix products, arithmetic and copies ran while one was open for 0% -> 0% of each run, Pallas kernels for 28% -> 27%
where the time goes in v4:
time: 35.4 us; the launch traced here: 35.1 us
  waiting for transfers between devices  11.1 us (31%)
  Pallas kernels  10.9 us (31%)
  starting transfers between devices  9.87 us (28%)
  local copies, waits for them, and re-layouts  2.42 us (7%)
  other arithmetic  0.7 us (2%)
    ppermute x9, waiting for transfers between devices, swapped(): lax.ppermute(value, axis, [(source, source ^ bit) for source in range(cou...  11.1 us
    pallas_call x5, Pallas kernels, pair_terms(): pl.pallas_call(functools.partial(kernel, width, vectors, min(512, points)...  10.9 us
    ppermute x9, starting transfers between devices, swapped(): lax.ppermute(value, axis, [(source, source ^ bit) for source in range(cou...  9.87 us
    unnamed x6, local copies, waits for them, and re-layouts  2.42 us
  transfers between devices with their start and end apart: 9, of which 5 were waited for; matrix products, arithmetic and copies ran while one was open for 0% of the time, Pallas kernels for 27%

profile of v4, /device:TPU:0, one launch (start us, length us, event | category | flops | bytes accessed | tf_op | source)
XLA Modules:
  0.0 35.1 jit_solution(2544343121681897189)
XLA Ops:
  0.0 0.0 copy-start
  0.0 0.9 %copy-done = f32[64,512]{1,0:T(8,128)S(1)} copy-done((f32[64,512]{1,0:T(8,128)S(1)}, f32[64,512]{1,0:T(8,128)}, u32[]{:S(2)}) %copy-start) | copy-done | bytes 131096
  0.9 0.0 copy-start.1
  0.9 0.8 %copy-done.1 = f32[16,512]{1,0:T(8,128)S(1)} copy-done((f32[16,512]{1,0:T(8,128)S(1)}, f32[16,512]{1,0:T(8,128)}, u32[]{:S(2)}) %copy-start.1) | copy-done | bytes 32792
  1.7 0.0 copy-start.2
  1.7 0.8 %copy-done.2 = f32[16,512]{1,0:T(8,128)S(1)} copy-done((f32[16,512]{1,0:T(8,128)S(1)}, f32[16,512]{1,0:T(8,128)}, u32[]{:S(2)}) %copy-start.2) | copy-done | bytes 32792
  2.4 0.5 %collective-permute-start = (f32[96,512]{1,0:T(8,128)S(1)}, f32[96,512]{1,0:T(8,128)S(1)}, u32[]{:S(2)}, u32[]{:S(2)}) collective-permute-start(f32[96,512]{1,0:T(8,128)S(1)} %shard_map.37.refs_0_.refs_2_), channel_id=1, source_target_pairs={{0,1},{1,0},{2,3},{3,2},{4,5},{5,4},{6,7},{7,6},{8,9},{9,8},{10,11... | collective-permute-start | bytes 589832 | tf_op jit(solution)/shard_map/ppermute | solution.py:17
  3.0 2.6 %collective-permute-start.3 = (f32[96,512]{1,0:T(8,128)S(1)}, f32[96,512]{1,0:T(8,128)S(1)}, u32[]{:S(2)}, u32[]{:S(2)}) collective-permute-start(f32[96,512]{1,0:T(8,128)S(1)} %shard_map.37.refs_0_.refs_2_), channel_id=1, source_target_pairs={{0,2},{1,3},{2,0},{3,1},{4,6},{5,7},{6,4},{7,5},{8,10},{9,11},{10,... | collective-permute-start | bytes 589832 | tf_op jit(solution)/shard_map/ppermute | solution.py:17
  5.6 2.6 %collective-permute-start.1 = (f32[96,512]{1,0:T(8,128)S(1)}, f32[96,512]{1,0:T(8,128)S(1)}, u32[]{:S(2)}, u32[]{:S(2)}) collective-permute-start(f32[96,512]{1,0:T(8,128)S(1)} %shard_map.37.refs_0_.refs_2_), channel_id=1, source_target_pairs={{0,8},{1,9},{2,10},{3,11},{4,12},{5,13},{6,14},{7,15},{8,0},{9,1},... | collective-permute-start | bytes 589832 | tf_op jit(solution)/shard_map/ppermute | solution.py:17
  8.1 1.6 %collective-permute-start.2 = (f32[96,512]{1,0:T(8,128)S(1)}, f32[96,512]{1,0:T(8,128)S(1)}, u32[]{:S(2)}, u32[]{:S(2)}) collective-permute-start(f32[96,512]{1,0:T(8,128)S(1)} %shard_map.37.refs_0_.refs_2_), channel_id=1, source_target_pairs={{0,4},{1,5},{2,6},{3,7},{4,0},{5,1},{6,2},{7,3},{8,12},{9,13},{10,... | collective-permute-start | bytes 589832 | tf_op jit(solution)/shard_map/ppermute | solution.py:17
  9.7 0.0 collective-permute-done.refs_1_
  9.7 1.3 %collective-permute-done.3.refs_3_ = f32[96,512]{1,0:T(8,128)S(1)} collective-permute-done((f32[96,512]{1,0:T(8,128)S(1)}, f32[96,512]{1,0:T(8,128)S(1)}, u32[]{:S(2)}, u32[]{:S(2)}) %collective-permute-start.3) | collective-permute-done | bytes 196640 | tf_op jit(solution)/shard_map/ppermute | solution.py:17
  11.0 2.6 %shard_map.38 = (f32[64,512]{1,0:T(8,128)S(1)}, f32[64,512]{1,0:T(8,128)S(1)}, bf16[512,208]{1,0:T(8,128)(2,1)S(1)}, bf16[512,96]{1,0:T(8,128)(2,1)S(1)}, bf16[5...) custom-call(f32[96,512]{1,0:T(8,128)S(1)} %shard_map.37.refs_0_.refs_2_, f32[96,512]{1,0:T(8,128)S(1)} %collective-permute-done.refs_1_, ...), custom_call_target="tpu_custom_call" | custom-call | flops 1 | bytes 1 | tf_op jit(solution)/shard_map/pallas_call | solution.py:120
  13.7 4.0 %collective-permute-done.1.refs_2_.refs_4_ = f32[96,512]{1,0:T(8,128)S(1)} collective-permute-done((f32[96,512]{1,0:T(8,128)S(1)}, f32[96,512]{1,0:T(8,128)S(1)}, u32[]{:S(2)}, u32[]{:S(2)}) %collective-permute-start.1) | collective-permute-done | bytes 196640 | tf_op jit(solution)/shard_map/ppermute | solution.py:17
  17.7 0.2 collective-permute-done.2.refs_0_
  17.9 0.0 collective-permute-start.5
  17.9 0.5 %collective-permute-start.4 = (f32[96,512]{1,0:T(8,128)S(1)}, f32[96,512]{1,0:T(8,128)S(1)}, u32[]{:S(2)}, u32[]{:S(2)}) collective-permute-start(f32[96,512]{1,0:T(8,128)S(1)} %collective-permute-done.1.refs_2_.refs_4_), channel_id=1, source_target_pairs={{0,2},{1,3},{2,0},{3,1},{4,6},{5,7},{6,4},{7,5},{8,10},{9,11},{10,... | collective-permute-start | bytes 589832 | tf_op jit(solution)/shard_map/ppermute | solution.py:17
  18.4 1.5 %shard_map.39 = (f32[64,512]{1,0:T(8,128)S(1)}, f32[64,512]{1,0:T(8,128)S(1)}) custom-call(f32[96,512]{1,0:T(8,128)S(1)} %shard_map.37.refs_0_.refs_2_, f32[96,512]{1,0:T(8,128)S(1)} %collective-permute-done.refs_1_, f32[96,512]{1,0:T(8,128)S(1)} %collective-permute-done.1.refs_2_.refs_4_, bf16[512,208]{1,0:T(8,128)(2,1)S(1)} %get-tuple-element.37.refs_3_, ...), custom_call_target="tpu_custom_call" | custom-call | flops 1 | bytes 1 | tf_op jit(solution)/shard_map/pallas_call | solution.py:120
  19.9 0.0 collective-permute-done.5.refs_1_
  19.9 3.7 %shard_map.40 = (f32[64,512]{1,0:T(8,128)S(1)}, f32[64,512]{1,0:T(8,128)S(1)}, bf16[512,208]{1,0:T(8,128)(2,1)S(1)}, bf16[512,96]{1,0:T(8,128)(2,1)S(1)}, bf16[5...) custom-call(f32[96,512]{1,0:T(8,128)S(1)} %collective-permute-done.2.refs_0_, ...), custom_call_target="tpu_custom_call" | custom-call | flops 1 | bytes 1 | tf_op jit(solution)/shard_map/pallas_call | solution.py:120
  23.7 1.6 %collective-permute-done.4.refs_2_ = f32[96,512]{1,0:T(8,128)S(1)} collective-permute-done((f32[96,512]{1,0:T(8,128)S(1)}, f32[96,512]{1,0:T(8,128)S(1)}, u32[]{:S(2)}, u32[]{:S(2)}) %collective-permute-start.4) | collective-permute-done | bytes 196640 | tf_op jit(solution)/shard_map/ppermute | solution.py:17
  25.3 1.5 %shard_map.42 = (f32[64,512]{1,0:T(8,128)S(1)}, f32[64,512]{1,0:T(8,128)S(1)}) custom-call(f32[96,512]{1,0:T(8,128)S(1)} %collective-permute-done.2.refs_0_, f32[96,512]{1,0:T(8,128)S(1)} %collective-permute-done.5.refs_1_, f32[96,512]{1,0:T(8,128)S(1)} %collective-permute-done.4.refs_2_, bf16[512,208]{1,0:T(8,128)(2,1)S(1)} %get-tuple-element.53.refs_3_, ...), custom_call_target="tpu_custom_call" | custom-call | flops 1 | bytes 1 | tf_op jit(solution)/shard_map/pallas_call | solution.py:120
  26.8 0.1 collective-permute-start.7
  26.8 1.5 %shard_map.41 = (f32[64,512]{1,0:T(8,128)S(1)}, f32[64,512]{1,0:T(8,128)S(1)}) custom-call(f32[96,512]{1,0:T(8,128)S(1)} %shard_map.37.refs_0_.refs_2_, f32[96,512]{1,0:T(8,128)S(1)} %collective-permute-done.refs_1_, f32[96,512]{1,0:T(8,128)S(1)} %collective-permute-done.4.refs_2_, bf16[512,208]{1,0:T(8,128)(2,1)S(1)} %get-tuple-element.37.refs_3_, ...), custom_call_target="tpu_custom_call" | custom-call | flops 1 | bytes 1 | tf_op jit(solution)/shard_map/pallas_call | solution.py:120
  28.4 0.6 %collective-permute-start.6 = (f32[64,512]{1,0:T(8,128)S(1)}, f32[64,512]{1,0:T(8,128)S(1)}, u32[]{:S(2)}, u32[]{:S(2)}) collective-permute-start(f32[64,512]{1,0:T(8,128)S(1)} %get-tuple-element.52), channel_id=1, source_target_pairs={{0,1},{1,0},{2,3},{3,2},{4,5},{5,4},{6,7},{7,6},{8,9},{9,8},{10,11... | collective-permute-start | bytes 393224 | tf_op jit(solution)/shard_map/ppermute | solution.py:17
  28.9 0.0 collective-permute-done.7
  29.0 1.5 %collective-permute-start.8 = (f32[64,512]{1,0:T(8,128)S(1)}, f32[64,512]{1,0:T(8,128)S(1)}, u32[]{:S(2)}, u32[]{:S(2)}) collective-permute-start(f32[64,512]{1,0:T(8,128)S(1)} %add.10), channel_id=1, source_target_pairs={{0,4},{1,5},{2,6},{3,7},{4,0},{5,1},{6,2},{7,3},{8,12},{9,13},{10,... | collective-permute-start | bytes 393224 | tf_op jit(solution)/shard_map/ppermute | solution.py:17
  30.5 0.0 collective-permute-done.6
  30.5 4.0 %collective-permute-done.8 = f32[64,512]{1,0:T(8,128)S(1)} collective-permute-done((f32[64,512]{1,0:T(8,128)S(1)}, f32[64,512]{1,0:T(8,128)S(1)}, u32[]{:S(2)}, u32[]{:S(2)}) %collective-permute-start.8) | collective-permute-done | bytes 131104 | tf_op jit(solution)/shard_map/ppermute | solution.py:17
  34.4 0.7 %add_add_fusion = f32[64,512]{1,0:T(8,128)} fusion(f32[64,512]{1,0:T(8,128)S(1)} %collective-permute-done.8, f32[64,512]{1,0:T(8,128)S(1)} %get-tuple-element.51, f32[64,512]{1,0:T(8,128)S(1)} %collective-permute-done.6), kind=kLoop, calls=%fused_computation | loop fusion | flops 65536 | bytes 524288 | tf_op jit(solution)/shard_map/add | solution.py:187
  (2 shorter events, 0.0 us)
Async XLA Ops:
  0.0 0.9 %copy-start = (f32[64,512]{1,0:T(8,128)S(1)}, f32[64,512]{1,0:T(8,128)}, u32[]{:S(2)}) copy-start(f32[64,512]{1,0:T(8,128)} %features_ref.1) | copy-start | bytes 393220
  0.9 0.8 %copy-start.1 = (f32[16,512]{1,0:T(8,128)S(1)}, f32[16,512]{1,0:T(8,128)}, u32[]{:S(2)}) copy-start(f32[16,512]{1,0:T(8,128)} %solves_ref.1) | copy-start | bytes 98308
  1.7 0.8 %copy-start.2 = (f32[16,512]{1,0:T(8,128)S(1)}, f32[16,512]{1,0:T(8,128)}, u32[]{:S(2)}) copy-start(f32[16,512]{1,0:T(8,128)} %probes_ref.1) | copy-start | bytes 98308
  2.4 7.3 %collective-permute-start = (f32[96,512]{1,0:T(8,128)S(1)}, f32[96,512]{1,0:T(8,128)S(1)}, u32[]{:S(2)}, u32[]{:S(2)}) collective-permute-start(f32[96,512]{1,0:T(8,128)S(1)} %shard_map.37.refs_0_.refs_2_), channel_id=1, source_target_pairs={{0,1},{1,0},{2,3},{3,2},{4,5},{5,4},{6,7},{7,6},{8,9},{9,8},{10,11... | collective-permute-start | bytes 589832 | tf_op jit(solution)/shard_map/ppermute | solution.py:17
  3.0 8.1 %collective-permute-start.3 = (f32[96,512]{1,0:T(8,128)S(1)}, f32[96,512]{1,0:T(8,128)S(1)}, u32[]{:S(2)}, u32[]{:S(2)}) collective-permute-start(f32[96,512]{1,0:T(8,128)S(1)} %shard_map.37.refs_0_.refs_2_), channel_id=1, source_target_pairs={{0,2},{1,3},{2,0},{3,1},{4,6},{5,7},{6,4},{7,5},{8,10},{9,11},{10,... | collective-permute-start | bytes 589832 | tf_op jit(solution)/shard_map/ppermute | solution.py:17
  5.6 12.2 %collective-permute-start.1 = (f32[96,512]{1,0:T(8,128)S(1)}, f32[96,512]{1,0:T(8,128)S(1)}, u32[]{:S(2)}, u32[]{:S(2)}) collective-permute-start(f32[96,512]{1,0:T(8,128)S(1)} %shard_map.37.refs_0_.refs_2_), channel_id=1, source_target_pairs={{0,8},{1,9},{2,10},{3,11},{4,12},{5,13},{6,14},{7,15},{8,0},{9,1},... | collective-permute-start | bytes 589832 | tf_op jit(solution)/shard_map/ppermute | solution.py:17
  8.1 9.8 %collective-permute-start.2 = (f32[96,512]{1,0:T(8,128)S(1)}, f32[96,512]{1,0:T(8,128)S(1)}, u32[]{:S(2)}, u32[]{:S(2)}) collective-permute-start(f32[96,512]{1,0:T(8,128)S(1)} %shard_map.37.refs_0_.refs_2_), channel_id=1, source_target_pairs={{0,4},{1,5},{2,6},{3,7},{4,0},{5,1},{6,2},{7,3},{8,12},{9,13},{10,... | collective-permute-start | bytes 589832 | tf_op jit(solution)/shard_map/ppermute | solution.py:17
  17.9 2.0 %collective-permute-start.5 = (f32[96,512]{1,0:T(8,128)S(1)}, f32[96,512]{1,0:T(8,128)S(1)}, u32[]{:S(2)}, u32[]{:S(2)}) collective-permute-start(f32[96,512]{1,0:T(8,128)S(1)} %collective-permute-done.2.refs_0_), channel_id=1, source_target_pairs={{0,1},{1,0},{2,3},{3,2},{4,5},{5,4},{6,7},{7,6},{8,9},{9,8},{10,11... | collective-permute-start | bytes 589832 | tf_op jit(solution)/shard_map/ppermute | solution.py:17
  17.9 7.3 %collective-permute-start.4 = (f32[96,512]{1,0:T(8,128)S(1)}, f32[96,512]{1,0:T(8,128)S(1)}, u32[]{:S(2)}, u32[]{:S(2)}) collective-permute-start(f32[96,512]{1,0:T(8,128)S(1)} %collective-permute-done.1.refs_2_.refs_4_), channel_id=1, source_target_pairs={{0,2},{1,3},{2,0},{3,1},{4,6},{5,7},{6,4},{7,5},{8,10},{9,11},{10,... | collective-permute-start | bytes 589832 | tf_op jit(solution)/shard_map/ppermute | solution.py:17
  26.8 2.2 %collective-permute-start.7 = (f32[64,512]{1,0:T(8,128)S(1)}, f32[64,512]{1,0:T(8,128)S(1)}, u32[]{:S(2)}, u32[]{:S(2)}) collective-permute-start(f32[64,512]{1,0:T(8,128)S(1)} %get-tuple-element.60), channel_id=1, source_target_pairs={{0,1},{1,0},{2,3},{3,2},{4,5},{5,4},{6,7},{7,6},{8,9},{9,8},{10,11... | collective-permute-start | bytes 393224 | tf_op jit(solution)/shard_map/ppermute | solution.py:17
  28.4 2.1 %collective-permute-start.6 = (f32[64,512]{1,0:T(8,128)S(1)}, f32[64,512]{1,0:T(8,128)S(1)}, u32[]{:S(2)}, u32[]{:S(2)}) collective-permute-start(f32[64,512]{1,0:T(8,128)S(1)} %get-tuple-element.52), channel_id=1, source_target_pairs={{0,1},{1,0},{2,3},{3,2},{4,5},{5,4},{6,7},{7,6},{8,9},{9,8},{10,11... | collective-permute-start | bytes 393224 | tf_op jit(solution)/shard_map/ppermute | solution.py:17
  29.0 5.5 %collective-permute-start.8 = (f32[64,512]{1,0:T(8,128)S(1)}, f32[64,512]{1,0:T(8,128)S(1)}, u32[]{:S(2)}, u32[]{:S(2)}) collective-permute-start(f32[64,512]{1,0:T(8,128)S(1)} %add.10), channel_id=1, source_target_pairs={{0,4},{1,5},{2,6},{3,7},{4,0},{5,1},{6,2},{7,3},{8,12},{9,13},{10,... | collective-permute-start | bytes 393224 | tf_op jit(solution)/shard_map/ppermute | solution.py:17

commit v5 on v4

--- a/solution.py
+++ b/solution.py
@@ -135,15 +135,24 @@
     width, points = features.shape
     vectors = solves.shape[0]
 
-    def body(features_ref, solves_ref, probes_ref, out_ref):
-        out_ref[:width] = features_ref[...]
-        out_ref[width : width + vectors] = solves_ref[...]
-        out_ref[width + vectors :] = probes_ref[...]
+    def body(features_ref, solves_ref, probes_ref, out_ref, arrived):
+        parts = ((features_ref, 0), (solves_ref, width), (probes_ref, width + vectors))
+        copies = [
+            pltpu.make_async_copy(ref, out_ref.at[pl.ds(start, ref.shape[0])], arrived.at[place])
+            for place, (ref, start) in enumerate(parts)
+        ]
+        for copy in copies:
+            copy.start()
+        for copy in copies:
+            copy.wait()
 
     return pl.pallas_call(
         body,
         out_shape=jax.ShapeDtypeStruct((width + 2 * vectors, points), jnp.float32),
-        compiler_params=pltpu.CompilerParams(vmem_limit_bytes=4 << 20),
+        in_specs=[pl.BlockSpec(memory_space=pltpu.HBM)] * 3,
+        out_specs=pl.BlockSpec(memory_space=pltpu.HBM),
+        scratch_shapes=[pltpu.SemaphoreType.DMA((3,))],
+        compiler_params=pltpu.CompilerParams(vmem_limit_bytes=60 << 20),
     )(features, solves, probes)
 
 
@@ -163,28 +172,29 @@
     direct = [swap(mine, bit) for bit in beside]
     sibling = swap(mine, 1)
 
-    def spread(block):
-        blocks = [block]
-        for bit in beside:
-            blocks += [swap(other, bit) for other in blocks]
-        return blocks
-
-    early = [mine] + direct
-    here, ready_here = terms([mine, sibling], early)
-    far, near, here = tied((far, near, here))
-    near_sibling = swap(near, 1)
-    far_columns = spread(far)
-    here, _ = terms([mine, sibling], [far], ready=ready_here, before=here)
-    near_sibling, here = tied((near_sibling, here))
-    there, ready_there = terms([near, near_sibling], early + [far])
-    last = far_columns[1:]
-    last[0], there = tied((last[0], there))
-    there, _ = terms([near, near_sibling], last, ready=ready_there, before=there)
-    here, _ = terms([mine, sibling], last, ready=ready_here, before=here)
-
-    toward_near = there[0] + swap(there[1], 1)
-    from_near = swap(toward_near, 4)
-    return here[0] + swap(here[1], 1) + from_near
+    here, ready_here = terms([mine], [mine, sibling])
+    *direct, here[0] = tied((*direct, here[0]))
+    direct_siblings = [swap(block, 1) for block in direct]
+    here, _ = terms([mine], direct, ready=ready_here, before=here)
+    far, near, here[0] = tied((far, near, here[0]))
+    last = []
+    for bit in beside:
+        last += [swap(block, bit) for block in [far] + last]
+    far_sibling = swap(far, 1)
+    here, _ = terms([mine], direct_siblings + [far], ready=ready_here, before=here)
+    early = [mine, sibling, *direct, *direct_siblings, far]
+    there, ready_there = terms([near], early)
+    last[0], here[0], there[0] = tied((last[0], here[0], there[0]))
+    last_siblings = [swap(block, 1) for block in last]
+    both = [mine, near]
+    ready = ready_here + ready_there
+    (toward_here, toward_there), _ = terms(
+        both, [far_sibling, *last], ready=ready, before=here + there
+    )
+    there, _ = terms([near], last_siblings, ready=ready_there, before=[toward_there])
+    from_near = swap(there[0], 4)
+    here, _ = terms([mine], last_siblings, ready=ready_here, before=[toward_here])
+    return here[0] + from_near
 
 
 def solution(mesh):

time: 35.4 us -> 39.1 us (1.10)
  Pallas kernels: 10.9 us -> 18.8 us
  waiting for transfers between devices: 11.1 us -> 8.9 us
  local copies, waits for them, and re-layouts: 2.42 us -> 0.96 us
    pallas_call x1, Pallas kernels: 0.01 us -> 7.08 us  [packed(): pl.pallas_call(body, out_shape=jax.ShapeDtypeStruct((width + 2 * vectors,...]
    ppermute x9, waiting for transfers between devices: 11.1 us -> 8.9 us  [swapped(): lax.ppermute(value, axis, [(source, source ^ bit) for source in range(cou...]
    unnamed x6 -> x4, local copies, waits for them, and re-layouts: 2.42 us -> 0.96 us
    pallas_call x5 -> x7, Pallas kernels: 10.9 us -> 11.7 us  [pair_terms(): pl.pallas_call(functools.partial(kernel, width, vectors, min(512, points)...]
  transfers between devices with their start and end apart: 9 -> 9, of which waited for: 5 -> 4; matrix products, arithmetic and copies ran while one was open for 0% -> 0% of each run, Pallas kernels for 27% -> 28%
where the time goes in v5:
time: 39.1 us; the launch traced here: 39 us
  Pallas kernels  18.8 us (48%)
  starting transfers between devices  9.53 us (24%)
  waiting for transfers between devices  8.9 us (23%)
  local copies, waits for them, and re-layouts  0.96 us (2%)
  other arithmetic  0.67 us (2%)
    pallas_call x7, Pallas kernels, pair_terms(): pl.pallas_call(functools.partial(kernel, width, vectors, min(512, points)...  11.7 us
    ppermute x9, starting transfers between devices, swapped(): lax.ppermute(value, axis, [(source, source ^ bit) for source in range(cou...  9.53 us
    ppermute x9, waiting for transfers between devices, swapped(): lax.ppermute(value, axis, [(source, source ^ bit) for source in range(cou...  8.9 us
    pallas_call x1, Pallas kernels, packed(): pl.pallas_call(body, out_shape=jax.ShapeDtypeStruct((width + 2 * vectors,...  7.08 us
    unnamed x4, local copies, waits for them, and re-layouts  0.96 us
  transfers between devices with their start and end apart: 9, of which 4 were waited for; matrix products, arithmetic and copies ran while one was open for 0% of the time, Pallas kernels for 28%

profile of v5, /device:TPU:0, one launch (start us, length us, event | category | flops | bytes accessed | tf_op | source)
XLA Modules:
  0.0 39.0 jit_solution(15316293022940773571)
XLA Ops:
  0.0 7.1 %shard_map.37.refs_0_.refs_1_ = f32[96,512]{1,0:T(8,128)} custom-call(f32[64,512]{1,0:T(8,128)} %features_ref.1, f32[16,512]{1,0:T(8,128)} %solves_ref.1, f32[16,512]{1,0:T(8,128)} %probes_ref.1), custom_call_target="tpu_custom_call" | custom-call | tf_op jit(solution)/shard_map/pallas_call | solution.py:149
  7.1 0.5 %collective-permute-start.3 = (f32[96,512]{1,0:T(8,128)}, f32[96,512]{1,0:T(8,128)S(1)}, u32[]{:S(2)}, u32[]{:S(2)}) collective-permute-start(f32[96,512]{1,0:T(8,128)} %shard_map.37.refs_0_.refs_1_), channel_id=1, source_target_pairs={{0,1},{1,0},{2,3},{3,2},{4,5},{5,4},{6,7},{7,6},{8,9},{9,8},{10,11... | collective-permute-start | bytes 589832 | tf_op jit(solution)/shard_map/ppermute | solution.py:17
  7.6 2.6 %collective-permute-start.2 = (f32[96,512]{1,0:T(8,128)}, f32[96,512]{1,0:T(8,128)S(1)}, u32[]{:S(2)}, u32[]{:S(2)}) collective-permute-start(f32[96,512]{1,0:T(8,128)} %shard_map.37.refs_0_.refs_1_), channel_id=1, source_target_pairs={{0,2},{1,3},{2,0},{3,1},{4,6},{5,7},{6,4},{7,5},{8,10},{9,11},{10,... | collective-permute-start | bytes 589832 | tf_op jit(solution)/shard_map/ppermute | solution.py:17
  10.2 2.6 %collective-permute-start = (f32[96,512]{1,0:T(8,128)}, f32[96,512]{1,0:T(8,128)S(1)}, u32[]{:S(2)}, u32[]{:S(2)}) collective-permute-start(f32[96,512]{1,0:T(8,128)} %shard_map.37.refs_0_.refs_1_), channel_id=1, source_target_pairs={{0,8},{1,9},{2,10},{3,11},{4,12},{5,13},{6,14},{7,15},{8,0},{9,1},... | collective-permute-start | bytes 589832 | tf_op jit(solution)/shard_map/ppermute | solution.py:17
  12.8 1.6 %collective-permute-start.1 = (f32[96,512]{1,0:T(8,128)}, f32[96,512]{1,0:T(8,128)S(1)}, u32[]{:S(2)}, u32[]{:S(2)}) collective-permute-start(f32[96,512]{1,0:T(8,128)} %shard_map.37.refs_0_.refs_1_), channel_id=1, source_target_pairs={{0,4},{1,5},{2,6},{3,7},{4,0},{5,1},{6,2},{7,3},{8,12},{9,13},{10,... | collective-permute-start | bytes 589832 | tf_op jit(solution)/shard_map/ppermute | solution.py:17
  14.4 0.0 collective-permute-done.3.refs_2_
  14.4 0.0 copy-start
  14.4 1.0 %copy-done = f32[96,512]{1,0:T(8,128)S(1)} copy-done((f32[96,512]{1,0:T(8,128)S(1)}, f32[96,512]{1,0:T(8,128)}, u32[]{:S(2)}) %copy-start) | copy-done | bytes 196632
  15.3 1.5 %shard_map.38 = (f32[64,512]{1,0:T(8,128)S(1)}, bf16[512,208]{1,0:T(8,128)(2,1)S(1)}, bf16[512,96]{1,0:T(8,128)(2,1)S(1)}) custom-call(f32[96,512]{1,0:T(8,128)S(1)} %copy-done, f32[96,512]{1,0:T(8,128)S(1)} %copy-done, f32[96,512]{1,0:T(8,128)S(1)} %collective-permute-done.3.refs_2_), custom_call_target="tpu_custom_call" | custom-call | flops 1 | bytes 1 | tf_op jit(solution)/shard_map/pallas_call | solution.py:120
  16.9 0.0 collective-permute-done.2.refs_1_.refs_3_
  16.9 0.1 collective-permute-start.5
  17.0 0.0 copy-start.1
  17.0 1.0 %shard_map.39.refs_5_ = f32[64,512]{1,0:T(8,128)S(1)} custom-call(f32[96,512]{1,0:T(8,128)S(1)} %copy-done, f32[96,512]{1,0:T(8,128)S(1)} %collective-permute-done.2.refs_1_.refs_3_, bf16[512,208]{1,0:T(8,128)(2,1)S(1)} %get-tuple-element.23.refs_2_.refs_3_.refs_4_, bf16[512,96]{1,0:T(8,128)(2,1)S(1)} %get-tuple-element.24.refs_3_.refs_4_.refs_5_, ...), custom_call_target="tpu_custom_call" | custom-call | flops 1 | bytes 1 | tf_op jit(solution)/shard_map/pallas_call | solution.py:120
  17.9 4.7 %collective-permute-done.refs_2_.refs_5_ = f32[96,512]{1,0:T(8,128)S(1)} collective-permute-done((f32[96,512]{1,0:T(8,128)}, f32[96,512]{1,0:T(8,128)S(1)}, u32[]{:S(2)}, u32[]{:S(2)}) %collective-permute-start) | collective-permute-done | bytes 196640 | tf_op jit(solution)/shard_map/ppermute | solution.py:17
  22.6 0.2 collective-permute-done.1.refs_0_.refs_1_
  22.8 0.5 %collective-permute-start.4 = (f32[96,512]{1,0:T(8,128)S(1)}, f32[96,512]{1,0:T(8,128)S(1)}, u32[]{:S(2)}, u32[]{:S(2)}) collective-permute-start(f32[96,512]{1,0:T(8,128)S(1)} %collective-permute-done.refs_2_.refs_5_), channel_id=1, source_target_pairs={{0,2},{1,3},{2,0},{3,1},{4,6},{5,7},{6,4},{7,5},{8,10},{9,11},{10,... | collective-permute-start | bytes 589832 | tf_op jit(solution)/shard_map/ppermute | solution.py:17
  23.3 0.0 collective-permute-start.7
  23.3 0.0 collective-permute-done.5.refs_1_.refs_4_
  23.3 0.0 copy-done.1
  23.3 3.2 %shard_map.41 = (f32[64,512]{1,0:T(8,128)S(1)}, bf16[512,208]{1,0:T(8,128)(2,1)S(1)}, bf16[512,96]{1,0:T(8,128)(2,1)S(1)}) custom-call(f32[96,512]{1,0:T(8,128)S(1)} %collective-permute-done.1.refs_0_.refs_1_, f32[96,512]{1,0:T(8,128)S(1)} %copy-done.1, f32[96,512]{1,0:T(8,128)S(1)} %collective-permute-done.3.refs_2_, ...), custom_call_target="tpu_custom_call" | custom-call | flops 1 | bytes 1 | tf_op jit(solution)/shard_map/pallas_call | solution.py:120
  26.5 1.5 %shard_map.40.refs_8_ = f32[64,512]{1,0:T(8,128)S(1)} custom-call(f32[96,512]{1,0:T(8,128)S(1)} %copy-done.1, f32[96,512]{1,0:T(8,128)S(1)} %collective-permute-done.5.refs_1_.refs_4_, f32[96,512]{1,0:T(8,128)S(1)} %collective-permute-done.refs_2_.refs_5_, bf16[512,208]{1,0:T(8,128)(2,1)S(1)} %get-tuple-element.23.refs_2_.refs_3_.refs_4_, ...), custom_call_target="tpu_custom_call" | custom-call | flops 1 | bytes 1 | tf_op jit(solution)/shard_map/pallas_call | solution.py:120
  28.0 0.7 %collective-permute-done.4.refs_3_ = f32[96,512]{1,0:T(8,128)S(1)} collective-permute-done((f32[96,512]{1,0:T(8,128)S(1)}, f32[96,512]{1,0:T(8,128)S(1)}, u32[]{:S(2)}, u32[]{:S(2)}) %collective-permute-start.4) | collective-permute-done | bytes 196640 | tf_op jit(solution)/shard_map/ppermute | solution.py:17
  28.7 0.0 collective-permute-start.6
  28.7 0.0 collective-permute-done.7.refs_2_
  28.7 2.6 %shard_map.42 = (f32[64,512]{1,0:T(8,128)S(1)}, f32[64,512]{1,0:T(8,128)S(1)}) custom-call(f32[96,512]{1,0:T(8,128)S(1)} %copy-done.1, f32[96,512]{1,0:T(8,128)S(1)} %collective-permute-done.1.refs_0_.refs_1_, f32[96,512]{1,0:T(8,128)S(1)} %collective-permute-done.7.refs_2_, f32[96,512]{1,0:T(8,128)S(1)} %collective-permute-done.4.refs_3_, ...), custom_call_target="tpu_custom_call" | custom-call | flops 1 | bytes 1 | tf_op jit(solution)/shard_map/pallas_call | solution.py:120
  31.4 0.0 collective-permute-done.6.refs_1_
  31.4 1.0 %shard_map.44 = f32[64,512]{1,0:T(8,128)S(1)} custom-call(f32[96,512]{1,0:T(8,128)S(1)} %collective-permute-done.1.refs_0_.refs_1_, f32[96,512]{1,0:T(8,128)S(1)} %collective-permute-done.6.refs_1_, bf16[512,208]{1,0:T(8,128)(2,1)S(1)} %get-tuple-element.31.refs_6_.refs_2_, bf16[512,96]{1,0:T(8,128)(2,1)S(1)} %get-tuple-element.32.refs_7_.refs_3_, ...), custom_call_target="tpu_custom_call" | custom-call | flops 1 | bytes 1 | tf_op jit(solution)/shard_map/pallas_call | solution.py:120
  32.3 1.7 %collective-permute-start.8 = (f32[64,512]{1,0:T(8,128)S(1)}, f32[64,512]{1,0:T(8,128)S(1)}, u32[]{:S(2)}, u32[]{:S(2)}) collective-permute-start(f32[64,512]{1,0:T(8,128)S(1)} %shard_map.44), channel_id=1, source_target_pairs={{0,4},{1,5},{2,6},{3,7},{4,0},{5,1},{6,2},{7,3},{8,12},{9,13},{10,... | collective-permute-start | bytes 393224 | tf_op jit(solution)/shard_map/ppermute | solution.py:17
  34.0 1.0 %shard_map.43 = f32[64,512]{1,0:T(8,128)S(1)} custom-call(f32[96,512]{1,0:T(8,128)S(1)} %copy-done.1, f32[96,512]{1,0:T(8,128)S(1)} %collective-permute-done.6.refs_1_, bf16[512,208]{1,0:T(8,128)(2,1)S(1)} %get-tuple-element.23.refs_2_.refs_3_.refs_4_, bf16[512,96]{1,0:T(8,128)(2,1)S(1)} %get-tuple-element.24.refs_3_.refs_4_.refs_5_, ...), custom_call_target="tpu_custom_call" | custom-call | flops 1 | bytes 1 | tf_op jit(solution)/shard_map/pallas_call | solution.py:120
  35.0 3.3 %collective-permute-done.8 = f32[64,512]{1,0:T(8,128)S(1)} collective-permute-done((f32[64,512]{1,0:T(8,128)S(1)}, f32[64,512]{1,0:T(8,128)S(1)}, u32[]{:S(2)}, u32[]{:S(2)}) %collective-permute-start.8) | collective-permute-done | bytes 131104 | tf_op jit(solution)/shard_map/ppermute | solution.py:17
  38.3 0.7 %add.3 = f32[64,512]{1,0:T(8,128)} add(f32[64,512]{1,0:T(8,128)S(1)} %shard_map.43, f32[64,512]{1,0:T(8,128)S(1)} %collective-permute-done.8) | non-fusion elementwise | flops 32768 | bytes 393216 | tf_op jit(solution)/shard_map/add | solution.py:197
Async XLA Ops:
  7.1 7.3 %collective-permute-start.3 = (f32[96,512]{1,0:T(8,128)}, f32[96,512]{1,0:T(8,128)S(1)}, u32[]{:S(2)}, u32[]{:S(2)}) collective-permute-start(f32[96,512]{1,0:T(8,128)} %shard_map.37.refs_0_.refs_1_), channel_id=1, source_target_pairs={{0,1},{1,0},{2,3},{3,2},{4,5},{5,4},{6,7},{7,6},{8,9},{9,8},{10,11... | collective-permute-start | bytes 589832 | tf_op jit(solution)/shard_map/ppermute | solution.py:17
  7.6 9.3 %collective-permute-start.2 = (f32[96,512]{1,0:T(8,128)}, f32[96,512]{1,0:T(8,128)S(1)}, u32[]{:S(2)}, u32[]{:S(2)}) collective-permute-start(f32[96,512]{1,0:T(8,128)} %shard_map.37.refs_0_.refs_1_), channel_id=1, source_target_pairs={{0,2},{1,3},{2,0},{3,1},{4,6},{5,7},{6,4},{7,5},{8,10},{9,11},{10,... | collective-permute-start | bytes 589832 | tf_op jit(solution)/shard_map/ppermute | solution.py:17
  10.2 12.4 %collective-permute-start = (f32[96,512]{1,0:T(8,128)}, f32[96,512]{1,0:T(8,128)S(1)}, u32[]{:S(2)}, u32[]{:S(2)}) collective-permute-start(f32[96,512]{1,0:T(8,128)} %shard_map.37.refs_0_.refs_1_), channel_id=1, source_target_pairs={{0,8},{1,9},{2,10},{3,11},{4,12},{5,13},{6,14},{7,15},{8,0},{9,1},... | collective-permute-start | bytes 589832 | tf_op jit(solution)/shard_map/ppermute | solution.py:17
  12.8 10.0 %collective-permute-start.1 = (f32[96,512]{1,0:T(8,128)}, f32[96,512]{1,0:T(8,128)S(1)}, u32[]{:S(2)}, u32[]{:S(2)}) collective-permute-start(f32[96,512]{1,0:T(8,128)} %shard_map.37.refs_0_.refs_1_), channel_id=1, source_target_pairs={{0,4},{1,5},{2,6},{3,7},{4,0},{5,1},{6,2},{7,3},{8,12},{9,13},{10,... | collective-permute-start | bytes 589832 | tf_op jit(solution)/shard_map/ppermute | solution.py:17
  14.4 1.0 %copy-start = (f32[96,512]{1,0:T(8,128)S(1)}, f32[96,512]{1,0:T(8,128)}, u32[]{:S(2)}) copy-start(f32[96,512]{1,0:T(8,128)} %shard_map.37.refs_0_.refs_1_) | copy-start | bytes 589828
  16.9 6.4 %collective-permute-start.5 = (f32[96,512]{1,0:T(8,128)S(1)}, f32[96,512]{1,0:T(8,128)S(1)}, u32[]{:S(2)}, u32[]{:S(2)}) collective-permute-start(f32[96,512]{1,0:T(8,128)S(1)} %collective-permute-done.2.refs_1_.refs_3_), channel_id=1, source_target_pairs={{0,1},{1,0},{2,3},{3,2},{4,5},{5,4},{6,7},{7,6},{8,9},{9,8},{10,11... | collective-permute-start | bytes 589832 | tf_op jit(solution)/shard_map/ppermute | solution.py:17
  17.0 6.3 %copy-start.1 = (f32[96,512]{1,0:T(8,128)S(1)}, f32[96,512]{1,0:T(8,128)}, u32[]{:S(2)}) copy-start(f32[96,512]{1,0:T(8,128)} %shard_map.37.refs_0_.refs_1_) | copy-start | bytes 589828
  22.8 5.9 %collective-permute-start.4 = (f32[96,512]{1,0:T(8,128)S(1)}, f32[96,512]{1,0:T(8,128)S(1)}, u32[]{:S(2)}, u32[]{:S(2)}) collective-permute-start(f32[96,512]{1,0:T(8,128)S(1)} %collective-permute-done.refs_2_.refs_5_), channel_id=1, source_target_pairs={{0,2},{1,3},{2,0},{3,1},{4,6},{5,7},{6,4},{7,5},{8,10},{9,11},{10,... | collective-permute-start | bytes 589832 | tf_op jit(solution)/shard_map/ppermute | solution.py:17
  23.3 5.5 %collective-permute-start.7 = (f32[96,512]{1,0:T(8,128)S(1)}, f32[96,512]{1,0:T(8,128)S(1)}, u32[]{:S(2)}, u32[]{:S(2)}) collective-permute-start(f32[96,512]{1,0:T(8,128)S(1)} %collective-permute-done.refs_2_.refs_5_), channel_id=1, source_target_pairs={{0,1},{1,0},{2,3},{3,2},{4,5},{5,4},{6,7},{7,6},{8,9},{9,8},{10,11... | collective-permute-start | bytes 589832 | tf_op jit(solution)/shard_map/ppermute | solution.py:17
  28.7 2.6 %collective-permute-start.6 = (f32[96,512]{1,0:T(8,128)S(1)}, f32[96,512]{1,0:T(8,128)S(1)}, u32[]{:S(2)}, u32[]{:S(2)}) collective-permute-start(f32[96,512]{1,0:T(8,128)S(1)} %collective-permute-done.4.refs_3_), channel_id=1, source_target_pairs={{0,1},{1,0},{2,3},{3,2},{4,5},{5,4},{6,7},{7,6},{8,9},{9,8},{10,11... | collective-permute-start | bytes 589832 | tf_op jit(solution)/shard_map/ppermute | solution.py:17
  32.3 6.0 %collective-permute-start.8 = (f32[64,512]{1,0:T(8,128)S(1)}, f32[64,512]{1,0:T(8,128)S(1)}, u32[]{:S(2)}, u32[]{:S(2)}) collective-permute-start(f32[64,512]{1,0:T(8,128)S(1)} %shard_map.44), channel_id=1, source_target_pairs={{0,4},{1,5},{2,6},{3,7},{4,0},{5,1},{6,2},{7,3},{8,12},{9,13},{10,... | collective-permute-start | bytes 393224 | tf_op jit(solution)/shard_map/ppermute | solution.py:17

commit v6 on v4

v6 whole, which is shorter than its diff:
```python
import functools

import jax
import jax.numpy as jnp
from jax import lax
from jax.experimental import pallas as pl
from jax.experimental.pallas import tpu as pltpu
from jax.sharding import PartitionSpec as P

LOG2E = 1.4426950408889634
NORM_ROWS = 16
ONES_ROWS = 16
VMEM_LIMIT = 24 << 20


def swapped(value, axis, bit):
    count = lax.axis_size(axis)
    return lax.ppermute(value, axis, [(source, source ^ bit) for source in range(count)])


def split2(value):
    high = value.astype(jnp.bfloat16)
    low = (value - high.astype(jnp.float32)).astype(jnp.bfloat16)
    return high, low


def term_weights(vectors):
    position = lax.broadcasted_iota(jnp.int32, (2 * vectors, 1), 0)
    first = (position == 0) | (position == vectors)
    return jnp.where(first, 0.5, -0.5 / (vectors - 1)).astype(jnp.float32)


def norm_rows(norms, first):
    high = norms.astype(jnp.bfloat16).astype(jnp.float32)
    rest = norms - high
    mid = rest.astype(jnp.bfloat16).astype(jnp.float32)
    row = lax.broadcasted_iota(jnp.int32, (NORM_ROWS, norms.shape[1]), 0)
    at, ones = (0, 3) if first else (3, 0)
    rows = jnp.where((row >= ones) & (row < ones + 3), 1.0, 0.0)
    for place, part in enumerate((high, mid, rest - mid)):
        rows = jnp.where(row == at + place, part, rows)
    return rows.astype(jnp.bfloat16)


def prepared_mine(block, width, vectors):
    feat = block[:width]
    scale = LOG2E / (2.0 * width)
    norms = jnp.sum(feat * feat, axis=0, keepdims=True) * -scale
    high, low = split2(feat * (2.0 * scale))
    dist = jnp.concatenate([high, low, high, norm_rows(norms, True)], 0)
    high, low = split2(block[width:] * term_weights(vectors))
    return dist, jnp.concatenate([high, low, high], 0)


def prepared_theirs(block, width, vectors):
    feat = block[:width]
    scale = LOG2E / (2.0 * width)
    norms = jnp.sum(feat * feat, axis=0, keepdims=True) * -scale
    high, low = split2(feat)
    dist = jnp.concatenate([high, high, low, norm_rows(norms, False)], 0)
    vecs = jnp.concatenate([block[width + vectors :], block[width : width + vectors]], 0)
    vec_high, vec_low = split2(vecs)
    pair = jnp.concatenate([vec_high, vec_high, vec_low], 0)
    ones = jnp.ones((ONES_ROWS, block.shape[1]), jnp.bfloat16)
    return dist.T, pair.T, jnp.concatenate([high, ones, low], 0)


def product(left, right):
    return jnp.dot(left, right, preferred_element_type=jnp.float32)


def block_terms(mine, theirs, width):
    dist_mine, pair_mine = mine
    dist_theirs, pair_theirs, pull = theirs
    coupling = jnp.exp2(product(dist_theirs, dist_mine)) * product(pair_theirs, pair_mine)
    high, low = split2(coupling)
    from_high = product(pull, high)
    from_low = product(pull[: width + ONES_ROWS], low)
    pulled = from_high[:width] + from_high[width + ONES_ROWS :] + from_low[:width]
    return pulled, from_high[width : width + 1] + from_low[width : width + 1]


def kernel(width, vectors, jobs, count, *refs):
    blocks, refs = refs[:count], refs[count:]
    before, out = refs[: -len(jobs)], refs[-len(jobs) :]
    used = sorted({theirs for _, columns in jobs for theirs in columns})
    theirs = {place: prepared_theirs(blocks[place][...], width, vectors) for place in used}
    for place, (row, columns) in enumerate(jobs):
        mine = prepared_mine(blocks[row][...], width, vectors)
        terms = [block_terms(mine, theirs[column], width) for column in columns]
        pulled = sum(term[0] for term in terms)
        sums = sum(term[1] for term in terms)
        value = (pulled - blocks[row][:width] * sums) / width
        out[place][...] = value + before[place][...] if place < len(before) else value


def pair_terms(jobs, width, vectors, before=()):
    blocks = []

    def place(block):
        for index, other in enumerate(blocks):
            if other is block:
                return index
        blocks.append(block)
        return len(blocks) - 1

    placed = [(place(row), [place(column) for column in columns]) for row, columns in jobs]
    points = blocks[0].shape[1]
    operands = blocks + list(before)
    out_shape = [jax.ShapeDtypeStruct((width, points), jnp.float32)] * len(jobs)
    return list(
        pl.pallas_call(
            functools.partial(kernel, width, vectors, placed, len(blocks)),
            out_shape=out_shape,
            in_specs=[pl.BlockSpec(memory_space=pltpu.VMEM)] * len(operands),
            out_specs=[pl.BlockSpec(memory_space=pltpu.VMEM)] * len(out_shape),
            compiler_params=pltpu.CompilerParams(vmem_limit_bytes=VMEM_LIMIT),
        )(*operands)
    )


def packed(features, solves, probes):
    width, points = features.shape
    vectors = solves.shape[0]

    def body(features_ref, solves_ref, probes_ref, out_ref):
        out_ref[:width] = features_ref[...]
        out_ref[width : width + vectors] = solves_ref[...]
        out_ref[width + vectors :] = probes_ref[...]

    return pl.pallas_call(
        body,
        out_shape=jax.ShapeDtypeStruct((width + 2 * vectors, points), jnp.float32),
        compiler_params=pltpu.CompilerParams(vmem_limit_bytes=60 << 20),
    )(features, solves, probes)


def local(features, solves, probes):
    width = features.shape[0]
    vectors = solves.shape[0]
    count = lax.axis_size("blk")
    terms = functools.partial(pair_terms, width=width, vectors=vectors)
    swap = lambda value, bit: swapped(value, "blk", bit)
    tied = lax.optimization_barrier

    top = count // 2
    beside = [1 << place for place in range(1, count.bit_length() - 2) if place != 2]
    mine = packed(features, solves, probes)
    sibling = swap(mine, 1)
    far = swap(mine, top)
    near = swap(mine, 4)
    direct = [swap(mine, bit) for bit in beside]

    here = terms([(mine, [mine, sibling])])
    far, here[0] = tied((far, here[0]))
    last = []
    for bit in beside:
        last += [swap(block, bit) for block in [far] + last]
    siblings = [swap(block, 1) for block in [far] + direct]
    both = terms(
        [(mine, [far] + direct), (near, [mine, sibling, far] + direct)],
        before=here,
    )
    both = terms([(mine, siblings), (near, siblings)], before=both)
    last[0], *both = tied((last[0], *both))
    last_siblings = [swap(block, 1) for block in last]
    here, there = terms([(mine, last), (near, last)], before=both)
    (there,) = terms([(near, last_siblings)], before=[there])
    from_near = swap(there, 4)
    (here,) = terms([(mine, last_siblings)], before=[here])
    return here + from_near


def solution(mesh):
    in_specs = (P(None, ("groups", "blk")), P(None, ("groups", "blk")), P(None, ("groups", "blk")))
    out_specs = P(None, ("groups", "blk"))
    return jax.shard_map(local, mesh=mesh, in_specs=in_specs, out_specs=out_specs, check_vma=False)
```

time: 35.4 us -> 33 us (0.932)
  waiting for transfers between devices: 11.1 us -> 9.23 us
  local copies, waits for them, and re-layouts: 2.42 us -> 0.96 us
  Pallas kernels: 10.9 us -> 11.9 us
    ppermute x9, waiting for transfers between devices: 11.1 us -> 9.23 us  [swapped(): lax.ppermute(value, axis, [(source, source ^ bit) for source in range(cou...]
    pallas_call x1, Pallas kernels: 0.01 us -> 1.62 us  [packed(): pl.pallas_call(body, out_shape=jax.ShapeDtypeStruct((width + 2 * vectors,...]
    unnamed x6 -> x4, local copies, waits for them, and re-layouts: 2.42 us -> 0.96 us
    pallas_call x5 -> x6, Pallas kernels: 10.9 us -> 10.3 us  [pair_terms(): pl.pallas_call(functools.partial(kernel, width, vectors, placed, len(bloc...]
  transfers between devices with their start and end apart: 9 -> 9, of which waited for: 5 -> 3; matrix products, arithmetic and copies ran while one was open for 0% -> 0% of each run, Pallas kernels for 27% -> 29%
where the time goes in v6:
time: 33 us; the launch traced here: 32.8 us
  Pallas kernels  11.9 us (36%)
  starting transfers between devices  10 us (30%)
  waiting for transfers between devices  9.23 us (28%)
  local copies, waits for them, and re-layouts  0.96 us (3%)
  other arithmetic  0.67 us (2%)
    pallas_call x6, Pallas kernels, pair_terms(): pl.pallas_call(functools.partial(kernel, width, vectors, placed, len(bloc...  10.3 us
    ppermute x9, starting transfers between devices, swapped(): lax.ppermute(value, axis, [(source, source ^ bit) for source in range(cou...  10 us
    ppermute x9, waiting for transfers between devices, swapped(): lax.ppermute(value, axis, [(source, source ^ bit) for source in range(cou...  9.23 us
    pallas_call x1, Pallas kernels, packed(): pl.pallas_call(body, out_shape=jax.ShapeDtypeStruct((width + 2 * vectors,...  1.62 us
    unnamed x4, local copies, waits for them, and re-layouts  0.96 us
    add x1, other arithmetic, local(): return here + from_near  0.67 us
  transfers between devices with their start and end apart: 9, of which 3 were waited for; matrix products, arithmetic and copies ran while one was open for 0% of the time, Pallas kernels for 29%

profile of v6, /device:TPU:0, one launch (start us, length us, event | category | flops | bytes accessed | tf_op | source)
XLA Modules:
  0.0 32.8 jit_solution(2645498227180955856)
XLA Ops:
  0.0 1.6 %shard_map.37.refs_0_ = f32[96,512]{1,0:T(8,128)} custom-call(f32[64,512]{1,0:T(8,128)} %features_ref.1, f32[16,512]{1,0:T(8,128)} %solves_ref.1, f32[16,512]{1,0:T(8,128)} %probes_ref.1), custom_call_target="tpu_custom_call" | custom-call | tf_op jit(solution)/shard_map/pallas_call | solution.py:131
  1.6 0.5 %collective-permute-start.1 = (f32[96,512]{1,0:T(8,128)}, f32[96,512]{1,0:T(8,128)S(1)}, u32[]{:S(2)}, u32[]{:S(2)}) collective-permute-start(f32[96,512]{1,0:T(8,128)} %shard_map.37.refs_0_), channel_id=1, source_target_pairs={{0,1},{1,0},{2,3},{3,2},{4,5},{5,4},{6,7},{7,6},{8,9},{9,8},{10,11... | collective-permute-start | bytes 589832 | tf_op jit(solution)/shard_map/ppermute | solution.py:18
  2.1 3.6 %collective-permute-start = (f32[96,512]{1,0:T(8,128)}, f32[96,512]{1,0:T(8,128)S(1)}, u32[]{:S(2)}, u32[]{:S(2)}) collective-permute-start(f32[96,512]{1,0:T(8,128)} %shard_map.37.refs_0_), channel_id=1, source_target_pairs={{0,8},{1,9},{2,10},{3,11},{4,12},{5,13},{6,14},{7,15},{8,0},{9,1},... | collective-permute-start | bytes 589832 | tf_op jit(solution)/shard_map/ppermute | solution.py:18
  5.7 1.5 %collective-permute-start.4 = (f32[96,512]{1,0:T(8,128)}, f32[96,512]{1,0:T(8,128)S(1)}, u32[]{:S(2)}, u32[]{:S(2)}) collective-permute-start(f32[96,512]{1,0:T(8,128)} %shard_map.37.refs_0_), channel_id=1, source_target_pairs={{0,2},{1,3},{2,0},{3,1},{4,6},{5,7},{6,4},{7,5},{8,10},{9,11},{10,... | collective-permute-start | bytes 589832 | tf_op jit(solution)/shard_map/ppermute | solution.py:18
  7.2 1.6 %collective-permute-start.6 = (f32[96,512]{1,0:T(8,128)}, f32[96,512]{1,0:T(8,128)S(1)}, u32[]{:S(2)}, u32[]{:S(2)}) collective-permute-start(f32[96,512]{1,0:T(8,128)} %shard_map.37.refs_0_), channel_id=1, source_target_pairs={{0,4},{1,5},{2,6},{3,7},{4,0},{5,1},{6,2},{7,3},{8,12},{9,13},{10,... | collective-permute-start | bytes 589832 | tf_op jit(solution)/shard_map/ppermute | solution.py:18
  8.8 0.0 collective-permute-done.1.refs_1_.refs_4_
  8.8 0.0 copy-start
  8.8 1.0 %copy-done = f32[96,512]{1,0:T(8,128)S(1)} copy-done((f32[96,512]{1,0:T(8,128)S(1)}, f32[96,512]{1,0:T(8,128)}, u32[]{:S(2)}) %copy-start) | copy-done | bytes 196632
  9.7 0.0 copy-start.1
  9.7 1.3 %shard_map.38.refs_5_ = f32[64,512]{1,0:T(8,128)S(1)} custom-call(f32[96,512]{1,0:T(8,128)S(1)} %copy-done, f32[96,512]{1,0:T(8,128)S(1)} %collective-permute-done.1.refs_1_.refs_4_), custom_call_target="tpu_custom_call" | custom-call | tf_op jit(solution)/shard_map/pallas_call | solution.py:112
  11.0 4.7 %collective-permute-done.refs_1_ = f32[96,512]{1,0:T(8,128)S(1)} collective-permute-done((f32[96,512]{1,0:T(8,128)}, f32[96,512]{1,0:T(8,128)S(1)}, u32[]{:S(2)}, u32[]{:S(2)}) %collective-permute-start) | collective-permute-done | bytes 196640 | tf_op jit(solution)/shard_map/ppermute | solution.py:18
  15.8 0.0 collective-permute-start.3
  15.8 0.0 collective-permute-done.4.refs_2_
  15.8 0.5 %collective-permute-start.5 = (f32[96,512]{1,0:T(8,128)S(1)}, f32[96,512]{1,0:T(8,128)S(1)}, u32[]{:S(2)}, u32[]{:S(2)}) collective-permute-start(f32[96,512]{1,0:T(8,128)S(1)} %collective-permute-done.4.refs_2_), channel_id=1, source_target_pairs={{0,1},{1,0},{2,3},{3,2},{4,5},{5,4},{6,7},{7,6},{8,9},{9,8},{10,11... | collective-permute-start | bytes 589832 | tf_op jit(solution)/shard_map/ppermute | solution.py:18
  16.3 1.6 %collective-permute-start.2 = (f32[96,512]{1,0:T(8,128)S(1)}, f32[96,512]{1,0:T(8,128)S(1)}, u32[]{:S(2)}, u32[]{:S(2)}) collective-permute-start(f32[96,512]{1,0:T(8,128)S(1)} %collective-permute-done.refs_1_), channel_id=1, source_target_pairs={{0,2},{1,3},{2,0},{3,1},{4,6},{5,7},{6,4},{7,5},{8,10},{9,11},{10,... | collective-permute-start | bytes 589832 | tf_op jit(solution)/shard_map/ppermute | solution.py:18
  17.8 0.0 collective-permute-done.6.refs_3_.refs_2_.refs_0_
  17.8 0.0 copy-done.1
  17.9 3.6 %shard_map.39 = (f32[64,512]{1,0:T(8,128)S(1)}, f32[64,512]{1,0:T(8,128)S(1)}) custom-call(f32[96,512]{1,0:T(8,128)S(1)} %copy-done.1, f32[96,512]{1,0:T(8,128)S(1)} %collective-permute-done.refs_1_, f32[96,512]{1,0:T(8,128)S(1)} %collective-permute-done.4.refs_2_, f32[96,512]{1,0:T(8,128)S(1)} %collective-permute-done.6.refs_3_.refs_2_.refs_0_, ...), custom_call_target="tpu_custom_call" | custom-call | tf_op jit(solution)/shard_map/pallas_call | solution.py:112
  21.5 0.0 collective-permute-done.3.refs_1_
  21.5 0.0 collective-permute-done.5.refs_2_
  21.5 2.5 %shard_map.40 = (f32[64,512]{1,0:T(8,128)S(1)}, f32[64,512]{1,0:T(8,128)S(1)}) custom-call(f32[96,512]{1,0:T(8,128)S(1)} %copy-done.1, f32[96,512]{1,0:T(8,128)S(1)} %collective-permute-done.3.refs_1_, f32[96,512]{1,0:T(8,128)S(1)} %collective-permute-done.5.refs_2_, f32[96,512]{1,0:T(8,128)S(1)} %collective-permute-done.6.refs_3_.refs_2_.refs_0_, ...), custom_call_target="tpu_custom_call" | custom-call | tf_op jit(solution)/shard_map/pallas_call | solution.py:112
  24.0 0.0 collective-permute-done.2.refs_1_
  24.0 0.1 collective-permute-start.7
  24.1 1.3 %shard_map.41 = (f32[64,512]{1,0:T(8,128)S(1)}, f32[64,512]{1,0:T(8,128)S(1)}) custom-call(f32[96,512]{1,0:T(8,128)S(1)} %copy-done.1, f32[96,512]{1,0:T(8,128)S(1)} %collective-permute-done.2.refs_1_, f32[96,512]{1,0:T(8,128)S(1)} %collective-permute-done.6.refs_3_.refs_2_.refs_0_, f32[64,512]{1,0:T(8,128)S(1)} %get-tuple-element.23.refs_3_, ...), custom_call_target="tpu_custom_call" | custom-call | tf_op jit(solution)/shard_map/pallas_call | solution.py:112
  25.4 0.1 collective-permute-done.7.refs_1_
  25.5 0.8 %shard_map.43 = f32[64,512]{1,0:T(8,128)S(1)} custom-call(f32[96,512]{1,0:T(8,128)S(1)} %collective-permute-done.6.refs_3_.refs_2_.refs_0_, f32[96,512]{1,0:T(8,128)S(1)} %collective-permute-done.7.refs_1_, f32[64,512]{1,0:T(8,128)S(1)} %get-tuple-element.26.refs_2_), custom_call_target="tpu_custom_call" | custom-call | tf_op jit(solution)/shard_map/pallas_call | solution.py:112
  26.3 0.7 %collective-permute-start.8 = (f32[64,512]{1,0:T(8,128)S(1)}, f32[64,512]{1,0:T(8,128)S(1)}, u32[]{:S(2)}, u32[]{:S(2)}) collective-permute-start(f32[64,512]{1,0:T(8,128)S(1)} %shard_map.43), channel_id=1, source_target_pairs={{0,4},{1,5},{2,6},{3,7},{4,0},{5,1},{6,2},{7,3},{8,12},{9,13},{10,... | collective-permute-start | bytes 393224 | tf_op jit(solution)/shard_map/ppermute | solution.py:18
  27.0 0.8 %shard_map.42 = f32[64,512]{1,0:T(8,128)S(1)} custom-call(f32[96,512]{1,0:T(8,128)S(1)} %copy-done.1, f32[96,512]{1,0:T(8,128)S(1)} %collective-permute-done.7.refs_1_, f32[64,512]{1,0:T(8,128)S(1)} %get-tuple-element.25.refs_2_), custom_call_target="tpu_custom_call" | custom-call | tf_op jit(solution)/shard_map/pallas_call | solution.py:112
  27.8 4.4 %collective-permute-done.8 = f32[64,512]{1,0:T(8,128)S(1)} collective-permute-done((f32[64,512]{1,0:T(8,128)S(1)}, f32[64,512]{1,0:T(8,128)S(1)}, u32[]{:S(2)}, u32[]{:S(2)}) %collective-permute-start.8) | collective-permute-done | bytes 131104 | tf_op jit(solution)/shard_map/ppermute | solution.py:18
  32.2 0.7 %add.3 = f32[64,512]{1,0:T(8,128)} add(f32[64,512]{1,0:T(8,128)S(1)} %shard_map.42, f32[64,512]{1,0:T(8,128)S(1)} %collective-permute-done.8) | non-fusion elementwise | flops 32768 | bytes 393216 | tf_op jit(solution)/shard_map/add | solution.py:171
Async XLA Ops:
  1.6 7.1 %collective-permute-start.1 = (f32[96,512]{1,0:T(8,128)}, f32[96,512]{1,0:T(8,128)S(1)}, u32[]{:S(2)}, u32[]{:S(2)}) collective-permute-start(f32[96,512]{1,0:T(8,128)} %shard_map.37.refs_0_), channel_id=1, source_target_pairs={{0,1},{1,0},{2,3},{3,2},{4,5},{5,4},{6,7},{7,6},{8,9},{9,8},{10,11... | collective-permute-start | bytes 589832 | tf_op jit(solution)/shard_map/ppermute | solution.py:18
  2.1 13.7 %collective-permute-start = (f32[96,512]{1,0:T(8,128)}, f32[96,512]{1,0:T(8,128)S(1)}, u32[]{:S(2)}, u32[]{:S(2)}) collective-permute-start(f32[96,512]{1,0:T(8,128)} %shard_map.37.refs_0_), channel_id=1, source_target_pairs={{0,8},{1,9},{2,10},{3,11},{4,12},{5,13},{6,14},{7,15},{8,0},{9,1},... | collective-permute-start | bytes 589832 | tf_op jit(solution)/shard_map/ppermute | solution.py:18
  5.7 10.1 %collective-permute-start.4 = (f32[96,512]{1,0:T(8,128)}, f32[96,512]{1,0:T(8,128)S(1)}, u32[]{:S(2)}, u32[]{:S(2)}) collective-permute-start(f32[96,512]{1,0:T(8,128)} %shard_map.37.refs_0_), channel_id=1, source_target_pairs={{0,2},{1,3},{2,0},{3,1},{4,6},{5,7},{6,4},{7,5},{8,10},{9,11},{10,... | collective-permute-start | bytes 589832 | tf_op jit(solution)/shard_map/ppermute | solution.py:18
  7.2 10.7 %collective-permute-start.6 = (f32[96,512]{1,0:T(8,128)}, f32[96,512]{1,0:T(8,128)S(1)}, u32[]{:S(2)}, u32[]{:S(2)}) collective-permute-start(f32[96,512]{1,0:T(8,128)} %shard_map.37.refs_0_), channel_id=1, source_target_pairs={{0,4},{1,5},{2,6},{3,7},{4,0},{5,1},{6,2},{7,3},{8,12},{9,13},{10,... | collective-permute-start | bytes 589832 | tf_op jit(solution)/shard_map/ppermute | solution.py:18
  8.8 1.0 %copy-start = (f32[96,512]{1,0:T(8,128)S(1)}, f32[96,512]{1,0:T(8,128)}, u32[]{:S(2)}) copy-start(f32[96,512]{1,0:T(8,128)} %shard_map.37.refs_0_) | copy-start | bytes 589828
  9.7 8.1 %copy-start.1 = (f32[96,512]{1,0:T(8,128)S(1)}, f32[96,512]{1,0:T(8,128)}, u32[]{:S(2)}) copy-start(f32[96,512]{1,0:T(8,128)} %shard_map.37.refs_0_) | copy-start | bytes 589828
  15.8 5.7 %collective-permute-start.3 = (f32[96,512]{1,0:T(8,128)S(1)}, f32[96,512]{1,0:T(8,128)S(1)}, u32[]{:S(2)}, u32[]{:S(2)}) collective-permute-start(f32[96,512]{1,0:T(8,128)S(1)} %collective-permute-done.refs_1_), channel_id=1, source_target_pairs={{0,1},{1,0},{2,3},{3,2},{4,5},{5,4},{6,7},{7,6},{8,9},{9,8},{10,11... | collective-permute-start | bytes 589832 | tf_op jit(solution)/shard_map/ppermute | solution.py:18
  15.8 5.7 %collective-permute-start.5 = (f32[96,512]{1,0:T(8,128)S(1)}, f32[96,512]{1,0:T(8,128)S(1)}, u32[]{:S(2)}, u32[]{:S(2)}) collective-permute-start(f32[96,512]{1,0:T(8,128)S(1)} %collective-permute-done.4.refs_2_), channel_id=1, source_target_pairs={{0,1},{1,0},{2,3},{3,2},{4,5},{5,4},{6,7},{7,6},{8,9},{9,8},{10,11... | collective-permute-start | bytes 589832 | tf_op jit(solution)/shard_map/ppermute | solution.py:18
  16.3 7.7 %collective-permute-start.2 = (f32[96,512]{1,0:T(8,128)S(1)}, f32[96,512]{1,0:T(8,128)S(1)}, u32[]{:S(2)}, u32[]{:S(2)}) collective-permute-start(f32[96,512]{1,0:T(8,128)S(1)} %collective-permute-done.refs_1_), channel_id=1, source_target_pairs={{0,2},{1,3},{2,0},{3,1},{4,6},{5,7},{6,4},{7,5},{8,10},{9,11},{10,... | collective-permute-start | bytes 589832 | tf_op jit(solution)/shard_map/ppermute | solution.py:18
  24.0 1.5 %collective-permute-start.7 = (f32[96,512]{1,0:T(8,128)S(1)}, f32[96,512]{1,0:T(8,128)S(1)}, u32[]{:S(2)}, u32[]{:S(2)}) collective-permute-start(f32[96,512]{1,0:T(8,128)S(1)} %collective-permute-done.2.refs_1_), channel_id=1, source_target_pairs={{0,1},{1,0},{2,3},{3,2},{4,5},{5,4},{6,7},{7,6},{8,9},{9,8},{10,11... | collective-permute-start | bytes 589832 | tf_op jit(solution)/shard_map/ppermute | solution.py:18
  26.3 5.9 %collective-permute-start.8 = (f32[64,512]{1,0:T(8,128)S(1)}, f32[64,512]{1,0:T(8,128)S(1)}, u32[]{:S(2)}, u32[]{:S(2)}) collective-permute-start(f32[64,512]{1,0:T(8,128)S(1)} %shard_map.43), channel_id=1, source_target_pairs={{0,4},{1,5},{2,6},{3,7},{4,0},{5,1},{6,2},{7,3},{8,12},{9,13},{10,... | collective-permute-start | bytes 393224 | tf_op jit(solution)/shard_map/ppermute | solution.py:18

commit v7 on v6

--- a/solution.py
+++ b/solution.py
@@ -10,6 +10,7 @@
 LOG2E = 1.4426950408889634
 NORM_ROWS = 16
 ONES_ROWS = 16
+CHUNK = 256
 VMEM_LIMIT = 24 << 20
 
 
@@ -69,15 +70,25 @@
     return jnp.dot(left, right, preferred_element_type=jnp.float32)
 
 
-def block_terms(mine, theirs, width):
-    dist_mine, pair_mine = mine
-    dist_theirs, pair_theirs, pull = theirs
-    coupling = jnp.exp2(product(dist_theirs, dist_mine)) * product(pair_theirs, pair_mine)
-    high, low = split2(coupling)
-    from_high = product(pull, high)
-    from_low = product(pull[: width + ONES_ROWS], low)
-    pulled = from_high[:width] + from_high[width + ONES_ROWS :] + from_low[:width]
-    return pulled, from_high[width : width + 1] + from_low[width : width + 1]
+def pulled_terms(mine, theirs, width):
+    points = mine[0].shape[1]
+    chunks = []
+    for start in range(0, points, CHUNK):
+        dist_mine, pair_mine = (part[:, start : start + CHUNK] for part in mine)
+        from_high = from_low = None
+        for dist_theirs, pair_theirs, pull in theirs:
+            for first in range(0, points, CHUNK):
+                rows = slice(first, first + CHUNK)
+                power = product(dist_theirs[rows], dist_mine)
+                coupling = jnp.exp2(power) * product(pair_theirs[rows], pair_mine)
+                high, low = split2(coupling)
+                term_high = product(pull[:, rows], high)
+                term_low = product(pull[: width + ONES_ROWS, rows], low)
+                from_high = term_high if from_high is None else from_high + term_high
+                from_low = term_low if from_low is None else from_low + term_low
+        pulled = from_high[:width] + from_high[width + ONES_ROWS :] + from_low[:width]
+        chunks.append((pulled, from_high[width : width + 1] + from_low[width : width + 1]))
+    return (jnp.concatenate(parts, 1) for parts in zip(*chunks))
 
 
 def kernel(width, vectors, jobs, count, *refs):
@@ -87,9 +98,7 @@
     theirs = {place: prepared_theirs(blocks[place][...], width, vectors) for place in used}
     for place, (row, columns) in enumerate(jobs):
         mine = prepared_mine(blocks[row][...], width, vectors)
-        terms = [block_terms(mine, theirs[column], width) for column in columns]
-        pulled = sum(term[0] for term in terms)
-        sums = sum(term[1] for term in terms)
+        pulled, sums = pulled_terms(mine, [theirs[column] for column in columns], width)
         value = (pulled - blocks[row][:width] * sums) / width
         out[place][...] = value + before[place][...] if place < len(before) else value
 

time: 33 us -> 34.6 us (1.048)
  Pallas kernels: 11.9 us -> 14 us
  waiting for transfers between devices: 9.23 us -> 8.66 us
    pallas_call x6, Pallas kernels: 10.3 us -> 12.4 us  [pair_terms(): pl.pallas_call(functools.partial(kernel, width, vectors, placed, len(bloc...]
    ppermute x9, waiting for transfers between devices: 9.23 us -> 8.66 us  [swapped(): lax.ppermute(value, axis, [(source, source ^ bit) for source in range(cou...]
  transfers between devices with their start and end apart: 9 -> 9, of which waited for: 3 -> 2; matrix products, arithmetic and copies ran while one was open for 0% -> 0% of each run, Pallas kernels for 29% -> 33%
where the time goes in v7:
time: 34.6 us; the launch traced here: 34.4 us
  Pallas kernels  14 us (40%)
  starting transfers between devices  10 us (29%)
  waiting for transfers between devices  8.66 us (25%)
  local copies, waits for them, and re-layouts  0.96 us (3%)
  other arithmetic  0.67 us (2%)
    pallas_call x6, Pallas kernels, pair_terms(): pl.pallas_call(functools.partial(kernel, width, vectors, placed, len(bloc...  12.4 us
    ppermute x9, starting transfers between devices, swapped(): lax.ppermute(value, axis, [(source, source ^ bit) for source in range(cou...  10 us
    ppermute x9, waiting for transfers between devices, swapped(): lax.ppermute(value, axis, [(source, source ^ bit) for source in range(cou...  8.66 us
    pallas_call x1, Pallas kernels, packed(): pl.pallas_call(body, out_shape=jax.ShapeDtypeStruct((width + 2 * vectors,...  1.62 us
    unnamed x4, local copies, waits for them, and re-layouts  0.96 us
  transfers between devices with their start and end apart: 9, of which 2 were waited for; matrix products, arithmetic and copies ran while one was open for 0% of the time, Pallas kernels for 33%

profile of v7, /device:TPU:0, one launch (start us, length us, event | category | flops | bytes accessed | tf_op | source)
XLA Modules:
  0.0 34.4 jit_solution(17581586127059222416)
XLA Ops:
  0.0 1.6 %shard_map.37.refs_0_ = f32[96,512]{1,0:T(8,128)} custom-call(f32[64,512]{1,0:T(8,128)} %features_ref.1, f32[16,512]{1,0:T(8,128)} %solves_ref.1, f32[16,512]{1,0:T(8,128)} %probes_ref.1), custom_call_target="tpu_custom_call" | custom-call | tf_op jit(solution)/shard_map/pallas_call | solution.py:140
  1.6 0.5 %collective-permute-start.1 = (f32[96,512]{1,0:T(8,128)}, f32[96,512]{1,0:T(8,128)S(1)}, u32[]{:S(2)}, u32[]{:S(2)}) collective-permute-start(f32[96,512]{1,0:T(8,128)} %shard_map.37.refs_0_), channel_id=1, source_target_pairs={{0,1},{1,0},{2,3},{3,2},{4,5},{5,4},{6,7},{7,6},{8,9},{9,8},{10,11... | collective-permute-start | bytes 589832 | tf_op jit(solution)/shard_map/ppermute | solution.py:19
  2.1 3.6 %collective-permute-start = (f32[96,512]{1,0:T(8,128)}, f32[96,512]{1,0:T(8,128)S(1)}, u32[]{:S(2)}, u32[]{:S(2)}) collective-permute-start(f32[96,512]{1,0:T(8,128)} %shard_map.37.refs_0_), channel_id=1, source_target_pairs={{0,8},{1,9},{2,10},{3,11},{4,12},{5,13},{6,14},{7,15},{8,0},{9,1},... | collective-permute-start | bytes 589832 | tf_op jit(solution)/shard_map/ppermute | solution.py:19
  5.7 1.5 %collective-permute-start.4 = (f32[96,512]{1,0:T(8,128)}, f32[96,512]{1,0:T(8,128)S(1)}, u32[]{:S(2)}, u32[]{:S(2)}) collective-permute-start(f32[96,512]{1,0:T(8,128)} %shard_map.37.refs_0_), channel_id=1, source_target_pairs={{0,2},{1,3},{2,0},{3,1},{4,6},{5,7},{6,4},{7,5},{8,10},{9,11},{10,... | collective-permute-start | bytes 589832 | tf_op jit(solution)/shard_map/ppermute | solution.py:19
  7.2 1.6 %collective-permute-start.6 = (f32[96,512]{1,0:T(8,128)}, f32[96,512]{1,0:T(8,128)S(1)}, u32[]{:S(2)}, u32[]{:S(2)}) collective-permute-start(f32[96,512]{1,0:T(8,128)} %shard_map.37.refs_0_), channel_id=1, source_target_pairs={{0,4},{1,5},{2,6},{3,7},{4,0},{5,1},{6,2},{7,3},{8,12},{9,13},{10,... | collective-permute-start | bytes 589832 | tf_op jit(solution)/shard_map/ppermute | solution.py:19
  8.8 0.0 collective-permute-done.1.refs_1_.refs_4_
  8.8 0.0 copy-start
  8.8 1.0 %copy-done = f32[96,512]{1,0:T(8,128)S(1)} copy-done((f32[96,512]{1,0:T(8,128)S(1)}, f32[96,512]{1,0:T(8,128)}, u32[]{:S(2)}) %copy-start) | copy-done | bytes 196632
  9.7 0.0 copy-start.1
  9.7 1.6 %shard_map.38.refs_5_ = f32[64,512]{1,0:T(8,128)S(1)} custom-call(f32[96,512]{1,0:T(8,128)S(1)} %copy-done, f32[96,512]{1,0:T(8,128)S(1)} %collective-permute-done.1.refs_1_.refs_4_), custom_call_target="tpu_custom_call" | custom-call | tf_op jit(solution)/shard_map/pallas_call | solution.py:121
  11.3 4.4 %collective-permute-done.refs_1_ = f32[96,512]{1,0:T(8,128)S(1)} collective-permute-done((f32[96,512]{1,0:T(8,128)}, f32[96,512]{1,0:T(8,128)S(1)}, u32[]{:S(2)}, u32[]{:S(2)}) %collective-permute-start) | collective-permute-done | bytes 196640 | tf_op jit(solution)/shard_map/ppermute | solution.py:19
  15.8 0.0 collective-permute-start.3
  15.8 0.0 collective-permute-done.4.refs_2_
  15.8 0.5 %collective-permute-start.5 = (f32[96,512]{1,0:T(8,128)S(1)}, f32[96,512]{1,0:T(8,128)S(1)}, u32[]{:S(2)}, u32[]{:S(2)}) collective-permute-start(f32[96,512]{1,0:T(8,128)S(1)} %collective-permute-done.4.refs_2_), channel_id=1, source_target_pairs={{0,1},{1,0},{2,3},{3,2},{4,5},{5,4},{6,7},{7,6},{8,9},{9,8},{10,11... | collective-permute-start | bytes 589832 | tf_op jit(solution)/shard_map/ppermute | solution.py:19
  16.3 1.6 %collective-permute-start.2 = (f32[96,512]{1,0:T(8,128)S(1)}, f32[96,512]{1,0:T(8,128)S(1)}, u32[]{:S(2)}, u32[]{:S(2)}) collective-permute-start(f32[96,512]{1,0:T(8,128)S(1)} %collective-permute-done.refs_1_), channel_id=1, source_target_pairs={{0,2},{1,3},{2,0},{3,1},{4,6},{5,7},{6,4},{7,5},{8,10},{9,11},{10,... | collective-permute-start | bytes 589832 | tf_op jit(solution)/shard_map/ppermute | solution.py:19
  17.8 0.0 collective-permute-done.6.refs_3_.refs_2_.refs_0_
  17.8 0.0 copy-done.1
  17.9 4.2 %shard_map.39 = (f32[64,512]{1,0:T(8,128)S(1)}, f32[64,512]{1,0:T(8,128)S(1)}) custom-call(f32[96,512]{1,0:T(8,128)S(1)} %copy-done.1, f32[96,512]{1,0:T(8,128)S(1)} %collective-permute-done.refs_1_, f32[96,512]{1,0:T(8,128)S(1)} %collective-permute-done.4.refs_2_, f32[96,512]{1,0:T(8,128)S(1)} %collective-permute-done.6.refs_3_.refs_2_.refs_0_, ...), custom_call_target="tpu_custom_call" | custom-call | tf_op jit(solution)/shard_map/pallas_call | solution.py:121
  22.0 0.0 collective-permute-done.3.refs_1_
  22.1 0.0 collective-permute-done.5.refs_2_
  22.1 2.9 %shard_map.40 = (f32[64,512]{1,0:T(8,128)S(1)}, f32[64,512]{1,0:T(8,128)S(1)}) custom-call(f32[96,512]{1,0:T(8,128)S(1)} %copy-done.1, f32[96,512]{1,0:T(8,128)S(1)} %collective-permute-done.3.refs_1_, f32[96,512]{1,0:T(8,128)S(1)} %collective-permute-done.5.refs_2_, f32[96,512]{1,0:T(8,128)S(1)} %collective-permute-done.6.refs_3_.refs_2_.refs_0_, ...), custom_call_target="tpu_custom_call" | custom-call | tf_op jit(solution)/shard_map/pallas_call | solution.py:121
  25.0 0.0 collective-permute-done.2.refs_1_
  25.0 0.1 collective-permute-start.7
  25.1 1.7 %shard_map.41 = (f32[64,512]{1,0:T(8,128)S(1)}, f32[64,512]{1,0:T(8,128)S(1)}) custom-call(f32[96,512]{1,0:T(8,128)S(1)} %copy-done.1, f32[96,512]{1,0:T(8,128)S(1)} %collective-permute-done.2.refs_1_, f32[96,512]{1,0:T(8,128)S(1)} %collective-permute-done.6.refs_3_.refs_2_.refs_0_, f32[64,512]{1,0:T(8,128)S(1)} %get-tuple-element.23.refs_3_, ...), custom_call_target="tpu_custom_call" | custom-call | tf_op jit(solution)/shard_map/pallas_call | solution.py:121
  26.8 0.0 collective-permute-done.7.refs_1_
  26.8 1.0 %shard_map.43 = f32[64,512]{1,0:T(8,128)S(1)} custom-call(f32[96,512]{1,0:T(8,128)S(1)} %collective-permute-done.6.refs_3_.refs_2_.refs_0_, f32[96,512]{1,0:T(8,128)S(1)} %collective-permute-done.7.refs_1_, f32[64,512]{1,0:T(8,128)S(1)} %get-tuple-element.26.refs_2_), custom_call_target="tpu_custom_call" | custom-call | tf_op jit(solution)/shard_map/pallas_call | solution.py:121
  27.8 0.7 %collective-permute-start.8 = (f32[64,512]{1,0:T(8,128)S(1)}, f32[64,512]{1,0:T(8,128)S(1)}, u32[]{:S(2)}, u32[]{:S(2)}) collective-permute-start(f32[64,512]{1,0:T(8,128)S(1)} %shard_map.43), channel_id=1, source_target_pairs={{0,4},{1,5},{2,6},{3,7},{4,0},{5,1},{6,2},{7,3},{8,12},{9,13},{10,... | collective-permute-start | bytes 393224 | tf_op jit(solution)/shard_map/ppermute | solution.py:19
  28.5 1.0 %shard_map.42 = f32[64,512]{1,0:T(8,128)S(1)} custom-call(f32[96,512]{1,0:T(8,128)S(1)} %copy-done.1, f32[96,512]{1,0:T(8,128)S(1)} %collective-permute-done.7.refs_1_, f32[64,512]{1,0:T(8,128)S(1)} %get-tuple-element.25.refs_2_), custom_call_target="tpu_custom_call" | custom-call | tf_op jit(solution)/shard_map/pallas_call | solution.py:121
  29.5 4.2 %collective-permute-done.8 = f32[64,512]{1,0:T(8,128)S(1)} collective-permute-done((f32[64,512]{1,0:T(8,128)S(1)}, f32[64,512]{1,0:T(8,128)S(1)}, u32[]{:S(2)}, u32[]{:S(2)}) %collective-permute-start.8) | collective-permute-done | bytes 131104 | tf_op jit(solution)/shard_map/ppermute | solution.py:19
  33.7 0.7 %add.3 = f32[64,512]{1,0:T(8,128)} add(f32[64,512]{1,0:T(8,128)S(1)} %shard_map.42, f32[64,512]{1,0:T(8,128)S(1)} %collective-permute-done.8) | non-fusion elementwise | flops 32768 | bytes 393216 | tf_op jit(solution)/shard_map/add | solution.py:180
Async XLA Ops:
  1.6 7.1 %collective-permute-start.1 = (f32[96,512]{1,0:T(8,128)}, f32[96,512]{1,0:T(8,128)S(1)}, u32[]{:S(2)}, u32[]{:S(2)}) collective-permute-start(f32[96,512]{1,0:T(8,128)} %shard_map.37.refs_0_), channel_id=1, source_target_pairs={{0,1},{1,0},{2,3},{3,2},{4,5},{5,4},{6,7},{7,6},{8,9},{9,8},{10,11... | collective-permute-start | bytes 589832 | tf_op jit(solution)/shard_map/ppermute | solution.py:19
  2.1 13.7 %collective-permute-start = (f32[96,512]{1,0:T(8,128)}, f32[96,512]{1,0:T(8,128)S(1)}, u32[]{:S(2)}, u32[]{:S(2)}) collective-permute-start(f32[96,512]{1,0:T(8,128)} %shard_map.37.refs_0_), channel_id=1, source_target_pairs={{0,8},{1,9},{2,10},{3,11},{4,12},{5,13},{6,14},{7,15},{8,0},{9,1},... | collective-permute-start | bytes 589832 | tf_op jit(solution)/shard_map/ppermute | solution.py:19
  5.7 10.1 %collective-permute-start.4 = (f32[96,512]{1,0:T(8,128)}, f32[96,512]{1,0:T(8,128)S(1)}, u32[]{:S(2)}, u32[]{:S(2)}) collective-permute-start(f32[96,512]{1,0:T(8,128)} %shard_map.37.refs_0_), channel_id=1, source_target_pairs={{0,2},{1,3},{2,0},{3,1},{4,6},{5,7},{6,4},{7,5},{8,10},{9,11},{10,... | collective-permute-start | bytes 589832 | tf_op jit(solution)/shard_map/ppermute | solution.py:19
  7.2 10.7 %collective-permute-start.6 = (f32[96,512]{1,0:T(8,128)}, f32[96,512]{1,0:T(8,128)S(1)}, u32[]{:S(2)}, u32[]{:S(2)}) collective-permute-start(f32[96,512]{1,0:T(8,128)} %shard_map.37.refs_0_), channel_id=1, source_target_pairs={{0,4},{1,5},{2,6},{3,7},{4,0},{5,1},{6,2},{7,3},{8,12},{9,13},{10,... | collective-permute-start | bytes 589832 | tf_op jit(solution)/shard_map/ppermute | solution.py:19
  8.8 1.0 %copy-start = (f32[96,512]{1,0:T(8,128)S(1)}, f32[96,512]{1,0:T(8,128)}, u32[]{:S(2)}) copy-start(f32[96,512]{1,0:T(8,128)} %shard_map.37.refs_0_) | copy-start | bytes 589828
  9.7 8.1 %copy-start.1 = (f32[96,512]{1,0:T(8,128)S(1)}, f32[96,512]{1,0:T(8,128)}, u32[]{:S(2)}) copy-start(f32[96,512]{1,0:T(8,128)} %shard_map.37.refs_0_) | copy-start | bytes 589828
  15.8 6.3 %collective-permute-start.3 = (f32[96,512]{1,0:T(8,128)S(1)}, f32[96,512]{1,0:T(8,128)S(1)}, u32[]{:S(2)}, u32[]{:S(2)}) collective-permute-start(f32[96,512]{1,0:T(8,128)S(1)} %collective-permute-done.refs_1_), channel_id=1, source_target_pairs={{0,1},{1,0},{2,3},{3,2},{4,5},{5,4},{6,7},{7,6},{8,9},{9,8},{10,11... | collective-permute-start | bytes 589832 | tf_op jit(solution)/shard_map/ppermute | solution.py:19
  15.8 6.3 %collective-permute-start.5 = (f32[96,512]{1,0:T(8,128)S(1)}, f32[96,512]{1,0:T(8,128)S(1)}, u32[]{:S(2)}, u32[]{:S(2)}) collective-permute-start(f32[96,512]{1,0:T(8,128)S(1)} %collective-permute-done.4.refs_2_), channel_id=1, source_target_pairs={{0,1},{1,0},{2,3},{3,2},{4,5},{5,4},{6,7},{7,6},{8,9},{9,8},{10,11... | collective-permute-start | bytes 589832 | tf_op jit(solution)/shard_map/ppermute | solution.py:19
  16.3 8.7 %collective-permute-start.2 = (f32[96,512]{1,0:T(8,128)S(1)}, f32[96,512]{1,0:T(8,128)S(1)}, u32[]{:S(2)}, u32[]{:S(2)}) collective-permute-start(f32[96,512]{1,0:T(8,128)S(1)} %collective-permute-done.refs_1_), channel_id=1, source_target_pairs={{0,2},{1,3},{2,0},{3,1},{4,6},{5,7},{6,4},{7,5},{8,10},{9,11},{10,... | collective-permute-start | bytes 589832 | tf_op jit(solution)/shard_map/ppermute | solution.py:19
  25.0 1.7 %collective-permute-start.7 = (f32[96,512]{1,0:T(8,128)S(1)}, f32[96,512]{1,0:T(8,128)S(1)}, u32[]{:S(2)}, u32[]{:S(2)}) collective-permute-start(f32[96,512]{1,0:T(8,128)S(1)} %collective-permute-done.2.refs_1_), channel_id=1, source_target_pairs={{0,1},{1,0},{2,3},{3,2},{4,5},{5,4},{6,7},{7,6},{8,9},{9,8},{10,11... | collective-permute-start | bytes 589832 | tf_op jit(solution)/shard_map/ppermute | solution.py:19
  27.8 6.0 %collective-permute-start.8 = (f32[64,512]{1,0:T(8,128)S(1)}, f32[64,512]{1,0:T(8,128)S(1)}, u32[]{:S(2)}, u32[]{:S(2)}) collective-permute-start(f32[64,512]{1,0:T(8,128)S(1)} %shard_map.43), channel_id=1, source_target_pairs={{0,4},{1,5},{2,6},{3,7},{4,0},{5,1},{6,2},{7,3},{8,12},{9,13},{10,... | collective-permute-start | bytes 393224 | tf_op jit(solution)/shard_map/ppermute | solution.py:19

commit v8 on v6

--- a/solution.py
+++ b/solution.py
@@ -69,7 +69,7 @@
     return jnp.dot(left, right, preferred_element_type=jnp.float32)
 
 
-def block_terms(mine, theirs, width):
+def pulled_terms(mine, theirs, width):
     dist_mine, pair_mine = mine
     dist_theirs, pair_theirs, pull = theirs
     coupling = jnp.exp2(product(dist_theirs, dist_mine)) * product(pair_theirs, pair_mine)
@@ -80,6 +80,11 @@
     return pulled, from_high[width : width + 1] + from_low[width : width + 1]
 
 
+def stacked(theirs):
+    dist, pair, pull = zip(*theirs)
+    return jnp.concatenate(dist, 0), jnp.concatenate(pair, 0), jnp.concatenate(pull, 1)
+
+
 def kernel(width, vectors, jobs, count, *refs):
     blocks, refs = refs[:count], refs[count:]
     before, out = refs[: -len(jobs)], refs[-len(jobs) :]
@@ -87,9 +92,7 @@
     theirs = {place: prepared_theirs(blocks[place][...], width, vectors) for place in used}
     for place, (row, columns) in enumerate(jobs):
         mine = prepared_mine(blocks[row][...], width, vectors)
-        terms = [block_terms(mine, theirs[column], width) for column in columns]
-        pulled = sum(term[0] for term in terms)
-        sums = sum(term[1] for term in terms)
+        pulled, sums = pulled_terms(mine, stacked([theirs[column] for column in columns]), width)
         value = (pulled - blocks[row][:width] * sums) / width
         out[place][...] = value + before[place][...] if place < len(before) else value
 
@@ -115,6 +118,11 @@
             in_specs=[pl.BlockSpec(memory_space=pltpu.VMEM)] * len(operands),
             out_specs=[pl.BlockSpec(memory_space=pltpu.VMEM)] * len(out_shape),
             compiler_params=pltpu.CompilerParams(vmem_limit_bytes=VMEM_LIMIT),
+            cost_estimate=pl.CostEstimate(
+                flops=2 * points * points * 2048 * sum(len(columns) for _, columns in jobs),
+                bytes_accessed=4 * points * 96 * len(operands),
+                transcendentals=points * points,
+            ),
         )(*operands)
     )
 
@@ -143,32 +151,39 @@
     swap = lambda value, bit: swapped(value, "blk", bit)
     tied = lax.optimization_barrier
 
-    top = count // 2
-    beside = [1 << place for place in range(1, count.bit_length() - 2) if place != 2]
+    beside = [1 << place for place in range(3, count.bit_length() - 1)]
     mine = packed(features, solves, probes)
     sibling = swap(mine, 1)
-    far = swap(mine, top)
-    near = swap(mine, 4)
-    direct = [swap(mine, bit) for bit in beside]
+    far = swap(mine, beside[-1])
+    sent, sibling = tied((mine, sibling))
+    near_y = swap(sent, 2)
+    near_z = swap(sent, 4)
 
-    here = terms([(mine, [mine, sibling])])
-    far, here[0] = tied((far, here[0]))
-    last = []
-    for bit in beside:
-        last += [swap(block, bit) for block in [far] + last]
-    siblings = [swap(block, 1) for block in [far] + direct]
-    both = terms(
-        [(mine, [far] + direct), (near, [mine, sibling, far] + direct)],
-        before=here,
-    )
-    both = terms([(mine, siblings), (near, siblings)], before=both)
-    last[0], *both = tied((last[0], *both))
-    last_siblings = [swap(block, 1) for block in last]
-    here, there = terms([(mine, last), (near, last)], before=both)
-    (there,) = terms([(near, last_siblings)], before=[there])
-    from_near = swap(there, 4)
-    (here,) = terms([(mine, last_siblings)], before=[here])
-    return here + from_near
+    home = [mine, sibling]
+    (here,) = terms([(mine, home)])
+    near_z, near_y, here = tied((near_z, near_y, here))
+    near_both = swap(near_z, 2)
+    toward_y, toward_z = terms([(near_y, home), (near_z, home)])
+    near_both, toward_y = tied((near_both, toward_y))
+    (toward_both,) = terms([(near_both, home)])
+
+    far, toward_both = tied((far, toward_both))
+    columns = [far]
+    for bit in reversed(beside[:-1]):
+        columns += [swap(block, bit) for block in [mine] + columns]
+    for block in columns:
+        other = swap(block, 1)
+        toward_both, toward_y, toward_z = terms(
+            [(near_both, [block]), (near_y, [block]), (near_z, [block])],
+            before=[toward_both, toward_y, toward_z],
+        )
+        other, toward_both = tied((other, toward_both))
+        toward_both, toward_y, toward_z = terms(
+            [(near_both, [other]), (near_y, [other]), (near_z, [other])],
+            before=[toward_both, toward_y, toward_z],
+        )
+        (here,) = terms([(mine, [block, other])], before=[here])
+    return here + swap(toward_both, 6) + swap(toward_y, 2) + swap(toward_z, 4)
 
 
 def solution(mesh):

time: 33 us -> 38.7 us (1.17)
  waiting for transfers between devices: 9.23 us -> 14.7 us
  starting transfers between devices: 10 us -> 11.3 us
  Pallas kernels: 11.9 us -> 10.8 us
    ppermute x9, waiting for transfers between devices: 9.23 us -> 14.7 us  [swapped(): lax.ppermute(value, axis, [(source, source ^ bit) for source in range(cou...]
    ppermute x9, starting transfers between devices: 10 us -> 11.3 us  [swapped(): lax.ppermute(value, axis, [(source, source ^ bit) for source in range(cou...]
    pallas_call x6, Pallas kernels: 10.3 us -> 9.15 us  [pair_terms(): pl.pallas_call(functools.partial(kernel, width, vectors, placed, len(bloc...]
  transfers between devices with their start and end apart: 9 -> 9, of which waited for: 3 -> 5; matrix products, arithmetic and copies ran while one was open for 0% -> 0% of each run, Pallas kernels for 29% -> 19%
where the time goes in v8:
time: 38.7 us; the launch traced here: 38.5 us
  waiting for transfers between devices  14.7 us (38%)
  starting transfers between devices  11.3 us (29%)
  Pallas kernels  10.8 us (28%)
  local copies, waits for them, and re-layouts  0.96 us (2%)
  other arithmetic  0.69 us (2%)
    ppermute x9, waiting for transfers between devices, swapped(): lax.ppermute(value, axis, [(source, source ^ bit) for source in range(cou...  14.7 us
    ppermute x9, starting transfers between devices, swapped(): lax.ppermute(value, axis, [(source, source ^ bit) for source in range(cou...  11.3 us
    pallas_call x6, Pallas kernels, pair_terms(): pl.pallas_call(functools.partial(kernel, width, vectors, placed, len(bloc...  9.15 us
    pallas_call x1, Pallas kernels, packed(): pl.pallas_call(body, out_shape=jax.ShapeDtypeStruct((width + 2 * vectors,...  1.62 us
    unnamed x4, local copies, waits for them, and re-layouts  0.96 us
  transfers between devices with their start and end apart: 9, of which 5 were waited for; matrix products, arithmetic and copies ran while one was open for 0% of the time, Pallas kernels for 19%

profile of v8, /device:TPU:0, one launch (start us, length us, event | category | flops | bytes accessed | tf_op | source)
XLA Modules:
  0.0 38.5 jit_solution(6980846379781597892)
XLA Ops:
  0.0 1.6 %shard_map.37.refs_0_.refs_1_ = f32[96,512]{1,0:T(8,128)} custom-call(f32[64,512]{1,0:T(8,128)} %features_ref.1, f32[16,512]{1,0:T(8,128)} %solves_ref.1, f32[16,512]{1,0:T(8,128)} %probes_ref.1), custom_call_target="tpu_custom_call" | custom-call | tf_op jit(solution)/shard_map/pallas_call | solution.py:139
  1.6 0.5 %collective-permute-start.1 = (f32[96,512]{1,0:T(8,128)}, f32[96,512]{1,0:T(8,128)S(1)}, u32[]{:S(2)}, u32[]{:S(2)}) collective-permute-start(f32[96,512]{1,0:T(8,128)} %shard_map.37.refs_0_.refs_1_), channel_id=1, source_target_pairs={{0,1},{1,0},{2,3},{3,2},{4,5},{5,4},{6,7},{7,6},{8,9},{9,8},{10,11... | collective-permute-start | bytes 589832 | tf_op jit(solution)/shard_map/ppermute | solution.py:18
  2.1 3.6 %collective-permute-start = (f32[96,512]{1,0:T(8,128)}, f32[96,512]{1,0:T(8,128)S(1)}, u32[]{:S(2)}, u32[]{:S(2)}) collective-permute-start(f32[96,512]{1,0:T(8,128)} %shard_map.37.refs_0_.refs_1_), channel_id=1, source_target_pairs={{0,8},{1,9},{2,10},{3,11},{4,12},{5,13},{6,14},{7,15},{8,0},{9,1},... | collective-permute-start | bytes 589832 | tf_op jit(solution)/shard_map/ppermute | solution.py:18
  5.7 0.0 collective-permute-done.1.refs_1_.refs_2_
  5.7 1.5 %collective-permute-start.3 = (f32[96,512]{1,0:T(8,128)}, f32[96,512]{1,0:T(8,128)S(1)}, u32[]{:S(2)}, u32[]{:S(2)}) collective-permute-start(f32[96,512]{1,0:T(8,128)} %shard_map.37.refs_0_.refs_1_), channel_id=1, source_target_pairs={{0,2},{1,3},{2,0},{3,1},{4,6},{5,7},{6,4},{7,5},{8,10},{9,11},{10,... | collective-permute-start | bytes 589832 | tf_op jit(solution)/shard_map/ppermute | solution.py:18
  7.2 1.6 %collective-permute-start.2 = (f32[96,512]{1,0:T(8,128)}, f32[96,512]{1,0:T(8,128)S(1)}, u32[]{:S(2)}, u32[]{:S(2)}) collective-permute-start(f32[96,512]{1,0:T(8,128)} %shard_map.37.refs_0_.refs_1_), channel_id=1, source_target_pairs={{0,4},{1,5},{2,6},{3,7},{4,0},{5,1},{6,2},{7,3},{8,12},{9,13},{10,... | collective-permute-start | bytes 589832 | tf_op jit(solution)/shard_map/ppermute | solution.py:18
  8.8 0.0 copy-start
  8.8 1.0 %copy-done = f32[96,512]{1,0:T(8,128)S(1)} copy-done((f32[96,512]{1,0:T(8,128)S(1)}, f32[96,512]{1,0:T(8,128)}, u32[]{:S(2)}) %copy-start) | copy-done | bytes 196632
  9.7 0.0 copy-start.1
  9.7 1.1 %shard_map.38.refs_3_ = f32[64,512]{1,0:T(8,128)S(1)} custom-call(f32[96,512]{1,0:T(8,128)S(1)} %copy-done, f32[96,512]{1,0:T(8,128)S(1)} %collective-permute-done.1.refs_1_.refs_2_), custom_call_target="tpu_custom_call" | custom-call | flops 2147483648 | bytes 393216 | tf_op jit(solution)/shard_map/pallas_call | solution.py:115
  10.8 2.1 %collective-permute-done.3.refs_0_.refs_2_ = f32[96,512]{1,0:T(8,128)S(1)} collective-permute-done((f32[96,512]{1,0:T(8,128)}, f32[96,512]{1,0:T(8,128)S(1)}, u32[]{:S(2)}, u32[]{:S(2)}) %collective-permute-start.3) | collective-permute-done | bytes 196640 | tf_op jit(solution)/shard_map/ppermute | solution.py:18
  12.9 4.3 %collective-permute-done.2.refs_3_ = f32[96,512]{1,0:T(8,128)S(1)} collective-permute-done((f32[96,512]{1,0:T(8,128)}, f32[96,512]{1,0:T(8,128)S(1)}, u32[]{:S(2)}, u32[]{:S(2)}) %collective-permute-start.2) | collective-permute-done | bytes 196640 | tf_op jit(solution)/shard_map/ppermute | solution.py:18
  17.2 0.6 %collective-permute-start.4 = (f32[96,512]{1,0:T(8,128)S(1)}, f32[96,512]{1,0:T(8,128)S(1)}, u32[]{:S(2)}, u32[]{:S(2)}) collective-permute-start(f32[96,512]{1,0:T(8,128)S(1)} %collective-permute-done.2.refs_3_), channel_id=1, source_target_pairs={{0,2},{1,3},{2,0},{3,1},{4,6},{5,7},{6,4},{7,5},{8,10},{9,11},{10,... | collective-permute-start | bytes 589832 | tf_op jit(solution)/shard_map/ppermute | solution.py:18
  17.8 0.0 copy-done.1
  17.8 2.0 %shard_map.39 = (f32[64,512]{1,0:T(8,128)S(1)}, f32[64,512]{1,0:T(8,128)S(1)}) custom-call(f32[96,512]{1,0:T(8,128)S(1)} %collective-permute-done.3.refs_0_.refs_2_, f32[96,512]{1,0:T(8,128)S(1)} %copy-done.1, f32[96,512]{1,0:T(8,128)S(1)} %collective-permute-done.1.refs_1_.refs_2_, f32[96,512]{1,0:T(8,128)S(1)} %collective-permute-done.2.refs_3_), custom_call_target="tpu_custom_call" | custom-call | flops 4294967296 | bytes 786432 | tf_op jit(solution)/shard_map/pallas_call | solution.py:115
  19.8 3.3 %collective-permute-done.4.refs_0_ = f32[96,512]{1,0:T(8,128)S(1)} collective-permute-done((f32[96,512]{1,0:T(8,128)S(1)}, f32[96,512]{1,0:T(8,128)S(1)}, u32[]{:S(2)}, u32[]{:S(2)}) %collective-permute-start.4) | collective-permute-done | bytes 196640 | tf_op jit(solution)/shard_map/ppermute | solution.py:18
  23.1 1.1 %shard_map.40.refs_4_ = f32[64,512]{1,0:T(8,128)S(1)} custom-call(f32[96,512]{1,0:T(8,128)S(1)} %collective-permute-done.4.refs_0_, f32[96,512]{1,0:T(8,128)S(1)} %copy-done.1, f32[96,512]{1,0:T(8,128)S(1)} %collective-permute-done.1.refs_1_.refs_2_), custom_call_target="tpu_custom_call" | custom-call | flops 2147483648 | bytes 589824 | tf_op jit(solution)/shard_map/pallas_call | solution.py:115
  24.2 0.0 collective-permute-done.refs_1_
  24.2 0.1 collective-permute-start.5
  24.3 1.9 %shard_map.41 = (f32[64,512]{1,0:T(8,128)S(1)}, f32[64,512]{1,0:T(8,128)S(1)}, f32[64,512]{1,0:T(8,128)S(1)}) custom-call(f32[96,512]{1,0:T(8,128)S(1)} %collective-permute-done.4.refs_0_, f32[96,512]{1,0:T(8,128)S(1)} %collective-permute-done.refs_1_, f32[96,512]{1,0:T(8,128)S(1)} %collective-permute-done.3.refs_0_.refs_2_, ...), custom_call_target="tpu_custom_call" | custom-call | flops 3221225472 | bytes 1376256 | tf_op jit(solution)/shard_map/pallas_call | solution.py:115
  26.2 0.0 collective-permute-done.5.refs_2_.refs_1_
  26.2 1.9 %shard_map.43 = (f32[64,512]{1,0:T(8,128)S(1)}, f32[64,512]{1,0:T(8,128)S(1)}, f32[64,512]{1,0:T(8,128)S(1)}) custom-call(f32[96,512]{1,0:T(8,128)S(1)} %collective-permute-done.4.refs_0_, f32[96,512]{1,0:T(8,128)S(1)} %collective-permute-done.5.refs_2_.refs_1_, f32[96,512]{1,0:T(8,128)S(1)} %collective-permute-done.3.refs_0_.refs_2_, ...), custom_call_target="tpu_custom_call" | custom-call | flops 3221225472 | bytes 1376256 | tf_op jit(solution)/shard_map/pallas_call | solution.py:115
  28.1 1.9 %collective-permute-start.6 = (f32[64,512]{1,0:T(8,128)S(1)}, f32[64,512]{1,0:T(8,128)S(1)}, u32[]{:S(2)}, u32[]{:S(2)}) collective-permute-start(f32[64,512]{1,0:T(8,128)S(1)} %get-tuple-element.40), channel_id=1, source_target_pairs={{0,6},{1,7},{2,4},{3,5},{4,2},{5,3},{6,0},{7,1},{8,14},{9,15},{10,... | collective-permute-start | bytes 393224 | tf_op jit(solution)/shard_map/ppermute | solution.py:18
  30.0 0.5 %collective-permute-start.7 = (f32[64,512]{1,0:T(8,128)S(1)}, f32[64,512]{1,0:T(8,128)S(1)}, u32[]{:S(2)}, u32[]{:S(2)}) collective-permute-start(f32[64,512]{1,0:T(8,128)S(1)} %get-tuple-element.41), channel_id=1, source_target_pairs={{0,2},{1,3},{2,0},{3,1},{4,6},{5,7},{6,4},{7,5},{8,10},{9,11},{10,... | collective-permute-start | bytes 393224 | tf_op jit(solution)/shard_map/ppermute | solution.py:18
  30.6 1.1 %collective-permute-start.8 = (f32[64,512]{1,0:T(8,128)S(1)}, f32[64,512]{1,0:T(8,128)S(1)}, u32[]{:S(2)}, u32[]{:S(2)}) collective-permute-start(f32[64,512]{1,0:T(8,128)S(1)} %get-tuple-element.42), channel_id=1, source_target_pairs={{0,4},{1,5},{2,6},{3,7},{4,0},{5,1},{6,2},{7,3},{8,12},{9,13},{10,... | collective-permute-start | bytes 393224 | tf_op jit(solution)/shard_map/ppermute | solution.py:18
  31.7 1.1 %shard_map.42 = f32[64,512]{1,0:T(8,128)S(1)} custom-call(f32[96,512]{1,0:T(8,128)S(1)} %copy-done.1, f32[96,512]{1,0:T(8,128)S(1)} %collective-permute-done.refs_1_, f32[96,512]{1,0:T(8,128)S(1)} %collective-permute-done.5.refs_2_.refs_1_, f32[64,512]{1,0:T(8,128)S(1)} %shard_map.38.refs_3_), custom_call_target="tpu_custom_call" | custom-call | flops 2147483648 | bytes 786432 | tf_op jit(solution)/shard_map/pallas_call | solution.py:115
  32.8 2.6 %collective-permute-done.6 = f32[64,512]{1,0:T(8,128)S(1)} collective-permute-done((f32[64,512]{1,0:T(8,128)S(1)}, f32[64,512]{1,0:T(8,128)S(1)}, u32[]{:S(2)}, u32[]{:S(2)}) %collective-permute-start.6) | collective-permute-done | bytes 131104 | tf_op jit(solution)/shard_map/ppermute | solution.py:18
  35.4 2.4 %collective-permute-done.7 = f32[64,512]{1,0:T(8,128)S(1)} collective-permute-done((f32[64,512]{1,0:T(8,128)S(1)}, f32[64,512]{1,0:T(8,128)S(1)}, u32[]{:S(2)}, u32[]{:S(2)}) %collective-permute-start.7) | collective-permute-done | bytes 131104 | tf_op jit(solution)/shard_map/ppermute | solution.py:18
  37.8 0.0 collective-permute-done.8
  37.8 0.7 %add_add_fusion = f32[64,512]{1,0:T(8,128)} fusion(f32[64,512]{1,0:T(8,128)S(1)} %collective-permute-done.8, f32[64,512]{1,0:T(8,128)S(1)} %collective-permute-done.7, f32[64,512]{1,0:T(8,128)S(1)} %shard_map.42, f32[64,512]{1,0:T(8,128)S(1)} %collective-permute-done.6), kind=kLoop, calls=%fused_computation | loop fusion | flops 98304 | bytes 655360 | tf_op jit(solution)/shard_map/add | solution.py:186
Async XLA Ops:
  1.6 4.0 %collective-permute-start.1 = (f32[96,512]{1,0:T(8,128)}, f32[96,512]{1,0:T(8,128)S(1)}, u32[]{:S(2)}, u32[]{:S(2)}) collective-permute-start(f32[96,512]{1,0:T(8,128)} %shard_map.37.refs_0_.refs_1_), channel_id=1, source_target_pairs={{0,1},{1,0},{2,3},{3,2},{4,5},{5,4},{6,7},{7,6},{8,9},{9,8},{10,11... | collective-permute-start | bytes 589832 | tf_op jit(solution)/shard_map/ppermute | solution.py:18
  2.1 22.2 %collective-permute-start = (f32[96,512]{1,0:T(8,128)}, f32[96,512]{1,0:T(8,128)S(1)}, u32[]{:S(2)}, u32[]{:S(2)}) collective-permute-start(f32[96,512]{1,0:T(8,128)} %shard_map.37.refs_0_.refs_1_), channel_id=1, source_target_pairs={{0,8},{1,9},{2,10},{3,11},{4,12},{5,13},{6,14},{7,15},{8,0},{9,1},... | collective-permute-start | bytes 589832 | tf_op jit(solution)/shard_map/ppermute | solution.py:18
  5.7 7.2 %collective-permute-start.3 = (f32[96,512]{1,0:T(8,128)}, f32[96,512]{1,0:T(8,128)S(1)}, u32[]{:S(2)}, u32[]{:S(2)}) collective-permute-start(f32[96,512]{1,0:T(8,128)} %shard_map.37.refs_0_.refs_1_), channel_id=1, source_target_pairs={{0,2},{1,3},{2,0},{3,1},{4,6},{5,7},{6,4},{7,5},{8,10},{9,11},{10,... | collective-permute-start | bytes 589832 | tf_op jit(solution)/shard_map/ppermute | solution.py:18
  7.2 10.0 %collective-permute-start.2 = (f32[96,512]{1,0:T(8,128)}, f32[96,512]{1,0:T(8,128)S(1)}, u32[]{:S(2)}, u32[]{:S(2)}) collective-permute-start(f32[96,512]{1,0:T(8,128)} %shard_map.37.refs_0_.refs_1_), channel_id=1, source_target_pairs={{0,4},{1,5},{2,6},{3,7},{4,0},{5,1},{6,2},{7,3},{8,12},{9,13},{10,... | collective-permute-start | bytes 589832 | tf_op jit(solution)/shard_map/ppermute | solution.py:18
  8.8 1.0 %copy-start = (f32[96,512]{1,0:T(8,128)S(1)}, f32[96,512]{1,0:T(8,128)}, u32[]{:S(2)}) copy-start(f32[96,512]{1,0:T(8,128)} %shard_map.37.refs_0_.refs_1_) | copy-start | bytes 589828
  9.7 8.0 %copy-start.1 = (f32[96,512]{1,0:T(8,128)S(1)}, f32[96,512]{1,0:T(8,128)}, u32[]{:S(2)}) copy-start(f32[96,512]{1,0:T(8,128)} %shard_map.37.refs_0_.refs_1_) | copy-start | bytes 589828
  17.2 5.9 %collective-permute-start.4 = (f32[96,512]{1,0:T(8,128)S(1)}, f32[96,512]{1,0:T(8,128)S(1)}, u32[]{:S(2)}, u32[]{:S(2)}) collective-permute-start(f32[96,512]{1,0:T(8,128)S(1)} %collective-permute-done.2.refs_3_), channel_id=1, source_target_pairs={{0,2},{1,3},{2,0},{3,1},{4,6},{5,7},{6,4},{7,5},{8,10},{9,11},{10,... | collective-permute-start | bytes 589832 | tf_op jit(solution)/shard_map/ppermute | solution.py:18
  24.2 2.0 %collective-permute-start.5 = (f32[96,512]{1,0:T(8,128)S(1)}, f32[96,512]{1,0:T(8,128)S(1)}, u32[]{:S(2)}, u32[]{:S(2)}) collective-permute-start(f32[96,512]{1,0:T(8,128)S(1)} %collective-permute-done.refs_1_), channel_id=1, source_target_pairs={{0,1},{1,0},{2,3},{3,2},{4,5},{5,4},{6,7},{7,6},{8,9},{9,8},{10,11... | collective-permute-start | bytes 589832 | tf_op jit(solution)/shard_map/ppermute | solution.py:18
  28.1 7.3 %collective-permute-start.6 = (f32[64,512]{1,0:T(8,128)S(1)}, f32[64,512]{1,0:T(8,128)S(1)}, u32[]{:S(2)}, u32[]{:S(2)}) collective-permute-start(f32[64,512]{1,0:T(8,128)S(1)} %get-tuple-element.40), channel_id=1, source_target_pairs={{0,6},{1,7},{2,4},{3,5},{4,2},{5,3},{6,0},{7,1},{8,14},{9,15},{10,... | collective-permute-start | bytes 393224 | tf_op jit(solution)/shard_map/ppermute | solution.py:18
  30.0 7.8 %collective-permute-start.7 = (f32[64,512]{1,0:T(8,128)S(1)}, f32[64,512]{1,0:T(8,128)S(1)}, u32[]{:S(2)}, u32[]{:S(2)}) collective-permute-start(f32[64,512]{1,0:T(8,128)S(1)} %get-tuple-element.41), channel_id=1, source_target_pairs={{0,2},{1,3},{2,0},{3,1},{4,6},{5,7},{6,4},{7,5},{8,10},{9,11},{10,... | collective-permute-start | bytes 393224 | tf_op jit(solution)/shard_map/ppermute | solution.py:18
  30.6 7.3 %collective-permute-start.8 = (f32[64,512]{1,0:T(8,128)S(1)}, f32[64,512]{1,0:T(8,128)S(1)}, u32[]{:S(2)}, u32[]{:S(2)}) collective-permute-start(f32[64,512]{1,0:T(8,128)S(1)} %get-tuple-element.42), channel_id=1, source_target_pairs={{0,4},{1,5},{2,6},{3,7},{4,0},{5,1},{6,2},{7,3},{8,12},{9,13},{10,... | collective-permute-start | bytes 393224 | tf_op jit(solution)/shard_map/ppermute | solution.py:18

commit v9 on v6

--- a/solution.py
+++ b/solution.py
@@ -10,6 +10,7 @@
 LOG2E = 1.4426950408889634
 NORM_ROWS = 16
 ONES_ROWS = 16
+STACK = 4
 VMEM_LIMIT = 24 << 20
 
 
@@ -69,7 +70,7 @@
     return jnp.dot(left, right, preferred_element_type=jnp.float32)
 
 
-def block_terms(mine, theirs, width):
+def pulled_terms(mine, theirs, width):
     dist_mine, pair_mine = mine
     dist_theirs, pair_theirs, pull = theirs
     coupling = jnp.exp2(product(dist_theirs, dist_mine)) * product(pair_theirs, pair_mine)
@@ -80,6 +81,11 @@
     return pulled, from_high[width : width + 1] + from_low[width : width + 1]
 
 
+def stacked(theirs):
+    dist, pair, pull = zip(*theirs)
+    return jnp.concatenate(dist, 0), jnp.concatenate(pair, 0), jnp.concatenate(pull, 1)
+
+
 def kernel(width, vectors, jobs, count, *refs):
     blocks, refs = refs[:count], refs[count:]
     before, out = refs[: -len(jobs)], refs[-len(jobs) :]
@@ -87,14 +93,16 @@
     theirs = {place: prepared_theirs(blocks[place][...], width, vectors) for place in used}
     for place, (row, columns) in enumerate(jobs):
         mine = prepared_mine(blocks[row][...], width, vectors)
-        terms = [block_terms(mine, theirs[column], width) for column in columns]
-        pulled = sum(term[0] for term in terms)
-        sums = sum(term[1] for term in terms)
+        parts = [
+            pulled_terms(mine, stacked([theirs[column] for column in columns[at : at + STACK]]), width)
+            for at in range(0, len(columns), STACK)
+        ]
+        pulled, sums = (sum(part) for part in zip(*parts))
         value = (pulled - blocks[row][:width] * sums) / width
         out[place][...] = value + before[place][...] if place < len(before) else value
 
 
-def pair_terms(jobs, width, vectors, before=()):
+def pair_terms(jobs, width, vectors, before=(), weight=2048):
     blocks = []
 
     def place(block):
@@ -115,6 +123,11 @@
             in_specs=[pl.BlockSpec(memory_space=pltpu.VMEM)] * len(operands),
             out_specs=[pl.BlockSpec(memory_space=pltpu.VMEM)] * len(out_shape),
             compiler_params=pltpu.CompilerParams(vmem_limit_bytes=VMEM_LIMIT),
+            cost_estimate=pl.CostEstimate(
+                flops=2 * points * points * weight * sum(len(columns) for _, columns in jobs),
+                bytes_accessed=4 * points * 96 * len(operands),
+                transcendentals=points * points,
+            ),
         )(*operands)
     )
 
@@ -143,31 +156,35 @@
     swap = lambda value, bit: swapped(value, "blk", bit)
     tied = lax.optimization_barrier
 
-    top = count // 2
-    beside = [1 << place for place in range(1, count.bit_length() - 2) if place != 2]
+    bits = [1 << place for place in range(count.bit_length() - 1)]
+    top, beside = bits[-1], [bit for bit in bits[:-1] if bit not in (1, 4)]
+    far_features = swap(features, top)
     mine = packed(features, solves, probes)
+    far_vectors = swap(mine[width:], top)
     sibling = swap(mine, 1)
-    far = swap(mine, top)
     near = swap(mine, 4)
     direct = [swap(mine, bit) for bit in beside]
 
-    here = terms([(mine, [mine, sibling])])
-    far, here[0] = tied((far, here[0]))
+    far_features, own = tied((far_features, mine))
+    (here,) = terms([(own, [own])], weight=512)
+    far_vectors, here = tied((far_vectors, here))
+    split = [far_features, far_vectors]
+    far = jnp.concatenate(split, 0)
     last = []
     for bit in beside:
-        last += [swap(block, bit) for block in [far] + last]
-    siblings = [swap(block, 1) for block in [far] + direct]
-    both = terms(
-        [(mine, [far] + direct), (near, [mine, sibling, far] + direct)],
-        before=here,
-    )
-    both = terms([(mine, siblings), (near, siblings)], before=both)
-    last[0], *both = tied((last[0], *both))
+        pieces = [split] + [[block[:width], block[width:]] for block in last]
+        last += [jnp.concatenate([swap(piece, bit) for piece in pair], 0) for pair in pieces]
+    first = [far] + direct
+    siblings = [swap(block, 1) for block in first]
+    (there,) = terms([(near, [mine, sibling] + first)], weight=64)
+    (there,) = terms([(near, siblings)], before=[there], weight=2048)
+    last[0], there = tied((last[0], there))
     last_siblings = [swap(block, 1) for block in last]
-    here, there = terms([(mine, last), (near, last)], before=both)
+    (there,) = terms([(near, last)], before=[there])
     (there,) = terms([(near, last_siblings)], before=[there])
     from_near = swap(there, 4)
-    (here,) = terms([(mine, last_siblings)], before=[here])
+    rest = [sibling] + first + siblings + last + last_siblings
+    (here,) = terms([(mine, rest)], before=[here])
     return here + from_near
 
 

time: 33 us -> 31 us (0.939)
  Pallas kernels: 11.9 us -> 10.5 us
  waiting for transfers between devices: 9.23 us -> 8.32 us
    pallas_call x6, Pallas kernels: 10.3 us -> 8.9 us  [pair_terms(): pl.pallas_call(functools.partial(kernel, width, vectors, placed, len(bloc...]
    unnamed x4 -> x3, local copies, waits for them, and re-layouts: 0.96 us -> 0.01 us
    ppermute x9 -> x11, waiting for transfers between devices: 9.23 us -> 8.32 us  [swapped(): lax.ppermute(value, axis, [(source, source ^ bit) for source in range(cou...]
    slice x0 -> x1, local copies, waits for them, and re-layouts: none -> 0.87 us  [local(): far_vectors = swap(mine[width:], top)]
    ppermute x9 -> x11, starting transfers between devices: 10 us -> 10.3 us  [swapped(): lax.ppermute(value, axis, [(source, source ^ bit) for source in range(cou...]
  transfers between devices with their start and end apart: 9 -> 11, of which waited for: 3 -> 5; matrix products, arithmetic and copies ran while one was open for 0% -> 3% of each run, Pallas kernels for 29% -> 28%
where the time goes in v9:
time: 31 us; the launch traced here: 30.8 us
  Pallas kernels  10.5 us (34%)
  starting transfers between devices  10.3 us (33%)
  waiting for transfers between devices  8.32 us (27%)
  local copies, waits for them, and re-layouts  0.89 us (3%)
  other arithmetic  0.69 us (2%)
    ppermute x11, starting transfers between devices, swapped(): lax.ppermute(value, axis, [(source, source ^ bit) for source in range(cou...  10.3 us
    pallas_call x6, Pallas kernels, pair_terms(): pl.pallas_call(functools.partial(kernel, width, vectors, placed, len(bloc...  8.9 us
    ppermute x11, waiting for transfers between devices, swapped(): lax.ppermute(value, axis, [(source, source ^ bit) for source in range(cou...  8.32 us
    pallas_call x1, Pallas kernels, packed(): pl.pallas_call(body, out_shape=jax.ShapeDtypeStruct((width + 2 * vectors,...  1.63 us
    slice x1, local copies, waits for them, and re-layouts, local(): far_vectors = swap(mine[width:], top)  0.87 us
    add x1, other arithmetic, local(): return here + from_near  0.67 us
  transfers between devices with their start and end apart: 11, of which 5 were waited for; matrix products, arithmetic and copies ran while one was open for 3% of the time, Pallas kernels for 28%

profile of v9, /device:TPU:0, one launch (start us, length us, event | category | flops | bytes accessed | tf_op | source)
XLA Modules:
  0.0 30.8 jit_solution(17499532982771134501)
XLA Ops:
  0.0 4.0 %collective-permute-start.1 = (f32[64,512]{1,0:T(8,128)}, f32[64,512]{1,0:T(8,128)S(1)}, u32[]{:S(2)}, u32[]{:S(2)}) collective-permute-start(f32[64,512]{1,0:T(8,128)} %features_ref.1), channel_id=1, source_target_pairs={{0,8},{1,9},{2,10},{3,11},{4,12},{5,13},{6,14},{7,15},{8,0},{9,1},... | collective-permute-start | bytes 393224 | tf_op jit(solution)/shard_map/ppermute | solution.py:19
  4.0 1.6 %shard_map.37.refs_0_.refs_1_ = f32[96,512]{1,0:T(8,128)} custom-call(f32[64,512]{1,0:T(8,128)} %features_ref.1, f32[16,512]{1,0:T(8,128)} %solves_ref.1, f32[16,512]{1,0:T(8,128)} %probes_ref.1), custom_call_target="tpu_custom_call" | custom-call | tf_op jit(solution)/shard_map/pallas_call | solution.py:144
  5.7 0.0 copy-start
  5.7 1.6 %collective-permute-start.8 = (f32[96,512]{1,0:T(8,128)}, f32[96,512]{1,0:T(8,128)S(1)}, u32[]{:S(2)}, u32[]{:S(2)}) collective-permute-start(f32[96,512]{1,0:T(8,128)} %shard_map.37.refs_0_.refs_1_), channel_id=1, source_target_pairs={{0,4},{1,5},{2,6},{3,7},{4,0},{5,1},{6,2},{7,3},{8,12},{9,13},{10,... | collective-permute-start | bytes 589832 | tf_op jit(solution)/shard_map/ppermute | solution.py:19
  7.3 1.5 %collective-permute-start.3 = (f32[96,512]{1,0:T(8,128)}, f32[96,512]{1,0:T(8,128)S(1)}, u32[]{:S(2)}, u32[]{:S(2)}) collective-permute-start(f32[96,512]{1,0:T(8,128)} %shard_map.37.refs_0_.refs_1_), channel_id=1, source_target_pairs={{0,2},{1,3},{2,0},{3,1},{4,6},{5,7},{6,4},{7,5},{8,10},{9,11},{10,... | collective-permute-start | bytes 589832 | tf_op jit(solution)/shard_map/ppermute | solution.py:19
  8.8 0.0 collective-permute-start
  8.8 0.9 %slice.4 = f32[32,512]{1,0:T(8,128)S(1)} slice(f32[96,512]{1,0:T(8,128)} %shard_map.37.refs_0_.refs_1_), slice={[64:96], [0:512]} | slice | bytes 131072 | tf_op jit(solution)/shard_map/slice | solution.py:163
  9.6 0.3 %collective-permute-start.2 = (f32[32,512]{1,0:T(8,128)S(1)}, f32[32,512]{1,0:T(8,128)S(1)}, u32[]{:S(2)}, u32[]{:S(2)}) collective-permute-start(f32[32,512]{1,0:T(8,128)S(1)} %slice.4), channel_id=1, source_target_pairs={{0,8},{1,9},{2,10},{3,11},{4,12},{5,13},{6,14},{7,15},{8,0},{9,1},... | collective-permute-start | bytes 196616 | tf_op jit(solution)/shard_map/ppermute | solution.py:19
  10.0 0.7 %collective-permute-done.1 = f32[64,512]{1,0:T(8,128)S(1)} collective-permute-done((f32[64,512]{1,0:T(8,128)}, f32[64,512]{1,0:T(8,128)S(1)}, u32[]{:S(2)}, u32[]{:S(2)}) %collective-permute-start.1) | collective-permute-done | bytes 131104 | tf_op jit(solution)/shard_map/ppermute | solution.py:19
  10.7 1.6 %collective-permute-start.6 = (f32[64,512]{1,0:T(8,128)S(1)}, f32[64,512]{1,0:T(8,128)S(1)}, u32[]{:S(2)}, u32[]{:S(2)}) collective-permute-start(f32[64,512]{1,0:T(8,128)S(1)} %collective-permute-done.1), channel_id=1, source_target_pairs={{0,2},{1,3},{2,0},{3,1},{4,6},{5,7},{6,4},{7,5},{8,10},{9,11},{10,... | collective-permute-start | bytes 393224 | tf_op jit(solution)/shard_map/ppermute | solution.py:19
  12.2 0.0 copy-done
  12.3 0.8 %shard_map.38.refs_8_ = f32[64,512]{1,0:T(8,128)S(1)} custom-call(f32[96,512]{1,0:T(8,128)S(1)} %copy-done), custom_call_target="tpu_custom_call" | custom-call | flops 268435456 | bytes 196608 | tf_op jit(solution)/shard_map/pallas_call | solution.py:120
  13.0 3.3 %collective-permute-done.2 = f32[32,512]{1,0:T(8,128)S(1)} collective-permute-done((f32[32,512]{1,0:T(8,128)S(1)}, f32[32,512]{1,0:T(8,128)S(1)}, u32[]{:S(2)}, u32[]{:S(2)}) %collective-permute-start.2) | collective-permute-done | bytes 65568 | tf_op jit(solution)/shard_map/ppermute | solution.py:19
  16.3 0.1 collective-permute-start.4
  16.4 0.0 collective-permute-done.3.refs_4_.refs_3_
  16.4 0.4 %collective-permute-start.5 = (f32[96,512]{1,0:T(8,128)S(1)}, f32[96,512]{1,0:T(8,128)S(1)}, u32[]{:S(2)}, u32[]{:S(2)}) collective-permute-start(f32[96,512]{1,0:T(8,128)S(1)} %collective-permute-done.3.refs_4_.refs_3_), channel_id=1, source_target_pairs={{0,1},{1,0},{2,3},{3,2},{4,5},{5,4},{6,7},{7,6},{8,9},{9,8},{10,11... | collective-permute-start | bytes 589832 | tf_op jit(solution)/shard_map/ppermute | solution.py:19
  16.8 0.0 collective-permute-done.8.refs_0_
  16.8 0.6 %collective-permute-start.7 = (f32[32,512]{1,0:T(8,128)S(1)}, f32[32,512]{1,0:T(8,128)S(1)}, u32[]{:S(2)}, u32[]{:S(2)}) collective-permute-start(f32[32,512]{1,0:T(8,128)S(1)} %collective-permute-done.2), channel_id=1, source_target_pairs={{0,2},{1,3},{2,0},{3,1},{4,6},{5,7},{6,4},{7,5},{8,10},{9,11},{10,... | collective-permute-start | bytes 196616 | tf_op jit(solution)/shard_map/ppermute | solution.py:19
  17.4 0.0 collective-permute-done.refs_2_.refs_1_
  17.4 2.0 %shard_map.39.refs_3_ = f32[64,512]{1,0:T(8,128)S(1)} custom-call(f32[96,512]{1,0:T(8,128)S(1)} %collective-permute-done.8.refs_0_, f32[96,512]{1,0:T(8,128)S(1)} %copy-done, f32[96,512]{1,0:T(8,128)S(1)} %collective-permute-done.refs_2_.refs_1_, f32[96,512]{1,0:T(8,128)S(1)} %constant_dynamic-update-slice_fusion.refs_3_.refs_2_, ...), custom_call_target="tpu_custom_call" | custom-call | flops 134217728 | bytes 983040 | tf_op jit(solution)/shard_map/pallas_call | solution.py:120
  19.5 1.6 %collective-permute-done.7 = f32[32,512]{1,0:T(8,128)S(1)} collective-permute-done((f32[32,512]{1,0:T(8,128)S(1)}, f32[32,512]{1,0:T(8,128)S(1)}, u32[]{:S(2)}, u32[]{:S(2)}) %collective-permute-start.7) | collective-permute-done | bytes 65568 | tf_op jit(solution)/shard_map/ppermute | solution.py:19
  21.1 0.0 collective-permute-done.6
  21.1 0.0 collective-permute-done.4.refs_1_.refs_4_
  21.1 0.0 collective-permute-done.5.refs_2_.refs_5_
  21.1 1.1 %shard_map.40.refs_2_ = f32[64,512]{1,0:T(8,128)S(1)} custom-call(f32[96,512]{1,0:T(8,128)S(1)} %collective-permute-done.8.refs_0_, f32[96,512]{1,0:T(8,128)S(1)} %collective-permute-done.4.refs_1_.refs_4_, f32[96,512]{1,0:T(8,128)S(1)} %collective-permute-done.5.refs_2_.refs_5_, f32[64,512]{1,0:T(8,128)S(1)} %shard_map.39.refs_3_), custom_call_target="tpu_custom_call" | custom-call | flops 2147483648 | bytes 786432 | tf_op jit(solution)/shard_map/pallas_call | solution.py:120
  22.3 0.1 collective-permute-start.9
  22.4 0.8 %shard_map.42.refs_2_ = f32[64,512]{1,0:T(8,128)S(1)} custom-call(f32[96,512]{1,0:T(8,128)S(1)} %collective-permute-done.8.refs_0_, f32[96,512]{1,0:T(8,128)S(1)} %pad_maximum_fusion.refs_6_.refs_1_, f32[64,512]{1,0:T(8,128)S(1)} %shard_map.40.refs_2_), custom_call_target="tpu_custom_call" | custom-call | flops 1073741824 | bytes 589824 | tf_op jit(solution)/shard_map/pallas_call | solution.py:120
  23.1 0.7 %collective-permute-done.9.refs_7_.refs_1_ = f32[96,512]{1,0:T(8,128)S(1)} collective-permute-done((f32[96,512]{1,0:T(8,128)S(1)}, f32[96,512]{1,0:T(8,128)S(1)}, u32[]{:S(2)}, u32[]{:S(2)}) %collective-permute-start.9) | collective-permute-done | bytes 196640 | tf_op jit(solution)/shard_map/ppermute | solution.py:19
  23.8 0.8 %shard_map.43 = f32[64,512]{1,0:T(8,128)S(1)} custom-call(f32[96,512]{1,0:T(8,128)S(1)} %collective-permute-done.8.refs_0_, f32[96,512]{1,0:T(8,128)S(1)} %collective-permute-done.9.refs_7_.refs_1_, f32[64,512]{1,0:T(8,128)S(1)} %shard_map.42.refs_2_), custom_call_target="tpu_custom_call" | custom-call | flops 1073741824 | bytes 589824 | tf_op jit(solution)/shard_map/pallas_call | solution.py:120
  24.6 0.1 collective-permute-start.10
  24.6 3.5 %shard_map.41 = f32[64,512]{1,0:T(8,128)S(1)} custom-call(f32[96,512]{1,0:T(8,128)S(1)} %copy-done, f32[96,512]{1,0:T(8,128)S(1)} %collective-permute-done.refs_2_.refs_1_, f32[96,512]{1,0:T(8,128)S(1)} %constant_dynamic-update-slice_fusion.refs_3_.refs_2_, f32[96,512]{1,0:T(8,128)S(1)} %collective-permute-done.3.refs_4_.refs_3_, ...), custom_call_target="tpu_custom_call" | custom-call | flops 7516192768 | bytes 1769472 | tf_op jit(solution)/shard_map/pallas_call | solution.py:120
  28.1 2.1 %collective-permute-done.10 = f32[64,512]{1,0:T(8,128)S(1)} collective-permute-done((f32[64,512]{1,0:T(8,128)S(1)}, f32[64,512]{1,0:T(8,128)S(1)}, u32[]{:S(2)}, u32[]{:S(2)}) %collective-permute-start.10) | collective-permute-done | bytes 131104 | tf_op jit(solution)/shard_map/ppermute | solution.py:19
  30.2 0.7 %add.3 = f32[64,512]{1,0:T(8,128)} add(f32[64,512]{1,0:T(8,128)S(1)} %shard_map.41, f32[64,512]{1,0:T(8,128)S(1)} %collective-permute-done.10) | non-fusion elementwise | flops 32768 | bytes 393216 | tf_op jit(solution)/shard_map/add | solution.py:188
  (3 shorter events, 0.0 us)
Async XLA Ops:
  0.0 10.7 %collective-permute-start.1 = (f32[64,512]{1,0:T(8,128)}, f32[64,512]{1,0:T(8,128)S(1)}, u32[]{:S(2)}, u32[]{:S(2)}) collective-permute-start(f32[64,512]{1,0:T(8,128)} %features_ref.1), channel_id=1, source_target_pairs={{0,8},{1,9},{2,10},{3,11},{4,12},{5,13},{6,14},{7,15},{8,0},{9,1},... | collective-permute-start | bytes 393224 | tf_op jit(solution)/shard_map/ppermute | solution.py:19
  5.7 6.6 %copy-start = (f32[96,512]{1,0:T(8,128)S(1)}, f32[96,512]{1,0:T(8,128)}, u32[]{:S(2)}) copy-start(f32[96,512]{1,0:T(8,128)} %shard_map.37.refs_0_.refs_1_) | copy-start | bytes 589828
  5.7 11.2 %collective-permute-start.8 = (f32[96,512]{1,0:T(8,128)}, f32[96,512]{1,0:T(8,128)S(1)}, u32[]{:S(2)}, u32[]{:S(2)}) collective-permute-start(f32[96,512]{1,0:T(8,128)} %shard_map.37.refs_0_.refs_1_), channel_id=1, source_target_pairs={{0,4},{1,5},{2,6},{3,7},{4,0},{5,1},{6,2},{7,3},{8,12},{9,13},{10,... | collective-permute-start | bytes 589832 | tf_op jit(solution)/shard_map/ppermute | solution.py:19
  7.3 9.1 %collective-permute-start.3 = (f32[96,512]{1,0:T(8,128)}, f32[96,512]{1,0:T(8,128)S(1)}, u32[]{:S(2)}, u32[]{:S(2)}) collective-permute-start(f32[96,512]{1,0:T(8,128)} %shard_map.37.refs_0_.refs_1_), channel_id=1, source_target_pairs={{0,2},{1,3},{2,0},{3,1},{4,6},{5,7},{6,4},{7,5},{8,10},{9,11},{10,... | collective-permute-start | bytes 589832 | tf_op jit(solution)/shard_map/ppermute | solution.py:19
  8.8 8.7 %collective-permute-start = (f32[96,512]{1,0:T(8,128)}, f32[96,512]{1,0:T(8,128)S(1)}, u32[]{:S(2)}, u32[]{:S(2)}) collective-permute-start(f32[96,512]{1,0:T(8,128)} %shard_map.37.refs_0_.refs_1_), channel_id=1, source_target_pairs={{0,1},{1,0},{2,3},{3,2},{4,5},{5,4},{6,7},{7,6},{8,9},{9,8},{10,11... | collective-permute-start | bytes 589832 | tf_op jit(solution)/shard_map/ppermute | solution.py:19
  9.6 6.7 %collective-permute-start.2 = (f32[32,512]{1,0:T(8,128)S(1)}, f32[32,512]{1,0:T(8,128)S(1)}, u32[]{:S(2)}, u32[]{:S(2)}) collective-permute-start(f32[32,512]{1,0:T(8,128)S(1)} %slice.4), channel_id=1, source_target_pairs={{0,8},{1,9},{2,10},{3,11},{4,12},{5,13},{6,14},{7,15},{8,0},{9,1},... | collective-permute-start | bytes 196616 | tf_op jit(solution)/shard_map/ppermute | solution.py:19
  10.7 10.5 %collective-permute-start.6 = (f32[64,512]{1,0:T(8,128)S(1)}, f32[64,512]{1,0:T(8,128)S(1)}, u32[]{:S(2)}, u32[]{:S(2)}) collective-permute-start(f32[64,512]{1,0:T(8,128)S(1)} %collective-permute-done.1), channel_id=1, source_target_pairs={{0,2},{1,3},{2,0},{3,1},{4,6},{5,7},{6,4},{7,5},{8,10},{9,11},{10,... | collective-permute-start | bytes 393224 | tf_op jit(solution)/shard_map/ppermute | solution.py:19
  16.3 4.8 %collective-permute-start.4 = (f32[96,512]{1,0:T(8,128)S(1)}, f32[96,512]{1,0:T(8,128)S(1)}, u32[]{:S(2)}, u32[]{:S(2)}) collective-permute-start(f32[96,512]{1,0:T(8,128)S(1)} %constant_dynamic-update-slice_fusion.refs_3_.refs_2_), channel_id=1, source_target_pairs={{0,1},{1,0},{2,3},{3,2},{4,5},{5,4},{6,7},{7,6},{8,9},{9,8},{10,11... | collective-permute-start | bytes 589832 | tf_op jit(solution)/shard_map/ppermute | solution.py:19
  16.4 4.7 %collective-permute-start.5 = (f32[96,512]{1,0:T(8,128)S(1)}, f32[96,512]{1,0:T(8,128)S(1)}, u32[]{:S(2)}, u32[]{:S(2)}) collective-permute-start(f32[96,512]{1,0:T(8,128)S(1)} %collective-permute-done.3.refs_4_.refs_3_), channel_id=1, source_target_pairs={{0,1},{1,0},{2,3},{3,2},{4,5},{5,4},{6,7},{7,6},{8,9},{9,8},{10,11... | collective-permute-start | bytes 589832 | tf_op jit(solution)/shard_map/ppermute | solution.py:19
  16.8 4.3 %collective-permute-start.7 = (f32[32,512]{1,0:T(8,128)S(1)}, f32[32,512]{1,0:T(8,128)S(1)}, u32[]{:S(2)}, u32[]{:S(2)}) collective-permute-start(f32[32,512]{1,0:T(8,128)S(1)} %collective-permute-done.2), channel_id=1, source_target_pairs={{0,2},{1,3},{2,0},{3,1},{4,6},{5,7},{6,4},{7,5},{8,10},{9,11},{10,... | collective-permute-start | bytes 196616 | tf_op jit(solution)/shard_map/ppermute | solution.py:19
  22.3 1.5 %collective-permute-start.9 = (f32[96,512]{1,0:T(8,128)S(1)}, f32[96,512]{1,0:T(8,128)S(1)}, u32[]{:S(2)}, u32[]{:S(2)}) collective-permute-start(f32[96,512]{1,0:T(8,128)S(1)} %pad_maximum_fusion.refs_6_.refs_1_), channel_id=1, source_target_pairs={{0,1},{1,0},{2,3},{3,2},{4,5},{5,4},{6,7},{7,6},{8,9},{9,8},{10,11... | collective-permute-start | bytes 589832 | tf_op jit(solution)/shard_map/ppermute | solution.py:19
  24.6 5.6 %collective-permute-start.10 = (f32[64,512]{1,0:T(8,128)S(1)}, f32[64,512]{1,0:T(8,128)S(1)}, u32[]{:S(2)}, u32[]{:S(2)}) collective-permute-start(f32[64,512]{1,0:T(8,128)S(1)} %shard_map.43), channel_id=1, source_target_pairs={{0,4},{1,5},{2,6},{3,7},{4,0},{5,1},{6,2},{7,3},{8,12},{9,13},{10,... | collective-permute-start | bytes 393224 | tf_op jit(solution)/shard_map/ppermute | solution.py:19

commit v10 on v9

--- a/solution.py
+++ b/solution.py
@@ -136,14 +136,18 @@
     width, points = features.shape
     vectors = solves.shape[0]
 
-    def body(features_ref, solves_ref, probes_ref, out_ref):
+    def body(features_ref, solves_ref, probes_ref, out_ref, vectors_ref):
         out_ref[:width] = features_ref[...]
-        out_ref[width : width + vectors] = solves_ref[...]
-        out_ref[width + vectors :] = probes_ref[...]
+        for first, ref in ((0, solves_ref), (vectors, probes_ref)):
+            out_ref[width + first : width + first + vectors] = ref[...]
+            vectors_ref[first : first + vectors] = ref[...]
 
     return pl.pallas_call(
         body,
-        out_shape=jax.ShapeDtypeStruct((width + 2 * vectors, points), jnp.float32),
+        out_shape=[
+            jax.ShapeDtypeStruct((rows, points), jnp.float32)
+            for rows in (width + 2 * vectors, 2 * vectors)
+        ],
         compiler_params=pltpu.CompilerParams(vmem_limit_bytes=60 << 20),
     )(features, solves, probes)
 
@@ -159,8 +163,8 @@
     bits = [1 << place for place in range(count.bit_length() - 1)]
     top, beside = bits[-1], [bit for bit in bits[:-1] if bit not in (1, 4)]
     far_features = swap(features, top)
-    mine = packed(features, solves, probes)
-    far_vectors = swap(mine[width:], top)
+    mine, my_vectors = packed(features, solves, probes)
+    far_vectors = swap(my_vectors, top)
     sibling = swap(mine, 1)
     near = swap(mine, 4)
     direct = [swap(mine, bit) for bit in beside]
@@ -176,7 +180,7 @@
         last += [jnp.concatenate([swap(piece, bit) for piece in pair], 0) for pair in pieces]
     first = [far] + direct
     siblings = [swap(block, 1) for block in first]
-    (there,) = terms([(near, [mine, sibling] + first)], weight=64)
+    (there,) = terms([(near, [mine, sibling] + first)], weight=512)
     (there,) = terms([(near, siblings)], before=[there], weight=2048)
     last[0], there = tied((last[0], there))
     last_siblings = [swap(block, 1) for block in last]

time: 31 us -> 30.8 us (level)
  waiting for transfers between devices: 8.32 us -> 7.25 us
  starting transfers between devices: 10.3 us -> 11.1 us
    ppermute x11, waiting for transfers between devices: 8.32 us -> 7.25 us  [swapped(): lax.ppermute(value, axis, [(source, source ^ bit) for source in range(cou...]
    unnamed x3 -> x5, local copies, waits for them, and re-layouts: 0.01 us -> 0.94 us
    slice x1 -> x0, local copies, waits for them, and re-layouts: 0.87 us -> none  [local(): far_vectors = swap(mine[width:], top)]
    ppermute x11, starting transfers between devices: 10.3 us -> 11.1 us  [swapped(): lax.ppermute(value, axis, [(source, source ^ bit) for source in range(cou...]
  transfers between devices with their start and end apart: 11 -> 11, of which waited for: 5 -> 4; matrix products, arithmetic and copies ran while one was open for 3% -> 0% of each run, Pallas kernels for 28% -> 28%
where the time goes in v10:
time: 30.8 us; the launch traced here: 30.7 us
  starting transfers between devices  11.1 us (36%)
  Pallas kernels  10.5 us (34%)
  waiting for transfers between devices  7.25 us (24%)
  local copies, waits for them, and re-layouts  0.95 us (3%)
  other arithmetic  0.69 us (2%)
    ppermute x11, starting transfers between devices, swapped(): lax.ppermute(value, axis, [(source, source ^ bit) for source in range(cou...  11.1 us
    pallas_call x6, Pallas kernels, pair_terms(): pl.pallas_call(functools.partial(kernel, width, vectors, placed, len(bloc...  8.89 us
    ppermute x11, waiting for transfers between devices, swapped(): lax.ppermute(value, axis, [(source, source ^ bit) for source in range(cou...  7.25 us
    pallas_call x1, Pallas kernels, packed(): pl.pallas_call(body, out_shape=[jax.ShapeDtypeStruct((rows, points), jnp....  1.65 us
    unnamed x5, local copies, waits for them, and re-layouts  0.94 us
    add x1, other arithmetic, local(): return here + from_near  0.67 us
  transfers between devices with their start and end apart: 11, of which 4 were waited for; matrix products, arithmetic and copies ran while one was open for 0% of the time, Pallas kernels for 28%

profile of v10, /device:TPU:0, one launch (start us, length us, event | category | flops | bytes accessed | tf_op | source)
XLA Modules:
  0.0 30.7 jit_solution(3340990601668432819)
XLA Ops:
  0.0 4.0 %collective-permute-start.1 = (f32[64,512]{1,0:T(8,128)}, f32[64,512]{1,0:T(8,128)S(1)}, u32[]{:S(2)}, u32[]{:S(2)}) collective-permute-start(f32[64,512]{1,0:T(8,128)} %features_ref.1), channel_id=1, source_target_pairs={{0,8},{1,9},{2,10},{3,11},{4,12},{5,13},{6,14},{7,15},{8,0},{9,1},... | collective-permute-start | bytes 393224 | tf_op jit(solution)/shard_map/ppermute | solution.py:19
  4.0 1.7 %shard_map.37 = (f32[96,512]{1,0:T(8,128)}, f32[32,512]{1,0:T(8,128)}) custom-call(f32[64,512]{1,0:T(8,128)} %features_ref.1, f32[16,512]{1,0:T(8,128)} %solves_ref.1, f32[16,512]{1,0:T(8,128)} %probes_ref.1), custom_call_target="tpu_custom_call" | custom-call | tf_op jit(solution)/shard_map/pallas_call | solution.py:145
  5.7 0.0 collective-permute-start.2
  5.7 1.9 %collective-permute-start.8 = (f32[96,512]{1,0:T(8,128)}, f32[96,512]{1,0:T(8,128)S(1)}, u32[]{:S(2)}, u32[]{:S(2)}) collective-permute-start(f32[96,512]{1,0:T(8,128)} %get-tuple-element.16.refs_0_.refs_1_), channel_id=1, source_target_pairs={{0,4},{1,5},{2,6},{3,7},{4,0},{5,1},{6,2},{7,3},{8,12},{9,13},{10,... | collective-permute-start | bytes 589832 | tf_op jit(solution)/shard_map/ppermute | solution.py:19
  7.6 1.5 %collective-permute-start.3 = (f32[96,512]{1,0:T(8,128)}, f32[96,512]{1,0:T(8,128)S(1)}, u32[]{:S(2)}, u32[]{:S(2)}) collective-permute-start(f32[96,512]{1,0:T(8,128)} %get-tuple-element.16.refs_0_.refs_1_), channel_id=1, source_target_pairs={{0,2},{1,3},{2,0},{3,1},{4,6},{5,7},{6,4},{7,5},{8,10},{9,11},{10,... | collective-permute-start | bytes 589832 | tf_op jit(solution)/shard_map/ppermute | solution.py:19
  9.1 0.0 collective-permute-start
  9.1 3.4 %collective-permute-done.1 = f32[64,512]{1,0:T(8,128)S(1)} collective-permute-done((f32[64,512]{1,0:T(8,128)}, f32[64,512]{1,0:T(8,128)S(1)}, u32[]{:S(2)}, u32[]{:S(2)}) %collective-permute-start.1) | collective-permute-done | bytes 131104 | tf_op jit(solution)/shard_map/ppermute | solution.py:19
  12.6 0.0 copy-start
  12.6 0.9 %copy-done = f32[96,512]{1,0:T(8,128)S(1)} copy-done((f32[96,512]{1,0:T(8,128)S(1)}, f32[96,512]{1,0:T(8,128)}, u32[]{:S(2)}) %copy-start) | copy-done | bytes 196632
  13.5 0.8 %shard_map.38.refs_8_ = f32[64,512]{1,0:T(8,128)S(1)} custom-call(f32[96,512]{1,0:T(8,128)S(1)} %copy-done), custom_call_target="tpu_custom_call" | custom-call | flops 268435456 | bytes 196608 | tf_op jit(solution)/shard_map/pallas_call | solution.py:120
  14.3 0.0 collective-permute-done.2
  14.3 1.7 %collective-permute-start.7 = (f32[32,512]{1,0:T(8,128)S(1)}, f32[32,512]{1,0:T(8,128)S(1)}, u32[]{:S(2)}, u32[]{:S(2)}) collective-permute-start(f32[32,512]{1,0:T(8,128)S(1)} %collective-permute-done.2), channel_id=1, source_target_pairs={{0,2},{1,3},{2,0},{3,1},{4,6},{5,7},{6,4},{7,5},{8,10},{9,11},{10,... | collective-permute-start | bytes 196616 | tf_op jit(solution)/shard_map/ppermute | solution.py:19
  16.0 0.4 %collective-permute-start.6 = (f32[64,512]{1,0:T(8,128)S(1)}, f32[64,512]{1,0:T(8,128)S(1)}, u32[]{:S(2)}, u32[]{:S(2)}) collective-permute-start(f32[64,512]{1,0:T(8,128)S(1)} %collective-permute-done.1), channel_id=1, source_target_pairs={{0,2},{1,3},{2,0},{3,1},{4,6},{5,7},{6,4},{7,5},{8,10},{9,11},{10,... | collective-permute-start | bytes 393224 | tf_op jit(solution)/shard_map/ppermute | solution.py:19
  16.4 0.0 collective-permute-done.8.refs_0_
  16.4 0.1 collective-permute-start.4
  16.5 0.0 collective-permute-done.3.refs_4_.refs_3_
  16.5 0.5 %collective-permute-start.5 = (f32[96,512]{1,0:T(8,128)S(1)}, f32[96,512]{1,0:T(8,128)S(1)}, u32[]{:S(2)}, u32[]{:S(2)}) collective-permute-start(f32[96,512]{1,0:T(8,128)S(1)} %collective-permute-done.3.refs_4_.refs_3_), channel_id=1, source_target_pairs={{0,1},{1,0},{2,3},{3,2},{4,5},{5,4},{6,7},{7,6},{8,9},{9,8},{10,11... | collective-permute-start | bytes 589832 | tf_op jit(solution)/shard_map/ppermute | solution.py:19
  17.0 0.0 collective-permute-done.refs_2_.refs_1_
  17.0 2.0 %shard_map.39.refs_3_ = f32[64,512]{1,0:T(8,128)S(1)} custom-call(f32[96,512]{1,0:T(8,128)S(1)} %collective-permute-done.8.refs_0_, f32[96,512]{1,0:T(8,128)S(1)} %copy-done, f32[96,512]{1,0:T(8,128)S(1)} %collective-permute-done.refs_2_.refs_1_, f32[96,512]{1,0:T(8,128)S(1)} %constant_dynamic-update-slice_fusion.refs_3_.refs_2_, ...), custom_call_target="tpu_custom_call" | custom-call | flops 1073741824 | bytes 983040 | tf_op jit(solution)/shard_map/pallas_call | solution.py:120
  19.0 0.0 collective-permute-done.7
  19.0 1.9 %collective-permute-done.6 = f32[64,512]{1,0:T(8,128)S(1)} collective-permute-done((f32[64,512]{1,0:T(8,128)S(1)}, f32[64,512]{1,0:T(8,128)S(1)}, u32[]{:S(2)}, u32[]{:S(2)}) %collective-permute-start.6) | collective-permute-done | bytes 131104 | tf_op jit(solution)/shard_map/ppermute | solution.py:19
  20.9 0.0 collective-permute-done.4.refs_1_.refs_4_
  21.0 0.0 collective-permute-done.5.refs_2_.refs_5_
  21.0 1.1 %shard_map.40.refs_2_ = f32[64,512]{1,0:T(8,128)S(1)} custom-call(f32[96,512]{1,0:T(8,128)S(1)} %collective-permute-done.8.refs_0_, f32[96,512]{1,0:T(8,128)S(1)} %collective-permute-done.4.refs_1_.refs_4_, f32[96,512]{1,0:T(8,128)S(1)} %collective-permute-done.5.refs_2_.refs_5_, f32[64,512]{1,0:T(8,128)S(1)} %shard_map.39.refs_3_), custom_call_target="tpu_custom_call" | custom-call | flops 2147483648 | bytes 786432 | tf_op jit(solution)/shard_map/pallas_call | solution.py:120
  22.1 0.1 collective-permute-start.9
  22.2 0.8 %shard_map.42.refs_2_ = f32[64,512]{1,0:T(8,128)S(1)} custom-call(f32[96,512]{1,0:T(8,128)S(1)} %collective-permute-done.8.refs_0_, f32[96,512]{1,0:T(8,128)S(1)} %pad_maximum_fusion.refs_6_.refs_1_, f32[64,512]{1,0:T(8,128)S(1)} %shard_map.40.refs_2_), custom_call_target="tpu_custom_call" | custom-call | flops 1073741824 | bytes 589824 | tf_op jit(solution)/shard_map/pallas_call | solution.py:120
  23.0 0.0 copy-start.1
  23.0 0.6 %collective-permute-done.9.refs_7_.refs_1_ = f32[96,512]{1,0:T(8,128)S(1)} collective-permute-done((f32[96,512]{1,0:T(8,128)S(1)}, f32[96,512]{1,0:T(8,128)S(1)}, u32[]{:S(2)}, u32[]{:S(2)}) %collective-permute-start.9) | collective-permute-done | bytes 196640 | tf_op jit(solution)/shard_map/ppermute | solution.py:19
  23.6 0.8 %shard_map.43 = f32[64,512]{1,0:T(8,128)S(1)} custom-call(f32[96,512]{1,0:T(8,128)S(1)} %collective-permute-done.8.refs_0_, f32[96,512]{1,0:T(8,128)S(1)} %collective-permute-done.9.refs_7_.refs_1_, f32[64,512]{1,0:T(8,128)S(1)} %shard_map.42.refs_2_), custom_call_target="tpu_custom_call" | custom-call | flops 1073741824 | bytes 589824 | tf_op jit(solution)/shard_map/pallas_call | solution.py:120
  24.4 0.9 %collective-permute-start.10 = (f32[64,512]{1,0:T(8,128)S(1)}, f32[64,512]{1,0:T(8,128)S(1)}, u32[]{:S(2)}, u32[]{:S(2)}) collective-permute-start(f32[64,512]{1,0:T(8,128)S(1)} %shard_map.43), channel_id=1, source_target_pairs={{0,4},{1,5},{2,6},{3,7},{4,0},{5,1},{6,2},{7,3},{8,12},{9,13},{10,... | collective-permute-start | bytes 393224 | tf_op jit(solution)/shard_map/ppermute | solution.py:19
  25.3 0.0 copy-done.1
  25.3 3.5 %shard_map.41 = f32[64,512]{1,0:T(8,128)S(1)} custom-call(f32[96,512]{1,0:T(8,128)S(1)} %copy-done.1, f32[96,512]{1,0:T(8,128)S(1)} %collective-permute-done.refs_2_.refs_1_, f32[96,512]{1,0:T(8,128)S(1)} %constant_dynamic-update-slice_fusion.refs_3_.refs_2_, f32[96,512]{1,0:T(8,128)S(1)} %collective-permute-done.3.refs_4_.refs_3_, ...), custom_call_target="tpu_custom_call" | custom-call | flops 7516192768 | bytes 1769472 | tf_op jit(solution)/shard_map/pallas_call | solution.py:120
  28.8 1.2 %collective-permute-done.10 = f32[64,512]{1,0:T(8,128)S(1)} collective-permute-done((f32[64,512]{1,0:T(8,128)S(1)}, f32[64,512]{1,0:T(8,128)S(1)}, u32[]{:S(2)}, u32[]{:S(2)}) %collective-permute-start.10) | collective-permute-done | bytes 131104 | tf_op jit(solution)/shard_map/ppermute | solution.py:19
  30.0 0.7 %add.3 = f32[64,512]{1,0:T(8,128)} add(f32[64,512]{1,0:T(8,128)S(1)} %shard_map.41, f32[64,512]{1,0:T(8,128)S(1)} %collective-permute-done.10) | non-fusion elementwise | flops 32768 | bytes 393216 | tf_op jit(solution)/shard_map/add | solution.py:192
  (3 shorter events, 0.0 us)
Async XLA Ops:
  0.0 12.6 %collective-permute-start.1 = (f32[64,512]{1,0:T(8,128)}, f32[64,512]{1,0:T(8,128)S(1)}, u32[]{:S(2)}, u32[]{:S(2)}) collective-permute-start(f32[64,512]{1,0:T(8,128)} %features_ref.1), channel_id=1, source_target_pairs={{0,8},{1,9},{2,10},{3,11},{4,12},{5,13},{6,14},{7,15},{8,0},{9,1},... | collective-permute-start | bytes 393224 | tf_op jit(solution)/shard_map/ppermute | solution.py:19
  5.7 8.6 %collective-permute-start.2 = (f32[32,512]{1,0:T(8,128)}, f32[32,512]{1,0:T(8,128)S(1)}, u32[]{:S(2)}, u32[]{:S(2)}) collective-permute-start(f32[32,512]{1,0:T(8,128)} %get-tuple-element.15), channel_id=1, source_target_pairs={{0,8},{1,9},{2,10},{3,11},{4,12},{5,13},{6,14},{7,15},{8,0},{9,1},... | collective-permute-start | bytes 196616 | tf_op jit(solution)/shard_map/ppermute | solution.py:19
  5.7 10.7 %collective-permute-start.8 = (f32[96,512]{1,0:T(8,128)}, f32[96,512]{1,0:T(8,128)S(1)}, u32[]{:S(2)}, u32[]{:S(2)}) collective-permute-start(f32[96,512]{1,0:T(8,128)} %get-tuple-element.16.refs_0_.refs_1_), channel_id=1, source_target_pairs={{0,4},{1,5},{2,6},{3,7},{4,0},{5,1},{6,2},{7,3},{8,12},{9,13},{10,... | collective-permute-start | bytes 589832 | tf_op jit(solution)/shard_map/ppermute | solution.py:19
  7.6 8.9 %collective-permute-start.3 = (f32[96,512]{1,0:T(8,128)}, f32[96,512]{1,0:T(8,128)S(1)}, u32[]{:S(2)}, u32[]{:S(2)}) collective-permute-start(f32[96,512]{1,0:T(8,128)} %get-tuple-element.16.refs_0_.refs_1_), channel_id=1, source_target_pairs={{0,2},{1,3},{2,0},{3,1},{4,6},{5,7},{6,4},{7,5},{8,10},{9,11},{10,... | collective-permute-start | bytes 589832 | tf_op jit(solution)/shard_map/ppermute | solution.py:19
  9.1 7.9 %collective-permute-start = (f32[96,512]{1,0:T(8,128)}, f32[96,512]{1,0:T(8,128)S(1)}, u32[]{:S(2)}, u32[]{:S(2)}) collective-permute-start(f32[96,512]{1,0:T(8,128)} %get-tuple-element.16.refs_0_.refs_1_), channel_id=1, source_target_pairs={{0,1},{1,0},{2,3},{3,2},{4,5},{5,4},{6,7},{7,6},{8,9},{9,8},{10,11... | collective-permute-start | bytes 589832 | tf_op jit(solution)/shard_map/ppermute | solution.py:19
  12.6 0.9 %copy-start = (f32[96,512]{1,0:T(8,128)S(1)}, f32[96,512]{1,0:T(8,128)}, u32[]{:S(2)}) copy-start(f32[96,512]{1,0:T(8,128)} %get-tuple-element.16.refs_0_.refs_1_) | copy-start | bytes 589828
  14.3 4.7 %collective-permute-start.7 = (f32[32,512]{1,0:T(8,128)S(1)}, f32[32,512]{1,0:T(8,128)S(1)}, u32[]{:S(2)}, u32[]{:S(2)}) collective-permute-start(f32[32,512]{1,0:T(8,128)S(1)} %collective-permute-done.2), channel_id=1, source_target_pairs={{0,2},{1,3},{2,0},{3,1},{4,6},{5,7},{6,4},{7,5},{8,10},{9,11},{10,... | collective-permute-start | bytes 196616 | tf_op jit(solution)/shard_map/ppermute | solution.py:19
  16.0 5.0 %collective-permute-start.6 = (f32[64,512]{1,0:T(8,128)S(1)}, f32[64,512]{1,0:T(8,128)S(1)}, u32[]{:S(2)}, u32[]{:S(2)}) collective-permute-start(f32[64,512]{1,0:T(8,128)S(1)} %collective-permute-done.1), channel_id=1, source_target_pairs={{0,2},{1,3},{2,0},{3,1},{4,6},{5,7},{6,4},{7,5},{8,10},{9,11},{10,... | collective-permute-start | bytes 393224 | tf_op jit(solution)/shard_map/ppermute | solution.py:19
  16.4 4.6 %collective-permute-start.4 = (f32[96,512]{1,0:T(8,128)S(1)}, f32[96,512]{1,0:T(8,128)S(1)}, u32[]{:S(2)}, u32[]{:S(2)}) collective-permute-start(f32[96,512]{1,0:T(8,128)S(1)} %constant_dynamic-update-slice_fusion.refs_3_.refs_2_), channel_id=1, source_target_pairs={{0,1},{1,0},{2,3},{3,2},{4,5},{5,4},{6,7},{7,6},{8,9},{9,8},{10,11... | collective-permute-start | bytes 589832 | tf_op jit(solution)/shard_map/ppermute | solution.py:19
  16.5 4.5 %collective-permute-start.5 = (f32[96,512]{1,0:T(8,128)S(1)}, f32[96,512]{1,0:T(8,128)S(1)}, u32[]{:S(2)}, u32[]{:S(2)}) collective-permute-start(f32[96,512]{1,0:T(8,128)S(1)} %collective-permute-done.3.refs_4_.refs_3_), channel_id=1, source_target_pairs={{0,1},{1,0},{2,3},{3,2},{4,5},{5,4},{6,7},{7,6},{8,9},{9,8},{10,11... | collective-permute-start | bytes 589832 | tf_op jit(solution)/shard_map/ppermute | solution.py:19
  22.1 1.5 %collective-permute-start.9 = (f32[96,512]{1,0:T(8,128)S(1)}, f32[96,512]{1,0:T(8,128)S(1)}, u32[]{:S(2)}, u32[]{:S(2)}) collective-permute-start(f32[96,512]{1,0:T(8,128)S(1)} %pad_maximum_fusion.refs_6_.refs_1_), channel_id=1, source_target_pairs={{0,1},{1,0},{2,3},{3,2},{4,5},{5,4},{6,7},{7,6},{8,9},{9,8},{10,11... | collective-permute-start | bytes 589832 | tf_op jit(solution)/shard_map/ppermute | solution.py:19
  23.0 2.3 %copy-start.1 = (f32[96,512]{1,0:T(8,128)S(1)}, f32[96,512]{1,0:T(8,128)}, u32[]{:S(2)}) copy-start(f32[96,512]{1,0:T(8,128)} %get-tuple-element.16.refs_0_.refs_1_) | copy-start | bytes 589828
  24.4 5.6 %collective-permute-start.10 = (f32[64,512]{1,0:T(8,128)S(1)}, f32[64,512]{1,0:T(8,128)S(1)}, u32[]{:S(2)}, u32[]{:S(2)}) collective-permute-start(f32[64,512]{1,0:T(8,128)S(1)} %shard_map.43), channel_id=1, source_target_pairs={{0,4},{1,5},{2,6},{3,7},{4,0},{5,1},{6,2},{7,3},{8,12},{9,13},{10,... | collective-permute-start | bytes 393224 | tf_op jit(solution)/shard_map/ppermute | solution.py:19

commit v11 on v10

--- a/solution.py
+++ b/solution.py
@@ -86,9 +86,10 @@
     return jnp.concatenate(dist, 0), jnp.concatenate(pair, 0), jnp.concatenate(pull, 1)
 
 
-def kernel(width, vectors, jobs, count, *refs):
+def kernel(width, vectors, jobs, count, pieces, *refs):
     blocks, refs = refs[:count], refs[count:]
-    before, out = refs[: -len(jobs)], refs[-len(jobs) :]
+    results = len(jobs) * pieces
+    before, out = refs[:-results], refs[-results:]
     used = sorted({theirs for _, columns in jobs for theirs in columns})
     theirs = {place: prepared_theirs(blocks[place][...], width, vectors) for place in used}
     for place, (row, columns) in enumerate(jobs):
@@ -99,10 +100,13 @@
         ]
         pulled, sums = (sum(part) for part in zip(*parts))
         value = (pulled - blocks[row][:width] * sums) / width
-        out[place][...] = value + before[place][...] if place < len(before) else value
-
-
-def pair_terms(jobs, width, vectors, before=(), weight=2048):
+        value = value + before[place][...] if place < len(before) else value
+        rows = width // pieces
+        for piece in range(pieces):
+            out[place * pieces + piece][...] = value[piece * rows : (piece + 1) * rows]
+
+
+def pair_terms(jobs, width, vectors, before=(), weight=2048, pieces=1):
     blocks = []
 
     def place(block):
@@ -115,10 +119,11 @@
     placed = [(place(row), [place(column) for column in columns]) for row, columns in jobs]
     points = blocks[0].shape[1]
     operands = blocks + list(before)
-    out_shape = [jax.ShapeDtypeStruct((width, points), jnp.float32)] * len(jobs)
+    shape = jax.ShapeDtypeStruct((width // pieces, points), jnp.float32)
+    out_shape = [shape] * (len(jobs) * pieces)
     return list(
         pl.pallas_call(
-            functools.partial(kernel, width, vectors, placed, len(blocks)),
+            functools.partial(kernel, width, vectors, placed, len(blocks), pieces),
             out_shape=out_shape,
             in_specs=[pl.BlockSpec(memory_space=pltpu.VMEM)] * len(operands),
             out_specs=[pl.BlockSpec(memory_space=pltpu.VMEM)] * len(out_shape),
@@ -169,26 +174,26 @@
     near = swap(mine, 4)
     direct = [swap(mine, bit) for bit in beside]
 
-    far_features, own = tied((far_features, mine))
-    (here,) = terms([(own, [own])], weight=512)
-    far_vectors, here = tied((far_vectors, here))
-    split = [far_features, far_vectors]
-    far = jnp.concatenate(split, 0)
+    (here,) = terms([(mine, [mine])], weight=64)
+    far_features, far_vectors, here = tied((far_features, far_vectors, here))
+    far = [far_features, far_vectors]
     last = []
     for bit in beside:
-        pieces = [split] + [[block[:width], block[width:]] for block in last]
-        last += [jnp.concatenate([swap(piece, bit) for piece in pair], 0) for pair in pieces]
-    first = [far] + direct
-    siblings = [swap(block, 1) for block in first]
-    (there,) = terms([(near, [mine, sibling] + first)], weight=512)
-    (there,) = terms([(near, siblings)], before=[there], weight=2048)
-    last[0], there = tied((last[0], there))
+        for pair in [far] + last:
+            last = last + [[swap(piece, bit) for piece in pair]]
+    first = [jnp.concatenate(far, 0)] + direct
+    (there,) = terms([(near, [mine, sibling] + first)], weight=2048)
+    swapped_first = swap(jnp.concatenate(first, 0), 1)
+    siblings = jnp.split(swapped_first, len(first), 0)
+    (there,) = terms([(near, siblings)], before=[there], weight=64)
+    *pieces, there = tied((*[piece for pair in last for piece in pair], there))
+    last = [jnp.concatenate(pieces[at : at + 2], 0) for at in range(0, len(pieces), 2)]
     last_siblings = [swap(block, 1) for block in last]
-    (there,) = terms([(near, last)], before=[there])
-    (there,) = terms([(near, last_siblings)], before=[there])
-    from_near = swap(there, 4)
+    (there,) = terms([(near, last)], before=[there], weight=64)
     rest = [sibling] + first + siblings + last + last_siblings
-    (here,) = terms([(mine, rest)], before=[here])
+    toward_near = terms([(near, last_siblings)], before=[there], weight=64, pieces=2)
+    from_near = jnp.concatenate([swap(piece, 4) for piece in toward_near], 0)
+    (here,) = terms([(mine, rest)], before=[here], weight=2048)
     return here + from_near
 
 

time: 30.8 us -> 28.8 us (0.935)
  waiting for transfers between devices: 7.25 us -> 4.48 us
  starting transfers between devices: 11.1 us -> 11.7 us
    ppermute x11, waiting for transfers between devices: 7.25 us -> 4.48 us  [swapped(): lax.ppermute(value, axis, [(source, source ^ bit) for source in range(cou...]
    ppermute x11, starting transfers between devices: 11.1 us -> 11.7 us  [swapped(): lax.ppermute(value, axis, [(source, source ^ bit) for source in range(cou...]
    unnamed x5 -> x4, local copies, waits for them, and re-layouts: 0.94 us -> 0.98 us
  transfers between devices with their start and end apart: 11 -> 11, of which waited for: 4 -> 4; matrix products, arithmetic and copies ran while one was open for 0% -> 0% of each run, Pallas kernels for 28% -> 34%
where the time goes in v11:
time: 28.8 us; the launch traced here: 28.6 us
  starting transfers between devices  11.7 us (41%)
  Pallas kernels  10.5 us (36%)
  waiting for transfers between devices  4.48 us (16%)
  local copies, waits for them, and re-layouts  1.02 us (4%)
  other arithmetic  0.7 us (2%)
    ppermute x11, starting transfers between devices, swapped(): lax.ppermute(value, axis, [(source, source ^ bit) for source in range(cou...  11.7 us
    pallas_call x6, Pallas kernels, pair_terms(): pl.pallas_call(functools.partial(kernel, width, vectors, placed, len(bloc...  8.89 us
    ppermute x11, waiting for transfers between devices, swapped(): lax.ppermute(value, axis, [(source, source ^ bit) for source in range(cou...  4.48 us
    pallas_call x1, Pallas kernels, packed(): pl.pallas_call(body, out_shape=[jax.ShapeDtypeStruct((rows, points), jnp....  1.65 us
    unnamed x4, local copies, waits for them, and re-layouts  0.98 us
    add x1, other arithmetic, local(): return here + from_near  0.67 us
  transfers between devices with their start and end apart: 11, of which 4 were waited for; matrix products, arithmetic and copies ran while one was open for 0% of the time, Pallas kernels for 34%

profile of v11, /device:TPU:0, one launch (start us, length us, event | category | flops | bytes accessed | tf_op | source)
XLA Modules:
  0.0 28.6 jit_solution(6468048817851181808)
XLA Ops:
  0.0 4.0 %collective-permute-start.1 = (f32[64,512]{1,0:T(8,128)}, f32[64,512]{1,0:T(8,128)S(1)}, u32[]{:S(2)}, u32[]{:S(2)}) collective-permute-start(f32[64,512]{1,0:T(8,128)} %features_ref.1), channel_id=1, source_target_pairs={{0,8},{1,9},{2,10},{3,11},{4,12},{5,13},{6,14},{7,15},{8,0},{9,1},... | collective-permute-start | bytes 393224 | tf_op jit(solution)/shard_map/ppermute | solution.py:19
  4.0 1.7 %shard_map.37 = (f32[96,512]{1,0:T(8,128)}, f32[32,512]{1,0:T(8,128)}) custom-call(f32[64,512]{1,0:T(8,128)} %features_ref.1, f32[16,512]{1,0:T(8,128)} %solves_ref.1, f32[16,512]{1,0:T(8,128)} %probes_ref.1), custom_call_target="tpu_custom_call" | custom-call | tf_op jit(solution)/shard_map/pallas_call | solution.py:150
  5.7 0.0 collective-permute-start.2
  5.7 0.0 collective-permute-start
  5.7 1.9 %collective-permute-start.3 = (f32[96,512]{1,0:T(8,128)}, f32[96,512]{1,0:T(8,128)S(1)}, u32[]{:S(2)}, u32[]{:S(2)}) collective-permute-start(f32[96,512]{1,0:T(8,128)} %get-tuple-element.15.refs_0_.refs_1_), channel_id=1, source_target_pairs={{0,2},{1,3},{2,0},{3,1},{4,6},{5,7},{6,4},{7,5},{8,10},{9,11},{10,... | collective-permute-start | bytes 589832 | tf_op jit(solution)/shard_map/ppermute | solution.py:19
  7.5 1.6 %collective-permute-start.7 = (f32[96,512]{1,0:T(8,128)}, f32[96,512]{1,0:T(8,128)S(1)}, u32[]{:S(2)}, u32[]{:S(2)}) collective-permute-start(f32[96,512]{1,0:T(8,128)} %get-tuple-element.15.refs_0_.refs_1_), channel_id=1, source_target_pairs={{0,4},{1,5},{2,6},{3,7},{4,0},{5,1},{6,2},{7,3},{8,12},{9,13},{10,... | collective-permute-start | bytes 589832 | tf_op jit(solution)/shard_map/ppermute | solution.py:19
  9.1 0.0 copy-start
  9.1 1.0 %copy-done = f32[96,512]{1,0:T(8,128)S(1)} copy-done((f32[96,512]{1,0:T(8,128)S(1)}, f32[96,512]{1,0:T(8,128)}, u32[]{:S(2)}) %copy-start) | copy-done | bytes 196632
  10.1 0.8 %shard_map.38.refs_8_ = f32[64,512]{1,0:T(8,128)S(1)} custom-call(f32[96,512]{1,0:T(8,128)S(1)} %copy-done), custom_call_target="tpu_custom_call" | custom-call | flops 33554432 | bytes 196608 | tf_op jit(solution)/shard_map/pallas_call | solution.py:125
  10.8 2.6 %collective-permute-done.2 = f32[32,512]{1,0:T(8,128)S(1)} collective-permute-done((f32[32,512]{1,0:T(8,128)}, f32[32,512]{1,0:T(8,128)S(1)}, u32[]{:S(2)}, u32[]{:S(2)}) %collective-permute-start.2) | collective-permute-done | bytes 65568 | tf_op jit(solution)/shard_map/ppermute | solution.py:19
  13.5 0.0 collective-permute-done.1
  13.5 1.5 %collective-permute-start.5 = (f32[64,512]{1,0:T(8,128)S(1)}, f32[64,512]{1,0:T(8,128)S(1)}, u32[]{:S(2)}, u32[]{:S(2)}) collective-permute-start(f32[64,512]{1,0:T(8,128)S(1)} %collective-permute-done.1), channel_id=1, source_target_pairs={{0,2},{1,3},{2,0},{3,1},{4,6},{5,7},{6,4},{7,5},{8,10},{9,11},{10,... | collective-permute-start | bytes 393224 | tf_op jit(solution)/shard_map/ppermute | solution.py:19
  15.0 0.5 %collective-permute-start.6 = (f32[32,512]{1,0:T(8,128)S(1)}, f32[32,512]{1,0:T(8,128)S(1)}, u32[]{:S(2)}, u32[]{:S(2)}) collective-permute-start(f32[32,512]{1,0:T(8,128)S(1)} %collective-permute-done.2), channel_id=1, source_target_pairs={{0,2},{1,3},{2,0},{3,1},{4,6},{5,7},{6,4},{7,5},{8,10},{9,11},{10,... | collective-permute-start | bytes 196616 | tf_op jit(solution)/shard_map/ppermute | solution.py:19
  15.5 0.0 collective-permute-done.3.refs_4_.refs_3_
  15.6 0.1 collective-permute-start.4
  15.7 0.0 collective-permute-done.refs_2_.refs_1_
  15.7 1.0 %collective-permute-done.7.refs_0_ = f32[96,512]{1,0:T(8,128)S(1)} collective-permute-done((f32[96,512]{1,0:T(8,128)}, f32[96,512]{1,0:T(8,128)S(1)}, u32[]{:S(2)}, u32[]{:S(2)}) %collective-permute-start.7) | collective-permute-done | bytes 196640 | tf_op jit(solution)/shard_map/ppermute | solution.py:19
  16.7 2.0 %shard_map.39.refs_3_ = f32[64,512]{1,0:T(8,128)S(1)} custom-call(f32[96,512]{1,0:T(8,128)S(1)} %collective-permute-done.7.refs_0_, f32[96,512]{1,0:T(8,128)S(1)} %copy-done, f32[96,512]{1,0:T(8,128)S(1)} %collective-permute-done.refs_2_.refs_1_, f32[96,512]{1,0:T(8,128)S(1)} %constant_dynamic-update-slice_fusion.refs_3_.refs_2_, ...), custom_call_target="tpu_custom_call" | custom-call | flops 4294967296 | bytes 983040 | tf_op jit(solution)/shard_map/pallas_call | solution.py:125
  18.7 0.0 collective-permute-done.4
  18.8 1.1 %shard_map.40.refs_2_ = f32[64,512]{1,0:T(8,128)S(1)} custom-call(f32[96,512]{1,0:T(8,128)S(1)} %collective-permute-done.7.refs_0_, f32[96,512]{1,0:T(8,128)S(1)} %get-tuple-element.26.refs_1_.refs_4_, f32[96,512]{1,0:T(8,128)S(1)} %get-tuple-element.25.refs_2_.refs_5_, f32[64,512]{1,0:T(8,128)S(1)} %shard_map.39.refs_3_), custom_call_target="tpu_custom_call" | custom-call | flops 67108864 | bytes 786432 | tf_op jit(solution)/shard_map/pallas_call | solution.py:125
  19.9 0.0 collective-permute-done.6
  19.9 0.0 collective-permute-done.5
  20.0 0.1 collective-permute-start.8
  20.0 0.8 %shard_map.42.refs_2_ = f32[64,512]{1,0:T(8,128)S(1)} custom-call(f32[96,512]{1,0:T(8,128)S(1)} %collective-permute-done.7.refs_0_, f32[96,512]{1,0:T(8,128)S(1)} %constant_dynamic-update-slice_fusion.2.refs_6_.refs_1_, f32[64,512]{1,0:T(8,128)S(1)} %shard_map.40.refs_2_), custom_call_target="tpu_custom_call" | custom-call | flops 33554432 | bytes 589824 | tf_op jit(solution)/shard_map/pallas_call | solution.py:125
  20.8 0.7 %collective-permute-done.8.refs_7_.refs_1_ = f32[96,512]{1,0:T(8,128)S(1)} collective-permute-done((f32[96,512]{1,0:T(8,128)S(1)}, f32[96,512]{1,0:T(8,128)S(1)}, u32[]{:S(2)}, u32[]{:S(2)}) %collective-permute-start.8) | collective-permute-done | bytes 196640 | tf_op jit(solution)/shard_map/ppermute | solution.py:19
  21.5 0.8 %shard_map.43 = (f32[32,512]{1,0:T(8,128)S(1)}, f32[32,512]{1,0:T(8,128)S(1)}) custom-call(f32[96,512]{1,0:T(8,128)S(1)} %collective-permute-done.7.refs_0_, f32[96,512]{1,0:T(8,128)S(1)} %collective-permute-done.8.refs_7_.refs_1_, f32[64,512]{1,0:T(8,128)S(1)} %shard_map.42.refs_2_), custom_call_target="tpu_custom_call" | custom-call | flops 33554432 | bytes 589824 | tf_op jit(solution)/shard_map/pallas_call | solution.py:125
  22.2 1.2 %collective-permute-start.10 = (f32[32,512]{1,0:T(8,128)S(1)}, f32[32,512]{1,0:T(8,128)S(1)}, u32[]{:S(2)}, u32[]{:S(2)}) collective-permute-start(f32[32,512]{1,0:T(8,128)S(1)} %get-tuple-element.24), channel_id=1, source_target_pairs={{0,4},{1,5},{2,6},{3,7},{4,0},{5,1},{6,2},{7,3},{8,12},{9,13},{10,... | collective-permute-start | bytes 196616 | tf_op jit(solution)/shard_map/ppermute | solution.py:19
  23.4 0.9 %collective-permute-start.9 = (f32[32,512]{1,0:T(8,128)S(1)}, f32[32,512]{1,0:T(8,128)S(1)}, u32[]{:S(2)}, u32[]{:S(2)}) collective-permute-start(f32[32,512]{1,0:T(8,128)S(1)} %get-tuple-element.23), channel_id=1, source_target_pairs={{0,4},{1,5},{2,6},{3,7},{4,0},{5,1},{6,2},{7,3},{8,12},{9,13},{10,... | collective-permute-start | bytes 196616 | tf_op jit(solution)/shard_map/ppermute | solution.py:19
  24.3 3.5 %shard_map.41 = f32[64,512]{1,0:T(8,128)S(1)} custom-call(f32[96,512]{1,0:T(8,128)S(1)} %copy-done, f32[96,512]{1,0:T(8,128)S(1)} %collective-permute-done.refs_2_.refs_1_, f32[96,512]{1,0:T(8,128)S(1)} %constant_dynamic-update-slice_fusion.refs_3_.refs_2_, f32[96,512]{1,0:T(8,128)S(1)} %collective-permute-done.3.refs_4_.refs_3_, ...), custom_call_target="tpu_custom_call" | custom-call | flops 7516192768 | bytes 1769472 | tf_op jit(solution)/shard_map/pallas_call | solution.py:125
  27.8 0.0 collective-permute-done.10
  27.8 0.2 collective-permute-done.9
  28.0 0.7 %maximum_add_fusion = f32[64,512]{1,0:T(8,128)} fusion(f32[64,512]{1,0:T(8,128)S(1)} %shard_map.41, f32[32,512]{1,0:T(8,128)S(1)} %collective-permute-done.10, f32[32,512]{1,0:T(8,128)S(1)} %collective-permute-done.9), kind=kLoop, calls=%fused_computation.1 | loop fusion | flops 65536 | bytes 393216 | tf_op jit(solution)/shard_map/add | solution.py:197
  (6 shorter events, 0.1 us)
Async XLA Ops:
  0.0 13.5 %collective-permute-start.1 = (f32[64,512]{1,0:T(8,128)}, f32[64,512]{1,0:T(8,128)S(1)}, u32[]{:S(2)}, u32[]{:S(2)}) collective-permute-start(f32[64,512]{1,0:T(8,128)} %features_ref.1), channel_id=1, source_target_pairs={{0,8},{1,9},{2,10},{3,11},{4,12},{5,13},{6,14},{7,15},{8,0},{9,1},... | collective-permute-start | bytes 393224 | tf_op jit(solution)/shard_map/ppermute | solution.py:19
  5.7 7.8 %collective-permute-start.2 = (f32[32,512]{1,0:T(8,128)}, f32[32,512]{1,0:T(8,128)S(1)}, u32[]{:S(2)}, u32[]{:S(2)}) collective-permute-start(f32[32,512]{1,0:T(8,128)} %get-tuple-element.16), channel_id=1, source_target_pairs={{0,8},{1,9},{2,10},{3,11},{4,12},{5,13},{6,14},{7,15},{8,0},{9,1},... | collective-permute-start | bytes 196616 | tf_op jit(solution)/shard_map/ppermute | solution.py:19
  5.7 10.0 %collective-permute-start = (f32[96,512]{1,0:T(8,128)}, f32[96,512]{1,0:T(8,128)S(1)}, u32[]{:S(2)}, u32[]{:S(2)}) collective-permute-start(f32[96,512]{1,0:T(8,128)} %get-tuple-element.15.refs_0_.refs_1_), channel_id=1, source_target_pairs={{0,1},{1,0},{2,3},{3,2},{4,5},{5,4},{6,7},{7,6},{8,9},{9,8},{10,11... | collective-permute-start | bytes 589832 | tf_op jit(solution)/shard_map/ppermute | solution.py:19
  5.7 9.8 %collective-permute-start.3 = (f32[96,512]{1,0:T(8,128)}, f32[96,512]{1,0:T(8,128)S(1)}, u32[]{:S(2)}, u32[]{:S(2)}) collective-permute-start(f32[96,512]{1,0:T(8,128)} %get-tuple-element.15.refs_0_.refs_1_), channel_id=1, source_target_pairs={{0,2},{1,3},{2,0},{3,1},{4,6},{5,7},{6,4},{7,5},{8,10},{9,11},{10,... | collective-permute-start | bytes 589832 | tf_op jit(solution)/shard_map/ppermute | solution.py:19
  7.5 9.1 %collective-permute-start.7 = (f32[96,512]{1,0:T(8,128)}, f32[96,512]{1,0:T(8,128)S(1)}, u32[]{:S(2)}, u32[]{:S(2)}) collective-permute-start(f32[96,512]{1,0:T(8,128)} %get-tuple-element.15.refs_0_.refs_1_), channel_id=1, source_target_pairs={{0,4},{1,5},{2,6},{3,7},{4,0},{5,1},{6,2},{7,3},{8,12},{9,13},{10,... | collective-permute-start | bytes 589832 | tf_op jit(solution)/shard_map/ppermute | solution.py:19
  9.1 1.0 %copy-start = (f32[96,512]{1,0:T(8,128)S(1)}, f32[96,512]{1,0:T(8,128)}, u32[]{:S(2)}) copy-start(f32[96,512]{1,0:T(8,128)} %get-tuple-element.15.refs_0_.refs_1_) | copy-start | bytes 589828
  13.5 6.4 %collective-permute-start.5 = (f32[64,512]{1,0:T(8,128)S(1)}, f32[64,512]{1,0:T(8,128)S(1)}, u32[]{:S(2)}, u32[]{:S(2)}) collective-permute-start(f32[64,512]{1,0:T(8,128)S(1)} %collective-permute-done.1), channel_id=1, source_target_pairs={{0,2},{1,3},{2,0},{3,1},{4,6},{5,7},{6,4},{7,5},{8,10},{9,11},{10,... | collective-permute-start | bytes 393224 | tf_op jit(solution)/shard_map/ppermute | solution.py:19
  15.0 4.9 %collective-permute-start.6 = (f32[32,512]{1,0:T(8,128)S(1)}, f32[32,512]{1,0:T(8,128)S(1)}, u32[]{:S(2)}, u32[]{:S(2)}) collective-permute-start(f32[32,512]{1,0:T(8,128)S(1)} %collective-permute-done.2), channel_id=1, source_target_pairs={{0,2},{1,3},{2,0},{3,1},{4,6},{5,7},{6,4},{7,5},{8,10},{9,11},{10,... | collective-permute-start | bytes 196616 | tf_op jit(solution)/shard_map/ppermute | solution.py:19
  15.6 3.2 %collective-permute-start.4 = (f32[192,512]{1,0:T(8,128)S(1)}, f32[192,512]{1,0:T(8,128)S(1)}, u32[]{:S(2)}, u32[]{:S(2)}) collective-permute-start(f32[192,512]{1,0:T(8,128)S(1)} %pad_maximum_fusion), channel_id=1, source_target_pairs={{0,1},{1,0},{2,3},{3,2},{4,5},{5,4},{6,7},{7,6},{8,9},{9,8},{10,11... | collective-permute-start | bytes 1179656 | tf_op jit(solution)/shard_map/ppermute | solution.py:19
  20.0 1.5 %collective-permute-start.8 = (f32[96,512]{1,0:T(8,128)S(1)}, f32[96,512]{1,0:T(8,128)S(1)}, u32[]{:S(2)}, u32[]{:S(2)}) collective-permute-start(f32[96,512]{1,0:T(8,128)S(1)} %constant_dynamic-update-slice_fusion.2.refs_6_.refs_1_), channel_id=1, source_target_pairs={{0,1},{1,0},{2,3},{3,2},{4,5},{5,4},{6,7},{7,6},{8,9},{9,8},{10,11... | collective-permute-start | bytes 589832 | tf_op jit(solution)/shard_map/ppermute | solution.py:19
  22.2 5.6 %collective-permute-start.10 = (f32[32,512]{1,0:T(8,128)S(1)}, f32[32,512]{1,0:T(8,128)S(1)}, u32[]{:S(2)}, u32[]{:S(2)}) collective-permute-start(f32[32,512]{1,0:T(8,128)S(1)} %get-tuple-element.24), channel_id=1, source_target_pairs={{0,4},{1,5},{2,6},{3,7},{4,0},{5,1},{6,2},{7,3},{8,12},{9,13},{10,... | collective-permute-start | bytes 196616 | tf_op jit(solution)/shard_map/ppermute | solution.py:19
  23.4 4.5 %collective-permute-start.9 = (f32[32,512]{1,0:T(8,128)S(1)}, f32[32,512]{1,0:T(8,128)S(1)}, u32[]{:S(2)}, u32[]{:S(2)}) collective-permute-start(f32[32,512]{1,0:T(8,128)S(1)} %get-tuple-element.23), channel_id=1, source_target_pairs={{0,4},{1,5},{2,6},{3,7},{4,0},{5,1},{6,2},{7,3},{8,12},{9,13},{10,... | collective-permute-start | bytes 196616 | tf_op jit(solution)/shard_map/ppermute | solution.py:19

commit v12 on v11

--- a/solution.py
+++ b/solution.py
@@ -174,25 +174,26 @@
     near = swap(mine, 4)
     direct = [swap(mine, bit) for bit in beside]
 
-    (here,) = terms([(mine, [mine])], weight=64)
+    (here,) = terms([(mine, [mine])], weight=512)
     far_features, far_vectors, here = tied((far_features, far_vectors, here))
     far = [far_features, far_vectors]
     last = []
     for bit in beside:
         for pair in [far] + last:
             last = last + [[swap(piece, bit) for piece in pair]]
+    (there,) = terms([(near, [mine])], weight=256)
+    *direct, there = tied((*direct, there))
     first = [jnp.concatenate(far, 0)] + direct
-    (there,) = terms([(near, [mine, sibling] + first)], weight=2048)
-    swapped_first = swap(jnp.concatenate(first, 0), 1)
-    siblings = jnp.split(swapped_first, len(first), 0)
-    (there,) = terms([(near, siblings)], before=[there], weight=64)
+    siblings = jnp.split(swap(jnp.concatenate(first, 0), 1), len(first), 0)
+    (there,) = terms([(near, [sibling] + first)], before=[there], weight=2048)
+    there, here = terms([(near, siblings), (mine, first)], before=[there, here], weight=64)
     *pieces, there = tied((*[piece for pair in last for piece in pair], there))
     last = [jnp.concatenate(pieces[at : at + 2], 0) for at in range(0, len(pieces), 2)]
     last_siblings = [swap(block, 1) for block in last]
-    (there,) = terms([(near, last)], before=[there], weight=64)
-    rest = [sibling] + first + siblings + last + last_siblings
+    there, here = terms([(near, last), (mine, last)], before=[there, here], weight=64)
     toward_near = terms([(near, last_siblings)], before=[there], weight=64, pieces=2)
     from_near = jnp.concatenate([swap(piece, 4) for piece in toward_near], 0)
+    rest = [sibling] + siblings + last_siblings
     (here,) = terms([(mine, rest)], before=[here], weight=2048)
     return here + from_near
 

time: 28.8 us -> 30.7 us (1.066)
  waiting for transfers between devices: 4.48 us -> 5.73 us
  Pallas kernels: 10.5 us -> 10.9 us
  starting transfers between devices: 11.7 us -> 12.1 us
    ppermute x11, waiting for transfers between devices: 4.48 us -> 5.73 us  [swapped(): lax.ppermute(value, axis, [(source, source ^ bit) for source in range(cou...]
    ppermute x11, starting transfers between devices: 11.7 us -> 12.1 us  [swapped(): lax.ppermute(value, axis, [(source, source ^ bit) for source in range(cou...]
    pallas_call x6 -> x7, Pallas kernels: 8.89 us -> 9.25 us  [pair_terms(): pl.pallas_call(functools.partial(kernel, width, vectors, placed, len(bloc...]
  transfers between devices with their start and end apart: 11 -> 11, of which waited for: 4 -> 4; matrix products, arithmetic and copies ran while one was open for 0% -> 0% of each run, Pallas kernels for 34% -> 33%
where the time goes in v12:
time: 30.7 us; the launch traced here: 30.6 us
  starting transfers between devices  12.1 us (39%)
  Pallas kernels  10.9 us (36%)
  waiting for transfers between devices  5.73 us (19%)
  local copies, waits for them, and re-layouts  0.99 us (3%)
  other arithmetic  0.7 us (2%)
    ppermute x11, starting transfers between devices, swapped(): lax.ppermute(value, axis, [(source, source ^ bit) for source in range(cou...  12.1 us
    pallas_call x7, Pallas kernels, pair_terms(): pl.pallas_call(functools.partial(kernel, width, vectors, placed, len(bloc...  9.25 us
    ppermute x11, waiting for transfers between devices, swapped(): lax.ppermute(value, axis, [(source, source ^ bit) for source in range(cou...  5.73 us
    pallas_call x1, Pallas kernels, packed(): pl.pallas_call(body, out_shape=[jax.ShapeDtypeStruct((rows, points), jnp....  1.65 us
    unnamed x4, local copies, waits for them, and re-layouts  0.95 us
    add x1, other arithmetic, local(): return here + from_near  0.67 us
  transfers between devices with their start and end apart: 11, of which 4 were waited for; matrix products, arithmetic and copies ran while one was open for 0% of the time, Pallas kernels for 33%

profile of v12, /device:TPU:0, one launch (start us, length us, event | category | flops | bytes accessed | tf_op | source)
XLA Modules:
  0.0 30.6 jit_solution(2965211832317037652)
XLA Ops:
  0.0 4.0 %collective-permute-start.1 = (f32[64,512]{1,0:T(8,128)}, f32[64,512]{1,0:T(8,128)S(1)}, u32[]{:S(2)}, u32[]{:S(2)}) collective-permute-start(f32[64,512]{1,0:T(8,128)} %features_ref.1), channel_id=1, source_target_pairs={{0,8},{1,9},{2,10},{3,11},{4,12},{5,13},{6,14},{7,15},{8,0},{9,1},... | collective-permute-start | bytes 393224 | tf_op jit(solution)/shard_map/ppermute | solution.py:19
  4.0 1.7 %shard_map.37 = (f32[96,512]{1,0:T(8,128)}, f32[32,512]{1,0:T(8,128)}) custom-call(f32[64,512]{1,0:T(8,128)} %features_ref.1, f32[16,512]{1,0:T(8,128)} %solves_ref.1, f32[16,512]{1,0:T(8,128)} %probes_ref.1), custom_call_target="tpu_custom_call" | custom-call | tf_op jit(solution)/shard_map/pallas_call | solution.py:150
  5.7 1.6 %collective-permute-start.4 = (f32[96,512]{1,0:T(8,128)}, f32[96,512]{1,0:T(8,128)S(1)}, u32[]{:S(2)}, u32[]{:S(2)}) collective-permute-start(f32[96,512]{1,0:T(8,128)} %get-tuple-element.21.refs_0_.refs_1_.refs_3_.refs_2_), channel_id=1, source_target_pairs={{0,4},{1,5},{2,6},{3,7},{4,0},{5,1},{6,2},{7,3},{8,12},{9,13},{10,... | collective-permute-start | bytes 589832 | tf_op jit(solution)/shard_map/ppermute | solution.py:19
  7.3 1.5 %collective-permute-start.3 = (f32[96,512]{1,0:T(8,128)}, f32[96,512]{1,0:T(8,128)S(1)}, u32[]{:S(2)}, u32[]{:S(2)}) collective-permute-start(f32[96,512]{1,0:T(8,128)} %get-tuple-element.21.refs_0_.refs_1_.refs_3_.refs_2_), channel_id=1, source_target_pairs={{0,2},{1,3},{2,0},{3,1},{4,6},{5,7},{6,4},{7,5},{8,10},{9,11},{10,... | collective-permute-start | bytes 589832 | tf_op jit(solution)/shard_map/ppermute | solution.py:19
  8.8 0.3 %collective-permute-start.2 = (f32[32,512]{1,0:T(8,128)}, f32[32,512]{1,0:T(8,128)S(1)}, u32[]{:S(2)}, u32[]{:S(2)}) collective-permute-start(f32[32,512]{1,0:T(8,128)} %get-tuple-element.22), channel_id=1, source_target_pairs={{0,8},{1,9},{2,10},{3,11},{4,12},{5,13},{6,14},{7,15},{8,0},{9,1},... | collective-permute-start | bytes 196616 | tf_op jit(solution)/shard_map/ppermute | solution.py:19
  9.1 0.0 collective-permute-start
  9.1 0.0 copy-start
  9.1 0.9 %copy-done = f32[96,512]{1,0:T(8,128)S(1)} copy-done((f32[96,512]{1,0:T(8,128)S(1)}, f32[96,512]{1,0:T(8,128)}, u32[]{:S(2)}) %copy-start) | copy-done | bytes 196632
  10.1 0.8 %shard_map.38.refs_7_ = f32[64,512]{1,0:T(8,128)S(1)} custom-call(f32[96,512]{1,0:T(8,128)S(1)} %copy-done), custom_call_target="tpu_custom_call" | custom-call | flops 268435456 | bytes 196608 | tf_op jit(solution)/shard_map/pallas_call | solution.py:125
  10.8 4.2 %collective-permute-done.2 = f32[32,512]{1,0:T(8,128)S(1)} collective-permute-done((f32[32,512]{1,0:T(8,128)}, f32[32,512]{1,0:T(8,128)S(1)}, u32[]{:S(2)}, u32[]{:S(2)}) %collective-permute-start.2) | collective-permute-done | bytes 65568 | tf_op jit(solution)/shard_map/ppermute | solution.py:19
  15.0 0.0 collective-permute-done.1
  15.0 0.3 collective-permute-start.6
  15.3 1.7 %collective-permute-start.7 = (f32[32,512]{1,0:T(8,128)S(1)}, f32[32,512]{1,0:T(8,128)S(1)}, u32[]{:S(2)}, u32[]{:S(2)}) collective-permute-start(f32[32,512]{1,0:T(8,128)S(1)} %collective-permute-done.2), channel_id=1, source_target_pairs={{0,2},{1,3},{2,0},{3,1},{4,6},{5,7},{6,4},{7,5},{8,10},{9,11},{10,... | collective-permute-start | bytes 196616 | tf_op jit(solution)/shard_map/ppermute | solution.py:19
  17.0 0.0 collective-permute-done.4.refs_0_
  17.0 0.8 %shard_map.39.refs_4_ = f32[64,512]{1,0:T(8,128)S(1)} custom-call(f32[96,512]{1,0:T(8,128)S(1)} %collective-permute-done.4.refs_0_, f32[96,512]{1,0:T(8,128)S(1)} %copy-done), custom_call_target="tpu_custom_call" | custom-call | flops 134217728 | bytes 393216 | tf_op jit(solution)/shard_map/pallas_call | solution.py:125
  17.8 0.0 collective-permute-done.3.refs_3_.refs_5_
  17.8 0.1 collective-permute-start.5
  17.9 0.0 collective-permute-done.refs_1_
  17.9 1.6 %shard_map.40.refs_6_ = f32[64,512]{1,0:T(8,128)S(1)} custom-call(f32[96,512]{1,0:T(8,128)S(1)} %collective-permute-done.4.refs_0_, f32[96,512]{1,0:T(8,128)S(1)} %collective-permute-done.refs_1_, f32[96,512]{1,0:T(8,128)S(1)} %constant_dynamic-update-slice_fusion.refs_2_.refs_4_, f32[96,512]{1,0:T(8,128)S(1)} %collective-permute-done.3.refs_3_.refs_5_, ...), custom_call_target="tpu_custom_call" | custom-call | flops 3221225472 | bytes 983040 | tf_op jit(solution)/shard_map/pallas_call | solution.py:125
  19.5 0.1 collective-permute-done.5
  19.7 2.0 %shard_map.41 = (f32[64,512]{1,0:T(8,128)S(1)}, f32[64,512]{1,0:T(8,128)S(1)}) custom-call(f32[96,512]{1,0:T(8,128)S(1)} %collective-permute-done.4.refs_0_, f32[96,512]{1,0:T(8,128)S(1)} %get-tuple-element.38.refs_1_.refs_2_, f32[96,512]{1,0:T(8,128)S(1)} %get-tuple-element.37.refs_2_.refs_3_, f32[96,512]{1,0:T(8,128)S(1)} %copy-done, ...), custom_call_target="tpu_custom_call" | custom-call | flops 134217728 | bytes 1572864 | tf_op jit(solution)/shard_map/pallas_call | solution.py:125
  21.7 0.0 collective-permute-done.7
  21.7 0.0 collective-permute-done.6
  21.8 0.5 %collective-permute-start.8 = (f32[96,512]{1,0:T(8,128)S(1)}, f32[96,512]{1,0:T(8,128)S(1)}, u32[]{:S(2)}, u32[]{:S(2)}) collective-permute-start(f32[96,512]{1,0:T(8,128)S(1)} %constant_dynamic-update-slice_fusion.2.refs_1_), channel_id=1, source_target_pairs={{0,1},{1,0},{2,3},{3,2},{4,5},{5,4},{6,7},{7,6},{8,9},{9,8},{10,11... | collective-permute-start | bytes 589832 | tf_op jit(solution)/shard_map/ppermute | solution.py:19
  22.2 1.3 %shard_map.42 = (f32[64,512]{1,0:T(8,128)S(1)}, f32[64,512]{1,0:T(8,128)S(1)}) custom-call(f32[96,512]{1,0:T(8,128)S(1)} %collective-permute-done.4.refs_0_, f32[96,512]{1,0:T(8,128)S(1)} %constant_dynamic-update-slice_fusion.2.refs_1_, f32[96,512]{1,0:T(8,128)S(1)} %copy-done, f32[64,512]{1,0:T(8,128)S(1)} %get-tuple-element.31.refs_3_, ...), custom_call_target="tpu_custom_call" | custom-call | flops 67108864 | bytes 983040 | tf_op jit(solution)/shard_map/pallas_call | solution.py:125
  23.6 0.0 collective-permute-done.8.refs_4_.refs_1_
  23.6 0.8 %shard_map.44 = (f32[32,512]{1,0:T(8,128)S(1)}, f32[32,512]{1,0:T(8,128)S(1)}) custom-call(f32[96,512]{1,0:T(8,128)S(1)} %collective-permute-done.4.refs_0_, f32[96,512]{1,0:T(8,128)S(1)} %collective-permute-done.8.refs_4_.refs_1_, f32[64,512]{1,0:T(8,128)S(1)} %get-tuple-element.34.refs_2_), custom_call_target="tpu_custom_call" | custom-call | flops 33554432 | bytes 589824 | tf_op jit(solution)/shard_map/pallas_call | solution.py:125
  24.3 0.2 collective-permute-start.10
  24.6 1.9 %collective-permute-start.9 = (f32[32,512]{1,0:T(8,128)S(1)}, f32[32,512]{1,0:T(8,128)S(1)}, u32[]{:S(2)}, u32[]{:S(2)}) collective-permute-start(f32[32,512]{1,0:T(8,128)S(1)} %get-tuple-element.35), channel_id=1, source_target_pairs={{0,4},{1,5},{2,6},{3,7},{4,0},{5,1},{6,2},{7,3},{8,12},{9,13},{10,... | collective-permute-start | bytes 196616 | tf_op jit(solution)/shard_map/ppermute | solution.py:19
  26.4 2.0 %shard_map.43 = f32[64,512]{1,0:T(8,128)S(1)} custom-call(f32[96,512]{1,0:T(8,128)S(1)} %copy-done, f32[96,512]{1,0:T(8,128)S(1)} %collective-permute-done.refs_1_, f32[96,512]{1,0:T(8,128)S(1)} %get-tuple-element.38.refs_1_.refs_2_, f32[96,512]{1,0:T(8,128)S(1)} %get-tuple-element.37.refs_2_.refs_3_, f32[96,512]{1,0:T(8,128)S(1)} %collective-permute-done.8.refs_4_.refs_1_, ...), custom_call_target="tpu_custom_call" | custom-call | flops 4294967296 | bytes 1179648 | tf_op jit(solution)/shard_map/pallas_call | solution.py:125
  28.5 0.7 %collective-permute-done.10 = f32[32,512]{1,0:T(8,128)S(1)} collective-permute-done((f32[32,512]{1,0:T(8,128)S(1)}, f32[32,512]{1,0:T(8,128)S(1)}, u32[]{:S(2)}, u32[]{:S(2)}) %collective-permute-start.10) | collective-permute-done | bytes 65568 | tf_op jit(solution)/shard_map/ppermute | solution.py:19
  29.2 0.7 %collective-permute-done.9 = f32[32,512]{1,0:T(8,128)S(1)} collective-permute-done((f32[32,512]{1,0:T(8,128)S(1)}, f32[32,512]{1,0:T(8,128)S(1)}, u32[]{:S(2)}, u32[]{:S(2)}) %collective-permute-start.9) | collective-permute-done | bytes 65568 | tf_op jit(solution)/shard_map/ppermute | solution.py:19
  29.9 0.7 %maximum_add_fusion = f32[64,512]{1,0:T(8,128)} fusion(f32[64,512]{1,0:T(8,128)S(1)} %shard_map.43, f32[32,512]{1,0:T(8,128)S(1)} %collective-permute-done.10, f32[32,512]{1,0:T(8,128)S(1)} %collective-permute-done.9), kind=kLoop, calls=%fused_computation.1 | loop fusion | flops 65536 | bytes 393216 | tf_op jit(solution)/shard_map/add | solution.py:198
  (6 shorter events, 0.1 us)
Async XLA Ops:
  0.0 15.0 %collective-permute-start.1 = (f32[64,512]{1,0:T(8,128)}, f32[64,512]{1,0:T(8,128)S(1)}, u32[]{:S(2)}, u32[]{:S(2)}) collective-permute-start(f32[64,512]{1,0:T(8,128)} %features_ref.1), channel_id=1, source_target_pairs={{0,8},{1,9},{2,10},{3,11},{4,12},{5,13},{6,14},{7,15},{8,0},{9,1},... | collective-permute-start | bytes 393224 | tf_op jit(solution)/shard_map/ppermute | solution.py:19
  5.7 11.3 %collective-permute-start.4 = (f32[96,512]{1,0:T(8,128)}, f32[96,512]{1,0:T(8,128)S(1)}, u32[]{:S(2)}, u32[]{:S(2)}) collective-permute-start(f32[96,512]{1,0:T(8,128)} %get-tuple-element.21.refs_0_.refs_1_.refs_3_.refs_2_), channel_id=1, source_target_pairs={{0,4},{1,5},{2,6},{3,7},{4,0},{5,1},{6,2},{7,3},{8,12},{9,13},{10,... | collective-permute-start | bytes 589832 | tf_op jit(solution)/shard_map/ppermute | solution.py:19
  7.3 10.5 %collective-permute-start.3 = (f32[96,512]{1,0:T(8,128)}, f32[96,512]{1,0:T(8,128)S(1)}, u32[]{:S(2)}, u32[]{:S(2)}) collective-permute-start(f32[96,512]{1,0:T(8,128)} %get-tuple-element.21.refs_0_.refs_1_.refs_3_.refs_2_), channel_id=1, source_target_pairs={{0,2},{1,3},{2,0},{3,1},{4,6},{5,7},{6,4},{7,5},{8,10},{9,11},{10,... | collective-permute-start | bytes 589832 | tf_op jit(solution)/shard_map/ppermute | solution.py:19
  8.8 6.2 %collective-permute-start.2 = (f32[32,512]{1,0:T(8,128)}, f32[32,512]{1,0:T(8,128)S(1)}, u32[]{:S(2)}, u32[]{:S(2)}) collective-permute-start(f32[32,512]{1,0:T(8,128)} %get-tuple-element.22), channel_id=1, source_target_pairs={{0,8},{1,9},{2,10},{3,11},{4,12},{5,13},{6,14},{7,15},{8,0},{9,1},... | collective-permute-start | bytes 196616 | tf_op jit(solution)/shard_map/ppermute | solution.py:19
  9.1 8.8 %collective-permute-start = (f32[96,512]{1,0:T(8,128)}, f32[96,512]{1,0:T(8,128)S(1)}, u32[]{:S(2)}, u32[]{:S(2)}) collective-permute-start(f32[96,512]{1,0:T(8,128)} %get-tuple-element.21.refs_0_.refs_1_.refs_3_.refs_2_), channel_id=1, source_target_pairs={{0,1},{1,0},{2,3},{3,2},{4,5},{5,4},{6,7},{7,6},{8,9},{9,8},{10,11... | collective-permute-start | bytes 589832 | tf_op jit(solution)/shard_map/ppermute | solution.py:19
  9.1 0.9 %copy-start = (f32[96,512]{1,0:T(8,128)S(1)}, f32[96,512]{1,0:T(8,128)}, u32[]{:S(2)}) copy-start(f32[96,512]{1,0:T(8,128)} %get-tuple-element.21.refs_0_.refs_1_.refs_3_.refs_2_) | copy-start | bytes 589828
  15.0 6.8 %collective-permute-start.6 = (f32[64,512]{1,0:T(8,128)S(1)}, f32[64,512]{1,0:T(8,128)S(1)}, u32[]{:S(2)}, u32[]{:S(2)}) collective-permute-start(f32[64,512]{1,0:T(8,128)S(1)} %collective-permute-done.1), channel_id=1, source_target_pairs={{0,2},{1,3},{2,0},{3,1},{4,6},{5,7},{6,4},{7,5},{8,10},{9,11},{10,... | collective-permute-start | bytes 393224 | tf_op jit(solution)/shard_map/ppermute | solution.py:19
  15.3 6.5 %collective-permute-start.7 = (f32[32,512]{1,0:T(8,128)S(1)}, f32[32,512]{1,0:T(8,128)S(1)}, u32[]{:S(2)}, u32[]{:S(2)}) collective-permute-start(f32[32,512]{1,0:T(8,128)S(1)} %collective-permute-done.2), channel_id=1, source_target_pairs={{0,2},{1,3},{2,0},{3,1},{4,6},{5,7},{6,4},{7,5},{8,10},{9,11},{10,... | collective-permute-start | bytes 196616 | tf_op jit(solution)/shard_map/ppermute | solution.py:19
  17.8 1.8 %collective-permute-start.5 = (f32[192,512]{1,0:T(8,128)S(1)}, f32[192,512]{1,0:T(8,128)S(1)}, u32[]{:S(2)}, u32[]{:S(2)}) collective-permute-start(f32[192,512]{1,0:T(8,128)S(1)} %pad_maximum_fusion), channel_id=1, source_target_pairs={{0,1},{1,0},{2,3},{3,2},{4,5},{5,4},{6,7},{7,6},{8,9},{9,8},{10,11... | collective-permute-start | bytes 1179656 | tf_op jit(solution)/shard_map/ppermute | solution.py:19
  21.8 1.8 %collective-permute-start.8 = (f32[96,512]{1,0:T(8,128)S(1)}, f32[96,512]{1,0:T(8,128)S(1)}, u32[]{:S(2)}, u32[]{:S(2)}) collective-permute-start(f32[96,512]{1,0:T(8,128)S(1)} %constant_dynamic-update-slice_fusion.2.refs_1_), channel_id=1, source_target_pairs={{0,1},{1,0},{2,3},{3,2},{4,5},{5,4},{6,7},{7,6},{8,9},{9,8},{10,11... | collective-permute-start | bytes 589832 | tf_op jit(solution)/shard_map/ppermute | solution.py:19
  24.3 4.9 %collective-permute-start.10 = (f32[32,512]{1,0:T(8,128)S(1)}, f32[32,512]{1,0:T(8,128)S(1)}, u32[]{:S(2)}, u32[]{:S(2)}) collective-permute-start(f32[32,512]{1,0:T(8,128)S(1)} %get-tuple-element.36), channel_id=1, source_target_pairs={{0,4},{1,5},{2,6},{3,7},{4,0},{5,1},{6,2},{7,3},{8,12},{9,13},{10,... | collective-permute-start | bytes 196616 | tf_op jit(solution)/shard_map/ppermute | solution.py:19
  24.6 5.4 %collective-permute-start.9 = (f32[32,512]{1,0:T(8,128)S(1)}, f32[32,512]{1,0:T(8,128)S(1)}, u32[]{:S(2)}, u32[]{:S(2)}) collective-permute-start(f32[32,512]{1,0:T(8,128)S(1)} %get-tuple-element.35), channel_id=1, source_target_pairs={{0,4},{1,5},{2,6},{3,7},{4,0},{5,1},{6,2},{7,3},{8,12},{9,13},{10,... | collective-permute-start | bytes 196616 | tf_op jit(solution)/shard_map/ppermute | solution.py:19

commit v13 on v12

--- a/solution.py
+++ b/solution.py
@@ -181,20 +181,21 @@
     for bit in beside:
         for pair in [far] + last:
             last = last + [[swap(piece, bit) for piece in pair]]
-    (there,) = terms([(near, [mine])], weight=256)
-    *direct, there = tied((*direct, there))
-    first = [jnp.concatenate(far, 0)] + direct
+    far = jnp.concatenate(far, 0)
+    (here,) = terms([(mine, [sibling, far])], before=[here], weight=256)
+    near, *direct, here = tied((near, *direct, here))
+    first = [far] + direct
     siblings = jnp.split(swap(jnp.concatenate(first, 0), 1), len(first), 0)
-    (there,) = terms([(near, [sibling] + first)], before=[there], weight=2048)
-    there, here = terms([(near, siblings), (mine, first)], before=[there, here], weight=64)
+    (there,) = terms([(near, [mine, sibling] + first)], weight=2048)
+    (there,) = terms([(near, siblings)], before=[there], weight=100000)
     *pieces, there = tied((*[piece for pair in last for piece in pair], there))
     last = [jnp.concatenate(pieces[at : at + 2], 0) for at in range(0, len(pieces), 2)]
     last_siblings = [swap(block, 1) for block in last]
     there, here = terms([(near, last), (mine, last)], before=[there, here], weight=64)
-    toward_near = terms([(near, last_siblings)], before=[there], weight=64, pieces=2)
+    toward_near = terms([(near, last_siblings)], before=[there], weight=8, pieces=2)
     from_near = jnp.concatenate([swap(piece, 4) for piece in toward_near], 0)
-    rest = [sibling] + siblings + last_siblings
-    (here,) = terms([(mine, rest)], before=[here], weight=2048)
+    rest = direct + siblings + last_siblings
+    (here,) = terms([(mine, rest)], before=[here], weight=100000)
     return here + from_near
 
 

time: 30.7 us -> 31 us (level)
  waiting for transfers between devices: 5.73 us -> 4.38 us
  other arithmetic: 0.7 us -> 1.57 us
  Pallas kernels: 10.9 us -> 11.5 us
    ppermute x11, waiting for transfers between devices: 5.73 us -> 4.38 us  [swapped(): lax.ppermute(value, axis, [(source, source ^ bit) for source in range(cou...]
    add x1, other arithmetic: 0.67 us -> 1.54 us  [local(): return here + from_near]
    pallas_call x7, Pallas kernels: 9.25 us -> 9.81 us  [pair_terms(): pl.pallas_call(functools.partial(kernel, width, vectors, placed, len(bloc...]
  transfers between devices with their start and end apart: 11 -> 11, of which waited for: 4 -> 3; matrix products, arithmetic and copies ran while one was open for 0% -> 0% of each run, Pallas kernels for 33% -> 33%
where the time goes in v13:
time: 31 us; the launch traced here: 30.8 us
  starting transfers between devices  12.2 us (39%)
  Pallas kernels  11.5 us (37%)
  waiting for transfers between devices  4.38 us (14%)
  other arithmetic  1.57 us (5%)
  local copies, waits for them, and re-layouts  1.02 us (3%)
    ppermute x11, starting transfers between devices, swapped(): lax.ppermute(value, axis, [(source, source ^ bit) for source in range(cou...  12.2 us
    pallas_call x7, Pallas kernels, pair_terms(): pl.pallas_call(functools.partial(kernel, width, vectors, placed, len(bloc...  9.81 us
    ppermute x11, waiting for transfers between devices, swapped(): lax.ppermute(value, axis, [(source, source ^ bit) for source in range(cou...  4.38 us
    pallas_call x1, Pallas kernels, packed(): pl.pallas_call(body, out_shape=[jax.ShapeDtypeStruct((rows, points), jnp....  1.65 us
    add x1, other arithmetic, local(): return here + from_near  1.54 us
    unnamed x4, local copies, waits for them, and re-layouts  0.98 us
  transfers between devices with their start and end apart: 11, of which 3 were waited for; matrix products, arithmetic and copies ran while one was open for 0% of the time, Pallas kernels for 33%

profile of v13, /device:TPU:0, one launch (start us, length us, event | category | flops | bytes accessed | tf_op | source)
XLA Modules:
  0.0 30.8 jit_solution(10138149887131213656)
XLA Ops:
  0.0 4.0 %collective-permute-start.3 = (f32[64,512]{1,0:T(8,128)}, f32[64,512]{1,0:T(8,128)S(1)}, u32[]{:S(2)}, u32[]{:S(2)}) collective-permute-start(f32[64,512]{1,0:T(8,128)} %features_ref.1), channel_id=1, source_target_pairs={{0,8},{1,9},{2,10},{3,11},{4,12},{5,13},{6,14},{7,15},{8,0},{9,1},... | collective-permute-start | bytes 393224 | tf_op jit(solution)/shard_map/ppermute | solution.py:19
  4.0 1.7 %shard_map.37 = (f32[96,512]{1,0:T(8,128)}, f32[32,512]{1,0:T(8,128)}) custom-call(f32[64,512]{1,0:T(8,128)} %features_ref.1, f32[16,512]{1,0:T(8,128)} %solves_ref.1, f32[16,512]{1,0:T(8,128)} %probes_ref.1), custom_call_target="tpu_custom_call" | custom-call | tf_op jit(solution)/shard_map/pallas_call | solution.py:150
  5.7 0.0 collective-permute-start.4
  5.7 0.0 collective-permute-start.2
  5.7 1.9 %collective-permute-start.1 = (f32[96,512]{1,0:T(8,128)}, f32[96,512]{1,0:T(8,128)S(1)}, u32[]{:S(2)}, u32[]{:S(2)}) collective-permute-start(f32[96,512]{1,0:T(8,128)} %get-tuple-element.20.refs_0_.refs_1_.refs_2_), channel_id=1, source_target_pairs={{0,2},{1,3},{2,0},{3,1},{4,6},{5,7},{6,4},{7,5},{8,10},{9,11},{10,... | collective-permute-start | bytes 589832 | tf_op jit(solution)/shard_map/ppermute | solution.py:19
  7.5 1.6 %collective-permute-start = (f32[96,512]{1,0:T(8,128)}, f32[96,512]{1,0:T(8,128)S(1)}, u32[]{:S(2)}, u32[]{:S(2)}) collective-permute-start(f32[96,512]{1,0:T(8,128)} %get-tuple-element.20.refs_0_.refs_1_.refs_2_), channel_id=1, source_target_pairs={{0,4},{1,5},{2,6},{3,7},{4,0},{5,1},{6,2},{7,3},{8,12},{9,13},{10,... | collective-permute-start | bytes 589832 | tf_op jit(solution)/shard_map/ppermute | solution.py:19
  9.1 0.0 copy-start
  9.1 1.0 %copy-done = f32[96,512]{1,0:T(8,128)S(1)} copy-done((f32[96,512]{1,0:T(8,128)S(1)}, f32[96,512]{1,0:T(8,128)}, u32[]{:S(2)}) %copy-start) | copy-done | bytes 196632
  10.1 0.8 %shard_map.38.refs_3_ = f32[64,512]{1,0:T(8,128)S(1)} custom-call(f32[96,512]{1,0:T(8,128)S(1)} %copy-done), custom_call_target="tpu_custom_call" | custom-call | flops 268435456 | bytes 196608 | tf_op jit(solution)/shard_map/pallas_call | solution.py:125
  10.8 2.6 %collective-permute-done.4 = f32[32,512]{1,0:T(8,128)S(1)} collective-permute-done((f32[32,512]{1,0:T(8,128)}, f32[32,512]{1,0:T(8,128)S(1)}, u32[]{:S(2)}, u32[]{:S(2)}) %collective-permute-start.4) | collective-permute-done | bytes 65568 | tf_op jit(solution)/shard_map/ppermute | solution.py:19
  13.5 0.0 collective-permute-done.3
  13.5 1.5 %collective-permute-start.6 = (f32[64,512]{1,0:T(8,128)S(1)}, f32[64,512]{1,0:T(8,128)S(1)}, u32[]{:S(2)}, u32[]{:S(2)}) collective-permute-start(f32[64,512]{1,0:T(8,128)S(1)} %collective-permute-done.3), channel_id=1, source_target_pairs={{0,2},{1,3},{2,0},{3,1},{4,6},{5,7},{6,4},{7,5},{8,10},{9,11},{10,... | collective-permute-start | bytes 393224 | tf_op jit(solution)/shard_map/ppermute | solution.py:19
  15.0 0.6 %collective-permute-start.7 = (f32[32,512]{1,0:T(8,128)S(1)}, f32[32,512]{1,0:T(8,128)S(1)}, u32[]{:S(2)}, u32[]{:S(2)}) collective-permute-start(f32[32,512]{1,0:T(8,128)S(1)} %collective-permute-done.4), channel_id=1, source_target_pairs={{0,2},{1,3},{2,0},{3,1},{4,6},{5,7},{6,4},{7,5},{8,10},{9,11},{10,... | collective-permute-start | bytes 196616 | tf_op jit(solution)/shard_map/ppermute | solution.py:19
  15.6 0.0 collective-permute-done.2.refs_1_.refs_2_
  15.6 1.1 %shard_map.39.refs_4_ = f32[64,512]{1,0:T(8,128)S(1)} custom-call(f32[96,512]{1,0:T(8,128)S(1)} %copy-done, f32[96,512]{1,0:T(8,128)S(1)} %collective-permute-done.2.refs_1_.refs_2_, f32[96,512]{1,0:T(8,128)S(1)} %constant_dynamic-update-slice_fusion.refs_2_.refs_3_, f32[64,512]{1,0:T(8,128)S(1)} %shard_map.38.refs_3_), custom_call_target="tpu_custom_call" | custom-call | flops 268435456 | bytes 786432 | tf_op jit(solution)/shard_map/pallas_call | solution.py:125
  16.7 0.0 collective-permute-done.1.refs_4_.refs_1_
  16.7 0.0 collective-permute-done.refs_0_
  16.8 0.1 collective-permute-start.5
  16.9 2.0 %shard_map.40.refs_3_ = f32[64,512]{1,0:T(8,128)S(1)} custom-call(f32[96,512]{1,0:T(8,128)S(1)} %collective-permute-done.refs_0_, f32[96,512]{1,0:T(8,128)S(1)} %copy-done, f32[96,512]{1,0:T(8,128)S(1)} %collective-permute-done.2.refs_1_.refs_2_, f32[96,512]{1,0:T(8,128)S(1)} %constant_dynamic-update-slice_fusion.refs_2_.refs_3_, ...), custom_call_target="tpu_custom_call" | custom-call | flops 4294967296 | bytes 983040 | tf_op jit(solution)/shard_map/pallas_call | solution.py:125
  18.9 0.0 collective-permute-done.5
  19.0 1.1 %shard_map.41.refs_3_ = f32[64,512]{1,0:T(8,128)S(1)} custom-call(f32[96,512]{1,0:T(8,128)S(1)} %collective-permute-done.refs_0_, f32[96,512]{1,0:T(8,128)S(1)} %get-tuple-element.36.refs_1_.refs_2_, f32[96,512]{1,0:T(8,128)S(1)} %get-tuple-element.35.refs_2_.refs_3_, f32[64,512]{1,0:T(8,128)S(1)} %shard_map.40.refs_3_), custom_call_target="tpu_custom_call" | custom-call | flops 104857600000 | bytes 786432 | tf_op jit(solution)/shard_map/pallas_call | solution.py:125
  20.1 0.0 collective-permute-done.7
  20.1 0.0 collective-permute-done.6
  20.1 0.6 %collective-permute-start.8 = (f32[96,512]{1,0:T(8,128)S(1)}, f32[96,512]{1,0:T(8,128)S(1)}, u32[]{:S(2)}, u32[]{:S(2)}) collective-permute-start(f32[96,512]{1,0:T(8,128)S(1)} %constant_dynamic-update-slice_fusion.2.refs_1_), channel_id=1, source_target_pairs={{0,1},{1,0},{2,3},{3,2},{4,5},{5,4},{6,7},{7,6},{8,9},{9,8},{10,11... | collective-permute-start | bytes 589832 | tf_op jit(solution)/shard_map/ppermute | solution.py:19
  20.7 1.3 %shard_map.42 = (f32[64,512]{1,0:T(8,128)S(1)}, f32[64,512]{1,0:T(8,128)S(1)}) custom-call(f32[96,512]{1,0:T(8,128)S(1)} %collective-permute-done.refs_0_, f32[96,512]{1,0:T(8,128)S(1)} %constant_dynamic-update-slice_fusion.2.refs_1_, f32[96,512]{1,0:T(8,128)S(1)} %copy-done, f32[64,512]{1,0:T(8,128)S(1)} %shard_map.41.refs_3_, f32[64,512]{1,0:T(8,128)S(1)} %shard_map.39.refs_4_), custom_call_target="tpu_custom_call" | custom-call | flops 67108864 | bytes 983040 | tf_op jit(solution)/shard_map/pallas_call | solution.py:125
  22.0 0.0 collective-permute-done.8.refs_4_.refs_1_
  22.0 1.4 %shard_map.44 = (f32[32,512]{1,0:T(8,128)}, f32[32,512]{1,0:T(8,128)}) custom-call(f32[96,512]{1,0:T(8,128)S(1)} %collective-permute-done.refs_0_, f32[96,512]{1,0:T(8,128)S(1)} %collective-permute-done.8.refs_4_.refs_1_, f32[64,512]{1,0:T(8,128)S(1)} %get-tuple-element.32.refs_2_), custom_call_target="tpu_custom_call" | custom-call | flops 4194304 | bytes 589824 | tf_op jit(solution)/shard_map/pallas_call | solution.py:125
  23.4 0.8 %collective-permute-start.9 = (f32[32,512]{1,0:T(8,128)}, f32[32,512]{1,0:T(8,128)}, u32[]{:S(2)}, u32[]{:S(2)}) collective-permute-start(f32[32,512]{1,0:T(8,128)} %get-tuple-element.33), channel_id=1, source_target_pairs={{0,4},{1,5},{2,6},{3,7},{4,0},{5,1},{6,2},{7,3},{8,12},{9,13},{10,... | collective-permute-start | bytes 196616 | tf_op jit(solution)/shard_map/ppermute | solution.py:19
  24.2 1.3 %collective-permute-start.10 = (f32[32,512]{1,0:T(8,128)}, f32[32,512]{1,0:T(8,128)}, u32[]{:S(2)}, u32[]{:S(2)}) collective-permute-start(f32[32,512]{1,0:T(8,128)} %get-tuple-element.34), channel_id=1, source_target_pairs={{0,4},{1,5},{2,6},{3,7},{4,0},{5,1},{6,2},{7,3},{8,12},{9,13},{10,... | collective-permute-start | bytes 196616 | tf_op jit(solution)/shard_map/ppermute | solution.py:19
  25.5 2.0 %shard_map.43 = f32[64,512]{1,0:T(8,128)S(1)} custom-call(f32[96,512]{1,0:T(8,128)S(1)} %copy-done, f32[96,512]{1,0:T(8,128)S(1)} %collective-permute-done.1.refs_4_.refs_1_, f32[96,512]{1,0:T(8,128)S(1)} %get-tuple-element.36.refs_1_.refs_2_, f32[96,512]{1,0:T(8,128)S(1)} %get-tuple-element.35.refs_2_.refs_3_, ...), custom_call_target="tpu_custom_call" | custom-call | flops 209715200000 | bytes 1179648 | tf_op jit(solution)/shard_map/pallas_call | solution.py:125
  27.5 1.0 %collective-permute-done.9 = f32[32,512]{1,0:T(8,128)} collective-permute-done((f32[32,512]{1,0:T(8,128)}, f32[32,512]{1,0:T(8,128)}, u32[]{:S(2)}, u32[]{:S(2)}) %collective-permute-start.9) | collective-permute-done | bytes 65568 | tf_op jit(solution)/shard_map/ppermute | solution.py:19
  28.6 0.7 %collective-permute-done.10 = f32[32,512]{1,0:T(8,128)} collective-permute-done((f32[32,512]{1,0:T(8,128)}, f32[32,512]{1,0:T(8,128)}, u32[]{:S(2)}, u32[]{:S(2)}) %collective-permute-start.10) | collective-permute-done | bytes 65568 | tf_op jit(solution)/shard_map/ppermute | solution.py:19
  29.3 1.5 %maximum_add_fusion = f32[64,512]{1,0:T(8,128)} fusion(f32[64,512]{1,0:T(8,128)S(1)} %shard_map.43, f32[32,512]{1,0:T(8,128)} %collective-permute-done.10, f32[32,512]{1,0:T(8,128)} %collective-permute-done.9), kind=kLoop, calls=%fused_computation.1 | loop fusion | flops 65536 | bytes 393216 | tf_op jit(solution)/shard_map/add | solution.py:199
  (6 shorter events, 0.1 us)
Async XLA Ops:
  0.0 13.5 %collective-permute-start.3 = (f32[64,512]{1,0:T(8,128)}, f32[64,512]{1,0:T(8,128)S(1)}, u32[]{:S(2)}, u32[]{:S(2)}) collective-permute-start(f32[64,512]{1,0:T(8,128)} %features_ref.1), channel_id=1, source_target_pairs={{0,8},{1,9},{2,10},{3,11},{4,12},{5,13},{6,14},{7,15},{8,0},{9,1},... | collective-permute-start | bytes 393224 | tf_op jit(solution)/shard_map/ppermute | solution.py:19
  5.7 7.8 %collective-permute-start.4 = (f32[32,512]{1,0:T(8,128)}, f32[32,512]{1,0:T(8,128)S(1)}, u32[]{:S(2)}, u32[]{:S(2)}) collective-permute-start(f32[32,512]{1,0:T(8,128)} %get-tuple-element.21), channel_id=1, source_target_pairs={{0,8},{1,9},{2,10},{3,11},{4,12},{5,13},{6,14},{7,15},{8,0},{9,1},... | collective-permute-start | bytes 196616 | tf_op jit(solution)/shard_map/ppermute | solution.py:19
  5.7 9.9 %collective-permute-start.2 = (f32[96,512]{1,0:T(8,128)}, f32[96,512]{1,0:T(8,128)S(1)}, u32[]{:S(2)}, u32[]{:S(2)}) collective-permute-start(f32[96,512]{1,0:T(8,128)} %get-tuple-element.20.refs_0_.refs_1_.refs_2_), channel_id=1, source_target_pairs={{0,1},{1,0},{2,3},{3,2},{4,5},{5,4},{6,7},{7,6},{8,9},{9,8},{10,11... | collective-permute-start | bytes 589832 | tf_op jit(solution)/shard_map/ppermute | solution.py:19
  5.7 11.0 %collective-permute-start.1 = (f32[96,512]{1,0:T(8,128)}, f32[96,512]{1,0:T(8,128)S(1)}, u32[]{:S(2)}, u32[]{:S(2)}) collective-permute-start(f32[96,512]{1,0:T(8,128)} %get-tuple-element.20.refs_0_.refs_1_.refs_2_), channel_id=1, source_target_pairs={{0,2},{1,3},{2,0},{3,1},{4,6},{5,7},{6,4},{7,5},{8,10},{9,11},{10,... | collective-permute-start | bytes 589832 | tf_op jit(solution)/shard_map/ppermute | solution.py:19
  7.5 9.2 %collective-permute-start = (f32[96,512]{1,0:T(8,128)}, f32[96,512]{1,0:T(8,128)S(1)}, u32[]{:S(2)}, u32[]{:S(2)}) collective-permute-start(f32[96,512]{1,0:T(8,128)} %get-tuple-element.20.refs_0_.refs_1_.refs_2_), channel_id=1, source_target_pairs={{0,4},{1,5},{2,6},{3,7},{4,0},{5,1},{6,2},{7,3},{8,12},{9,13},{10,... | collective-permute-start | bytes 589832 | tf_op jit(solution)/shard_map/ppermute | solution.py:19
  9.1 1.0 %copy-start = (f32[96,512]{1,0:T(8,128)S(1)}, f32[96,512]{1,0:T(8,128)}, u32[]{:S(2)}) copy-start(f32[96,512]{1,0:T(8,128)} %get-tuple-element.20.refs_0_.refs_1_.refs_2_) | copy-start | bytes 589828
  13.5 6.6 %collective-permute-start.6 = (f32[64,512]{1,0:T(8,128)S(1)}, f32[64,512]{1,0:T(8,128)S(1)}, u32[]{:S(2)}, u32[]{:S(2)}) collective-permute-start(f32[64,512]{1,0:T(8,128)S(1)} %collective-permute-done.3), channel_id=1, source_target_pairs={{0,2},{1,3},{2,0},{3,1},{4,6},{5,7},{6,4},{7,5},{8,10},{9,11},{10,... | collective-permute-start | bytes 393224 | tf_op jit(solution)/shard_map/ppermute | solution.py:19
  15.0 5.1 %collective-permute-start.7 = (f32[32,512]{1,0:T(8,128)S(1)}, f32[32,512]{1,0:T(8,128)S(1)}, u32[]{:S(2)}, u32[]{:S(2)}) collective-permute-start(f32[32,512]{1,0:T(8,128)S(1)} %collective-permute-done.4), channel_id=1, source_target_pairs={{0,2},{1,3},{2,0},{3,1},{4,6},{5,7},{6,4},{7,5},{8,10},{9,11},{10,... | collective-permute-start | bytes 196616 | tf_op jit(solution)/shard_map/ppermute | solution.py:19
  16.8 2.1 %collective-permute-start.5 = (f32[192,512]{1,0:T(8,128)S(1)}, f32[192,512]{1,0:T(8,128)S(1)}, u32[]{:S(2)}, u32[]{:S(2)}) collective-permute-start(f32[192,512]{1,0:T(8,128)S(1)} %pad_maximum_fusion), channel_id=1, source_target_pairs={{0,1},{1,0},{2,3},{3,2},{4,5},{5,4},{6,7},{7,6},{8,9},{9,8},{10,11... | collective-permute-start | bytes 1179656 | tf_op jit(solution)/shard_map/ppermute | solution.py:19
  20.1 1.9 %collective-permute-start.8 = (f32[96,512]{1,0:T(8,128)S(1)}, f32[96,512]{1,0:T(8,128)S(1)}, u32[]{:S(2)}, u32[]{:S(2)}) collective-permute-start(f32[96,512]{1,0:T(8,128)S(1)} %constant_dynamic-update-slice_fusion.2.refs_1_), channel_id=1, source_target_pairs={{0,1},{1,0},{2,3},{3,2},{4,5},{5,4},{6,7},{7,6},{8,9},{9,8},{10,11... | collective-permute-start | bytes 589832 | tf_op jit(solution)/shard_map/ppermute | solution.py:19
  23.4 5.1 %collective-permute-start.9 = (f32[32,512]{1,0:T(8,128)}, f32[32,512]{1,0:T(8,128)}, u32[]{:S(2)}, u32[]{:S(2)}) collective-permute-start(f32[32,512]{1,0:T(8,128)} %get-tuple-element.33), channel_id=1, source_target_pairs={{0,4},{1,5},{2,6},{3,7},{4,0},{5,1},{6,2},{7,3},{8,12},{9,13},{10,... | collective-permute-start | bytes 196616 | tf_op jit(solution)/shard_map/ppermute | solution.py:19
  24.2 5.0 %collective-permute-start.10 = (f32[32,512]{1,0:T(8,128)}, f32[32,512]{1,0:T(8,128)}, u32[]{:S(2)}, u32[]{:S(2)}) collective-permute-start(f32[32,512]{1,0:T(8,128)} %get-tuple-element.34), channel_id=1, source_target_pairs={{0,4},{1,5},{2,6},{3,7},{4,0},{5,1},{6,2},{7,3},{8,12},{9,13},{10,... | collective-permute-start | bytes 196616 | tf_op jit(solution)/shard_map/ppermute | solution.py:19

commit v14 on v12

--- a/solution.py
+++ b/solution.py
@@ -174,25 +174,23 @@
     near = swap(mine, 4)
     direct = [swap(mine, bit) for bit in beside]
 
-    (here,) = terms([(mine, [mine])], weight=512)
+    (here,) = terms([(mine, [mine])], weight=1024)
     far_features, far_vectors, here = tied((far_features, far_vectors, here))
     far = [far_features, far_vectors]
     last = []
     for bit in beside:
         for pair in [far] + last:
             last = last + [[swap(piece, bit) for piece in pair]]
-    (there,) = terms([(near, [mine])], weight=256)
-    *direct, there = tied((*direct, there))
     first = [jnp.concatenate(far, 0)] + direct
-    siblings = jnp.split(swap(jnp.concatenate(first, 0), 1), len(first), 0)
-    (there,) = terms([(near, [sibling] + first)], before=[there], weight=2048)
-    there, here = terms([(near, siblings), (mine, first)], before=[there, here], weight=64)
+    siblings = [swap(block, 1) for block in first]
+    (there,) = terms([(near, [mine, sibling] + first)], weight=1024)
+    there, here = terms([(near, siblings), (mine, first)], before=[there, here], weight=2048)
     *pieces, there = tied((*[piece for pair in last for piece in pair], there))
     last = [jnp.concatenate(pieces[at : at + 2], 0) for at in range(0, len(pieces), 2)]
     last_siblings = [swap(block, 1) for block in last]
     there, here = terms([(near, last), (mine, last)], before=[there, here], weight=64)
-    toward_near = terms([(near, last_siblings)], before=[there], weight=64, pieces=2)
-    from_near = jnp.concatenate([swap(piece, 4) for piece in toward_near], 0)
+    (there,) = terms([(near, last_siblings)], before=[there], weight=2048)
+    from_near = swap(there, 4)
     rest = [sibling] + siblings + last_siblings
     (here,) = terms([(mine, rest)], before=[here], weight=2048)
     return here + from_near

time: 30.7 us -> 29.3 us (0.954)
  starting transfers between devices: 12.1 us -> 11.3 us
  waiting for transfers between devices: 5.73 us -> 5.38 us
    ppermute x11, starting transfers between devices: 12.1 us -> 11.3 us  [swapped(): lax.ppermute(value, axis, [(source, source ^ bit) for source in range(cou...]
    ppermute x11, waiting for transfers between devices: 5.73 us -> 5.38 us  [swapped(): lax.ppermute(value, axis, [(source, source ^ bit) for source in range(cou...]
    pallas_call x7 -> x6, Pallas kernels: 9.25 us -> 8.96 us  [pair_terms(): pl.pallas_call(functools.partial(kernel, width, vectors, placed, len(bloc...]
    unnamed x4 -> x6, local copies, waits for them, and re-layouts: 0.95 us -> 0.98 us
  transfers between devices with their start and end apart: 11 -> 11, of which waited for: 4 -> 2; matrix products, arithmetic and copies ran while one was open for 0% -> 0% of each run, Pallas kernels for 33% -> 34%
where the time goes in v14:
time: 29.3 us; the launch traced here: 29.1 us
  starting transfers between devices  11.3 us (39%)
  Pallas kernels  10.6 us (36%)
  waiting for transfers between devices  5.38 us (18%)
  local copies, waits for them, and re-layouts  1 us (3%)
  other arithmetic  0.67 us (2%)
    ppermute x11, starting transfers between devices, swapped(): lax.ppermute(value, axis, [(source, source ^ bit) for source in range(cou...  11.3 us
    pallas_call x6, Pallas kernels, pair_terms(): pl.pallas_call(functools.partial(kernel, width, vectors, placed, len(bloc...  8.96 us
    ppermute x11, waiting for transfers between devices, swapped(): lax.ppermute(value, axis, [(source, source ^ bit) for source in range(cou...  5.38 us
    pallas_call x1, Pallas kernels, packed(): pl.pallas_call(body, out_shape=[jax.ShapeDtypeStruct((rows, points), jnp....  1.65 us
    unnamed x6, local copies, waits for them, and re-layouts  0.98 us
    add x1, other arithmetic, local(): return here + from_near  0.67 us
  transfers between devices with their start and end apart: 11, of which 2 were waited for; matrix products, arithmetic and copies ran while one was open for 0% of the time, Pallas kernels for 34%

profile of v14, /device:TPU:0, one launch (start us, length us, event | category | flops | bytes accessed | tf_op | source)
XLA Modules:
  0.0 29.1 jit_solution(15846764949466070915)
XLA Ops:
  0.0 4.0 %collective-permute-start.1 = (f32[64,512]{1,0:T(8,128)}, f32[64,512]{1,0:T(8,128)S(1)}, u32[]{:S(2)}, u32[]{:S(2)}) collective-permute-start(f32[64,512]{1,0:T(8,128)} %features_ref.1), channel_id=1, source_target_pairs={{0,8},{1,9},{2,10},{3,11},{4,12},{5,13},{6,14},{7,15},{8,0},{9,1},... | collective-permute-start | bytes 393224 | tf_op jit(solution)/shard_map/ppermute | solution.py:19
  4.0 1.7 %shard_map.37 = (f32[96,512]{1,0:T(8,128)}, f32[32,512]{1,0:T(8,128)}) custom-call(f32[64,512]{1,0:T(8,128)} %features_ref.1, f32[16,512]{1,0:T(8,128)} %solves_ref.1, f32[16,512]{1,0:T(8,128)} %probes_ref.1), custom_call_target="tpu_custom_call" | custom-call | tf_op jit(solution)/shard_map/pallas_call | solution.py:150
  5.7 0.0 collective-permute-start.2
  5.7 1.9 %collective-permute-start.8 = (f32[96,512]{1,0:T(8,128)}, f32[96,512]{1,0:T(8,128)S(1)}, u32[]{:S(2)}, u32[]{:S(2)}) collective-permute-start(f32[96,512]{1,0:T(8,128)} %get-tuple-element.17.refs_0_.refs_1_.refs_3_.refs_2_), channel_id=1, source_target_pairs={{0,4},{1,5},{2,6},{3,7},{4,0},{5,1},{6,2},{7,3},{8,12},{9,13},{10,... | collective-permute-start | bytes 589832 | tf_op jit(solution)/shard_map/ppermute | solution.py:19
  7.6 1.5 %collective-permute-start.4 = (f32[96,512]{1,0:T(8,128)}, f32[96,512]{1,0:T(8,128)S(1)}, u32[]{:S(2)}, u32[]{:S(2)}) collective-permute-start(f32[96,512]{1,0:T(8,128)} %get-tuple-element.17.refs_0_.refs_1_.refs_3_.refs_2_), channel_id=1, source_target_pairs={{0,2},{1,3},{2,0},{3,1},{4,6},{5,7},{6,4},{7,5},{8,10},{9,11},{10,... | collective-permute-start | bytes 589832 | tf_op jit(solution)/shard_map/ppermute | solution.py:19
  9.1 0.0 collective-permute-start
  9.1 0.0 copy-start
  9.1 1.0 %copy-done = f32[96,512]{1,0:T(8,128)S(1)} copy-done((f32[96,512]{1,0:T(8,128)S(1)}, f32[96,512]{1,0:T(8,128)}, u32[]{:S(2)}) %copy-start) | copy-done | bytes 196632
  10.1 0.8 %shard_map.38.refs_7_ = f32[64,512]{1,0:T(8,128)S(1)} custom-call(f32[96,512]{1,0:T(8,128)S(1)} %copy-done), custom_call_target="tpu_custom_call" | custom-call | flops 536870912 | bytes 196608 | tf_op jit(solution)/shard_map/pallas_call | solution.py:125
  10.8 2.6 %collective-permute-done.2 = f32[32,512]{1,0:T(8,128)S(1)} collective-permute-done((f32[32,512]{1,0:T(8,128)}, f32[32,512]{1,0:T(8,128)S(1)}, u32[]{:S(2)}, u32[]{:S(2)}) %collective-permute-start.2) | collective-permute-done | bytes 65568 | tf_op jit(solution)/shard_map/ppermute | solution.py:19
  13.5 0.0 collective-permute-done.1
  13.5 1.6 %collective-permute-start.7 = (f32[32,512]{1,0:T(8,128)S(1)}, f32[32,512]{1,0:T(8,128)S(1)}, u32[]{:S(2)}, u32[]{:S(2)}) collective-permute-start(f32[32,512]{1,0:T(8,128)S(1)} %collective-permute-done.2), channel_id=1, source_target_pairs={{0,2},{1,3},{2,0},{3,1},{4,6},{5,7},{6,4},{7,5},{8,10},{9,11},{10,... | collective-permute-start | bytes 196616 | tf_op jit(solution)/shard_map/ppermute | solution.py:19
  15.0 0.5 %collective-permute-start.6 = (f32[64,512]{1,0:T(8,128)S(1)}, f32[64,512]{1,0:T(8,128)S(1)}, u32[]{:S(2)}, u32[]{:S(2)}) collective-permute-start(f32[64,512]{1,0:T(8,128)S(1)} %collective-permute-done.1), channel_id=1, source_target_pairs={{0,2},{1,3},{2,0},{3,1},{4,6},{5,7},{6,4},{7,5},{8,10},{9,11},{10,... | collective-permute-start | bytes 393224 | tf_op jit(solution)/shard_map/ppermute | solution.py:19
  15.5 0.0 collective-permute-done.8.refs_0_
  15.5 0.1 collective-permute-start.3
  15.6 0.0 collective-permute-done.4.refs_4_.refs_5_
  15.6 0.5 %collective-permute-start.5 = (f32[96,512]{1,0:T(8,128)S(1)}, f32[96,512]{1,0:T(8,128)S(1)}, u32[]{:S(2)}, u32[]{:S(2)}) collective-permute-start(f32[96,512]{1,0:T(8,128)S(1)} %collective-permute-done.4.refs_4_.refs_5_), channel_id=1, source_target_pairs={{0,1},{1,0},{2,3},{3,2},{4,5},{5,4},{6,7},{7,6},{8,9},{9,8},{10,11... | collective-permute-start | bytes 589832 | tf_op jit(solution)/shard_map/ppermute | solution.py:19
  16.1 0.0 collective-permute-done.refs_2_.refs_1_
  16.1 2.0 %shard_map.39.refs_6_ = f32[64,512]{1,0:T(8,128)S(1)} custom-call(f32[96,512]{1,0:T(8,128)S(1)} %collective-permute-done.8.refs_0_, f32[96,512]{1,0:T(8,128)S(1)} %copy-done, f32[96,512]{1,0:T(8,128)S(1)} %collective-permute-done.refs_2_.refs_1_, f32[96,512]{1,0:T(8,128)S(1)} %constant_dynamic-update-slice_fusion.refs_3_.refs_4_, ...), custom_call_target="tpu_custom_call" | custom-call | flops 2147483648 | bytes 983040 | tf_op jit(solution)/shard_map/pallas_call | solution.py:125
  18.2 0.0 collective-permute-done.3.refs_1_.refs_2_
  18.2 0.0 collective-permute-done.5.refs_2_.refs_3_
  18.2 2.0 %shard_map.40 = (f32[64,512]{1,0:T(8,128)S(1)}, f32[64,512]{1,0:T(8,128)S(1)}) custom-call(f32[96,512]{1,0:T(8,128)S(1)} %collective-permute-done.8.refs_0_, f32[96,512]{1,0:T(8,128)S(1)} %collective-permute-done.3.refs_1_.refs_2_, f32[96,512]{1,0:T(8,128)S(1)} %collective-permute-done.5.refs_2_.refs_3_, f32[96,512]{1,0:T(8,128)S(1)} %copy-done, ...), custom_call_target="tpu_custom_call" | custom-call | flops 4294967296 | bytes 1572864 | tf_op jit(solution)/shard_map/pallas_call | solution.py:125
  20.2 0.0 collective-permute-done.7
  20.2 0.0 collective-permute-done.6
  20.3 0.2 collective-permute-start.9
  20.4 1.3 %shard_map.41 = (f32[64,512]{1,0:T(8,128)S(1)}, f32[64,512]{1,0:T(8,128)S(1)}) custom-call(f32[96,512]{1,0:T(8,128)S(1)} %collective-permute-done.8.refs_0_, f32[96,512]{1,0:T(8,128)S(1)} %constant_dynamic-update-slice_fusion.2.refs_1_, f32[96,512]{1,0:T(8,128)S(1)} %copy-done, f32[64,512]{1,0:T(8,128)S(1)} %get-tuple-element.25.refs_3_, ...), custom_call_target="tpu_custom_call" | custom-call | flops 67108864 | bytes 983040 | tf_op jit(solution)/shard_map/pallas_call | solution.py:125
  21.8 0.0 collective-permute-done.9.refs_4_.refs_1_
  21.8 0.0 copy-start.1
  21.8 0.8 %shard_map.43 = f32[64,512]{1,0:T(8,128)S(1)} custom-call(f32[96,512]{1,0:T(8,128)S(1)} %collective-permute-done.8.refs_0_, f32[96,512]{1,0:T(8,128)S(1)} %collective-permute-done.9.refs_4_.refs_1_, f32[64,512]{1,0:T(8,128)S(1)} %get-tuple-element.28.refs_2_), custom_call_target="tpu_custom_call" | custom-call | flops 1073741824 | bytes 589824 | tf_op jit(solution)/shard_map/pallas_call | solution.py:125
  22.6 1.1 %collective-permute-start.10 = (f32[64,512]{1,0:T(8,128)S(1)}, f32[64,512]{1,0:T(8,128)S(1)}, u32[]{:S(2)}, u32[]{:S(2)}) collective-permute-start(f32[64,512]{1,0:T(8,128)S(1)} %shard_map.43), channel_id=1, source_target_pairs={{0,4},{1,5},{2,6},{3,7},{4,0},{5,1},{6,2},{7,3},{8,12},{9,13},{10,... | collective-permute-start | bytes 393224 | tf_op jit(solution)/shard_map/ppermute | solution.py:19
  23.7 0.0 copy-done.1
  23.7 2.0 %shard_map.42 = f32[64,512]{1,0:T(8,128)S(1)} custom-call(f32[96,512]{1,0:T(8,128)S(1)} %copy-done.1, f32[96,512]{1,0:T(8,128)S(1)} %collective-permute-done.refs_2_.refs_1_, f32[96,512]{1,0:T(8,128)S(1)} %collective-permute-done.3.refs_1_.refs_2_, f32[96,512]{1,0:T(8,128)S(1)} %collective-permute-done.5.refs_2_.refs_3_, ...), custom_call_target="tpu_custom_call" | custom-call | flops 4294967296 | bytes 1179648 | tf_op jit(solution)/shard_map/pallas_call | solution.py:125
  25.7 2.7 %collective-permute-done.10 = f32[64,512]{1,0:T(8,128)S(1)} collective-permute-done((f32[64,512]{1,0:T(8,128)S(1)}, f32[64,512]{1,0:T(8,128)S(1)}, u32[]{:S(2)}, u32[]{:S(2)}) %collective-permute-start.10) | collective-permute-done | bytes 131104 | tf_op jit(solution)/shard_map/ppermute | solution.py:19
  28.5 0.7 %add.3 = f32[64,512]{1,0:T(8,128)} add(f32[64,512]{1,0:T(8,128)S(1)} %shard_map.42, f32[64,512]{1,0:T(8,128)S(1)} %collective-permute-done.10) | non-fusion elementwise | flops 32768 | bytes 393216 | tf_op jit(solution)/shard_map/add | solution.py:196
  (4 shorter events, 0.0 us)
Async XLA Ops:
  0.0 13.5 %collective-permute-start.1 = (f32[64,512]{1,0:T(8,128)}, f32[64,512]{1,0:T(8,128)S(1)}, u32[]{:S(2)}, u32[]{:S(2)}) collective-permute-start(f32[64,512]{1,0:T(8,128)} %features_ref.1), channel_id=1, source_target_pairs={{0,8},{1,9},{2,10},{3,11},{4,12},{5,13},{6,14},{7,15},{8,0},{9,1},... | collective-permute-start | bytes 393224 | tf_op jit(solution)/shard_map/ppermute | solution.py:19
  5.7 7.8 %collective-permute-start.2 = (f32[32,512]{1,0:T(8,128)}, f32[32,512]{1,0:T(8,128)S(1)}, u32[]{:S(2)}, u32[]{:S(2)}) collective-permute-start(f32[32,512]{1,0:T(8,128)} %get-tuple-element.18), channel_id=1, source_target_pairs={{0,8},{1,9},{2,10},{3,11},{4,12},{5,13},{6,14},{7,15},{8,0},{9,1},... | collective-permute-start | bytes 196616 | tf_op jit(solution)/shard_map/ppermute | solution.py:19
  5.7 9.8 %collective-permute-start.8 = (f32[96,512]{1,0:T(8,128)}, f32[96,512]{1,0:T(8,128)S(1)}, u32[]{:S(2)}, u32[]{:S(2)}) collective-permute-start(f32[96,512]{1,0:T(8,128)} %get-tuple-element.17.refs_0_.refs_1_.refs_3_.refs_2_), channel_id=1, source_target_pairs={{0,4},{1,5},{2,6},{3,7},{4,0},{5,1},{6,2},{7,3},{8,12},{9,13},{10,... | collective-permute-start | bytes 589832 | tf_op jit(solution)/shard_map/ppermute | solution.py:19
  7.6 8.0 %collective-permute-start.4 = (f32[96,512]{1,0:T(8,128)}, f32[96,512]{1,0:T(8,128)S(1)}, u32[]{:S(2)}, u32[]{:S(2)}) collective-permute-start(f32[96,512]{1,0:T(8,128)} %get-tuple-element.17.refs_0_.refs_1_.refs_3_.refs_2_), channel_id=1, source_target_pairs={{0,2},{1,3},{2,0},{3,1},{4,6},{5,7},{6,4},{7,5},{8,10},{9,11},{10,... | collective-permute-start | bytes 589832 | tf_op jit(solution)/shard_map/ppermute | solution.py:19
  9.1 7.0 %collective-permute-start = (f32[96,512]{1,0:T(8,128)}, f32[96,512]{1,0:T(8,128)S(1)}, u32[]{:S(2)}, u32[]{:S(2)}) collective-permute-start(f32[96,512]{1,0:T(8,128)} %get-tuple-element.17.refs_0_.refs_1_.refs_3_.refs_2_), channel_id=1, source_target_pairs={{0,1},{1,0},{2,3},{3,2},{4,5},{5,4},{6,7},{7,6},{8,9},{9,8},{10,11... | collective-permute-start | bytes 589832 | tf_op jit(solution)/shard_map/ppermute | solution.py:19
  9.1 1.0 %copy-start = (f32[96,512]{1,0:T(8,128)S(1)}, f32[96,512]{1,0:T(8,128)}, u32[]{:S(2)}) copy-start(f32[96,512]{1,0:T(8,128)} %get-tuple-element.17.refs_0_.refs_1_.refs_3_.refs_2_) | copy-start | bytes 589828
  13.5 6.8 %collective-permute-start.7 = (f32[32,512]{1,0:T(8,128)S(1)}, f32[32,512]{1,0:T(8,128)S(1)}, u32[]{:S(2)}, u32[]{:S(2)}) collective-permute-start(f32[32,512]{1,0:T(8,128)S(1)} %collective-permute-done.2), channel_id=1, source_target_pairs={{0,2},{1,3},{2,0},{3,1},{4,6},{5,7},{6,4},{7,5},{8,10},{9,11},{10,... | collective-permute-start | bytes 196616 | tf_op jit(solution)/shard_map/ppermute | solution.py:19
  15.0 5.2 %collective-permute-start.6 = (f32[64,512]{1,0:T(8,128)S(1)}, f32[64,512]{1,0:T(8,128)S(1)}, u32[]{:S(2)}, u32[]{:S(2)}) collective-permute-start(f32[64,512]{1,0:T(8,128)S(1)} %collective-permute-done.1), channel_id=1, source_target_pairs={{0,2},{1,3},{2,0},{3,1},{4,6},{5,7},{6,4},{7,5},{8,10},{9,11},{10,... | collective-permute-start | bytes 393224 | tf_op jit(solution)/shard_map/ppermute | solution.py:19
  15.5 2.6 %collective-permute-start.3 = (f32[96,512]{1,0:T(8,128)S(1)}, f32[96,512]{1,0:T(8,128)S(1)}, u32[]{:S(2)}, u32[]{:S(2)}) collective-permute-start(f32[96,512]{1,0:T(8,128)S(1)} %constant_dynamic-update-slice_fusion.refs_3_.refs_4_), channel_id=1, source_target_pairs={{0,1},{1,0},{2,3},{3,2},{4,5},{5,4},{6,7},{7,6},{8,9},{9,8},{10,11... | collective-permute-start | bytes 589832 | tf_op jit(solution)/shard_map/ppermute | solution.py:19
  15.6 2.5 %collective-permute-start.5 = (f32[96,512]{1,0:T(8,128)S(1)}, f32[96,512]{1,0:T(8,128)S(1)}, u32[]{:S(2)}, u32[]{:S(2)}) collective-permute-start(f32[96,512]{1,0:T(8,128)S(1)} %collective-permute-done.4.refs_4_.refs_5_), channel_id=1, source_target_pairs={{0,1},{1,0},{2,3},{3,2},{4,5},{5,4},{6,7},{7,6},{8,9},{9,8},{10,11... | collective-permute-start | bytes 589832 | tf_op jit(solution)/shard_map/ppermute | solution.py:19
  20.3 1.5 %collective-permute-start.9 = (f32[96,512]{1,0:T(8,128)S(1)}, f32[96,512]{1,0:T(8,128)S(1)}, u32[]{:S(2)}, u32[]{:S(2)}) collective-permute-start(f32[96,512]{1,0:T(8,128)S(1)} %constant_dynamic-update-slice_fusion.2.refs_1_), channel_id=1, source_target_pairs={{0,1},{1,0},{2,3},{3,2},{4,5},{5,4},{6,7},{7,6},{8,9},{9,8},{10,11... | collective-permute-start | bytes 589832 | tf_op jit(solution)/shard_map/ppermute | solution.py:19
  21.8 1.9 %copy-start.1 = (f32[96,512]{1,0:T(8,128)S(1)}, f32[96,512]{1,0:T(8,128)}, u32[]{:S(2)}) copy-start(f32[96,512]{1,0:T(8,128)} %get-tuple-element.17.refs_0_.refs_1_.refs_3_.refs_2_) | copy-start | bytes 589828
  22.6 5.9 %collective-permute-start.10 = (f32[64,512]{1,0:T(8,128)S(1)}, f32[64,512]{1,0:T(8,128)S(1)}, u32[]{:S(2)}, u32[]{:S(2)}) collective-permute-start(f32[64,512]{1,0:T(8,128)S(1)} %shard_map.43), channel_id=1, source_target_pairs={{0,4},{1,5},{2,6},{3,7},{4,0},{5,1},{6,2},{7,3},{8,12},{9,13},{10,... | collective-permute-start | bytes 393224 | tf_op jit(solution)/shard_map/ppermute | solution.py:19

commit v15 on v14

--- a/solution.py
+++ b/solution.py
@@ -184,14 +184,14 @@
     first = [jnp.concatenate(far, 0)] + direct
     siblings = [swap(block, 1) for block in first]
     (there,) = terms([(near, [mine, sibling] + first)], weight=1024)
-    there, here = terms([(near, siblings), (mine, first)], before=[there, here], weight=2048)
+    (there,) = terms([(near, siblings)], before=[there], weight=512)
     *pieces, there = tied((*[piece for pair in last for piece in pair], there))
     last = [jnp.concatenate(pieces[at : at + 2], 0) for at in range(0, len(pieces), 2)]
     last_siblings = [swap(block, 1) for block in last]
     there, here = terms([(near, last), (mine, last)], before=[there, here], weight=64)
-    (there,) = terms([(near, last_siblings)], before=[there], weight=2048)
-    from_near = swap(there, 4)
-    rest = [sibling] + siblings + last_siblings
+    toward_near = terms([(near, last_siblings)], before=[there], weight=64, pieces=2)
+    from_near = jnp.concatenate([swap(piece, 4) for piece in toward_near], 0)
+    rest = [sibling] + first + siblings + last_siblings
     (here,) = terms([(mine, rest)], before=[here], weight=2048)
     return here + from_near
 

time: 29.3 us -> 29 us (0.990)
  waiting for transfers between devices: 5.38 us -> 4.18 us
  starting transfers between devices: 11.3 us -> 12.2 us
    ppermute x11 -> x12, waiting for transfers between devices: 5.38 us -> 4.18 us  [swapped(): lax.ppermute(value, axis, [(source, source ^ bit) for source in range(cou...]
    ppermute x11 -> x12, starting transfers between devices: 11.3 us -> 12.2 us  [swapped(): lax.ppermute(value, axis, [(source, source ^ bit) for source in range(cou...]
    unnamed x6 -> x4, local copies, waits for them, and re-layouts: 0.98 us -> 0.98 us
  transfers between devices with their start and end apart: 11 -> 12, of which waited for: 2 -> 4; matrix products, arithmetic and copies ran while one was open for 0% -> 0% of each run, Pallas kernels for 34% -> 34%
where the time goes in v15:
time: 29 us; the launch traced here: 28.9 us
  starting transfers between devices  12.2 us (42%)
  Pallas kernels  10.7 us (37%)
  waiting for transfers between devices  4.18 us (14%)
  local copies, waits for them, and re-layouts  0.99 us (3%)
  other arithmetic  0.67 us (2%)
    ppermute x12, starting transfers between devices, swapped(): lax.ppermute(value, axis, [(source, source ^ bit) for source in range(cou...  12.2 us
    pallas_call x6, Pallas kernels, pair_terms(): pl.pallas_call(functools.partial(kernel, width, vectors, placed, len(bloc...  9.02 us
    ppermute x12, waiting for transfers between devices, swapped(): lax.ppermute(value, axis, [(source, source ^ bit) for source in range(cou...  4.18 us
    pallas_call x1, Pallas kernels, packed(): pl.pallas_call(body, out_shape=[jax.ShapeDtypeStruct((rows, points), jnp....  1.65 us
    unnamed x4, local copies, waits for them, and re-layouts  0.98 us
    add x1, other arithmetic, local(): return here + from_near  0.67 us
  transfers between devices with their start and end apart: 12, of which 4 were waited for; matrix products, arithmetic and copies ran while one was open for 0% of the time, Pallas kernels for 34%

profile of v15, /device:TPU:0, one launch (start us, length us, event | category | flops | bytes accessed | tf_op | source)
XLA Modules:
  0.0 28.9 jit_solution(4905694125352758529)
XLA Ops:
  0.0 4.0 %collective-permute-start.1 = (f32[64,512]{1,0:T(8,128)}, f32[64,512]{1,0:T(8,128)S(1)}, u32[]{:S(2)}, u32[]{:S(2)}) collective-permute-start(f32[64,512]{1,0:T(8,128)} %features_ref.1), channel_id=1, source_target_pairs={{0,8},{1,9},{2,10},{3,11},{4,12},{5,13},{6,14},{7,15},{8,0},{9,1},... | collective-permute-start | bytes 393224 | tf_op jit(solution)/shard_map/ppermute | solution.py:19
  4.0 1.7 %shard_map.37 = (f32[96,512]{1,0:T(8,128)}, f32[32,512]{1,0:T(8,128)}) custom-call(f32[64,512]{1,0:T(8,128)} %features_ref.1, f32[16,512]{1,0:T(8,128)} %solves_ref.1, f32[16,512]{1,0:T(8,128)} %probes_ref.1), custom_call_target="tpu_custom_call" | custom-call | tf_op jit(solution)/shard_map/pallas_call | solution.py:150
  5.7 0.0 collective-permute-start.2
  5.7 1.9 %collective-permute-start.8 = (f32[96,512]{1,0:T(8,128)}, f32[96,512]{1,0:T(8,128)S(1)}, u32[]{:S(2)}, u32[]{:S(2)}) collective-permute-start(f32[96,512]{1,0:T(8,128)} %get-tuple-element.17.refs_0_.refs_1_.refs_2_), channel_id=1, source_target_pairs={{0,4},{1,5},{2,6},{3,7},{4,0},{5,1},{6,2},{7,3},{8,12},{9,13},{10,... | collective-permute-start | bytes 589832 | tf_op jit(solution)/shard_map/ppermute | solution.py:19
  7.6 1.5 %collective-permute-start.3 = (f32[96,512]{1,0:T(8,128)}, f32[96,512]{1,0:T(8,128)S(1)}, u32[]{:S(2)}, u32[]{:S(2)}) collective-permute-start(f32[96,512]{1,0:T(8,128)} %get-tuple-element.17.refs_0_.refs_1_.refs_2_), channel_id=1, source_target_pairs={{0,2},{1,3},{2,0},{3,1},{4,6},{5,7},{6,4},{7,5},{8,10},{9,11},{10,... | collective-permute-start | bytes 589832 | tf_op jit(solution)/shard_map/ppermute | solution.py:19
  9.1 0.0 collective-permute-start
  9.1 0.0 copy-start
  9.1 1.0 %copy-done = f32[96,512]{1,0:T(8,128)S(1)} copy-done((f32[96,512]{1,0:T(8,128)S(1)}, f32[96,512]{1,0:T(8,128)}, u32[]{:S(2)}) %copy-start) | copy-done | bytes 196632
  10.1 0.8 %shard_map.38.refs_4_ = f32[64,512]{1,0:T(8,128)S(1)} custom-call(f32[96,512]{1,0:T(8,128)S(1)} %copy-done), custom_call_target="tpu_custom_call" | custom-call | flops 536870912 | bytes 196608 | tf_op jit(solution)/shard_map/pallas_call | solution.py:125
  10.8 2.6 %collective-permute-done.2 = f32[32,512]{1,0:T(8,128)S(1)} collective-permute-done((f32[32,512]{1,0:T(8,128)}, f32[32,512]{1,0:T(8,128)S(1)}, u32[]{:S(2)}, u32[]{:S(2)}) %collective-permute-start.2) | collective-permute-done | bytes 65568 | tf_op jit(solution)/shard_map/ppermute | solution.py:19
  13.5 0.0 collective-permute-done.1
  13.5 1.6 %collective-permute-start.7 = (f32[32,512]{1,0:T(8,128)S(1)}, f32[32,512]{1,0:T(8,128)S(1)}, u32[]{:S(2)}, u32[]{:S(2)}) collective-permute-start(f32[32,512]{1,0:T(8,128)S(1)} %collective-permute-done.2), channel_id=1, source_target_pairs={{0,2},{1,3},{2,0},{3,1},{4,6},{5,7},{6,4},{7,5},{8,10},{9,11},{10,... | collective-permute-start | bytes 196616 | tf_op jit(solution)/shard_map/ppermute | solution.py:19
  15.0 0.5 %collective-permute-start.6 = (f32[64,512]{1,0:T(8,128)S(1)}, f32[64,512]{1,0:T(8,128)S(1)}, u32[]{:S(2)}, u32[]{:S(2)}) collective-permute-start(f32[64,512]{1,0:T(8,128)S(1)} %collective-permute-done.1), channel_id=1, source_target_pairs={{0,2},{1,3},{2,0},{3,1},{4,6},{5,7},{6,4},{7,5},{8,10},{9,11},{10,... | collective-permute-start | bytes 393224 | tf_op jit(solution)/shard_map/ppermute | solution.py:19
  15.5 0.0 collective-permute-done.8.refs_0_
  15.5 0.1 collective-permute-start.4
  15.6 0.0 collective-permute-done.3.refs_4_.refs_3_
  15.6 0.5 %collective-permute-start.5 = (f32[96,512]{1,0:T(8,128)S(1)}, f32[96,512]{1,0:T(8,128)S(1)}, u32[]{:S(2)}, u32[]{:S(2)}) collective-permute-start(f32[96,512]{1,0:T(8,128)S(1)} %collective-permute-done.3.refs_4_.refs_3_), channel_id=1, source_target_pairs={{0,1},{1,0},{2,3},{3,2},{4,5},{5,4},{6,7},{7,6},{8,9},{9,8},{10,11... | collective-permute-start | bytes 589832 | tf_op jit(solution)/shard_map/ppermute | solution.py:19
  16.1 0.0 collective-permute-done.refs_2_.refs_1_
  16.1 2.0 %shard_map.39.refs_3_ = f32[64,512]{1,0:T(8,128)S(1)} custom-call(f32[96,512]{1,0:T(8,128)S(1)} %collective-permute-done.8.refs_0_, f32[96,512]{1,0:T(8,128)S(1)} %copy-done, f32[96,512]{1,0:T(8,128)S(1)} %collective-permute-done.refs_2_.refs_1_, f32[96,512]{1,0:T(8,128)S(1)} %constant_dynamic-update-slice_fusion.refs_3_.refs_2_, ...), custom_call_target="tpu_custom_call" | custom-call | flops 2147483648 | bytes 983040 | tf_op jit(solution)/shard_map/pallas_call | solution.py:125
  18.2 0.0 collective-permute-done.4.refs_1_.refs_4_
  18.2 0.0 collective-permute-done.5.refs_2_.refs_5_
  18.2 1.1 %shard_map.40.refs_3_ = f32[64,512]{1,0:T(8,128)S(1)} custom-call(f32[96,512]{1,0:T(8,128)S(1)} %collective-permute-done.8.refs_0_, f32[96,512]{1,0:T(8,128)S(1)} %collective-permute-done.4.refs_1_.refs_4_, f32[96,512]{1,0:T(8,128)S(1)} %collective-permute-done.5.refs_2_.refs_5_, f32[64,512]{1,0:T(8,128)S(1)} %shard_map.39.refs_3_), custom_call_target="tpu_custom_call" | custom-call | flops 536870912 | bytes 786432 | tf_op jit(solution)/shard_map/pallas_call | solution.py:125
  19.3 0.0 collective-permute-done.7
  19.3 0.7 %collective-permute-done.6 = f32[64,512]{1,0:T(8,128)S(1)} collective-permute-done((f32[64,512]{1,0:T(8,128)S(1)}, f32[64,512]{1,0:T(8,128)S(1)}, u32[]{:S(2)}, u32[]{:S(2)}) %collective-permute-start.6) | collective-permute-done | bytes 131104 | tf_op jit(solution)/shard_map/ppermute | solution.py:19
  20.0 0.1 collective-permute-start.9
  20.1 1.3 %shard_map.41 = (f32[64,512]{1,0:T(8,128)S(1)}, f32[64,512]{1,0:T(8,128)S(1)}) custom-call(f32[96,512]{1,0:T(8,128)S(1)} %collective-permute-done.8.refs_0_, f32[96,512]{1,0:T(8,128)S(1)} %constant_dynamic-update-slice_fusion.2.refs_1_, f32[96,512]{1,0:T(8,128)S(1)} %copy-done, f32[64,512]{1,0:T(8,128)S(1)} %shard_map.40.refs_3_, ...), custom_call_target="tpu_custom_call" | custom-call | flops 67108864 | bytes 983040 | tf_op jit(solution)/shard_map/pallas_call | solution.py:125
  21.4 0.1 collective-permute-done.9.refs_6_.refs_1_
  21.5 0.8 %shard_map.43 = (f32[32,512]{1,0:T(8,128)S(1)}, f32[32,512]{1,0:T(8,128)S(1)}) custom-call(f32[96,512]{1,0:T(8,128)S(1)} %collective-permute-done.8.refs_0_, f32[96,512]{1,0:T(8,128)S(1)} %collective-permute-done.9.refs_6_.refs_1_, f32[64,512]{1,0:T(8,128)S(1)} %get-tuple-element.26.refs_2_), custom_call_target="tpu_custom_call" | custom-call | flops 33554432 | bytes 589824 | tf_op jit(solution)/shard_map/pallas_call | solution.py:125
  22.3 1.4 %collective-permute-start.10 = (f32[32,512]{1,0:T(8,128)S(1)}, f32[32,512]{1,0:T(8,128)S(1)}, u32[]{:S(2)}, u32[]{:S(2)}) collective-permute-start(f32[32,512]{1,0:T(8,128)S(1)} %get-tuple-element.27), channel_id=1, source_target_pairs={{0,4},{1,5},{2,6},{3,7},{4,0},{5,1},{6,2},{7,3},{8,12},{9,13},{10,... | collective-permute-start | bytes 196616 | tf_op jit(solution)/shard_map/ppermute | solution.py:19
  23.7 0.7 %collective-permute-start.11 = (f32[32,512]{1,0:T(8,128)S(1)}, f32[32,512]{1,0:T(8,128)S(1)}, u32[]{:S(2)}, u32[]{:S(2)}) collective-permute-start(f32[32,512]{1,0:T(8,128)S(1)} %get-tuple-element.28), channel_id=1, source_target_pairs={{0,4},{1,5},{2,6},{3,7},{4,0},{5,1},{6,2},{7,3},{8,12},{9,13},{10,... | collective-permute-start | bytes 196616 | tf_op jit(solution)/shard_map/ppermute | solution.py:19
  24.4 3.0 %shard_map.42 = f32[64,512]{1,0:T(8,128)S(1)} custom-call(f32[96,512]{1,0:T(8,128)S(1)} %copy-done, f32[96,512]{1,0:T(8,128)S(1)} %collective-permute-done.refs_2_.refs_1_, f32[96,512]{1,0:T(8,128)S(1)} %constant_dynamic-update-slice_fusion.refs_3_.refs_2_, f32[96,512]{1,0:T(8,128)S(1)} %collective-permute-done.3.refs_4_.refs_3_, ...), custom_call_target="tpu_custom_call" | custom-call | flops 6442450944 | bytes 1572864 | tf_op jit(solution)/shard_map/pallas_call | solution.py:125
  27.4 0.0 collective-permute-done.10
  27.5 0.8 %collective-permute-done.11 = f32[32,512]{1,0:T(8,128)S(1)} collective-permute-done((f32[32,512]{1,0:T(8,128)S(1)}, f32[32,512]{1,0:T(8,128)S(1)}, u32[]{:S(2)}, u32[]{:S(2)}) %collective-permute-start.11) | collective-permute-done | bytes 65568 | tf_op jit(solution)/shard_map/ppermute | solution.py:19
  28.2 0.7 %maximum_add_fusion = f32[64,512]{1,0:T(8,128)} fusion(f32[64,512]{1,0:T(8,128)S(1)} %shard_map.42, f32[32,512]{1,0:T(8,128)S(1)} %collective-permute-done.11, f32[32,512]{1,0:T(8,128)S(1)} %collective-permute-done.10), kind=kLoop, calls=%fused_computation | loop fusion | flops 65536 | bytes 393216 | tf_op jit(solution)/shard_map/add | solution.py:196
  (4 shorter events, 0.0 us)
Async XLA Ops:
  0.0 13.5 %collective-permute-start.1 = (f32[64,512]{1,0:T(8,128)}, f32[64,512]{1,0:T(8,128)S(1)}, u32[]{:S(2)}, u32[]{:S(2)}) collective-permute-start(f32[64,512]{1,0:T(8,128)} %features_ref.1), channel_id=1, source_target_pairs={{0,8},{1,9},{2,10},{3,11},{4,12},{5,13},{6,14},{7,15},{8,0},{9,1},... | collective-permute-start | bytes 393224 | tf_op jit(solution)/shard_map/ppermute | solution.py:19
  5.7 7.8 %collective-permute-start.2 = (f32[32,512]{1,0:T(8,128)}, f32[32,512]{1,0:T(8,128)S(1)}, u32[]{:S(2)}, u32[]{:S(2)}) collective-permute-start(f32[32,512]{1,0:T(8,128)} %get-tuple-element.18), channel_id=1, source_target_pairs={{0,8},{1,9},{2,10},{3,11},{4,12},{5,13},{6,14},{7,15},{8,0},{9,1},... | collective-permute-start | bytes 196616 | tf_op jit(solution)/shard_map/ppermute | solution.py:19
  5.7 9.8 %collective-permute-start.8 = (f32[96,512]{1,0:T(8,128)}, f32[96,512]{1,0:T(8,128)S(1)}, u32[]{:S(2)}, u32[]{:S(2)}) collective-permute-start(f32[96,512]{1,0:T(8,128)} %get-tuple-element.17.refs_0_.refs_1_.refs_2_), channel_id=1, source_target_pairs={{0,4},{1,5},{2,6},{3,7},{4,0},{5,1},{6,2},{7,3},{8,12},{9,13},{10,... | collective-permute-start | bytes 589832 | tf_op jit(solution)/shard_map/ppermute | solution.py:19
  7.6 8.0 %collective-permute-start.3 = (f32[96,512]{1,0:T(8,128)}, f32[96,512]{1,0:T(8,128)S(1)}, u32[]{:S(2)}, u32[]{:S(2)}) collective-permute-start(f32[96,512]{1,0:T(8,128)} %get-tuple-element.17.refs_0_.refs_1_.refs_2_), channel_id=1, source_target_pairs={{0,2},{1,3},{2,0},{3,1},{4,6},{5,7},{6,4},{7,5},{8,10},{9,11},{10,... | collective-permute-start | bytes 589832 | tf_op jit(solution)/shard_map/ppermute | solution.py:19
  9.1 7.0 %collective-permute-start = (f32[96,512]{1,0:T(8,128)}, f32[96,512]{1,0:T(8,128)S(1)}, u32[]{:S(2)}, u32[]{:S(2)}) collective-permute-start(f32[96,512]{1,0:T(8,128)} %get-tuple-element.17.refs_0_.refs_1_.refs_2_), channel_id=1, source_target_pairs={{0,1},{1,0},{2,3},{3,2},{4,5},{5,4},{6,7},{7,6},{8,9},{9,8},{10,11... | collective-permute-start | bytes 589832 | tf_op jit(solution)/shard_map/ppermute | solution.py:19
  9.1 1.0 %copy-start = (f32[96,512]{1,0:T(8,128)S(1)}, f32[96,512]{1,0:T(8,128)}, u32[]{:S(2)}) copy-start(f32[96,512]{1,0:T(8,128)} %get-tuple-element.17.refs_0_.refs_1_.refs_2_) | copy-start | bytes 589828
  13.5 5.8 %collective-permute-start.7 = (f32[32,512]{1,0:T(8,128)S(1)}, f32[32,512]{1,0:T(8,128)S(1)}, u32[]{:S(2)}, u32[]{:S(2)}) collective-permute-start(f32[32,512]{1,0:T(8,128)S(1)} %collective-permute-done.2), channel_id=1, source_target_pairs={{0,2},{1,3},{2,0},{3,1},{4,6},{5,7},{6,4},{7,5},{8,10},{9,11},{10,... | collective-permute-start | bytes 196616 | tf_op jit(solution)/shard_map/ppermute | solution.py:19
  15.0 5.0 %collective-permute-start.6 = (f32[64,512]{1,0:T(8,128)S(1)}, f32[64,512]{1,0:T(8,128)S(1)}, u32[]{:S(2)}, u32[]{:S(2)}) collective-permute-start(f32[64,512]{1,0:T(8,128)S(1)} %collective-permute-done.1), channel_id=1, source_target_pairs={{0,2},{1,3},{2,0},{3,1},{4,6},{5,7},{6,4},{7,5},{8,10},{9,11},{10,... | collective-permute-start | bytes 393224 | tf_op jit(solution)/shard_map/ppermute | solution.py:19
  15.5 2.6 %collective-permute-start.4 = (f32[96,512]{1,0:T(8,128)S(1)}, f32[96,512]{1,0:T(8,128)S(1)}, u32[]{:S(2)}, u32[]{:S(2)}) collective-permute-start(f32[96,512]{1,0:T(8,128)S(1)} %constant_dynamic-update-slice_fusion.refs_3_.refs_2_), channel_id=1, source_target_pairs={{0,1},{1,0},{2,3},{3,2},{4,5},{5,4},{6,7},{7,6},{8,9},{9,8},{10,11... | collective-permute-start | bytes 589832 | tf_op jit(solution)/shard_map/ppermute | solution.py:19
  15.6 2.5 %collective-permute-start.5 = (f32[96,512]{1,0:T(8,128)S(1)}, f32[96,512]{1,0:T(8,128)S(1)}, u32[]{:S(2)}, u32[]{:S(2)}) collective-permute-start(f32[96,512]{1,0:T(8,128)S(1)} %collective-permute-done.3.refs_4_.refs_3_), channel_id=1, source_target_pairs={{0,1},{1,0},{2,3},{3,2},{4,5},{5,4},{6,7},{7,6},{8,9},{9,8},{10,11... | collective-permute-start | bytes 589832 | tf_op jit(solution)/shard_map/ppermute | solution.py:19
  20.0 1.5 %collective-permute-start.9 = (f32[96,512]{1,0:T(8,128)S(1)}, f32[96,512]{1,0:T(8,128)S(1)}, u32[]{:S(2)}, u32[]{:S(2)}) collective-permute-start(f32[96,512]{1,0:T(8,128)S(1)} %constant_dynamic-update-slice_fusion.2.refs_1_), channel_id=1, source_target_pairs={{0,1},{1,0},{2,3},{3,2},{4,5},{5,4},{6,7},{7,6},{8,9},{9,8},{10,11... | collective-permute-start | bytes 589832 | tf_op jit(solution)/shard_map/ppermute | solution.py:19
  22.3 5.1 %collective-permute-start.10 = (f32[32,512]{1,0:T(8,128)S(1)}, f32[32,512]{1,0:T(8,128)S(1)}, u32[]{:S(2)}, u32[]{:S(2)}) collective-permute-start(f32[32,512]{1,0:T(8,128)S(1)} %get-tuple-element.27), channel_id=1, source_target_pairs={{0,4},{1,5},{2,6},{3,7},{4,0},{5,1},{6,2},{7,3},{8,12},{9,13},{10,... | collective-permute-start | bytes 196616 | tf_op jit(solution)/shard_map/ppermute | solution.py:19
  23.7 4.5 %collective-permute-start.11 = (f32[32,512]{1,0:T(8,128)S(1)}, f32[32,512]{1,0:T(8,128)S(1)}, u32[]{:S(2)}, u32[]{:S(2)}) collective-permute-start(f32[32,512]{1,0:T(8,128)S(1)} %get-tuple-element.28), channel_id=1, source_target_pairs={{0,4},{1,5},{2,6},{3,7},{4,0},{5,1},{6,2},{7,3},{8,12},{9,13},{10,... | collective-permute-start | bytes 196616 | tf_op jit(solution)/shard_map/ppermute | solution.py:19

commit v16 on v15

--- a/solution.py
+++ b/solution.py
@@ -141,18 +141,14 @@
     width, points = features.shape
     vectors = solves.shape[0]
 
-    def body(features_ref, solves_ref, probes_ref, out_ref, vectors_ref):
+    def body(features_ref, solves_ref, probes_ref, out_ref):
         out_ref[:width] = features_ref[...]
-        for first, ref in ((0, solves_ref), (vectors, probes_ref)):
-            out_ref[width + first : width + first + vectors] = ref[...]
-            vectors_ref[first : first + vectors] = ref[...]
+        out_ref[width : width + vectors] = solves_ref[...]
+        out_ref[width + vectors :] = probes_ref[...]
 
     return pl.pallas_call(
         body,
-        out_shape=[
-            jax.ShapeDtypeStruct((rows, points), jnp.float32)
-            for rows in (width + 2 * vectors, 2 * vectors)
-        ],
+        out_shape=jax.ShapeDtypeStruct((width + 2 * vectors, points), jnp.float32),
         compiler_params=pltpu.CompilerParams(vmem_limit_bytes=60 << 20),
     )(features, solves, probes)
 
@@ -168,15 +164,16 @@
     bits = [1 << place for place in range(count.bit_length() - 1)]
     top, beside = bits[-1], [bit for bit in bits[:-1] if bit not in (1, 4)]
     far_features = swap(features, top)
-    mine, my_vectors = packed(features, solves, probes)
-    far_vectors = swap(my_vectors, top)
+    far_vectors = [swap(part, top) for part in (solves, probes)]
+    mine = packed(features, solves, probes)
     sibling = swap(mine, 1)
     near = swap(mine, 4)
     direct = [swap(mine, bit) for bit in beside]
 
-    (here,) = terms([(mine, [mine])], weight=1024)
-    far_features, far_vectors, here = tied((far_features, far_vectors, here))
-    far = [far_features, far_vectors]
+    far_features, own = tied((far_features, mine))
+    (here,) = terms([(own, [own])], weight=1024)
+    *far_vectors, here = tied((*far_vectors, here))
+    far = [far_features, jnp.concatenate(far_vectors, 0)]
     last = []
     for bit in beside:
         for pair in [far] + last:
@@ -189,8 +186,8 @@
     last = [jnp.concatenate(pieces[at : at + 2], 0) for at in range(0, len(pieces), 2)]
     last_siblings = [swap(block, 1) for block in last]
     there, here = terms([(near, last), (mine, last)], before=[there, here], weight=64)
-    toward_near = terms([(near, last_siblings)], before=[there], weight=64, pieces=2)
-    from_near = jnp.concatenate([swap(piece, 4) for piece in toward_near], 0)
+    toward_near = terms([(near, last_siblings)], before=[there], weight=64)
+    from_near = swap(toward_near[0], 4)
     rest = [sibling] + first + siblings + last_siblings
     (here,) = terms([(mine, rest)], before=[here], weight=2048)
     return here + from_near

time: 29 us -> 30.1 us (1.038)
  waiting for transfers between devices: 4.18 us -> 5.59 us
  local copies, waits for them, and re-layouts: 0.99 us -> 0.04 us
  starting transfers between devices: 12.2 us -> 12.9 us
    ppermute x12, waiting for transfers between devices: 4.18 us -> 5.59 us  [swapped(): lax.ppermute(value, axis, [(source, source ^ bit) for source in range(cou...]
    unnamed x4 -> x5, local copies, waits for them, and re-layouts: 0.98 us -> 0.03 us
    ppermute x12, starting transfers between devices: 12.2 us -> 12.9 us  [swapped(): lax.ppermute(value, axis, [(source, source ^ bit) for source in range(cou...]
  transfers between devices with their start and end apart: 12 -> 12, of which waited for: 4 -> 4; matrix products, arithmetic and copies ran while one was open for 0% -> 0% of each run, Pallas kernels for 34% -> 33%
where the time goes in v16:
time: 30.1 us; the launch traced here: 30 us
  starting transfers between devices  12.9 us (43%)
  Pallas kernels  10.7 us (36%)
  waiting for transfers between devices  5.59 us (19%)
  other arithmetic  0.68 us (2%)
    ppermute x12, starting transfers between devices, swapped(): lax.ppermute(value, axis, [(source, source ^ bit) for source in range(cou...  12.9 us
    pallas_call x6, Pallas kernels, pair_terms(): pl.pallas_call(functools.partial(kernel, width, vectors, placed, len(bloc...  9.04 us
    ppermute x12, waiting for transfers between devices, swapped(): lax.ppermute(value, axis, [(source, source ^ bit) for source in range(cou...  5.59 us
    pallas_call x1, Pallas kernels, packed(): pl.pallas_call(body, out_shape=jax.ShapeDtypeStruct((width + 2 * vectors,...  1.62 us
    add x1, other arithmetic, local(): return here + from_near  0.67 us
  transfers between devices with their start and end apart: 12, of which 4 were waited for; matrix products, arithmetic and copies ran while one was open for 0% of the time, Pallas kernels for 33%

profile of v16, /device:TPU:0, one launch (start us, length us, event | category | flops | bytes accessed | tf_op | source)
XLA Modules:
  0.0 30.0 jit_solution(5865453807628875690)
XLA Ops:
  0.0 4.0 %collective-permute-start.1 = (f32[64,512]{1,0:T(8,128)}, f32[64,512]{1,0:T(8,128)S(1)}, u32[]{:S(2)}, u32[]{:S(2)}) collective-permute-start(f32[64,512]{1,0:T(8,128)} %features_ref.1), channel_id=1, source_target_pairs={{0,8},{1,9},{2,10},{3,11},{4,12},{5,13},{6,14},{7,15},{8,0},{9,1},... | collective-permute-start | bytes 393224 | tf_op jit(solution)/shard_map/ppermute | solution.py:19
  4.0 0.0 collective-permute-start.2
  4.1 2.9 %collective-permute-start.3 = (f32[16,512]{1,0:T(8,128)}, f32[16,512]{1,0:T(8,128)S(1)}, u32[]{:S(2)}, u32[]{:S(2)}) collective-permute-start(f32[16,512]{1,0:T(8,128)} %probes_ref.1), channel_id=1, source_target_pairs={{0,8},{1,9},{2,10},{3,11},{4,12},{5,13},{6,14},{7,15},{8,0},{9,1},... | collective-permute-start | bytes 98312 | tf_op jit(solution)/shard_map/ppermute | solution.py:19
  7.0 1.6 %shard_map.37.refs_0_.refs_1_.refs_2_ = f32[96,512]{1,0:T(8,128)} custom-call(f32[64,512]{1,0:T(8,128)} %features_ref.1, f32[16,512]{1,0:T(8,128)} %solves_ref.1, f32[16,512]{1,0:T(8,128)} %probes_ref.1), custom_call_target="tpu_custom_call" | custom-call | tf_op jit(solution)/shard_map/pallas_call | solution.py:149
  8.6 0.0 copy-start
  8.6 1.6 %collective-permute-start.9 = (f32[96,512]{1,0:T(8,128)}, f32[96,512]{1,0:T(8,128)S(1)}, u32[]{:S(2)}, u32[]{:S(2)}) collective-permute-start(f32[96,512]{1,0:T(8,128)} %shard_map.37.refs_0_.refs_1_.refs_2_), channel_id=1, source_target_pairs={{0,4},{1,5},{2,6},{3,7},{4,0},{5,1},{6,2},{7,3},{8,12},{9,13},{10,... | collective-permute-start | bytes 589832 | tf_op jit(solution)/shard_map/ppermute | solution.py:19
  10.2 1.5 %collective-permute-start.4 = (f32[96,512]{1,0:T(8,128)}, f32[96,512]{1,0:T(8,128)S(1)}, u32[]{:S(2)}, u32[]{:S(2)}) collective-permute-start(f32[96,512]{1,0:T(8,128)} %shard_map.37.refs_0_.refs_1_.refs_2_), channel_id=1, source_target_pairs={{0,2},{1,3},{2,0},{3,1},{4,6},{5,7},{6,4},{7,5},{8,10},{9,11},{10,... | collective-permute-start | bytes 589832 | tf_op jit(solution)/shard_map/ppermute | solution.py:19
  11.7 1.1 %collective-permute-done.1 = f32[64,512]{1,0:T(8,128)S(1)} collective-permute-done((f32[64,512]{1,0:T(8,128)}, f32[64,512]{1,0:T(8,128)S(1)}, u32[]{:S(2)}, u32[]{:S(2)}) %collective-permute-start.1) | collective-permute-done | bytes 131104 | tf_op jit(solution)/shard_map/ppermute | solution.py:19
  12.8 0.0 collective-permute-start
  12.8 0.0 copy-done
  12.8 0.8 %shard_map.38.refs_4_ = f32[64,512]{1,0:T(8,128)S(1)} custom-call(f32[96,512]{1,0:T(8,128)S(1)} %copy-done), custom_call_target="tpu_custom_call" | custom-call | flops 536870912 | bytes 196608 | tf_op jit(solution)/shard_map/pallas_call | solution.py:125
  13.6 0.0 collective-permute-done.2
  13.6 1.6 %collective-permute-start.7 = (f32[64,512]{1,0:T(8,128)S(1)}, f32[64,512]{1,0:T(8,128)S(1)}, u32[]{:S(2)}, u32[]{:S(2)}) collective-permute-start(f32[64,512]{1,0:T(8,128)S(1)} %collective-permute-done.1), channel_id=1, source_target_pairs={{0,2},{1,3},{2,0},{3,1},{4,6},{5,7},{6,4},{7,5},{8,10},{9,11},{10,... | collective-permute-start | bytes 393224 | tf_op jit(solution)/shard_map/ppermute | solution.py:19
  15.2 0.0 collective-permute-done.3
  15.2 0.5 %collective-permute-start.8 = (f32[32,512]{1,0:T(8,128)S(1)}, f32[32,512]{1,0:T(8,128)S(1)}, u32[]{:S(2)}, u32[]{:S(2)}) collective-permute-start(f32[32,512]{1,0:T(8,128)S(1)} %pad_maximum_fusion), channel_id=1, source_target_pairs={{0,2},{1,3},{2,0},{3,1},{4,6},{5,7},{6,4},{7,5},{8,10},{9,11},{10,... | collective-permute-start | bytes 196616 | tf_op jit(solution)/shard_map/ppermute | solution.py:19
  15.7 1.6 %collective-permute-done.9.refs_0_ = f32[96,512]{1,0:T(8,128)S(1)} collective-permute-done((f32[96,512]{1,0:T(8,128)}, f32[96,512]{1,0:T(8,128)S(1)}, u32[]{:S(2)}, u32[]{:S(2)}) %collective-permute-start.9) | collective-permute-done | bytes 196640 | tf_op jit(solution)/shard_map/ppermute | solution.py:19
  17.4 0.0 collective-permute-start.5
  17.4 0.0 collective-permute-done.4.refs_4_.refs_3_
  17.4 0.5 %collective-permute-start.6 = (f32[96,512]{1,0:T(8,128)S(1)}, f32[96,512]{1,0:T(8,128)S(1)}, u32[]{:S(2)}, u32[]{:S(2)}) collective-permute-start(f32[96,512]{1,0:T(8,128)S(1)} %collective-permute-done.4.refs_4_.refs_3_), channel_id=1, source_target_pairs={{0,1},{1,0},{2,3},{3,2},{4,5},{5,4},{6,7},{7,6},{8,9},{9,8},{10,11... | collective-permute-start | bytes 589832 | tf_op jit(solution)/shard_map/ppermute | solution.py:19
  17.9 0.0 collective-permute-done.refs_2_.refs_1_
  17.9 2.0 %shard_map.39.refs_3_ = f32[64,512]{1,0:T(8,128)S(1)} custom-call(f32[96,512]{1,0:T(8,128)S(1)} %collective-permute-done.9.refs_0_, f32[96,512]{1,0:T(8,128)S(1)} %copy-done, f32[96,512]{1,0:T(8,128)S(1)} %collective-permute-done.refs_2_.refs_1_, f32[96,512]{1,0:T(8,128)S(1)} %constant_dynamic-update-slice_fusion.refs_3_.refs_2_, ...), custom_call_target="tpu_custom_call" | custom-call | flops 2147483648 | bytes 983040 | tf_op jit(solution)/shard_map/pallas_call | solution.py:125
  19.9 0.0 collective-permute-done.5.refs_1_.refs_4_
  19.9 0.0 collective-permute-done.6.refs_2_.refs_5_
  19.9 1.1 %shard_map.40.refs_3_ = f32[64,512]{1,0:T(8,128)S(1)} custom-call(f32[96,512]{1,0:T(8,128)S(1)} %collective-permute-done.9.refs_0_, f32[96,512]{1,0:T(8,128)S(1)} %collective-permute-done.5.refs_1_.refs_4_, f32[96,512]{1,0:T(8,128)S(1)} %collective-permute-done.6.refs_2_.refs_5_, f32[64,512]{1,0:T(8,128)S(1)} %shard_map.39.refs_3_), custom_call_target="tpu_custom_call" | custom-call | flops 536870912 | bytes 786432 | tf_op jit(solution)/shard_map/pallas_call | solution.py:125
  21.1 0.0 collective-permute-done.8
  21.1 0.0 collective-permute-done.7
  21.1 0.1 collective-permute-start.10
  21.2 1.3 %shard_map.41 = (f32[64,512]{1,0:T(8,128)S(1)}, f32[64,512]{1,0:T(8,128)S(1)}) custom-call(f32[96,512]{1,0:T(8,128)S(1)} %collective-permute-done.9.refs_0_, f32[96,512]{1,0:T(8,128)S(1)} %constant_dynamic-update-slice_fusion.3.refs_1_, f32[96,512]{1,0:T(8,128)S(1)} %copy-done, f32[64,512]{1,0:T(8,128)S(1)} %shard_map.40.refs_3_, ...), custom_call_target="tpu_custom_call" | custom-call | flops 67108864 | bytes 983040 | tf_op jit(solution)/shard_map/pallas_call | solution.py:125
  22.5 0.1 collective-permute-done.10.refs_6_.refs_1_
  22.6 0.8 %shard_map.43 = f32[64,512]{1,0:T(8,128)S(1)} custom-call(f32[96,512]{1,0:T(8,128)S(1)} %collective-permute-done.9.refs_0_, f32[96,512]{1,0:T(8,128)S(1)} %collective-permute-done.10.refs_6_.refs_1_, f32[64,512]{1,0:T(8,128)S(1)} %get-tuple-element.24.refs_2_), custom_call_target="tpu_custom_call" | custom-call | flops 33554432 | bytes 589824 | tf_op jit(solution)/shard_map/pallas_call | solution.py:125
  23.4 0.1 collective-permute-start.11
  23.5 3.0 %shard_map.42 = f32[64,512]{1,0:T(8,128)S(1)} custom-call(f32[96,512]{1,0:T(8,128)S(1)} %copy-done, f32[96,512]{1,0:T(8,128)S(1)} %collective-permute-done.refs_2_.refs_1_, f32[96,512]{1,0:T(8,128)S(1)} %constant_dynamic-update-slice_fusion.refs_3_.refs_2_, f32[96,512]{1,0:T(8,128)S(1)} %collective-permute-done.4.refs_4_.refs_3_, ...), custom_call_target="tpu_custom_call" | custom-call | flops 6442450944 | bytes 1572864 | tf_op jit(solution)/shard_map/pallas_call | solution.py:125
  26.5 2.8 %collective-permute-done.11 = f32[64,512]{1,0:T(8,128)S(1)} collective-permute-done((f32[64,512]{1,0:T(8,128)S(1)}, f32[64,512]{1,0:T(8,128)S(1)}, u32[]{:S(2)}, u32[]{:S(2)}) %collective-permute-start.11) | collective-permute-done | bytes 131104 | tf_op jit(solution)/shard_map/ppermute | solution.py:19
  29.3 0.7 %add.3 = f32[64,512]{1,0:T(8,128)} add(f32[64,512]{1,0:T(8,128)S(1)} %shard_map.42, f32[64,512]{1,0:T(8,128)S(1)} %collective-permute-done.11) | non-fusion elementwise | flops 32768 | bytes 393216 | tf_op jit(solution)/shard_map/add | solution.py:193
  (6 shorter events, 0.0 us)
Async XLA Ops:
  0.0 12.8 %collective-permute-start.1 = (f32[64,512]{1,0:T(8,128)}, f32[64,512]{1,0:T(8,128)S(1)}, u32[]{:S(2)}, u32[]{:S(2)}) collective-permute-start(f32[64,512]{1,0:T(8,128)} %features_ref.1), channel_id=1, source_target_pairs={{0,8},{1,9},{2,10},{3,11},{4,12},{5,13},{6,14},{7,15},{8,0},{9,1},... | collective-permute-start | bytes 393224 | tf_op jit(solution)/shard_map/ppermute | solution.py:19
  4.0 9.5 %collective-permute-start.2 = (f32[16,512]{1,0:T(8,128)}, f32[16,512]{1,0:T(8,128)S(1)}, u32[]{:S(2)}, u32[]{:S(2)}) collective-permute-start(f32[16,512]{1,0:T(8,128)} %solves_ref.1), channel_id=1, source_target_pairs={{0,8},{1,9},{2,10},{3,11},{4,12},{5,13},{6,14},{7,15},{8,0},{9,1},... | collective-permute-start | bytes 98312 | tf_op jit(solution)/shard_map/ppermute | solution.py:19
  4.1 11.1 %collective-permute-start.3 = (f32[16,512]{1,0:T(8,128)}, f32[16,512]{1,0:T(8,128)S(1)}, u32[]{:S(2)}, u32[]{:S(2)}) collective-permute-start(f32[16,512]{1,0:T(8,128)} %probes_ref.1), channel_id=1, source_target_pairs={{0,8},{1,9},{2,10},{3,11},{4,12},{5,13},{6,14},{7,15},{8,0},{9,1},... | collective-permute-start | bytes 98312 | tf_op jit(solution)/shard_map/ppermute | solution.py:19
  8.6 4.2 %copy-start = (f32[96,512]{1,0:T(8,128)S(1)}, f32[96,512]{1,0:T(8,128)}, u32[]{:S(2)}) copy-start(f32[96,512]{1,0:T(8,128)} %shard_map.37.refs_0_.refs_1_.refs_2_) | copy-start | bytes 589828
  8.6 8.8 %collective-permute-start.9 = (f32[96,512]{1,0:T(8,128)}, f32[96,512]{1,0:T(8,128)S(1)}, u32[]{:S(2)}, u32[]{:S(2)}) collective-permute-start(f32[96,512]{1,0:T(8,128)} %shard_map.37.refs_0_.refs_1_.refs_2_), channel_id=1, source_target_pairs={{0,4},{1,5},{2,6},{3,7},{4,0},{5,1},{6,2},{7,3},{8,12},{9,13},{10,... | collective-permute-start | bytes 589832 | tf_op jit(solution)/shard_map/ppermute | solution.py:19
  10.2 7.2 %collective-permute-start.4 = (f32[96,512]{1,0:T(8,128)}, f32[96,512]{1,0:T(8,128)S(1)}, u32[]{:S(2)}, u32[]{:S(2)}) collective-permute-start(f32[96,512]{1,0:T(8,128)} %shard_map.37.refs_0_.refs_1_.refs_2_), channel_id=1, source_target_pairs={{0,2},{1,3},{2,0},{3,1},{4,6},{5,7},{6,4},{7,5},{8,10},{9,11},{10,... | collective-permute-start | bytes 589832 | tf_op jit(solution)/shard_map/ppermute | solution.py:19
  12.8 5.1 %collective-permute-start = (f32[96,512]{1,0:T(8,128)}, f32[96,512]{1,0:T(8,128)S(1)}, u32[]{:S(2)}, u32[]{:S(2)}) collective-permute-start(f32[96,512]{1,0:T(8,128)} %shard_map.37.refs_0_.refs_1_.refs_2_), channel_id=1, source_target_pairs={{0,1},{1,0},{2,3},{3,2},{4,5},{5,4},{6,7},{7,6},{8,9},{9,8},{10,11... | collective-permute-start | bytes 589832 | tf_op jit(solution)/shard_map/ppermute | solution.py:19
  13.6 7.5 %collective-permute-start.7 = (f32[64,512]{1,0:T(8,128)S(1)}, f32[64,512]{1,0:T(8,128)S(1)}, u32[]{:S(2)}, u32[]{:S(2)}) collective-permute-start(f32[64,512]{1,0:T(8,128)S(1)} %collective-permute-done.1), channel_id=1, source_target_pairs={{0,2},{1,3},{2,0},{3,1},{4,6},{5,7},{6,4},{7,5},{8,10},{9,11},{10,... | collective-permute-start | bytes 393224 | tf_op jit(solution)/shard_map/ppermute | solution.py:19
  15.2 5.9 %collective-permute-start.8 = (f32[32,512]{1,0:T(8,128)S(1)}, f32[32,512]{1,0:T(8,128)S(1)}, u32[]{:S(2)}, u32[]{:S(2)}) collective-permute-start(f32[32,512]{1,0:T(8,128)S(1)} %pad_maximum_fusion), channel_id=1, source_target_pairs={{0,2},{1,3},{2,0},{3,1},{4,6},{5,7},{6,4},{7,5},{8,10},{9,11},{10,... | collective-permute-start | bytes 196616 | tf_op jit(solution)/shard_map/ppermute | solution.py:19
  17.4 2.6 %collective-permute-start.5 = (f32[96,512]{1,0:T(8,128)S(1)}, f32[96,512]{1,0:T(8,128)S(1)}, u32[]{:S(2)}, u32[]{:S(2)}) collective-permute-start(f32[96,512]{1,0:T(8,128)S(1)} %constant_dynamic-update-slice_fusion.refs_3_.refs_2_), channel_id=1, source_target_pairs={{0,1},{1,0},{2,3},{3,2},{4,5},{5,4},{6,7},{7,6},{8,9},{9,8},{10,11... | collective-permute-start | bytes 589832 | tf_op jit(solution)/shard_map/ppermute | solution.py:19
  17.4 2.6 %collective-permute-start.6 = (f32[96,512]{1,0:T(8,128)S(1)}, f32[96,512]{1,0:T(8,128)S(1)}, u32[]{:S(2)}, u32[]{:S(2)}) collective-permute-start(f32[96,512]{1,0:T(8,128)S(1)} %collective-permute-done.4.refs_4_.refs_3_), channel_id=1, source_target_pairs={{0,1},{1,0},{2,3},{3,2},{4,5},{5,4},{6,7},{7,6},{8,9},{9,8},{10,11... | collective-permute-start | bytes 589832 | tf_op jit(solution)/shard_map/ppermute | solution.py:19
  21.1 1.5 %collective-permute-start.10 = (f32[96,512]{1,0:T(8,128)S(1)}, f32[96,512]{1,0:T(8,128)S(1)}, u32[]{:S(2)}, u32[]{:S(2)}) collective-permute-start(f32[96,512]{1,0:T(8,128)S(1)} %constant_dynamic-update-slice_fusion.3.refs_1_), channel_id=1, source_target_pairs={{0,1},{1,0},{2,3},{3,2},{4,5},{5,4},{6,7},{7,6},{8,9},{9,8},{10,11... | collective-permute-start | bytes 589832 | tf_op jit(solution)/shard_map/ppermute | solution.py:19
  23.4 5.9 %collective-permute-start.11 = (f32[64,512]{1,0:T(8,128)S(1)}, f32[64,512]{1,0:T(8,128)S(1)}, u32[]{:S(2)}, u32[]{:S(2)}) collective-permute-start(f32[64,512]{1,0:T(8,128)S(1)} %shard_map.43), channel_id=1, source_target_pairs={{0,4},{1,5},{2,6},{3,7},{4,0},{5,1},{6,2},{7,3},{8,12},{9,13},{10,... | collective-permute-start | bytes 393224 | tf_op jit(solution)/shard_map/ppermute | solution.py:19

commit v17 on v15

--- a/solution.py
+++ b/solution.py
@@ -174,24 +174,27 @@
     near = swap(mine, 4)
     direct = [swap(mine, bit) for bit in beside]
 
-    (here,) = terms([(mine, [mine])], weight=1024)
-    far_features, far_vectors, here = tied((far_features, far_vectors, here))
+    far_features, own = tied((far_features, mine))
+    (here,) = terms([(own, [own])], weight=2048)
+    near, here = tied((near, here))
+    (there,) = terms([(near, [mine, sibling] + direct)], weight=1024)
+    far_vectors, there = tied((far_vectors, there))
     far = [far_features, far_vectors]
     last = []
     for bit in beside:
         for pair in [far] + last:
             last = last + [[swap(piece, bit) for piece in pair]]
     first = [jnp.concatenate(far, 0)] + direct
-    siblings = [swap(block, 1) for block in first]
-    (there,) = terms([(near, [mine, sibling] + first)], weight=1024)
-    (there,) = terms([(near, siblings)], before=[there], weight=512)
+    siblings = jnp.split(swap(jnp.concatenate(first, 0), 1), len(first), 0)
+    there, here = terms([(near, first[:1]), (mine, first[:1])], before=[there, here], weight=30000)
+    (there,) = terms([(near, siblings)], before=[there], weight=8)
     *pieces, there = tied((*[piece for pair in last for piece in pair], there))
     last = [jnp.concatenate(pieces[at : at + 2], 0) for at in range(0, len(pieces), 2)]
     last_siblings = [swap(block, 1) for block in last]
     there, here = terms([(near, last), (mine, last)], before=[there, here], weight=64)
-    toward_near = terms([(near, last_siblings)], before=[there], weight=64, pieces=2)
-    from_near = jnp.concatenate([swap(piece, 4) for piece in toward_near], 0)
-    rest = [sibling] + first + siblings + last_siblings
+    (toward_near,) = terms([(near, last_siblings)], before=[there], weight=64)
+    from_near = swap(toward_near, 4)
+    rest = [sibling] + direct + siblings + last_siblings
     (here,) = terms([(mine, rest)], before=[here], weight=2048)
     return here + from_near
 

time: 29 us -> 30.5 us (1.052)
  waiting for transfers between devices: 4.18 us -> 5.96 us
  starting transfers between devices: 12.2 us -> 11.4 us
  Pallas kernels: 10.7 us -> 11.2 us
    ppermute x12 -> x10, waiting for transfers between devices: 4.18 us -> 5.96 us  [swapped(): lax.ppermute(value, axis, [(source, source ^ bit) for source in range(cou...]
    ppermute x12 -> x10, starting transfers between devices: 12.2 us -> 11.4 us  [swapped(): lax.ppermute(value, axis, [(source, source ^ bit) for source in range(cou...]
    pallas_call x6 -> x7, Pallas kernels: 9.02 us -> 9.53 us  [pair_terms(): pl.pallas_call(functools.partial(kernel, width, vectors, placed, len(bloc...]
    unnamed x4 -> x3, local copies, waits for them, and re-layouts: 0.98 us -> 0.94 us
  transfers between devices with their start and end apart: 12 -> 10, of which waited for: 4 -> 5; matrix products, arithmetic and copies ran while one was open for 0% -> 0% of each run, Pallas kernels for 34% -> 34%
where the time goes in v17:
time: 30.5 us; the launch traced here: 30.4 us
  starting transfers between devices  11.4 us (37%)
  Pallas kernels  11.2 us (37%)
  waiting for transfers between devices  5.96 us (20%)
  local copies, waits for them, and re-layouts  0.97 us (3%)
  other arithmetic  0.72 us (2%)
    ppermute x10, starting transfers between devices, swapped(): lax.ppermute(value, axis, [(source, source ^ bit) for source in range(cou...  11.4 us
    pallas_call x7, Pallas kernels, pair_terms(): pl.pallas_call(functools.partial(kernel, width, vectors, placed, len(bloc...  9.53 us
    ppermute x10, waiting for transfers between devices, swapped(): lax.ppermute(value, axis, [(source, source ^ bit) for source in range(cou...  5.96 us
    pallas_call x1, Pallas kernels, packed(): pl.pallas_call(body, out_shape=[jax.ShapeDtypeStruct((rows, points), jnp....  1.65 us
    unnamed x3, local copies, waits for them, and re-layouts  0.94 us
    add x1, other arithmetic, local(): return here + from_near  0.67 us
  transfers between devices with their start and end apart: 10, of which 5 were waited for; matrix products, arithmetic and copies ran while one was open for 0% of the time, Pallas kernels for 34%

profile of v17, /device:TPU:0, one launch (start us, length us, event | category | flops | bytes accessed | tf_op | source)
XLA Modules:
  0.0 30.4 jit_solution(6590610072855910545)
XLA Ops:
  0.0 4.0 %collective-permute-start.2 = (f32[64,512]{1,0:T(8,128)}, f32[64,512]{1,0:T(8,128)S(1)}, u32[]{:S(2)}, u32[]{:S(2)}) collective-permute-start(f32[64,512]{1,0:T(8,128)} %features_ref.1), channel_id=1, source_target_pairs={{0,8},{1,9},{2,10},{3,11},{4,12},{5,13},{6,14},{7,15},{8,0},{9,1},... | collective-permute-start | bytes 393224 | tf_op jit(solution)/shard_map/ppermute | solution.py:19
  4.0 1.7 %shard_map.37 = (f32[96,512]{1,0:T(8,128)}, f32[32,512]{1,0:T(8,128)}) custom-call(f32[64,512]{1,0:T(8,128)} %features_ref.1, f32[16,512]{1,0:T(8,128)} %solves_ref.1, f32[16,512]{1,0:T(8,128)} %probes_ref.1), custom_call_target="tpu_custom_call" | custom-call | tf_op jit(solution)/shard_map/pallas_call | solution.py:150
  5.7 1.6 %collective-permute-start.4 = (f32[96,512]{1,0:T(8,128)}, f32[96,512]{1,0:T(8,128)S(1)}, u32[]{:S(2)}, u32[]{:S(2)}) collective-permute-start(f32[96,512]{1,0:T(8,128)} %get-tuple-element.23.refs_0_.refs_1_.refs_2_), channel_id=1, source_target_pairs={{0,4},{1,5},{2,6},{3,7},{4,0},{5,1},{6,2},{7,3},{8,12},{9,13},{10,... | collective-permute-start | bytes 589832 | tf_op jit(solution)/shard_map/ppermute | solution.py:19
  7.3 1.5 %collective-permute-start.1 = (f32[96,512]{1,0:T(8,128)}, f32[96,512]{1,0:T(8,128)S(1)}, u32[]{:S(2)}, u32[]{:S(2)}) collective-permute-start(f32[96,512]{1,0:T(8,128)} %get-tuple-element.23.refs_0_.refs_1_.refs_2_), channel_id=1, source_target_pairs={{0,2},{1,3},{2,0},{3,1},{4,6},{5,7},{6,4},{7,5},{8,10},{9,11},{10,... | collective-permute-start | bytes 589832 | tf_op jit(solution)/shard_map/ppermute | solution.py:19
  8.8 0.0 collective-permute-start
  8.8 0.3 %collective-permute-start.3 = (f32[32,512]{1,0:T(8,128)}, f32[32,512]{1,0:T(8,128)S(1)}, u32[]{:S(2)}, u32[]{:S(2)}) collective-permute-start(f32[32,512]{1,0:T(8,128)} %get-tuple-element.22), channel_id=1, source_target_pairs={{0,8},{1,9},{2,10},{3,11},{4,12},{5,13},{6,14},{7,15},{8,0},{9,1},... | collective-permute-start | bytes 196616 | tf_op jit(solution)/shard_map/ppermute | solution.py:19
  9.1 1.5 %collective-permute-done.2 = f32[64,512]{1,0:T(8,128)S(1)} collective-permute-done((f32[64,512]{1,0:T(8,128)}, f32[64,512]{1,0:T(8,128)S(1)}, u32[]{:S(2)}, u32[]{:S(2)}) %collective-permute-start.2) | collective-permute-done | bytes 131104 | tf_op jit(solution)/shard_map/ppermute | solution.py:19
  10.7 1.6 %collective-permute-start.6 = (f32[64,512]{1,0:T(8,128)S(1)}, f32[64,512]{1,0:T(8,128)S(1)}, u32[]{:S(2)}, u32[]{:S(2)}) collective-permute-start(f32[64,512]{1,0:T(8,128)S(1)} %collective-permute-done.2), channel_id=1, source_target_pairs={{0,2},{1,3},{2,0},{3,1},{4,6},{5,7},{6,4},{7,5},{8,10},{9,11},{10,... | collective-permute-start | bytes 393224 | tf_op jit(solution)/shard_map/ppermute | solution.py:19
  12.2 0.0 copy-start
  12.2 0.9 %copy-done = f32[96,512]{1,0:T(8,128)S(1)} copy-done((f32[96,512]{1,0:T(8,128)S(1)}, f32[96,512]{1,0:T(8,128)}, u32[]{:S(2)}) %copy-start) | copy-done | bytes 196632
  13.2 0.8 %shard_map.38.refs_4_ = f32[64,512]{1,0:T(8,128)S(1)} custom-call(f32[96,512]{1,0:T(8,128)S(1)} %copy-done), custom_call_target="tpu_custom_call" | custom-call | flops 1073741824 | bytes 196608 | tf_op jit(solution)/shard_map/pallas_call | solution.py:125
  13.9 0.1 collective-permute-done.4.refs_0_
  14.0 0.9 %collective-permute-done.1.refs_3_.refs_2_ = f32[96,512]{1,0:T(8,128)S(1)} collective-permute-done((f32[96,512]{1,0:T(8,128)}, f32[96,512]{1,0:T(8,128)S(1)}, u32[]{:S(2)}, u32[]{:S(2)}) %collective-permute-start.1) | collective-permute-done | bytes 196640 | tf_op jit(solution)/shard_map/ppermute | solution.py:19
  14.9 0.0 collective-permute-done.refs_2_.refs_1_
  14.9 1.6 %shard_map.39.refs_3_ = f32[64,512]{1,0:T(8,128)S(1)} custom-call(f32[96,512]{1,0:T(8,128)S(1)} %collective-permute-done.4.refs_0_, f32[96,512]{1,0:T(8,128)S(1)} %copy-done, f32[96,512]{1,0:T(8,128)S(1)} %collective-permute-done.refs_2_.refs_1_, f32[96,512]{1,0:T(8,128)S(1)} %collective-permute-done.1.refs_3_.refs_2_), custom_call_target="tpu_custom_call" | custom-call | flops 1610612736 | bytes 786432 | tf_op jit(solution)/shard_map/pallas_call | solution.py:125
  16.5 0.0 collective-permute-done.3
  16.5 2.0 %collective-permute-start.7 = (f32[32,512]{1,0:T(8,128)S(1)}, f32[32,512]{1,0:T(8,128)S(1)}, u32[]{:S(2)}, u32[]{:S(2)}) collective-permute-start(f32[32,512]{1,0:T(8,128)S(1)} %collective-permute-done.3), channel_id=1, source_target_pairs={{0,2},{1,3},{2,0},{3,1},{4,6},{5,7},{6,4},{7,5},{8,10},{9,11},{10,... | collective-permute-start | bytes 196616 | tf_op jit(solution)/shard_map/ppermute | solution.py:19
  18.5 0.1 collective-permute-start.5
  18.6 1.3 %shard_map.40 = (f32[64,512]{1,0:T(8,128)S(1)}, f32[64,512]{1,0:T(8,128)S(1)}) custom-call(f32[96,512]{1,0:T(8,128)S(1)} %collective-permute-done.4.refs_0_, f32[96,512]{1,0:T(8,128)S(1)} %pad_maximum_fusion.1.refs_1_, f32[96,512]{1,0:T(8,128)S(1)} %copy-done, f32[64,512]{1,0:T(8,128)S(1)} %shard_map.39.refs_3_, f32[64,512]{1,0:T(8,128)S(1)} %shard_map.38.refs_4_), custom_call_target="tpu_custom_call" | custom-call | flops 31457280000 | bytes 983040 | tf_op jit(solution)/shard_map/pallas_call | solution.py:125
  19.9 0.4 %collective-permute-done.5 = f32[192,512]{1,0:T(8,128)S(1)} collective-permute-done((f32[192,512]{1,0:T(8,128)S(1)}, f32[192,512]{1,0:T(8,128)S(1)}, u32[]{:S(2)}, u32[]{:S(2)}) %collective-permute-start.5) | collective-permute-done | bytes 393248 | tf_op jit(solution)/shard_map/ppermute | solution.py:19
  20.3 1.1 %shard_map.41.refs_3_ = f32[64,512]{1,0:T(8,128)S(1)} custom-call(f32[96,512]{1,0:T(8,128)S(1)} %collective-permute-done.4.refs_0_, f32[96,512]{1,0:T(8,128)S(1)} %get-tuple-element.36.refs_1_.refs_3_, f32[96,512]{1,0:T(8,128)S(1)} %get-tuple-element.35.refs_2_.refs_4_, f32[64,512]{1,0:T(8,128)S(1)} %get-tuple-element.28.refs_3_), custom_call_target="tpu_custom_call" | custom-call | flops 8388608 | bytes 786432 | tf_op jit(solution)/shard_map/pallas_call | solution.py:125
  21.5 0.0 collective-permute-done.6
  21.5 0.0 collective-permute-done.7
  21.5 0.2 collective-permute-start.8
  21.7 1.3 %shard_map.42 = (f32[64,512]{1,0:T(8,128)S(1)}, f32[64,512]{1,0:T(8,128)S(1)}) custom-call(f32[96,512]{1,0:T(8,128)S(1)} %collective-permute-done.4.refs_0_, f32[96,512]{1,0:T(8,128)S(1)} %constant_dynamic-update-slice_fusion.refs_1_, f32[96,512]{1,0:T(8,128)S(1)} %copy-done, f32[64,512]{1,0:T(8,128)S(1)} %shard_map.41.refs_3_, ...), custom_call_target="tpu_custom_call" | custom-call | flops 67108864 | bytes 983040 | tf_op jit(solution)/shard_map/pallas_call | solution.py:125
  23.1 0.0 collective-permute-done.8.refs_5_.refs_1_
  23.1 0.8 %shard_map.44 = f32[64,512]{1,0:T(8,128)S(1)} custom-call(f32[96,512]{1,0:T(8,128)S(1)} %collective-permute-done.4.refs_0_, f32[96,512]{1,0:T(8,128)S(1)} %collective-permute-done.8.refs_5_.refs_1_, f32[64,512]{1,0:T(8,128)S(1)} %get-tuple-element.34.refs_2_), custom_call_target="tpu_custom_call" | custom-call | flops 33554432 | bytes 589824 | tf_op jit(solution)/shard_map/pallas_call | solution.py:125
  23.8 0.1 collective-permute-start.9
  23.9 2.7 %shard_map.43 = f32[64,512]{1,0:T(8,128)S(1)} custom-call(f32[96,512]{1,0:T(8,128)S(1)} %copy-done, f32[96,512]{1,0:T(8,128)S(1)} %collective-permute-done.refs_2_.refs_1_, f32[96,512]{1,0:T(8,128)S(1)} %collective-permute-done.1.refs_3_.refs_2_, f32[96,512]{1,0:T(8,128)S(1)} %get-tuple-element.36.refs_1_.refs_3_, ...), custom_call_target="tpu_custom_call" | custom-call | flops 5368709120 | bytes 1376256 | tf_op jit(solution)/shard_map/pallas_call | solution.py:125
  26.6 3.1 %collective-permute-done.9 = f32[64,512]{1,0:T(8,128)S(1)} collective-permute-done((f32[64,512]{1,0:T(8,128)S(1)}, f32[64,512]{1,0:T(8,128)S(1)}, u32[]{:S(2)}, u32[]{:S(2)}) %collective-permute-start.9) | collective-permute-done | bytes 131104 | tf_op jit(solution)/shard_map/ppermute | solution.py:19
  29.7 0.7 %add.3 = f32[64,512]{1,0:T(8,128)} add(f32[64,512]{1,0:T(8,128)S(1)} %shard_map.43, f32[64,512]{1,0:T(8,128)S(1)} %collective-permute-done.9) | non-fusion elementwise | flops 32768 | bytes 393216 | tf_op jit(solution)/shard_map/add | solution.py:199
  (5 shorter events, 0.1 us)
Async XLA Ops:
  0.0 10.7 %collective-permute-start.2 = (f32[64,512]{1,0:T(8,128)}, f32[64,512]{1,0:T(8,128)S(1)}, u32[]{:S(2)}, u32[]{:S(2)}) collective-permute-start(f32[64,512]{1,0:T(8,128)} %features_ref.1), channel_id=1, source_target_pairs={{0,8},{1,9},{2,10},{3,11},{4,12},{5,13},{6,14},{7,15},{8,0},{9,1},... | collective-permute-start | bytes 393224 | tf_op jit(solution)/shard_map/ppermute | solution.py:19
  5.7 8.3 %collective-permute-start.4 = (f32[96,512]{1,0:T(8,128)}, f32[96,512]{1,0:T(8,128)S(1)}, u32[]{:S(2)}, u32[]{:S(2)}) collective-permute-start(f32[96,512]{1,0:T(8,128)} %get-tuple-element.23.refs_0_.refs_1_.refs_2_), channel_id=1, source_target_pairs={{0,4},{1,5},{2,6},{3,7},{4,0},{5,1},{6,2},{7,3},{8,12},{9,13},{10,... | collective-permute-start | bytes 589832 | tf_op jit(solution)/shard_map/ppermute | solution.py:19
  7.3 7.6 %collective-permute-start.1 = (f32[96,512]{1,0:T(8,128)}, f32[96,512]{1,0:T(8,128)S(1)}, u32[]{:S(2)}, u32[]{:S(2)}) collective-permute-start(f32[96,512]{1,0:T(8,128)} %get-tuple-element.23.refs_0_.refs_1_.refs_2_), channel_id=1, source_target_pairs={{0,2},{1,3},{2,0},{3,1},{4,6},{5,7},{6,4},{7,5},{8,10},{9,11},{10,... | collective-permute-start | bytes 589832 | tf_op jit(solution)/shard_map/ppermute | solution.py:19
  8.8 6.1 %collective-permute-start = (f32[96,512]{1,0:T(8,128)}, f32[96,512]{1,0:T(8,128)S(1)}, u32[]{:S(2)}, u32[]{:S(2)}) collective-permute-start(f32[96,512]{1,0:T(8,128)} %get-tuple-element.23.refs_0_.refs_1_.refs_2_), channel_id=1, source_target_pairs={{0,1},{1,0},{2,3},{3,2},{4,5},{5,4},{6,7},{7,6},{8,9},{9,8},{10,11... | collective-permute-start | bytes 589832 | tf_op jit(solution)/shard_map/ppermute | solution.py:19
  8.8 7.7 %collective-permute-start.3 = (f32[32,512]{1,0:T(8,128)}, f32[32,512]{1,0:T(8,128)S(1)}, u32[]{:S(2)}, u32[]{:S(2)}) collective-permute-start(f32[32,512]{1,0:T(8,128)} %get-tuple-element.22), channel_id=1, source_target_pairs={{0,8},{1,9},{2,10},{3,11},{4,12},{5,13},{6,14},{7,15},{8,0},{9,1},... | collective-permute-start | bytes 196616 | tf_op jit(solution)/shard_map/ppermute | solution.py:19
  10.7 10.8 %collective-permute-start.6 = (f32[64,512]{1,0:T(8,128)S(1)}, f32[64,512]{1,0:T(8,128)S(1)}, u32[]{:S(2)}, u32[]{:S(2)}) collective-permute-start(f32[64,512]{1,0:T(8,128)S(1)} %collective-permute-done.2), channel_id=1, source_target_pairs={{0,2},{1,3},{2,0},{3,1},{4,6},{5,7},{6,4},{7,5},{8,10},{9,11},{10,... | collective-permute-start | bytes 393224 | tf_op jit(solution)/shard_map/ppermute | solution.py:19
  12.2 0.9 %copy-start = (f32[96,512]{1,0:T(8,128)S(1)}, f32[96,512]{1,0:T(8,128)}, u32[]{:S(2)}) copy-start(f32[96,512]{1,0:T(8,128)} %get-tuple-element.23.refs_0_.refs_1_.refs_2_) | copy-start | bytes 589828
  16.5 5.0 %collective-permute-start.7 = (f32[32,512]{1,0:T(8,128)S(1)}, f32[32,512]{1,0:T(8,128)S(1)}, u32[]{:S(2)}, u32[]{:S(2)}) collective-permute-start(f32[32,512]{1,0:T(8,128)S(1)} %collective-permute-done.3), channel_id=1, source_target_pairs={{0,2},{1,3},{2,0},{3,1},{4,6},{5,7},{6,4},{7,5},{8,10},{9,11},{10,... | collective-permute-start | bytes 196616 | tf_op jit(solution)/shard_map/ppermute | solution.py:19
  18.5 1.8 %collective-permute-start.5 = (f32[192,512]{1,0:T(8,128)S(1)}, f32[192,512]{1,0:T(8,128)S(1)}, u32[]{:S(2)}, u32[]{:S(2)}) collective-permute-start(f32[192,512]{1,0:T(8,128)S(1)} %pad_maximum_fusion), channel_id=1, source_target_pairs={{0,1},{1,0},{2,3},{3,2},{4,5},{5,4},{6,7},{7,6},{8,9},{9,8},{10,11... | collective-permute-start | bytes 1179656 | tf_op jit(solution)/shard_map/ppermute | solution.py:19
  21.5 1.5 %collective-permute-start.8 = (f32[96,512]{1,0:T(8,128)S(1)}, f32[96,512]{1,0:T(8,128)S(1)}, u32[]{:S(2)}, u32[]{:S(2)}) collective-permute-start(f32[96,512]{1,0:T(8,128)S(1)} %constant_dynamic-update-slice_fusion.refs_1_), channel_id=1, source_target_pairs={{0,1},{1,0},{2,3},{3,2},{4,5},{5,4},{6,7},{7,6},{8,9},{9,8},{10,11... | collective-permute-start | bytes 589832 | tf_op jit(solution)/shard_map/ppermute | solution.py:19
  23.8 5.8 %collective-permute-start.9 = (f32[64,512]{1,0:T(8,128)S(1)}, f32[64,512]{1,0:T(8,128)S(1)}, u32[]{:S(2)}, u32[]{:S(2)}) collective-permute-start(f32[64,512]{1,0:T(8,128)S(1)} %shard_map.44), channel_id=1, source_target_pairs={{0,4},{1,5},{2,6},{3,7},{4,0},{5,1},{6,2},{7,3},{8,12},{9,13},{10,... | collective-permute-start | bytes 393224 | tf_op jit(solution)/shard_map/ppermute | solution.py:19

commit v18 on v15

--- a/solution.py
+++ b/solution.py
@@ -63,17 +63,23 @@
     vec_high, vec_low = split2(vecs)
     pair = jnp.concatenate([vec_high, vec_high, vec_low], 0)
     ones = jnp.ones((ONES_ROWS, block.shape[1]), jnp.bfloat16)
-    return dist.T, pair.T, jnp.concatenate([high, ones, low], 0)
+    return dist, pair, jnp.concatenate([high, ones, low], 0)
 
 
 def product(left, right):
     return jnp.dot(left, right, preferred_element_type=jnp.float32)
+
+
+def pair_product(left, right):
+    first = (((0,), (0,)), ((), ()))
+    return lax.dot_general(left, right, first, preferred_element_type=jnp.float32)
 
 
 def pulled_terms(mine, theirs, width):
     dist_mine, pair_mine = mine
     dist_theirs, pair_theirs, pull = theirs
-    coupling = jnp.exp2(product(dist_theirs, dist_mine)) * product(pair_theirs, pair_mine)
+    power = pair_product(dist_theirs, dist_mine)
+    coupling = jnp.exp2(power) * pair_product(pair_theirs, pair_mine)
     high, low = split2(coupling)
     from_high = product(pull, high)
     from_low = product(pull[: width + ONES_ROWS], low)
@@ -83,7 +89,7 @@
 
 def stacked(theirs):
     dist, pair, pull = zip(*theirs)
-    return jnp.concatenate(dist, 0), jnp.concatenate(pair, 0), jnp.concatenate(pull, 1)
+    return tuple(jnp.concatenate(part, 1) for part in (dist, pair, pull))
 
 
 def kernel(width, vectors, jobs, count, pieces, *refs):

time: 29 us -> 29 us (level)
  no operation moved by 1% of the time
where the time goes in v18:
time: 29 us; the launch traced here: 28.9 us
  starting transfers between devices  12.2 us (42%)
  Pallas kernels  10.7 us (37%)
  waiting for transfers between devices  4.18 us (14%)
  local copies, waits for them, and re-layouts  0.99 us (3%)
  other arithmetic  0.67 us (2%)
    ppermute x12, starting transfers between devices, swapped(): lax.ppermute(value, axis, [(source, source ^ bit) for source in range(cou...  12.2 us
    pallas_call x6, Pallas kernels, pair_terms(): pl.pallas_call(functools.partial(kernel, width, vectors, placed, len(bloc...  9.02 us
    ppermute x12, waiting for transfers between devices, swapped(): lax.ppermute(value, axis, [(source, source ^ bit) for source in range(cou...  4.18 us
    pallas_call x1, Pallas kernels, packed(): pl.pallas_call(body, out_shape=[jax.ShapeDtypeStruct((rows, points), jnp....  1.65 us
    unnamed x4, local copies, waits for them, and re-layouts  0.98 us
    add x1, other arithmetic, local(): return here + from_near  0.67 us
  transfers between devices with their start and end apart: 12, of which 4 were waited for; matrix products, arithmetic and copies ran while one was open for 0% of the time, Pallas kernels for 34%

profile of v18, /device:TPU:0, one launch (start us, length us, event | category | flops | bytes accessed | tf_op | source)
XLA Modules:
  0.0 28.9 jit_solution(4905694125352758529)
XLA Ops:
  0.0 4.0 %collective-permute-start.1 = (f32[64,512]{1,0:T(8,128)}, f32[64,512]{1,0:T(8,128)S(1)}, u32[]{:S(2)}, u32[]{:S(2)}) collective-permute-start(f32[64,512]{1,0:T(8,128)} %features_ref.1), channel_id=1, source_target_pairs={{0,8},{1,9},{2,10},{3,11},{4,12},{5,13},{6,14},{7,15},{8,0},{9,1},... | collective-permute-start | bytes 393224 | tf_op jit(solution)/shard_map/ppermute | solution.py:19
  4.0 1.7 %shard_map.37 = (f32[96,512]{1,0:T(8,128)}, f32[32,512]{1,0:T(8,128)}) custom-call(f32[64,512]{1,0:T(8,128)} %features_ref.1, f32[16,512]{1,0:T(8,128)} %solves_ref.1, f32[16,512]{1,0:T(8,128)} %probes_ref.1), custom_call_target="tpu_custom_call" | custom-call | tf_op jit(solution)/shard_map/pallas_call | solution.py:156
  5.7 0.0 collective-permute-start.2
  5.7 1.9 %collective-permute-start.8 = (f32[96,512]{1,0:T(8,128)}, f32[96,512]{1,0:T(8,128)S(1)}, u32[]{:S(2)}, u32[]{:S(2)}) collective-permute-start(f32[96,512]{1,0:T(8,128)} %get-tuple-element.17.refs_0_.refs_1_.refs_2_), channel_id=1, source_target_pairs={{0,4},{1,5},{2,6},{3,7},{4,0},{5,1},{6,2},{7,3},{8,12},{9,13},{10,... | collective-permute-start | bytes 589832 | tf_op jit(solution)/shard_map/ppermute | solution.py:19
  7.6 1.5 %collective-permute-start.3 = (f32[96,512]{1,0:T(8,128)}, f32[96,512]{1,0:T(8,128)S(1)}, u32[]{:S(2)}, u32[]{:S(2)}) collective-permute-start(f32[96,512]{1,0:T(8,128)} %get-tuple-element.17.refs_0_.refs_1_.refs_2_), channel_id=1, source_target_pairs={{0,2},{1,3},{2,0},{3,1},{4,6},{5,7},{6,4},{7,5},{8,10},{9,11},{10,... | collective-permute-start | bytes 589832 | tf_op jit(solution)/shard_map/ppermute | solution.py:19
  9.1 0.0 collective-permute-start
  9.1 0.0 copy-start
  9.1 1.0 %copy-done = f32[96,512]{1,0:T(8,128)S(1)} copy-done((f32[96,512]{1,0:T(8,128)S(1)}, f32[96,512]{1,0:T(8,128)}, u32[]{:S(2)}) %copy-start) | copy-done | bytes 196632
  10.1 0.8 %shard_map.38.refs_4_ = f32[64,512]{1,0:T(8,128)S(1)} custom-call(f32[96,512]{1,0:T(8,128)S(1)} %copy-done), custom_call_target="tpu_custom_call" | custom-call | flops 536870912 | bytes 196608 | tf_op jit(solution)/shard_map/pallas_call | solution.py:131
  10.8 2.6 %collective-permute-done.2 = f32[32,512]{1,0:T(8,128)S(1)} collective-permute-done((f32[32,512]{1,0:T(8,128)}, f32[32,512]{1,0:T(8,128)S(1)}, u32[]{:S(2)}, u32[]{:S(2)}) %collective-permute-start.2) | collective-permute-done | bytes 65568 | tf_op jit(solution)/shard_map/ppermute | solution.py:19
  13.5 0.0 collective-permute-done.1
  13.5 1.6 %collective-permute-start.7 = (f32[32,512]{1,0:T(8,128)S(1)}, f32[32,512]{1,0:T(8,128)S(1)}, u32[]{:S(2)}, u32[]{:S(2)}) collective-permute-start(f32[32,512]{1,0:T(8,128)S(1)} %collective-permute-done.2), channel_id=1, source_target_pairs={{0,2},{1,3},{2,0},{3,1},{4,6},{5,7},{6,4},{7,5},{8,10},{9,11},{10,... | collective-permute-start | bytes 196616 | tf_op jit(solution)/shard_map/ppermute | solution.py:19
  15.0 0.5 %collective-permute-start.6 = (f32[64,512]{1,0:T(8,128)S(1)}, f32[64,512]{1,0:T(8,128)S(1)}, u32[]{:S(2)}, u32[]{:S(2)}) collective-permute-start(f32[64,512]{1,0:T(8,128)S(1)} %collective-permute-done.1), channel_id=1, source_target_pairs={{0,2},{1,3},{2,0},{3,1},{4,6},{5,7},{6,4},{7,5},{8,10},{9,11},{10,... | collective-permute-start | bytes 393224 | tf_op jit(solution)/shard_map/ppermute | solution.py:19
  15.5 0.0 collective-permute-done.8.refs_0_
  15.5 0.1 collective-permute-start.4
  15.6 0.0 collective-permute-done.3.refs_4_.refs_3_
  15.6 0.5 %collective-permute-start.5 = (f32[96,512]{1,0:T(8,128)S(1)}, f32[96,512]{1,0:T(8,128)S(1)}, u32[]{:S(2)}, u32[]{:S(2)}) collective-permute-start(f32[96,512]{1,0:T(8,128)S(1)} %collective-permute-done.3.refs_4_.refs_3_), channel_id=1, source_target_pairs={{0,1},{1,0},{2,3},{3,2},{4,5},{5,4},{6,7},{7,6},{8,9},{9,8},{10,11... | collective-permute-start | bytes 589832 | tf_op jit(solution)/shard_map/ppermute | solution.py:19
  16.1 0.0 collective-permute-done.refs_2_.refs_1_
  16.1 2.0 %shard_map.39.refs_3_ = f32[64,512]{1,0:T(8,128)S(1)} custom-call(f32[96,512]{1,0:T(8,128)S(1)} %collective-permute-done.8.refs_0_, f32[96,512]{1,0:T(8,128)S(1)} %copy-done, f32[96,512]{1,0:T(8,128)S(1)} %collective-permute-done.refs_2_.refs_1_, f32[96,512]{1,0:T(8,128)S(1)} %constant_dynamic-update-slice_fusion.refs_3_.refs_2_, ...), custom_call_target="tpu_custom_call" | custom-call | flops 2147483648 | bytes 983040 | tf_op jit(solution)/shard_map/pallas_call | solution.py:131
  18.2 0.0 collective-permute-done.4.refs_1_.refs_4_
  18.2 0.0 collective-permute-done.5.refs_2_.refs_5_
  18.2 1.1 %shard_map.40.refs_3_ = f32[64,512]{1,0:T(8,128)S(1)} custom-call(f32[96,512]{1,0:T(8,128)S(1)} %collective-permute-done.8.refs_0_, f32[96,512]{1,0:T(8,128)S(1)} %collective-permute-done.4.refs_1_.refs_4_, f32[96,512]{1,0:T(8,128)S(1)} %collective-permute-done.5.refs_2_.refs_5_, f32[64,512]{1,0:T(8,128)S(1)} %shard_map.39.refs_3_), custom_call_target="tpu_custom_call" | custom-call | flops 536870912 | bytes 786432 | tf_op jit(solution)/shard_map/pallas_call | solution.py:131
  19.3 0.0 collective-permute-done.7
  19.3 0.7 %collective-permute-done.6 = f32[64,512]{1,0:T(8,128)S(1)} collective-permute-done((f32[64,512]{1,0:T(8,128)S(1)}, f32[64,512]{1,0:T(8,128)S(1)}, u32[]{:S(2)}, u32[]{:S(2)}) %collective-permute-start.6) | collective-permute-done | bytes 131104 | tf_op jit(solution)/shard_map/ppermute | solution.py:19
  20.0 0.1 collective-permute-start.9
  20.1 1.3 %shard_map.41 = (f32[64,512]{1,0:T(8,128)S(1)}, f32[64,512]{1,0:T(8,128)S(1)}) custom-call(f32[96,512]{1,0:T(8,128)S(1)} %collective-permute-done.8.refs_0_, f32[96,512]{1,0:T(8,128)S(1)} %constant_dynamic-update-slice_fusion.2.refs_1_, f32[96,512]{1,0:T(8,128)S(1)} %copy-done, f32[64,512]{1,0:T(8,128)S(1)} %shard_map.40.refs_3_, ...), custom_call_target="tpu_custom_call" | custom-call | flops 67108864 | bytes 983040 | tf_op jit(solution)/shard_map/pallas_call | solution.py:131
  21.4 0.1 collective-permute-done.9.refs_6_.refs_1_
  21.5 0.8 %shard_map.43 = (f32[32,512]{1,0:T(8,128)S(1)}, f32[32,512]{1,0:T(8,128)S(1)}) custom-call(f32[96,512]{1,0:T(8,128)S(1)} %collective-permute-done.8.refs_0_, f32[96,512]{1,0:T(8,128)S(1)} %collective-permute-done.9.refs_6_.refs_1_, f32[64,512]{1,0:T(8,128)S(1)} %get-tuple-element.26.refs_2_), custom_call_target="tpu_custom_call" | custom-call | flops 33554432 | bytes 589824 | tf_op jit(solution)/shard_map/pallas_call | solution.py:131
  22.3 1.4 %collective-permute-start.10 = (f32[32,512]{1,0:T(8,128)S(1)}, f32[32,512]{1,0:T(8,128)S(1)}, u32[]{:S(2)}, u32[]{:S(2)}) collective-permute-start(f32[32,512]{1,0:T(8,128)S(1)} %get-tuple-element.27), channel_id=1, source_target_pairs={{0,4},{1,5},{2,6},{3,7},{4,0},{5,1},{6,2},{7,3},{8,12},{9,13},{10,... | collective-permute-start | bytes 196616 | tf_op jit(solution)/shard_map/ppermute | solution.py:19
  23.7 0.7 %collective-permute-start.11 = (f32[32,512]{1,0:T(8,128)S(1)}, f32[32,512]{1,0:T(8,128)S(1)}, u32[]{:S(2)}, u32[]{:S(2)}) collective-permute-start(f32[32,512]{1,0:T(8,128)S(1)} %get-tuple-element.28), channel_id=1, source_target_pairs={{0,4},{1,5},{2,6},{3,7},{4,0},{5,1},{6,2},{7,3},{8,12},{9,13},{10,... | collective-permute-start | bytes 196616 | tf_op jit(solution)/shard_map/ppermute | solution.py:19
  24.4 3.0 %shard_map.42 = f32[64,512]{1,0:T(8,128)S(1)} custom-call(f32[96,512]{1,0:T(8,128)S(1)} %copy-done, f32[96,512]{1,0:T(8,128)S(1)} %collective-permute-done.refs_2_.refs_1_, f32[96,512]{1,0:T(8,128)S(1)} %constant_dynamic-update-slice_fusion.refs_3_.refs_2_, f32[96,512]{1,0:T(8,128)S(1)} %collective-permute-done.3.refs_4_.refs_3_, ...), custom_call_target="tpu_custom_call" | custom-call | flops 6442450944 | bytes 1572864 | tf_op jit(solution)/shard_map/pallas_call | solution.py:131
  27.4 0.0 collective-permute-done.10
  27.5 0.8 %collective-permute-done.11 = f32[32,512]{1,0:T(8,128)S(1)} collective-permute-done((f32[32,512]{1,0:T(8,128)S(1)}, f32[32,512]{1,0:T(8,128)S(1)}, u32[]{:S(2)}, u32[]{:S(2)}) %collective-permute-start.11) | collective-permute-done | bytes 65568 | tf_op jit(solution)/shard_map/ppermute | solution.py:19
  28.2 0.7 %maximum_add_fusion = f32[64,512]{1,0:T(8,128)} fusion(f32[64,512]{1,0:T(8,128)S(1)} %shard_map.42, f32[32,512]{1,0:T(8,128)S(1)} %collective-permute-done.11, f32[32,512]{1,0:T(8,128)S(1)} %collective-permute-done.10), kind=kLoop, calls=%fused_computation | loop fusion | flops 65536 | bytes 393216 | tf_op jit(solution)/shard_map/add | solution.py:202
  (4 shorter events, 0.0 us)
Async XLA Ops:
  0.0 13.5 %collective-permute-start.1 = (f32[64,512]{1,0:T(8,128)}, f32[64,512]{1,0:T(8,128)S(1)}, u32[]{:S(2)}, u32[]{:S(2)}) collective-permute-start(f32[64,512]{1,0:T(8,128)} %features_ref.1), channel_id=1, source_target_pairs={{0,8},{1,9},{2,10},{3,11},{4,12},{5,13},{6,14},{7,15},{8,0},{9,1},... | collective-permute-start | bytes 393224 | tf_op jit(solution)/shard_map/ppermute | solution.py:19
  5.7 7.8 %collective-permute-start.2 = (f32[32,512]{1,0:T(8,128)}, f32[32,512]{1,0:T(8,128)S(1)}, u32[]{:S(2)}, u32[]{:S(2)}) collective-permute-start(f32[32,512]{1,0:T(8,128)} %get-tuple-element.18), channel_id=1, source_target_pairs={{0,8},{1,9},{2,10},{3,11},{4,12},{5,13},{6,14},{7,15},{8,0},{9,1},... | collective-permute-start | bytes 196616 | tf_op jit(solution)/shard_map/ppermute | solution.py:19
  5.7 9.8 %collective-permute-start.8 = (f32[96,512]{1,0:T(8,128)}, f32[96,512]{1,0:T(8,128)S(1)}, u32[]{:S(2)}, u32[]{:S(2)}) collective-permute-start(f32[96,512]{1,0:T(8,128)} %get-tuple-element.17.refs_0_.refs_1_.refs_2_), channel_id=1, source_target_pairs={{0,4},{1,5},{2,6},{3,7},{4,0},{5,1},{6,2},{7,3},{8,12},{9,13},{10,... | collective-permute-start | bytes 589832 | tf_op jit(solution)/shard_map/ppermute | solution.py:19
  7.6 8.0 %collective-permute-start.3 = (f32[96,512]{1,0:T(8,128)}, f32[96,512]{1,0:T(8,128)S(1)}, u32[]{:S(2)}, u32[]{:S(2)}) collective-permute-start(f32[96,512]{1,0:T(8,128)} %get-tuple-element.17.refs_0_.refs_1_.refs_2_), channel_id=1, source_target_pairs={{0,2},{1,3},{2,0},{3,1},{4,6},{5,7},{6,4},{7,5},{8,10},{9,11},{10,... | collective-permute-start | bytes 589832 | tf_op jit(solution)/shard_map/ppermute | solution.py:19
  9.1 7.0 %collective-permute-start = (f32[96,512]{1,0:T(8,128)}, f32[96,512]{1,0:T(8,128)S(1)}, u32[]{:S(2)}, u32[]{:S(2)}) collective-permute-start(f32[96,512]{1,0:T(8,128)} %get-tuple-element.17.refs_0_.refs_1_.refs_2_), channel_id=1, source_target_pairs={{0,1},{1,0},{2,3},{3,2},{4,5},{5,4},{6,7},{7,6},{8,9},{9,8},{10,11... | collective-permute-start | bytes 589832 | tf_op jit(solution)/shard_map/ppermute | solution.py:19
  9.1 1.0 %copy-start = (f32[96,512]{1,0:T(8,128)S(1)}, f32[96,512]{1,0:T(8,128)}, u32[]{:S(2)}) copy-start(f32[96,512]{1,0:T(8,128)} %get-tuple-element.17.refs_0_.refs_1_.refs_2_) | copy-start | bytes 589828
  13.5 5.8 %collective-permute-start.7 = (f32[32,512]{1,0:T(8,128)S(1)}, f32[32,512]{1,0:T(8,128)S(1)}, u32[]{:S(2)}, u32[]{:S(2)}) collective-permute-start(f32[32,512]{1,0:T(8,128)S(1)} %collective-permute-done.2), channel_id=1, source_target_pairs={{0,2},{1,3},{2,0},{3,1},{4,6},{5,7},{6,4},{7,5},{8,10},{9,11},{10,... | collective-permute-start | bytes 196616 | tf_op jit(solution)/shard_map/ppermute | solution.py:19
  15.0 5.0 %collective-permute-start.6 = (f32[64,512]{1,0:T(8,128)S(1)}, f32[64,512]{1,0:T(8,128)S(1)}, u32[]{:S(2)}, u32[]{:S(2)}) collective-permute-start(f32[64,512]{1,0:T(8,128)S(1)} %collective-permute-done.1), channel_id=1, source_target_pairs={{0,2},{1,3},{2,0},{3,1},{4,6},{5,7},{6,4},{7,5},{8,10},{9,11},{10,... | collective-permute-start | bytes 393224 | tf_op jit(solution)/shard_map/ppermute | solution.py:19
  15.5 2.6 %collective-permute-start.4 = (f32[96,512]{1,0:T(8,128)S(1)}, f32[96,512]{1,0:T(8,128)S(1)}, u32[]{:S(2)}, u32[]{:S(2)}) collective-permute-start(f32[96,512]{1,0:T(8,128)S(1)} %constant_dynamic-update-slice_fusion.refs_3_.refs_2_), channel_id=1, source_target_pairs={{0,1},{1,0},{2,3},{3,2},{4,5},{5,4},{6,7},{7,6},{8,9},{9,8},{10,11... | collective-permute-start | bytes 589832 | tf_op jit(solution)/shard_map/ppermute | solution.py:19
  15.6 2.5 %collective-permute-start.5 = (f32[96,512]{1,0:T(8,128)S(1)}, f32[96,512]{1,0:T(8,128)S(1)}, u32[]{:S(2)}, u32[]{:S(2)}) collective-permute-start(f32[96,512]{1,0:T(8,128)S(1)} %collective-permute-done.3.refs_4_.refs_3_), channel_id=1, source_target_pairs={{0,1},{1,0},{2,3},{3,2},{4,5},{5,4},{6,7},{7,6},{8,9},{9,8},{10,11... | collective-permute-start | bytes 589832 | tf_op jit(solution)/shard_map/ppermute | solution.py:19
  20.0 1.5 %collective-permute-start.9 = (f32[96,512]{1,0:T(8,128)S(1)}, f32[96,512]{1,0:T(8,128)S(1)}, u32[]{:S(2)}, u32[]{:S(2)}) collective-permute-start(f32[96,512]{1,0:T(8,128)S(1)} %constant_dynamic-update-slice_fusion.2.refs_1_), channel_id=1, source_target_pairs={{0,1},{1,0},{2,3},{3,2},{4,5},{5,4},{6,7},{7,6},{8,9},{9,8},{10,11... | collective-permute-start | bytes 589832 | tf_op jit(solution)/shard_map/ppermute | solution.py:19
  22.3 5.1 %collective-permute-start.10 = (f32[32,512]{1,0:T(8,128)S(1)}, f32[32,512]{1,0:T(8,128)S(1)}, u32[]{:S(2)}, u32[]{:S(2)}) collective-permute-start(f32[32,512]{1,0:T(8,128)S(1)} %get-tuple-element.27), channel_id=1, source_target_pairs={{0,4},{1,5},{2,6},{3,7},{4,0},{5,1},{6,2},{7,3},{8,12},{9,13},{10,... | collective-permute-start | bytes 196616 | tf_op jit(solution)/shard_map/ppermute | solution.py:19
  23.7 4.5 %collective-permute-start.11 = (f32[32,512]{1,0:T(8,128)S(1)}, f32[32,512]{1,0:T(8,128)S(1)}, u32[]{:S(2)}, u32[]{:S(2)}) collective-permute-start(f32[32,512]{1,0:T(8,128)S(1)} %get-tuple-element.28), channel_id=1, source_target_pairs={{0,4},{1,5},{2,6},{3,7},{4,0},{5,1},{6,2},{7,3},{8,12},{9,13},{10,... | collective-permute-start | bytes 196616 | tf_op jit(solution)/shard_map/ppermute | solution.py:19

commit v19 on v15

--- a/solution.py
+++ b/solution.py
@@ -86,27 +86,24 @@
     return jnp.concatenate(dist, 0), jnp.concatenate(pair, 0), jnp.concatenate(pull, 1)
 
 
-def kernel(width, vectors, jobs, count, pieces, *refs):
+def kernel(width, vectors, jobs, count, span, *refs):
     blocks, refs = refs[:count], refs[count:]
-    results = len(jobs) * pieces
-    before, out = refs[:-results], refs[-results:]
+    before, out = refs[: -len(jobs)], refs[-len(jobs) :]
     used = sorted({theirs for _, columns in jobs for theirs in columns})
     theirs = {place: prepared_theirs(blocks[place][...], width, vectors) for place in used}
     for place, (row, columns) in enumerate(jobs):
-        mine = prepared_mine(blocks[row][...], width, vectors)
+        block = blocks[row][:, span]
+        mine = prepared_mine(block, width, vectors)
         parts = [
             pulled_terms(mine, stacked([theirs[column] for column in columns[at : at + STACK]]), width)
             for at in range(0, len(columns), STACK)
         ]
         pulled, sums = (sum(part) for part in zip(*parts))
-        value = (pulled - blocks[row][:width] * sums) / width
-        value = value + before[place][...] if place < len(before) else value
-        rows = width // pieces
-        for piece in range(pieces):
-            out[place * pieces + piece][...] = value[piece * rows : (piece + 1) * rows]
-
-
-def pair_terms(jobs, width, vectors, before=(), weight=2048, pieces=1):
+        value = (pulled - block[:width] * sums) / width
+        out[place][...] = value + before[place][:, span] if place < len(before) else value
+
+
+def pair_terms(jobs, width, vectors, before=(), weight=2048, span=None):
     blocks = []
 
     def place(block):
@@ -119,11 +116,11 @@
     placed = [(place(row), [place(column) for column in columns]) for row, columns in jobs]
     points = blocks[0].shape[1]
     operands = blocks + list(before)
-    shape = jax.ShapeDtypeStruct((width // pieces, points), jnp.float32)
-    out_shape = [shape] * (len(jobs) * pieces)
+    first, count = span or (0, points)
+    out_shape = [jax.ShapeDtypeStruct((width, count), jnp.float32)] * len(jobs)
     return list(
         pl.pallas_call(
-            functools.partial(kernel, width, vectors, placed, len(blocks), pieces),
+            functools.partial(kernel, width, vectors, placed, len(blocks), pl.ds(first, count)),
             out_shape=out_shape,
             in_specs=[pl.BlockSpec(memory_space=pltpu.VMEM)] * len(operands),
             out_specs=[pl.BlockSpec(memory_space=pltpu.VMEM)] * len(out_shape),
@@ -189,11 +186,15 @@
     last = [jnp.concatenate(pieces[at : at + 2], 0) for at in range(0, len(pieces), 2)]
     last_siblings = [swap(block, 1) for block in last]
     there, here = terms([(near, last), (mine, last)], before=[there, here], weight=64)
-    toward_near = terms([(near, last_siblings)], before=[there], weight=64, pieces=2)
-    from_near = jnp.concatenate([swap(piece, 4) for piece in toward_near], 0)
-    rest = [sibling] + first + siblings + last_siblings
-    (here,) = terms([(mine, rest)], before=[here], weight=2048)
-    return here + from_near
+    half = mine.shape[1] // 2
+    (first_half,) = terms([(near, last_siblings)], before=[there], weight=64, span=(0, half))
+    last_siblings[0], first_half = tied((last_siblings[0], first_half))
+    (second_half,) = terms([(near, last_siblings)], before=[there], weight=8, span=(half, half))
+    from_near = [swap(piece, 4) for piece in (first_half, second_half)]
+    (here,) = terms([(mine, [sibling] + first)], before=[here], weight=8)
+    from_near[0], here = tied((from_near[0], here))
+    (here,) = terms([(mine, siblings + last_siblings)], before=[here], weight=8)
+    return here + jnp.concatenate(from_near, 1)
 
 
 def solution(mesh):

time: 29 us -> 29.6 us (1.021)
  Pallas kernels: 10.7 us -> 11.3 us
  waiting for transfers between devices: 4.18 us -> 3.62 us
    pallas_call x6 -> x8, Pallas kernels: 9.02 us -> 9.62 us  [pair_terms(): pl.pallas_call(functools.partial(kernel, width, vectors, placed, len(bloc...]
    ppermute x12, waiting for transfers between devices: 4.18 us -> 3.62 us  [swapped(): lax.ppermute(value, axis, [(source, source ^ bit) for source in range(cou...]
    unnamed x4 -> x6, local copies, waits for them, and re-layouts: 0.98 us -> 1.18 us
  transfers between devices with their start and end apart: 12 -> 12, of which waited for: 4 -> 4; matrix products, arithmetic and copies ran while one was open for 0% -> 0% of each run, Pallas kernels for 34% -> 36%
where the time goes in v19:
time: 29.6 us; the launch traced here: 29.2 us
  starting transfers between devices  12.3 us (42%)
  Pallas kernels  11.3 us (38%)
  waiting for transfers between devices  3.62 us (12%)
  local copies, waits for them, and re-layouts  1.19 us (4%)
  other arithmetic  0.67 us (2%)
    ppermute x12, starting transfers between devices, swapped(): lax.ppermute(value, axis, [(source, source ^ bit) for source in range(cou...  12.3 us
    pallas_call x8, Pallas kernels, pair_terms(): pl.pallas_call(functools.partial(kernel, width, vectors, placed, len(bloc...  9.62 us
    ppermute x12, waiting for transfers between devices, swapped(): lax.ppermute(value, axis, [(source, source ^ bit) for source in range(cou...  3.62 us
    pallas_call x1, Pallas kernels, packed(): pl.pallas_call(body, out_shape=[jax.ShapeDtypeStruct((rows, points), jnp....  1.65 us
    unnamed x6, local copies, waits for them, and re-layouts  1.18 us
    add x1, other arithmetic, local(): return here + jnp.concatenate(from_near, 1)  0.67 us
  transfers between devices with their start and end apart: 12, of which 4 were waited for; matrix products, arithmetic and copies ran while one was open for 0% of the time, Pallas kernels for 36%

profile of v19, /device:TPU:0, one launch (start us, length us, event | category | flops | bytes accessed | tf_op | source)
XLA Modules:
  0.0 29.2 jit_solution(9565371355501325946)
XLA Ops:
  0.0 4.0 %collective-permute-start = (f32[64,512]{1,0:T(8,128)}, f32[64,512]{1,0:T(8,128)S(1)}, u32[]{:S(2)}, u32[]{:S(2)}) collective-permute-start(f32[64,512]{1,0:T(8,128)} %features_ref.1), channel_id=1, source_target_pairs={{0,8},{1,9},{2,10},{3,11},{4,12},{5,13},{6,14},{7,15},{8,0},{9,1},... | collective-permute-start | bytes 393224 | tf_op jit(solution)/shard_map/ppermute | solution.py:19
  4.0 1.7 %shard_map.37 = (f32[96,512]{1,0:T(8,128)}, f32[32,512]{1,0:T(8,128)}) custom-call(f32[64,512]{1,0:T(8,128)} %features_ref.1, f32[16,512]{1,0:T(8,128)} %solves_ref.1, f32[16,512]{1,0:T(8,128)} %probes_ref.1), custom_call_target="tpu_custom_call" | custom-call | tf_op jit(solution)/shard_map/pallas_call | solution.py:147
  5.7 0.0 collective-permute-start.1
  5.7 0.0 collective-permute-start.8
  5.7 1.9 %collective-permute-start.7 = (f32[96,512]{1,0:T(8,128)}, f32[96,512]{1,0:T(8,128)S(1)}, u32[]{:S(2)}, u32[]{:S(2)}) collective-permute-start(f32[96,512]{1,0:T(8,128)} %get-tuple-element.19.refs_0_.refs_1_.refs_2_), channel_id=1, source_target_pairs={{0,4},{1,5},{2,6},{3,7},{4,0},{5,1},{6,2},{7,3},{8,12},{9,13},{10,... | collective-permute-start | bytes 589832 | tf_op jit(solution)/shard_map/ppermute | solution.py:19
  7.6 1.5 %collective-permute-start.3 = (f32[96,512]{1,0:T(8,128)}, f32[96,512]{1,0:T(8,128)S(1)}, u32[]{:S(2)}, u32[]{:S(2)}) collective-permute-start(f32[96,512]{1,0:T(8,128)} %get-tuple-element.19.refs_0_.refs_1_.refs_2_), channel_id=1, source_target_pairs={{0,2},{1,3},{2,0},{3,1},{4,6},{5,7},{6,4},{7,5},{8,10},{9,11},{10,... | collective-permute-start | bytes 589832 | tf_op jit(solution)/shard_map/ppermute | solution.py:19
  9.1 0.0 copy-start
  9.1 1.0 %copy-done = f32[96,512]{1,0:T(8,128)S(1)} copy-done((f32[96,512]{1,0:T(8,128)S(1)}, f32[96,512]{1,0:T(8,128)}, u32[]{:S(2)}) %copy-start) | copy-done | bytes 196632
  10.1 0.8 %shard_map.38.refs_4_ = f32[64,512]{1,0:T(8,128)S(1)} custom-call(f32[96,512]{1,0:T(8,128)S(1)} %copy-done), custom_call_target="tpu_custom_call" | custom-call | flops 536870912 | bytes 196608 | tf_op jit(solution)/shard_map/pallas_call | solution.py:122
  10.8 2.6 %collective-permute-done.1 = f32[32,512]{1,0:T(8,128)S(1)} collective-permute-done((f32[32,512]{1,0:T(8,128)}, f32[32,512]{1,0:T(8,128)S(1)}, u32[]{:S(2)}, u32[]{:S(2)}) %collective-permute-start.1) | collective-permute-done | bytes 65568 | tf_op jit(solution)/shard_map/ppermute | solution.py:19
  13.4 0.0 collective-permute-done
  13.4 1.6 %collective-permute-start.6 = (f32[32,512]{1,0:T(8,128)S(1)}, f32[32,512]{1,0:T(8,128)S(1)}, u32[]{:S(2)}, u32[]{:S(2)}) collective-permute-start(f32[32,512]{1,0:T(8,128)S(1)} %collective-permute-done.1), channel_id=1, source_target_pairs={{0,2},{1,3},{2,0},{3,1},{4,6},{5,7},{6,4},{7,5},{8,10},{9,11},{10,... | collective-permute-start | bytes 196616 | tf_op jit(solution)/shard_map/ppermute | solution.py:19
  15.0 0.5 %collective-permute-start.5 = (f32[64,512]{1,0:T(8,128)S(1)}, f32[64,512]{1,0:T(8,128)S(1)}, u32[]{:S(2)}, u32[]{:S(2)}) collective-permute-start(f32[64,512]{1,0:T(8,128)S(1)} %collective-permute-done), channel_id=1, source_target_pairs={{0,2},{1,3},{2,0},{3,1},{4,6},{5,7},{6,4},{7,5},{8,10},{9,11},{10,... | collective-permute-start | bytes 393224 | tf_op jit(solution)/shard_map/ppermute | solution.py:19
  15.5 0.0 collective-permute-done.8.refs_2_.refs_1_
  15.5 0.1 collective-permute-start.2
  15.6 0.0 collective-permute-done.3.refs_4_.refs_3_
  15.6 0.5 %collective-permute-start.4 = (f32[96,512]{1,0:T(8,128)S(1)}, f32[96,512]{1,0:T(8,128)S(1)}, u32[]{:S(2)}, u32[]{:S(2)}) collective-permute-start(f32[96,512]{1,0:T(8,128)S(1)} %collective-permute-done.3.refs_4_.refs_3_), channel_id=1, source_target_pairs={{0,1},{1,0},{2,3},{3,2},{4,5},{5,4},{6,7},{7,6},{8,9},{9,8},{10,11... | collective-permute-start | bytes 589832 | tf_op jit(solution)/shard_map/ppermute | solution.py:19
  16.1 0.1 collective-permute-done.7.refs_0_
  16.2 2.0 %shard_map.39.refs_3_ = f32[64,512]{1,0:T(8,128)S(1)} custom-call(f32[96,512]{1,0:T(8,128)S(1)} %collective-permute-done.7.refs_0_, f32[96,512]{1,0:T(8,128)S(1)} %copy-done, f32[96,512]{1,0:T(8,128)S(1)} %collective-permute-done.8.refs_2_.refs_1_, f32[96,512]{1,0:T(8,128)S(1)} %constant_dynamic-update-slice_fusion.refs_3_.refs_2_, ...), custom_call_target="tpu_custom_call" | custom-call | flops 2147483648 | bytes 983040 | tf_op jit(solution)/shard_map/pallas_call | solution.py:122
  18.2 0.0 collective-permute-done.2.refs_1_
  18.2 0.0 collective-permute-done.4.refs_2_
  18.2 1.1 %shard_map.40.refs_3_ = f32[64,512]{1,0:T(8,128)S(1)} custom-call(f32[96,512]{1,0:T(8,128)S(1)} %collective-permute-done.7.refs_0_, f32[96,512]{1,0:T(8,128)S(1)} %collective-permute-done.2.refs_1_, f32[96,512]{1,0:T(8,128)S(1)} %collective-permute-done.4.refs_2_, f32[64,512]{1,0:T(8,128)S(1)} %shard_map.39.refs_3_), custom_call_target="tpu_custom_call" | custom-call | flops 536870912 | bytes 786432 | tf_op jit(solution)/shard_map/pallas_call | solution.py:122
  19.3 0.0 copy-start.1
  19.4 0.0 collective-permute-done.6
  19.4 0.6 %collective-permute-done.5 = f32[64,512]{1,0:T(8,128)S(1)} collective-permute-done((f32[64,512]{1,0:T(8,128)S(1)}, f32[64,512]{1,0:T(8,128)S(1)}, u32[]{:S(2)}, u32[]{:S(2)}) %collective-permute-start.5) | collective-permute-done | bytes 131104 | tf_op jit(solution)/shard_map/ppermute | solution.py:19
  20.0 0.1 collective-permute-start.9
  20.1 0.2 copy-done.1
  20.3 1.3 %shard_map.41 = (f32[64,512]{1,0:T(8,128)S(1)}, f32[64,512]{1,0:T(8,128)S(1)}) custom-call(f32[96,512]{1,0:T(8,128)S(1)} %collective-permute-done.7.refs_0_, f32[96,512]{1,0:T(8,128)S(1)} %constant_dynamic-update-slice_fusion.2.refs_1_, f32[96,512]{1,0:T(8,128)S(1)} %copy-done.1, f32[64,512]{1,0:T(8,128)S(1)} %shard_map.40.refs_3_, ...), custom_call_target="tpu_custom_call" | custom-call | flops 67108864 | bytes 983040 | tf_op jit(solution)/shard_map/pallas_call | solution.py:122
  21.6 0.0 collective-permute-done.9.refs_1_.refs_3_
  21.6 0.6 %shard_map.42 = f32[64,256]{1,0:T(8,128)S(1)} custom-call(f32[96,512]{1,0:T(8,128)S(1)} %collective-permute-done.7.refs_0_, f32[96,512]{1,0:T(8,128)S(1)} %collective-permute-done.9.refs_1_.refs_3_, f32[64,512]{1,0:T(8,128)S(1)} %get-tuple-element.27.refs_2_), custom_call_target="tpu_custom_call" | custom-call | flops 33554432 | bytes 589824 | tf_op jit(solution)/shard_map/pallas_call | solution.py:122
  22.3 1.3 %collective-permute-start.10 = (f32[64,256]{1,0:T(8,128)S(1)}, f32[64,256]{1,0:T(8,128)S(1)}, u32[]{:S(2)}, u32[]{:S(2)}) collective-permute-start(f32[64,256]{1,0:T(8,128)S(1)} %shard_map.42), channel_id=1, source_target_pairs={{0,4},{1,5},{2,6},{3,7},{4,0},{5,1},{6,2},{7,3},{8,12},{9,13},{10,... | collective-permute-start | bytes 196616 | tf_op jit(solution)/shard_map/ppermute | solution.py:19
  23.6 0.6 %shard_map.45 = f32[64,256]{1,0:T(8,128)S(1)} custom-call(f32[96,512]{1,0:T(8,128)S(1)} %collective-permute-done.7.refs_0_, f32[96,512]{1,0:T(8,128)S(1)} %collective-permute-done.9.refs_1_.refs_3_, f32[64,512]{1,0:T(8,128)S(1)} %get-tuple-element.27.refs_2_), custom_call_target="tpu_custom_call" | custom-call | flops 4194304 | bytes 589824 | tf_op jit(solution)/shard_map/pallas_call | solution.py:122
  24.2 0.9 %collective-permute-start.11 = (f32[64,256]{1,0:T(8,128)S(1)}, f32[64,256]{1,0:T(8,128)S(1)}, u32[]{:S(2)}, u32[]{:S(2)}) collective-permute-start(f32[64,256]{1,0:T(8,128)S(1)} %shard_map.45), channel_id=1, source_target_pairs={{0,4},{1,5},{2,6},{3,7},{4,0},{5,1},{6,2},{7,3},{8,12},{9,13},{10,... | collective-permute-start | bytes 196616 | tf_op jit(solution)/shard_map/ppermute | solution.py:19
  25.1 1.6 %shard_map.43.refs_4_ = f32[64,512]{1,0:T(8,128)S(1)} custom-call(f32[96,512]{1,0:T(8,128)S(1)} %copy-done.1, f32[96,512]{1,0:T(8,128)S(1)} %collective-permute-done.8.refs_2_.refs_1_, f32[96,512]{1,0:T(8,128)S(1)} %constant_dynamic-update-slice_fusion.refs_3_.refs_2_, f32[96,512]{1,0:T(8,128)S(1)} %collective-permute-done.3.refs_4_.refs_3_, ...), custom_call_target="tpu_custom_call" | custom-call | flops 12582912 | bytes 983040 | tf_op jit(solution)/shard_map/pallas_call | solution.py:122
  26.6 0.0 collective-permute-done.10
  26.7 1.6 %shard_map.44 = f32[64,512]{1,0:T(8,128)S(1)} custom-call(f32[96,512]{1,0:T(8,128)S(1)} %copy-done.1, f32[96,512]{1,0:T(8,128)S(1)} %collective-permute-done.2.refs_1_, f32[96,512]{1,0:T(8,128)S(1)} %collective-permute-done.4.refs_2_, f32[96,512]{1,0:T(8,128)S(1)} %collective-permute-done.9.refs_1_.refs_3_, f32[64,512]{1,0:T(8,128)S(1)} %shard_map.43.refs_4_), custom_call_target="tpu_custom_call" | custom-call | flops 12582912 | bytes 983040 | tf_op jit(solution)/shard_map/pallas_call | solution.py:122
  28.2 0.3 %collective-permute-done.11 = f32[64,256]{1,0:T(8,128)S(1)} collective-permute-done((f32[64,256]{1,0:T(8,128)S(1)}, f32[64,256]{1,0:T(8,128)S(1)}, u32[]{:S(2)}, u32[]{:S(2)}) %collective-permute-start.11) | collective-permute-done | bytes 65568 | tf_op jit(solution)/shard_map/ppermute | solution.py:19
  28.6 0.7 %maximum_add_fusion = f32[64,512]{1,0:T(8,128)} fusion(f32[64,512]{1,0:T(8,128)S(1)} %shard_map.44, f32[64,256]{1,0:T(8,128)S(1)} %collective-permute-done.11, f32[64,256]{1,0:T(8,128)S(1)} %collective-permute-done.10), kind=kLoop, calls=%fused_computation | loop fusion | flops 65536 | bytes 393216 | tf_op jit(solution)/shard_map/add | solution.py:197
  (4 shorter events, 0.0 us)
Async XLA Ops:
  0.0 13.4 %collective-permute-start = (f32[64,512]{1,0:T(8,128)}, f32[64,512]{1,0:T(8,128)S(1)}, u32[]{:S(2)}, u32[]{:S(2)}) collective-permute-start(f32[64,512]{1,0:T(8,128)} %features_ref.1), channel_id=1, source_target_pairs={{0,8},{1,9},{2,10},{3,11},{4,12},{5,13},{6,14},{7,15},{8,0},{9,1},... | collective-permute-start | bytes 393224 | tf_op jit(solution)/shard_map/ppermute | solution.py:19
  5.7 7.7 %collective-permute-start.1 = (f32[32,512]{1,0:T(8,128)}, f32[32,512]{1,0:T(8,128)S(1)}, u32[]{:S(2)}, u32[]{:S(2)}) collective-permute-start(f32[32,512]{1,0:T(8,128)} %get-tuple-element.20), channel_id=1, source_target_pairs={{0,8},{1,9},{2,10},{3,11},{4,12},{5,13},{6,14},{7,15},{8,0},{9,1},... | collective-permute-start | bytes 196616 | tf_op jit(solution)/shard_map/ppermute | solution.py:19
  5.7 9.8 %collective-permute-start.8 = (f32[96,512]{1,0:T(8,128)}, f32[96,512]{1,0:T(8,128)S(1)}, u32[]{:S(2)}, u32[]{:S(2)}) collective-permute-start(f32[96,512]{1,0:T(8,128)} %get-tuple-element.19.refs_0_.refs_1_.refs_2_), channel_id=1, source_target_pairs={{0,1},{1,0},{2,3},{3,2},{4,5},{5,4},{6,7},{7,6},{8,9},{9,8},{10,11... | collective-permute-start | bytes 589832 | tf_op jit(solution)/shard_map/ppermute | solution.py:19
  5.7 10.5 %collective-permute-start.7 = (f32[96,512]{1,0:T(8,128)}, f32[96,512]{1,0:T(8,128)S(1)}, u32[]{:S(2)}, u32[]{:S(2)}) collective-permute-start(f32[96,512]{1,0:T(8,128)} %get-tuple-element.19.refs_0_.refs_1_.refs_2_), channel_id=1, source_target_pairs={{0,4},{1,5},{2,6},{3,7},{4,0},{5,1},{6,2},{7,3},{8,12},{9,13},{10,... | collective-permute-start | bytes 589832 | tf_op jit(solution)/shard_map/ppermute | solution.py:19
  7.6 8.0 %collective-permute-start.3 = (f32[96,512]{1,0:T(8,128)}, f32[96,512]{1,0:T(8,128)S(1)}, u32[]{:S(2)}, u32[]{:S(2)}) collective-permute-start(f32[96,512]{1,0:T(8,128)} %get-tuple-element.19.refs_0_.refs_1_.refs_2_), channel_id=1, source_target_pairs={{0,2},{1,3},{2,0},{3,1},{4,6},{5,7},{6,4},{7,5},{8,10},{9,11},{10,... | collective-permute-start | bytes 589832 | tf_op jit(solution)/shard_map/ppermute | solution.py:19
  9.1 1.0 %copy-start = (f32[96,512]{1,0:T(8,128)S(1)}, f32[96,512]{1,0:T(8,128)}, u32[]{:S(2)}) copy-start(f32[96,512]{1,0:T(8,128)} %get-tuple-element.19.refs_0_.refs_1_.refs_2_) | copy-start | bytes 589828
  13.4 5.9 %collective-permute-start.6 = (f32[32,512]{1,0:T(8,128)S(1)}, f32[32,512]{1,0:T(8,128)S(1)}, u32[]{:S(2)}, u32[]{:S(2)}) collective-permute-start(f32[32,512]{1,0:T(8,128)S(1)} %collective-permute-done.1), channel_id=1, source_target_pairs={{0,2},{1,3},{2,0},{3,1},{4,6},{5,7},{6,4},{7,5},{8,10},{9,11},{10,... | collective-permute-start | bytes 196616 | tf_op jit(solution)/shard_map/ppermute | solution.py:19
  15.0 5.0 %collective-permute-start.5 = (f32[64,512]{1,0:T(8,128)S(1)}, f32[64,512]{1,0:T(8,128)S(1)}, u32[]{:S(2)}, u32[]{:S(2)}) collective-permute-start(f32[64,512]{1,0:T(8,128)S(1)} %collective-permute-done), channel_id=1, source_target_pairs={{0,2},{1,3},{2,0},{3,1},{4,6},{5,7},{6,4},{7,5},{8,10},{9,11},{10,... | collective-permute-start | bytes 393224 | tf_op jit(solution)/shard_map/ppermute | solution.py:19
  15.5 2.7 %collective-permute-start.2 = (f32[96,512]{1,0:T(8,128)S(1)}, f32[96,512]{1,0:T(8,128)S(1)}, u32[]{:S(2)}, u32[]{:S(2)}) collective-permute-start(f32[96,512]{1,0:T(8,128)S(1)} %constant_dynamic-update-slice_fusion.refs_3_.refs_2_), channel_id=1, source_target_pairs={{0,1},{1,0},{2,3},{3,2},{4,5},{5,4},{6,7},{7,6},{8,9},{9,8},{10,11... | collective-permute-start | bytes 589832 | tf_op jit(solution)/shard_map/ppermute | solution.py:19
  15.6 2.6 %collective-permute-start.4 = (f32[96,512]{1,0:T(8,128)S(1)}, f32[96,512]{1,0:T(8,128)S(1)}, u32[]{:S(2)}, u32[]{:S(2)}) collective-permute-start(f32[96,512]{1,0:T(8,128)S(1)} %collective-permute-done.3.refs_4_.refs_3_), channel_id=1, source_target_pairs={{0,1},{1,0},{2,3},{3,2},{4,5},{5,4},{6,7},{7,6},{8,9},{9,8},{10,11... | collective-permute-start | bytes 589832 | tf_op jit(solution)/shard_map/ppermute | solution.py:19
  19.3 0.9 %copy-start.1 = (f32[96,512]{1,0:T(8,128)S(1)}, f32[96,512]{1,0:T(8,128)}, u32[]{:S(2)}) copy-start(f32[96,512]{1,0:T(8,128)} %get-tuple-element.19.refs_0_.refs_1_.refs_2_) | copy-start | bytes 589828
  20.0 1.6 %collective-permute-start.9 = (f32[96,512]{1,0:T(8,128)S(1)}, f32[96,512]{1,0:T(8,128)S(1)}, u32[]{:S(2)}, u32[]{:S(2)}) collective-permute-start(f32[96,512]{1,0:T(8,128)S(1)} %constant_dynamic-update-slice_fusion.2.refs_1_), channel_id=1, source_target_pairs={{0,1},{1,0},{2,3},{3,2},{4,5},{5,4},{6,7},{7,6},{8,9},{9,8},{10,11... | collective-permute-start | bytes 589832 | tf_op jit(solution)/shard_map/ppermute | solution.py:19
  22.3 4.4 %collective-permute-start.10 = (f32[64,256]{1,0:T(8,128)S(1)}, f32[64,256]{1,0:T(8,128)S(1)}, u32[]{:S(2)}, u32[]{:S(2)}) collective-permute-start(f32[64,256]{1,0:T(8,128)S(1)} %shard_map.42), channel_id=1, source_target_pairs={{0,4},{1,5},{2,6},{3,7},{4,0},{5,1},{6,2},{7,3},{8,12},{9,13},{10,... | collective-permute-start | bytes 196616 | tf_op jit(solution)/shard_map/ppermute | solution.py:19
  24.2 4.3 %collective-permute-start.11 = (f32[64,256]{1,0:T(8,128)S(1)}, f32[64,256]{1,0:T(8,128)S(1)}, u32[]{:S(2)}, u32[]{:S(2)}) collective-permute-start(f32[64,256]{1,0:T(8,128)S(1)} %shard_map.45), channel_id=1, source_target_pairs={{0,4},{1,5},{2,6},{3,7},{4,0},{5,1},{6,2},{7,3},{8,12},{9,13},{10,... | collective-permute-start | bytes 196616 | tf_op jit(solution)/shard_map/ppermute | solution.py:19

commit v20 on v19

--- a/solution.py
+++ b/solution.py
@@ -11,7 +11,7 @@
 NORM_ROWS = 16
 ONES_ROWS = 16
 STACK = 4
-VMEM_LIMIT = 24 << 20
+VMEM_LIMIT = 16 << 20
 
 
 def swapped(value, axis, bit):
@@ -185,15 +185,15 @@
     *pieces, there = tied((*[piece for pair in last for piece in pair], there))
     last = [jnp.concatenate(pieces[at : at + 2], 0) for at in range(0, len(pieces), 2)]
     last_siblings = [swap(block, 1) for block in last]
-    there, here = terms([(near, last), (mine, last)], before=[there, here], weight=64)
+    (there,) = terms([(near, last)], before=[there], weight=64)
     half = mine.shape[1] // 2
     (first_half,) = terms([(near, last_siblings)], before=[there], weight=64, span=(0, half))
     last_siblings[0], first_half = tied((last_siblings[0], first_half))
     (second_half,) = terms([(near, last_siblings)], before=[there], weight=8, span=(half, half))
     from_near = [swap(piece, 4) for piece in (first_half, second_half)]
-    (here,) = terms([(mine, [sibling] + first)], before=[here], weight=8)
+    (here,) = terms([(mine, first + siblings[:1])], before=[here], weight=8)
     from_near[0], here = tied((from_near[0], here))
-    (here,) = terms([(mine, siblings + last_siblings)], before=[here], weight=8)
+    (here,) = terms([(mine, [sibling] + siblings[1:] + last + last_siblings)], before=[here], weight=8)
     return here + jnp.concatenate(from_near, 1)
 
 

time: 29.6 us -> 29.5 us (level)
  waiting for transfers between devices: 3.62 us -> 4.01 us
    ppermute x12, waiting for transfers between devices: 3.62 us -> 4.01 us  [swapped(): lax.ppermute(value, axis, [(source, source ^ bit) for source in range(cou...]
  transfers between devices with their start and end apart: 12 -> 12, of which waited for: 4 -> 3; matrix products, arithmetic and copies ran while one was open for 0% -> 0% of each run, Pallas kernels for 36% -> 36%
where the time goes in v20:
time: 29.5 us; the launch traced here: 29.3 us
  starting transfers between devices  12.3 us (42%)
  Pallas kernels  11.2 us (38%)
  waiting for transfers between devices  4.01 us (14%)
  local copies, waits for them, and re-layouts  0.99 us (3%)
  other arithmetic  0.67 us (2%)
    ppermute x12, starting transfers between devices, swapped(): lax.ppermute(value, axis, [(source, source ^ bit) for source in range(cou...  12.3 us
    pallas_call x8, Pallas kernels, pair_terms(): pl.pallas_call(functools.partial(kernel, width, vectors, placed, len(bloc...  9.52 us
    ppermute x12, waiting for transfers between devices, swapped(): lax.ppermute(value, axis, [(source, source ^ bit) for source in range(cou...  4.01 us
    pallas_call x1, Pallas kernels, packed(): pl.pallas_call(body, out_shape=[jax.ShapeDtypeStruct((rows, points), jnp....  1.65 us
    unnamed x6, local copies, waits for them, and re-layouts  0.98 us
    add x1, other arithmetic, local(): return here + jnp.concatenate(from_near, 1)  0.67 us
  transfers between devices with their start and end apart: 12, of which 3 were waited for; matrix products, arithmetic and copies ran while one was open for 0% of the time, Pallas kernels for 36%

profile of v20, /device:TPU:0, one launch (start us, length us, event | category | flops | bytes accessed | tf_op | source)
XLA Modules:
  0.0 29.3 jit_solution(14676950492190236654)
XLA Ops:
  0.0 4.0 %collective-permute-start.3 = (f32[64,512]{1,0:T(8,128)}, f32[64,512]{1,0:T(8,128)S(1)}, u32[]{:S(2)}, u32[]{:S(2)}) collective-permute-start(f32[64,512]{1,0:T(8,128)} %features_ref.1), channel_id=1, source_target_pairs={{0,8},{1,9},{2,10},{3,11},{4,12},{5,13},{6,14},{7,15},{8,0},{9,1},... | collective-permute-start | bytes 393224 | tf_op jit(solution)/shard_map/ppermute | solution.py:19
  4.0 1.7 %shard_map.37 = (f32[96,512]{1,0:T(8,128)}, f32[32,512]{1,0:T(8,128)}) custom-call(f32[64,512]{1,0:T(8,128)} %features_ref.1, f32[16,512]{1,0:T(8,128)} %solves_ref.1, f32[16,512]{1,0:T(8,128)} %probes_ref.1), custom_call_target="tpu_custom_call" | custom-call | tf_op jit(solution)/shard_map/pallas_call | solution.py:147
  5.7 0.0 collective-permute-start.4
  5.7 1.9 %collective-permute-start.7 = (f32[96,512]{1,0:T(8,128)}, f32[96,512]{1,0:T(8,128)S(1)}, u32[]{:S(2)}, u32[]{:S(2)}) collective-permute-start(f32[96,512]{1,0:T(8,128)} %get-tuple-element.17.refs_0_.refs_1_), channel_id=1, source_target_pairs={{0,4},{1,5},{2,6},{3,7},{4,0},{5,1},{6,2},{7,3},{8,12},{9,13},{10,... | collective-permute-start | bytes 589832 | tf_op jit(solution)/shard_map/ppermute | solution.py:19
  7.6 1.5 %collective-permute-start.1 = (f32[96,512]{1,0:T(8,128)}, f32[96,512]{1,0:T(8,128)S(1)}, u32[]{:S(2)}, u32[]{:S(2)}) collective-permute-start(f32[96,512]{1,0:T(8,128)} %get-tuple-element.17.refs_0_.refs_1_), channel_id=1, source_target_pairs={{0,2},{1,3},{2,0},{3,1},{4,6},{5,7},{6,4},{7,5},{8,10},{9,11},{10,... | collective-permute-start | bytes 589832 | tf_op jit(solution)/shard_map/ppermute | solution.py:19
  9.1 0.0 collective-permute-start
  9.1 0.0 copy-start
  9.1 1.0 %copy-done = f32[96,512]{1,0:T(8,128)S(1)} copy-done((f32[96,512]{1,0:T(8,128)S(1)}, f32[96,512]{1,0:T(8,128)}, u32[]{:S(2)}) %copy-start) | copy-done | bytes 196632
  10.1 0.8 %shard_map.38.refs_4_ = f32[64,512]{1,0:T(8,128)S(1)} custom-call(f32[96,512]{1,0:T(8,128)S(1)} %copy-done), custom_call_target="tpu_custom_call" | custom-call | flops 536870912 | bytes 196608 | tf_op jit(solution)/shard_map/pallas_call | solution.py:122
  10.8 2.6 %collective-permute-done.4 = f32[32,512]{1,0:T(8,128)S(1)} collective-permute-done((f32[32,512]{1,0:T(8,128)}, f32[32,512]{1,0:T(8,128)S(1)}, u32[]{:S(2)}, u32[]{:S(2)}) %collective-permute-start.4) | collective-permute-done | bytes 65568 | tf_op jit(solution)/shard_map/ppermute | solution.py:19
  13.5 0.0 collective-permute-done.3
  13.5 1.6 %collective-permute-start.6 = (f32[32,512]{1,0:T(8,128)S(1)}, f32[32,512]{1,0:T(8,128)S(1)}, u32[]{:S(2)}, u32[]{:S(2)}) collective-permute-start(f32[32,512]{1,0:T(8,128)S(1)} %collective-permute-done.4), channel_id=1, source_target_pairs={{0,2},{1,3},{2,0},{3,1},{4,6},{5,7},{6,4},{7,5},{8,10},{9,11},{10,... | collective-permute-start | bytes 196616 | tf_op jit(solution)/shard_map/ppermute | solution.py:19
  15.0 0.5 %collective-permute-start.5 = (f32[64,512]{1,0:T(8,128)S(1)}, f32[64,512]{1,0:T(8,128)S(1)}, u32[]{:S(2)}, u32[]{:S(2)}) collective-permute-start(f32[64,512]{1,0:T(8,128)S(1)} %collective-permute-done.3), channel_id=1, source_target_pairs={{0,2},{1,3},{2,0},{3,1},{4,6},{5,7},{6,4},{7,5},{8,10},{9,11},{10,... | collective-permute-start | bytes 393224 | tf_op jit(solution)/shard_map/ppermute | solution.py:19
  15.5 0.0 collective-permute-done.7.refs_0_
  15.5 0.1 collective-permute-start.8
  15.6 0.0 collective-permute-done.1.refs_4_.refs_2_
  15.6 0.5 %collective-permute-start.2 = (f32[96,512]{1,0:T(8,128)S(1)}, f32[96,512]{1,0:T(8,128)S(1)}, u32[]{:S(2)}, u32[]{:S(2)}) collective-permute-start(f32[96,512]{1,0:T(8,128)S(1)} %collective-permute-done.1.refs_4_.refs_2_), channel_id=1, source_target_pairs={{0,1},{1,0},{2,3},{3,2},{4,5},{5,4},{6,7},{7,6},{8,9},{9,8},{10,11... | collective-permute-start | bytes 589832 | tf_op jit(solution)/shard_map/ppermute | solution.py:19
  16.1 0.0 collective-permute-done.refs_2_.refs_1_
  16.1 2.0 %shard_map.39.refs_3_ = f32[64,512]{1,0:T(8,128)S(1)} custom-call(f32[96,512]{1,0:T(8,128)S(1)} %collective-permute-done.7.refs_0_, f32[96,512]{1,0:T(8,128)S(1)} %copy-done, f32[96,512]{1,0:T(8,128)S(1)} %collective-permute-done.refs_2_.refs_1_, f32[96,512]{1,0:T(8,128)S(1)} %constant_dynamic-update-slice_fusion.refs_3_.refs_1_, ...), custom_call_target="tpu_custom_call" | custom-call | flops 2147483648 | bytes 983040 | tf_op jit(solution)/shard_map/pallas_call | solution.py:122
  18.1 0.0 collective-permute-done.8.refs_1_.refs_3_
  18.1 0.0 collective-permute-done.2.refs_2_
  18.2 1.1 %shard_map.40.refs_2_ = f32[64,512]{1,0:T(8,128)S(1)} custom-call(f32[96,512]{1,0:T(8,128)S(1)} %collective-permute-done.7.refs_0_, f32[96,512]{1,0:T(8,128)S(1)} %collective-permute-done.8.refs_1_.refs_3_, f32[96,512]{1,0:T(8,128)S(1)} %collective-permute-done.2.refs_2_, f32[64,512]{1,0:T(8,128)S(1)} %shard_map.39.refs_3_), custom_call_target="tpu_custom_call" | custom-call | flops 536870912 | bytes 786432 | tf_op jit(solution)/shard_map/pallas_call | solution.py:122
  19.3 0.0 collective-permute-done.6
  19.3 0.7 %collective-permute-done.5 = f32[64,512]{1,0:T(8,128)S(1)} collective-permute-done((f32[64,512]{1,0:T(8,128)S(1)}, f32[64,512]{1,0:T(8,128)S(1)}, u32[]{:S(2)}, u32[]{:S(2)}) %collective-permute-start.5) | collective-permute-done | bytes 131104 | tf_op jit(solution)/shard_map/ppermute | solution.py:19
  20.0 0.1 collective-permute-start.9
  20.1 0.8 %shard_map.41.refs_2_ = f32[64,512]{1,0:T(8,128)S(1)} custom-call(f32[96,512]{1,0:T(8,128)S(1)} %collective-permute-done.7.refs_0_, f32[96,512]{1,0:T(8,128)S(1)} %constant_dynamic-update-slice_fusion.2.refs_1_.refs_3_, f32[64,512]{1,0:T(8,128)S(1)} %shard_map.40.refs_2_), custom_call_target="tpu_custom_call" | custom-call | flops 33554432 | bytes 589824 | tf_op jit(solution)/shard_map/pallas_call | solution.py:122
  20.9 0.7 %collective-permute-done.9.refs_1_.refs_4_ = f32[96,512]{1,0:T(8,128)S(1)} collective-permute-done((f32[96,512]{1,0:T(8,128)S(1)}, f32[96,512]{1,0:T(8,128)S(1)}, u32[]{:S(2)}, u32[]{:S(2)}) %collective-permute-start.9) | collective-permute-done | bytes 196640 | tf_op jit(solution)/shard_map/ppermute | solution.py:19
  21.5 0.6 %shard_map.42 = f32[64,256]{1,0:T(8,128)S(1)} custom-call(f32[96,512]{1,0:T(8,128)S(1)} %collective-permute-done.7.refs_0_, f32[96,512]{1,0:T(8,128)S(1)} %collective-permute-done.9.refs_1_.refs_4_, f32[64,512]{1,0:T(8,128)S(1)} %shard_map.41.refs_2_), custom_call_target="tpu_custom_call" | custom-call | flops 33554432 | bytes 589824 | tf_op jit(solution)/shard_map/pallas_call | solution.py:122
  22.2 0.0 copy-start.1
  22.2 1.4 %collective-permute-start.10 = (f32[64,256]{1,0:T(8,128)S(1)}, f32[64,256]{1,0:T(8,128)S(1)}, u32[]{:S(2)}, u32[]{:S(2)}) collective-permute-start(f32[64,256]{1,0:T(8,128)S(1)} %shard_map.42), channel_id=1, source_target_pairs={{0,4},{1,5},{2,6},{3,7},{4,0},{5,1},{6,2},{7,3},{8,12},{9,13},{10,... | collective-permute-start | bytes 196616 | tf_op jit(solution)/shard_map/ppermute | solution.py:19
  23.6 0.6 %shard_map.45 = f32[64,256]{1,0:T(8,128)S(1)} custom-call(f32[96,512]{1,0:T(8,128)S(1)} %collective-permute-done.7.refs_0_, f32[96,512]{1,0:T(8,128)S(1)} %collective-permute-done.9.refs_1_.refs_4_, f32[64,512]{1,0:T(8,128)S(1)} %shard_map.41.refs_2_), custom_call_target="tpu_custom_call" | custom-call | flops 4194304 | bytes 589824 | tf_op jit(solution)/shard_map/pallas_call | solution.py:122
  24.2 0.8 %collective-permute-start.11 = (f32[64,256]{1,0:T(8,128)S(1)}, f32[64,256]{1,0:T(8,128)S(1)}, u32[]{:S(2)}, u32[]{:S(2)}) collective-permute-start(f32[64,256]{1,0:T(8,128)S(1)} %shard_map.45), channel_id=1, source_target_pairs={{0,4},{1,5},{2,6},{3,7},{4,0},{5,1},{6,2},{7,3},{8,12},{9,13},{10,... | collective-permute-start | bytes 196616 | tf_op jit(solution)/shard_map/ppermute | solution.py:19
  25.0 0.0 copy-done.1
  25.0 1.6 %shard_map.43.refs_5_ = f32[64,512]{1,0:T(8,128)S(1)} custom-call(f32[96,512]{1,0:T(8,128)S(1)} %copy-done.1, f32[96,512]{1,0:T(8,128)S(1)} %constant_dynamic-update-slice_fusion.refs_3_.refs_1_, f32[96,512]{1,0:T(8,128)S(1)} %collective-permute-done.1.refs_4_.refs_2_, f32[96,512]{1,0:T(8,128)S(1)} %collective-permute-done.8.refs_1_.refs_3_, ...), custom_call_target="tpu_custom_call" | custom-call | flops 12582912 | bytes 983040 | tf_op jit(solution)/shard_map/pallas_call | solution.py:122
  26.6 0.0 collective-permute-done.10
  26.6 2.0 %shard_map.44 = f32[64,512]{1,0:T(8,128)S(1)} custom-call(f32[96,512]{1,0:T(8,128)S(1)} %copy-done.1, f32[96,512]{1,0:T(8,128)S(1)} %collective-permute-done.refs_2_.refs_1_, f32[96,512]{1,0:T(8,128)S(1)} %collective-permute-done.2.refs_2_, f32[96,512]{1,0:T(8,128)S(1)} %constant_dynamic-update-slice_fusion.2.refs_1_.refs_3_, ...), custom_call_target="tpu_custom_call" | custom-call | flops 16777216 | bytes 1179648 | tf_op jit(solution)/shard_map/pallas_call | solution.py:122
  28.6 0.0 collective-permute-done.11
  28.6 0.7 %maximum_add_fusion = f32[64,512]{1,0:T(8,128)} fusion(f32[64,512]{1,0:T(8,128)S(1)} %shard_map.44, f32[64,256]{1,0:T(8,128)S(1)} %collective-permute-done.11, f32[64,256]{1,0:T(8,128)S(1)} %collective-permute-done.10), kind=kLoop, calls=%fused_computation | loop fusion | flops 65536 | bytes 393216 | tf_op jit(solution)/shard_map/add | solution.py:197
  (4 shorter events, 0.0 us)
Async XLA Ops:
  0.0 13.5 %collective-permute-start.3 = (f32[64,512]{1,0:T(8,128)}, f32[64,512]{1,0:T(8,128)S(1)}, u32[]{:S(2)}, u32[]{:S(2)}) collective-permute-start(f32[64,512]{1,0:T(8,128)} %features_ref.1), channel_id=1, source_target_pairs={{0,8},{1,9},{2,10},{3,11},{4,12},{5,13},{6,14},{7,15},{8,0},{9,1},... | collective-permute-start | bytes 393224 | tf_op jit(solution)/shard_map/ppermute | solution.py:19
  5.7 7.8 %collective-permute-start.4 = (f32[32,512]{1,0:T(8,128)}, f32[32,512]{1,0:T(8,128)S(1)}, u32[]{:S(2)}, u32[]{:S(2)}) collective-permute-start(f32[32,512]{1,0:T(8,128)} %get-tuple-element.18), channel_id=1, source_target_pairs={{0,8},{1,9},{2,10},{3,11},{4,12},{5,13},{6,14},{7,15},{8,0},{9,1},... | collective-permute-start | bytes 196616 | tf_op jit(solution)/shard_map/ppermute | solution.py:19
  5.7 9.8 %collective-permute-start.7 = (f32[96,512]{1,0:T(8,128)}, f32[96,512]{1,0:T(8,128)S(1)}, u32[]{:S(2)}, u32[]{:S(2)}) collective-permute-start(f32[96,512]{1,0:T(8,128)} %get-tuple-element.17.refs_0_.refs_1_), channel_id=1, source_target_pairs={{0,4},{1,5},{2,6},{3,7},{4,0},{5,1},{6,2},{7,3},{8,12},{9,13},{10,... | collective-permute-start | bytes 589832 | tf_op jit(solution)/shard_map/ppermute | solution.py:19
  7.6 8.0 %collective-permute-start.1 = (f32[96,512]{1,0:T(8,128)}, f32[96,512]{1,0:T(8,128)S(1)}, u32[]{:S(2)}, u32[]{:S(2)}) collective-permute-start(f32[96,512]{1,0:T(8,128)} %get-tuple-element.17.refs_0_.refs_1_), channel_id=1, source_target_pairs={{0,2},{1,3},{2,0},{3,1},{4,6},{5,7},{6,4},{7,5},{8,10},{9,11},{10,... | collective-permute-start | bytes 589832 | tf_op jit(solution)/shard_map/ppermute | solution.py:19
  9.1 7.0 %collective-permute-start = (f32[96,512]{1,0:T(8,128)}, f32[96,512]{1,0:T(8,128)S(1)}, u32[]{:S(2)}, u32[]{:S(2)}) collective-permute-start(f32[96,512]{1,0:T(8,128)} %get-tuple-element.17.refs_0_.refs_1_), channel_id=1, source_target_pairs={{0,1},{1,0},{2,3},{3,2},{4,5},{5,4},{6,7},{7,6},{8,9},{9,8},{10,11... | collective-permute-start | bytes 589832 | tf_op jit(solution)/shard_map/ppermute | solution.py:19
  9.1 1.0 %copy-start = (f32[96,512]{1,0:T(8,128)S(1)}, f32[96,512]{1,0:T(8,128)}, u32[]{:S(2)}) copy-start(f32[96,512]{1,0:T(8,128)} %get-tuple-element.17.refs_0_.refs_1_) | copy-start | bytes 589828
  13.5 5.8 %collective-permute-start.6 = (f32[32,512]{1,0:T(8,128)S(1)}, f32[32,512]{1,0:T(8,128)S(1)}, u32[]{:S(2)}, u32[]{:S(2)}) collective-permute-start(f32[32,512]{1,0:T(8,128)S(1)} %collective-permute-done.4), channel_id=1, source_target_pairs={{0,2},{1,3},{2,0},{3,1},{4,6},{5,7},{6,4},{7,5},{8,10},{9,11},{10,... | collective-permute-start | bytes 196616 | tf_op jit(solution)/shard_map/ppermute | solution.py:19
  15.0 5.0 %collective-permute-start.5 = (f32[64,512]{1,0:T(8,128)S(1)}, f32[64,512]{1,0:T(8,128)S(1)}, u32[]{:S(2)}, u32[]{:S(2)}) collective-permute-start(f32[64,512]{1,0:T(8,128)S(1)} %collective-permute-done.3), channel_id=1, source_target_pairs={{0,2},{1,3},{2,0},{3,1},{4,6},{5,7},{6,4},{7,5},{8,10},{9,11},{10,... | collective-permute-start | bytes 393224 | tf_op jit(solution)/shard_map/ppermute | solution.py:19
  15.5 2.6 %collective-permute-start.8 = (f32[96,512]{1,0:T(8,128)S(1)}, f32[96,512]{1,0:T(8,128)S(1)}, u32[]{:S(2)}, u32[]{:S(2)}) collective-permute-start(f32[96,512]{1,0:T(8,128)S(1)} %constant_dynamic-update-slice_fusion.refs_3_.refs_1_), channel_id=1, source_target_pairs={{0,1},{1,0},{2,3},{3,2},{4,5},{5,4},{6,7},{7,6},{8,9},{9,8},{10,11... | collective-permute-start | bytes 589832 | tf_op jit(solution)/shard_map/ppermute | solution.py:19
  15.6 2.5 %collective-permute-start.2 = (f32[96,512]{1,0:T(8,128)S(1)}, f32[96,512]{1,0:T(8,128)S(1)}, u32[]{:S(2)}, u32[]{:S(2)}) collective-permute-start(f32[96,512]{1,0:T(8,128)S(1)} %collective-permute-done.1.refs_4_.refs_2_), channel_id=1, source_target_pairs={{0,1},{1,0},{2,3},{3,2},{4,5},{5,4},{6,7},{7,6},{8,9},{9,8},{10,11... | collective-permute-start | bytes 589832 | tf_op jit(solution)/shard_map/ppermute | solution.py:19
  20.0 1.5 %collective-permute-start.9 = (f32[96,512]{1,0:T(8,128)S(1)}, f32[96,512]{1,0:T(8,128)S(1)}, u32[]{:S(2)}, u32[]{:S(2)}) collective-permute-start(f32[96,512]{1,0:T(8,128)S(1)} %constant_dynamic-update-slice_fusion.2.refs_1_.refs_3_), channel_id=1, source_target_pairs={{0,1},{1,0},{2,3},{3,2},{4,5},{5,4},{6,7},{7,6},{8,9},{9,8},{10,11... | collective-permute-start | bytes 589832 | tf_op jit(solution)/shard_map/ppermute | solution.py:19
  22.2 2.8 %copy-start.1 = (f32[96,512]{1,0:T(8,128)S(1)}, f32[96,512]{1,0:T(8,128)}, u32[]{:S(2)}) copy-start(f32[96,512]{1,0:T(8,128)} %get-tuple-element.17.refs_0_.refs_1_) | copy-start | bytes 589828
  22.2 4.4 %collective-permute-start.10 = (f32[64,256]{1,0:T(8,128)S(1)}, f32[64,256]{1,0:T(8,128)S(1)}, u32[]{:S(2)}, u32[]{:S(2)}) collective-permute-start(f32[64,256]{1,0:T(8,128)S(1)} %shard_map.42), channel_id=1, source_target_pairs={{0,4},{1,5},{2,6},{3,7},{4,0},{5,1},{6,2},{7,3},{8,12},{9,13},{10,... | collective-permute-start | bytes 196616 | tf_op jit(solution)/shard_map/ppermute | solution.py:19
  24.2 4.4 %collective-permute-start.11 = (f32[64,256]{1,0:T(8,128)S(1)}, f32[64,256]{1,0:T(8,128)S(1)}, u32[]{:S(2)}, u32[]{:S(2)}) collective-permute-start(f32[64,256]{1,0:T(8,128)S(1)} %shard_map.45), channel_id=1, source_target_pairs={{0,4},{1,5},{2,6},{3,7},{4,0},{5,1},{6,2},{7,3},{8,12},{9,13},{10,... | collective-permute-start | bytes 196616 | tf_op jit(solution)/shard_map/ppermute | solution.py:19

commit v21 on v13

--- a/solution.py
+++ b/solution.py
@@ -187,15 +187,15 @@
     first = [far] + direct
     siblings = jnp.split(swap(jnp.concatenate(first, 0), 1), len(first), 0)
     (there,) = terms([(near, [mine, sibling] + first)], weight=2048)
-    (there,) = terms([(near, siblings)], before=[there], weight=100000)
+    (there,) = terms([(near, siblings)], before=[there], weight=64)
     *pieces, there = tied((*[piece for pair in last for piece in pair], there))
     last = [jnp.concatenate(pieces[at : at + 2], 0) for at in range(0, len(pieces), 2)]
     last_siblings = [swap(block, 1) for block in last]
     there, here = terms([(near, last), (mine, last)], before=[there, here], weight=64)
-    toward_near = terms([(near, last_siblings)], before=[there], weight=8, pieces=2)
+    toward_near = terms([(near, last_siblings)], before=[there], weight=64, pieces=2)
     from_near = jnp.concatenate([swap(piece, 4) for piece in toward_near], 0)
     rest = direct + siblings + last_siblings
-    (here,) = terms([(mine, rest)], before=[here], weight=100000)
+    (here,) = terms([(mine, rest)], before=[here], weight=2048)
     return here + from_near
 
 

time: 31 us -> 29.2 us (0.942)
  other arithmetic: 1.57 us -> 0.7 us
  Pallas kernels: 11.5 us -> 10.8 us
    add x1, other arithmetic: 1.54 us -> 0.67 us  [local(): return here + from_near]
    pallas_call x7, Pallas kernels: 9.81 us -> 9.16 us  [pair_terms(): pl.pallas_call(functools.partial(kernel, width, vectors, placed, len(bloc...]
  transfers between devices with their start and end apart: 11 -> 11, of which waited for: 3 -> 3; matrix products, arithmetic and copies ran while one was open for 0% -> 0% of each run, Pallas kernels for 33% -> 35%
where the time goes in v21:
time: 29.2 us; the launch traced here: 29 us
  starting transfers between devices  12.3 us (42%)
  Pallas kernels  10.8 us (37%)
  waiting for transfers between devices  4.07 us (14%)
  local copies, waits for them, and re-layouts  1.02 us (3%)
  other arithmetic  0.7 us (2%)
    ppermute x11, starting transfers between devices, swapped(): lax.ppermute(value, axis, [(source, source ^ bit) for source in range(cou...  12.3 us
    pallas_call x7, Pallas kernels, pair_terms(): pl.pallas_call(functools.partial(kernel, width, vectors, placed, len(bloc...  9.16 us
    ppermute x11, waiting for transfers between devices, swapped(): lax.ppermute(value, axis, [(source, source ^ bit) for source in range(cou...  4.07 us
    pallas_call x1, Pallas kernels, packed(): pl.pallas_call(body, out_shape=[jax.ShapeDtypeStruct((rows, points), jnp....  1.65 us
    unnamed x4, local copies, waits for them, and re-layouts  0.98 us
    add x1, other arithmetic, local(): return here + from_near  0.67 us
  transfers between devices with their start and end apart: 11, of which 3 were waited for; matrix products, arithmetic and copies ran while one was open for 0% of the time, Pallas kernels for 35%

profile of v21, /device:TPU:0, one launch (start us, length us, event | category | flops | bytes accessed | tf_op | source)
XLA Modules:
  0.0 29.0 jit_solution(2057308075982477606)
XLA Ops:
  0.0 4.0 %collective-permute-start.3 = (f32[64,512]{1,0:T(8,128)}, f32[64,512]{1,0:T(8,128)S(1)}, u32[]{:S(2)}, u32[]{:S(2)}) collective-permute-start(f32[64,512]{1,0:T(8,128)} %features_ref.1), channel_id=1, source_target_pairs={{0,8},{1,9},{2,10},{3,11},{4,12},{5,13},{6,14},{7,15},{8,0},{9,1},... | collective-permute-start | bytes 393224 | tf_op jit(solution)/shard_map/ppermute | solution.py:19
  4.0 1.7 %shard_map.37 = (f32[96,512]{1,0:T(8,128)}, f32[32,512]{1,0:T(8,128)}) custom-call(f32[64,512]{1,0:T(8,128)} %features_ref.1, f32[16,512]{1,0:T(8,128)} %solves_ref.1, f32[16,512]{1,0:T(8,128)} %probes_ref.1), custom_call_target="tpu_custom_call" | custom-call | tf_op jit(solution)/shard_map/pallas_call | solution.py:150
  5.7 0.0 collective-permute-start.4
  5.7 0.0 collective-permute-start.2
  5.7 1.9 %collective-permute-start.1 = (f32[96,512]{1,0:T(8,128)}, f32[96,512]{1,0:T(8,128)S(1)}, u32[]{:S(2)}, u32[]{:S(2)}) collective-permute-start(f32[96,512]{1,0:T(8,128)} %get-tuple-element.20.refs_0_.refs_1_.refs_2_), channel_id=1, source_target_pairs={{0,2},{1,3},{2,0},{3,1},{4,6},{5,7},{6,4},{7,5},{8,10},{9,11},{10,... | collective-permute-start | bytes 589832 | tf_op jit(solution)/shard_map/ppermute | solution.py:19
  7.5 1.6 %collective-permute-start = (f32[96,512]{1,0:T(8,128)}, f32[96,512]{1,0:T(8,128)S(1)}, u32[]{:S(2)}, u32[]{:S(2)}) collective-permute-start(f32[96,512]{1,0:T(8,128)} %get-tuple-element.20.refs_0_.refs_1_.refs_2_), channel_id=1, source_target_pairs={{0,4},{1,5},{2,6},{3,7},{4,0},{5,1},{6,2},{7,3},{8,12},{9,13},{10,... | collective-permute-start | bytes 589832 | tf_op jit(solution)/shard_map/ppermute | solution.py:19
  9.1 0.0 copy-start
  9.1 1.0 %copy-done = f32[96,512]{1,0:T(8,128)S(1)} copy-done((f32[96,512]{1,0:T(8,128)S(1)}, f32[96,512]{1,0:T(8,128)}, u32[]{:S(2)}) %copy-start) | copy-done | bytes 196632
  10.1 0.8 %shard_map.38.refs_3_ = f32[64,512]{1,0:T(8,128)S(1)} custom-call(f32[96,512]{1,0:T(8,128)S(1)} %copy-done), custom_call_target="tpu_custom_call" | custom-call | flops 268435456 | bytes 196608 | tf_op jit(solution)/shard_map/pallas_call | solution.py:125
  10.8 2.6 %collective-permute-done.4 = f32[32,512]{1,0:T(8,128)S(1)} collective-permute-done((f32[32,512]{1,0:T(8,128)}, f32[32,512]{1,0:T(8,128)S(1)}, u32[]{:S(2)}, u32[]{:S(2)}) %collective-permute-start.4) | collective-permute-done | bytes 65568 | tf_op jit(solution)/shard_map/ppermute | solution.py:19
  13.5 0.0 collective-permute-done.3
  13.5 1.5 %collective-permute-start.6 = (f32[64,512]{1,0:T(8,128)S(1)}, f32[64,512]{1,0:T(8,128)S(1)}, u32[]{:S(2)}, u32[]{:S(2)}) collective-permute-start(f32[64,512]{1,0:T(8,128)S(1)} %collective-permute-done.3), channel_id=1, source_target_pairs={{0,2},{1,3},{2,0},{3,1},{4,6},{5,7},{6,4},{7,5},{8,10},{9,11},{10,... | collective-permute-start | bytes 393224 | tf_op jit(solution)/shard_map/ppermute | solution.py:19
  15.0 0.6 %collective-permute-start.7 = (f32[32,512]{1,0:T(8,128)S(1)}, f32[32,512]{1,0:T(8,128)S(1)}, u32[]{:S(2)}, u32[]{:S(2)}) collective-permute-start(f32[32,512]{1,0:T(8,128)S(1)} %collective-permute-done.4), channel_id=1, source_target_pairs={{0,2},{1,3},{2,0},{3,1},{4,6},{5,7},{6,4},{7,5},{8,10},{9,11},{10,... | collective-permute-start | bytes 196616 | tf_op jit(solution)/shard_map/ppermute | solution.py:19
  15.6 0.0 collective-permute-done.2.refs_1_.refs_2_
  15.6 1.1 %shard_map.39.refs_4_ = f32[64,512]{1,0:T(8,128)S(1)} custom-call(f32[96,512]{1,0:T(8,128)S(1)} %copy-done, f32[96,512]{1,0:T(8,128)S(1)} %collective-permute-done.2.refs_1_.refs_2_, f32[96,512]{1,0:T(8,128)S(1)} %constant_dynamic-update-slice_fusion.refs_2_.refs_3_, f32[64,512]{1,0:T(8,128)S(1)} %shard_map.38.refs_3_), custom_call_target="tpu_custom_call" | custom-call | flops 268435456 | bytes 786432 | tf_op jit(solution)/shard_map/pallas_call | solution.py:125
  16.7 0.0 collective-permute-done.1.refs_4_.refs_1_
  16.7 0.0 collective-permute-done.refs_0_
  16.8 0.1 collective-permute-start.5
  16.9 2.0 %shard_map.40.refs_3_ = f32[64,512]{1,0:T(8,128)S(1)} custom-call(f32[96,512]{1,0:T(8,128)S(1)} %collective-permute-done.refs_0_, f32[96,512]{1,0:T(8,128)S(1)} %copy-done, f32[96,512]{1,0:T(8,128)S(1)} %collective-permute-done.2.refs_1_.refs_2_, f32[96,512]{1,0:T(8,128)S(1)} %constant_dynamic-update-slice_fusion.refs_2_.refs_3_, ...), custom_call_target="tpu_custom_call" | custom-call | flops 4294967296 | bytes 983040 | tf_op jit(solution)/shard_map/pallas_call | solution.py:125
  18.9 0.0 collective-permute-done.5
  19.0 1.1 %shard_map.41.refs_3_ = f32[64,512]{1,0:T(8,128)S(1)} custom-call(f32[96,512]{1,0:T(8,128)S(1)} %collective-permute-done.refs_0_, f32[96,512]{1,0:T(8,128)S(1)} %get-tuple-element.36.refs_1_.refs_2_, f32[96,512]{1,0:T(8,128)S(1)} %get-tuple-element.35.refs_2_.refs_3_, f32[64,512]{1,0:T(8,128)S(1)} %shard_map.40.refs_3_), custom_call_target="tpu_custom_call" | custom-call | flops 67108864 | bytes 786432 | tf_op jit(solution)/shard_map/pallas_call | solution.py:125
  20.1 0.0 collective-permute-done.7
  20.1 0.0 collective-permute-done.6
  20.1 0.6 %collective-permute-start.8 = (f32[96,512]{1,0:T(8,128)S(1)}, f32[96,512]{1,0:T(8,128)S(1)}, u32[]{:S(2)}, u32[]{:S(2)}) collective-permute-start(f32[96,512]{1,0:T(8,128)S(1)} %constant_dynamic-update-slice_fusion.2.refs_1_), channel_id=1, source_target_pairs={{0,1},{1,0},{2,3},{3,2},{4,5},{5,4},{6,7},{7,6},{8,9},{9,8},{10,11... | collective-permute-start | bytes 589832 | tf_op jit(solution)/shard_map/ppermute | solution.py:19
  20.7 1.3 %shard_map.42 = (f32[64,512]{1,0:T(8,128)S(1)}, f32[64,512]{1,0:T(8,128)S(1)}) custom-call(f32[96,512]{1,0:T(8,128)S(1)} %collective-permute-done.refs_0_, f32[96,512]{1,0:T(8,128)S(1)} %constant_dynamic-update-slice_fusion.2.refs_1_, f32[96,512]{1,0:T(8,128)S(1)} %copy-done, f32[64,512]{1,0:T(8,128)S(1)} %shard_map.41.refs_3_, f32[64,512]{1,0:T(8,128)S(1)} %shard_map.39.refs_4_), custom_call_target="tpu_custom_call" | custom-call | flops 67108864 | bytes 983040 | tf_op jit(solution)/shard_map/pallas_call | solution.py:125
  22.0 0.0 collective-permute-done.8.refs_4_.refs_1_
  22.0 0.8 %shard_map.44 = (f32[32,512]{1,0:T(8,128)S(1)}, f32[32,512]{1,0:T(8,128)S(1)}) custom-call(f32[96,512]{1,0:T(8,128)S(1)} %collective-permute-done.refs_0_, f32[96,512]{1,0:T(8,128)S(1)} %collective-permute-done.8.refs_4_.refs_1_, f32[64,512]{1,0:T(8,128)S(1)} %get-tuple-element.32.refs_2_), custom_call_target="tpu_custom_call" | custom-call | flops 33554432 | bytes 589824 | tf_op jit(solution)/shard_map/pallas_call | solution.py:125
  22.8 0.8 %collective-permute-start.9 = (f32[32,512]{1,0:T(8,128)S(1)}, f32[32,512]{1,0:T(8,128)S(1)}, u32[]{:S(2)}, u32[]{:S(2)}) collective-permute-start(f32[32,512]{1,0:T(8,128)S(1)} %get-tuple-element.33), channel_id=1, source_target_pairs={{0,4},{1,5},{2,6},{3,7},{4,0},{5,1},{6,2},{7,3},{8,12},{9,13},{10,... | collective-permute-start | bytes 196616 | tf_op jit(solution)/shard_map/ppermute | solution.py:19
  23.6 1.3 %collective-permute-start.10 = (f32[32,512]{1,0:T(8,128)S(1)}, f32[32,512]{1,0:T(8,128)S(1)}, u32[]{:S(2)}, u32[]{:S(2)}) collective-permute-start(f32[32,512]{1,0:T(8,128)S(1)} %get-tuple-element.34), channel_id=1, source_target_pairs={{0,4},{1,5},{2,6},{3,7},{4,0},{5,1},{6,2},{7,3},{8,12},{9,13},{10,... | collective-permute-start | bytes 196616 | tf_op jit(solution)/shard_map/ppermute | solution.py:19
  24.9 2.0 %shard_map.43 = f32[64,512]{1,0:T(8,128)S(1)} custom-call(f32[96,512]{1,0:T(8,128)S(1)} %copy-done, f32[96,512]{1,0:T(8,128)S(1)} %collective-permute-done.1.refs_4_.refs_1_, f32[96,512]{1,0:T(8,128)S(1)} %get-tuple-element.36.refs_1_.refs_2_, f32[96,512]{1,0:T(8,128)S(1)} %get-tuple-element.35.refs_2_.refs_3_, ...), custom_call_target="tpu_custom_call" | custom-call | flops 4294967296 | bytes 1179648 | tf_op jit(solution)/shard_map/pallas_call | solution.py:125
  26.9 0.7 %collective-permute-done.9 = f32[32,512]{1,0:T(8,128)S(1)} collective-permute-done((f32[32,512]{1,0:T(8,128)S(1)}, f32[32,512]{1,0:T(8,128)S(1)}, u32[]{:S(2)}, u32[]{:S(2)}) %collective-permute-start.9) | collective-permute-done | bytes 65568 | tf_op jit(solution)/shard_map/ppermute | solution.py:19
  27.7 0.7 %collective-permute-done.10 = f32[32,512]{1,0:T(8,128)S(1)} collective-permute-done((f32[32,512]{1,0:T(8,128)S(1)}, f32[32,512]{1,0:T(8,128)S(1)}, u32[]{:S(2)}, u32[]{:S(2)}) %collective-permute-start.10) | collective-permute-done | bytes 65568 | tf_op jit(solution)/shard_map/ppermute | solution.py:19
  28.4 0.7 %maximum_add_fusion = f32[64,512]{1,0:T(8,128)} fusion(f32[64,512]{1,0:T(8,128)S(1)} %shard_map.43, f32[32,512]{1,0:T(8,128)S(1)} %collective-permute-done.10, f32[32,512]{1,0:T(8,128)S(1)} %collective-permute-done.9), kind=kLoop, calls=%fused_computation.1 | loop fusion | flops 65536 | bytes 393216 | tf_op jit(solution)/shard_map/add | solution.py:199
  (6 shorter events, 0.1 us)
Async XLA Ops:
  0.0 13.5 %collective-permute-start.3 = (f32[64,512]{1,0:T(8,128)}, f32[64,512]{1,0:T(8,128)S(1)}, u32[]{:S(2)}, u32[]{:S(2)}) collective-permute-start(f32[64,512]{1,0:T(8,128)} %features_ref.1), channel_id=1, source_target_pairs={{0,8},{1,9},{2,10},{3,11},{4,12},{5,13},{6,14},{7,15},{8,0},{9,1},... | collective-permute-start | bytes 393224 | tf_op jit(solution)/shard_map/ppermute | solution.py:19
  5.7 7.8 %collective-permute-start.4 = (f32[32,512]{1,0:T(8,128)}, f32[32,512]{1,0:T(8,128)S(1)}, u32[]{:S(2)}, u32[]{:S(2)}) collective-permute-start(f32[32,512]{1,0:T(8,128)} %get-tuple-element.21), channel_id=1, source_target_pairs={{0,8},{1,9},{2,10},{3,11},{4,12},{5,13},{6,14},{7,15},{8,0},{9,1},... | collective-permute-start | bytes 196616 | tf_op jit(solution)/shard_map/ppermute | solution.py:19
  5.7 9.9 %collective-permute-start.2 = (f32[96,512]{1,0:T(8,128)}, f32[96,512]{1,0:T(8,128)S(1)}, u32[]{:S(2)}, u32[]{:S(2)}) collective-permute-start(f32[96,512]{1,0:T(8,128)} %get-tuple-element.20.refs_0_.refs_1_.refs_2_), channel_id=1, source_target_pairs={{0,1},{1,0},{2,3},{3,2},{4,5},{5,4},{6,7},{7,6},{8,9},{9,8},{10,11... | collective-permute-start | bytes 589832 | tf_op jit(solution)/shard_map/ppermute | solution.py:19
  5.7 11.0 %collective-permute-start.1 = (f32[96,512]{1,0:T(8,128)}, f32[96,512]{1,0:T(8,128)S(1)}, u32[]{:S(2)}, u32[]{:S(2)}) collective-permute-start(f32[96,512]{1,0:T(8,128)} %get-tuple-element.20.refs_0_.refs_1_.refs_2_), channel_id=1, source_target_pairs={{0,2},{1,3},{2,0},{3,1},{4,6},{5,7},{6,4},{7,5},{8,10},{9,11},{10,... | collective-permute-start | bytes 589832 | tf_op jit(solution)/shard_map/ppermute | solution.py:19
  7.5 9.2 %collective-permute-start = (f32[96,512]{1,0:T(8,128)}, f32[96,512]{1,0:T(8,128)S(1)}, u32[]{:S(2)}, u32[]{:S(2)}) collective-permute-start(f32[96,512]{1,0:T(8,128)} %get-tuple-element.20.refs_0_.refs_1_.refs_2_), channel_id=1, source_target_pairs={{0,4},{1,5},{2,6},{3,7},{4,0},{5,1},{6,2},{7,3},{8,12},{9,13},{10,... | collective-permute-start | bytes 589832 | tf_op jit(solution)/shard_map/ppermute | solution.py:19
  9.1 1.0 %copy-start = (f32[96,512]{1,0:T(8,128)S(1)}, f32[96,512]{1,0:T(8,128)}, u32[]{:S(2)}) copy-start(f32[96,512]{1,0:T(8,128)} %get-tuple-element.20.refs_0_.refs_1_.refs_2_) | copy-start | bytes 589828
  13.5 6.6 %collective-permute-start.6 = (f32[64,512]{1,0:T(8,128)S(1)}, f32[64,512]{1,0:T(8,128)S(1)}, u32[]{:S(2)}, u32[]{:S(2)}) collective-permute-start(f32[64,512]{1,0:T(8,128)S(1)} %collective-permute-done.3), channel_id=1, source_target_pairs={{0,2},{1,3},{2,0},{3,1},{4,6},{5,7},{6,4},{7,5},{8,10},{9,11},{10,... | collective-permute-start | bytes 393224 | tf_op jit(solution)/shard_map/ppermute | solution.py:19
  15.0 5.1 %collective-permute-start.7 = (f32[32,512]{1,0:T(8,128)S(1)}, f32[32,512]{1,0:T(8,128)S(1)}, u32[]{:S(2)}, u32[]{:S(2)}) collective-permute-start(f32[32,512]{1,0:T(8,128)S(1)} %collective-permute-done.4), channel_id=1, source_target_pairs={{0,2},{1,3},{2,0},{3,1},{4,6},{5,7},{6,4},{7,5},{8,10},{9,11},{10,... | collective-permute-start | bytes 196616 | tf_op jit(solution)/shard_map/ppermute | solution.py:19
  16.8 2.1 %collective-permute-start.5 = (f32[192,512]{1,0:T(8,128)S(1)}, f32[192,512]{1,0:T(8,128)S(1)}, u32[]{:S(2)}, u32[]{:S(2)}) collective-permute-start(f32[192,512]{1,0:T(8,128)S(1)} %pad_maximum_fusion), channel_id=1, source_target_pairs={{0,1},{1,0},{2,3},{3,2},{4,5},{5,4},{6,7},{7,6},{8,9},{9,8},{10,11... | collective-permute-start | bytes 1179656 | tf_op jit(solution)/shard_map/ppermute | solution.py:19
  20.1 1.9 %collective-permute-start.8 = (f32[96,512]{1,0:T(8,128)S(1)}, f32[96,512]{1,0:T(8,128)S(1)}, u32[]{:S(2)}, u32[]{:S(2)}) collective-permute-start(f32[96,512]{1,0:T(8,128)S(1)} %constant_dynamic-update-slice_fusion.2.refs_1_), channel_id=1, source_target_pairs={{0,1},{1,0},{2,3},{3,2},{4,5},{5,4},{6,7},{7,6},{8,9},{9,8},{10,11... | collective-permute-start | bytes 589832 | tf_op jit(solution)/shard_map/ppermute | solution.py:19
  22.8 4.9 %collective-permute-start.9 = (f32[32,512]{1,0:T(8,128)S(1)}, f32[32,512]{1,0:T(8,128)S(1)}, u32[]{:S(2)}, u32[]{:S(2)}) collective-permute-start(f32[32,512]{1,0:T(8,128)S(1)} %get-tuple-element.33), channel_id=1, source_target_pairs={{0,4},{1,5},{2,6},{3,7},{4,0},{5,1},{6,2},{7,3},{8,12},{9,13},{10,... | collective-permute-start | bytes 196616 | tf_op jit(solution)/shard_map/ppermute | solution.py:19
  23.6 4.7 %collective-permute-start.10 = (f32[32,512]{1,0:T(8,128)S(1)}, f32[32,512]{1,0:T(8,128)S(1)}, u32[]{:S(2)}, u32[]{:S(2)}) collective-permute-start(f32[32,512]{1,0:T(8,128)S(1)} %get-tuple-element.34), channel_id=1, source_target_pairs={{0,4},{1,5},{2,6},{3,7},{4,0},{5,1},{6,2},{7,3},{8,12},{9,13},{10,... | collective-permute-start | bytes 196616 | tf_op jit(solution)/shard_map/ppermute | solution.py:19

commit v22 on v21

--- a/solution.py
+++ b/solution.py
@@ -174,7 +174,7 @@
     near = swap(mine, 4)
     direct = [swap(mine, bit) for bit in beside]
 
-    (here,) = terms([(mine, [mine])], weight=512)
+    (here,) = terms([(mine, [mine])], weight=64)
     far_features, far_vectors, here = tied((far_features, far_vectors, here))
     far = [far_features, far_vectors]
     last = []
@@ -182,8 +182,8 @@
         for pair in [far] + last:
             last = last + [[swap(piece, bit) for piece in pair]]
     far = jnp.concatenate(far, 0)
-    (here,) = terms([(mine, [sibling, far])], before=[here], weight=256)
-    near, *direct, here = tied((near, *direct, here))
+    (here,) = terms([(mine, [far])], before=[here], weight=2048)
+    near, sibling, *direct, here = tied((near, sibling, *direct, here))
     first = [far] + direct
     siblings = jnp.split(swap(jnp.concatenate(first, 0), 1), len(first), 0)
     (there,) = terms([(near, [mine, sibling] + first)], weight=2048)
@@ -191,10 +191,10 @@
     *pieces, there = tied((*[piece for pair in last for piece in pair], there))
     last = [jnp.concatenate(pieces[at : at + 2], 0) for at in range(0, len(pieces), 2)]
     last_siblings = [swap(block, 1) for block in last]
-    there, here = terms([(near, last), (mine, last)], before=[there, here], weight=64)
+    (there,) = terms([(near, last)], before=[there], weight=64)
     toward_near = terms([(near, last_siblings)], before=[there], weight=64, pieces=2)
     from_near = jnp.concatenate([swap(piece, 4) for piece in toward_near], 0)
-    rest = direct + siblings + last_siblings
+    rest = [sibling] + direct + siblings + last + last_siblings
     (here,) = terms([(mine, rest)], before=[here], weight=2048)
     return here + from_near
 

time: 29.2 us -> 29.3 us (level)
  transfers between devices with their start and end apart: 11 -> 11, of which waited for: 3 -> 4; matrix products, arithmetic and copies ran while one was open for 0% -> 0% of each run, Pallas kernels for 35% -> 35%
where the time goes in v22:
time: 29.3 us; the launch traced here: 29.2 us
  starting transfers between devices  12.3 us (42%)
  Pallas kernels  10.9 us (37%)
  waiting for transfers between devices  4.11 us (14%)
  local copies, waits for them, and re-layouts  1.02 us (3%)
  other arithmetic  0.7 us (2%)
    ppermute x11, starting transfers between devices, swapped(): lax.ppermute(value, axis, [(source, source ^ bit) for source in range(cou...  12.3 us
    pallas_call x7, Pallas kernels, pair_terms(): pl.pallas_call(functools.partial(kernel, width, vectors, placed, len(bloc...  9.22 us
    ppermute x11, waiting for transfers between devices, swapped(): lax.ppermute(value, axis, [(source, source ^ bit) for source in range(cou...  4.11 us
    pallas_call x1, Pallas kernels, packed(): pl.pallas_call(body, out_shape=[jax.ShapeDtypeStruct((rows, points), jnp....  1.65 us
    unnamed x4, local copies, waits for them, and re-layouts  0.98 us
    add x1, other arithmetic, local(): return here + from_near  0.67 us
  transfers between devices with their start and end apart: 11, of which 4 were waited for; matrix products, arithmetic and copies ran while one was open for 0% of the time, Pallas kernels for 35%

profile of v22, /device:TPU:0, one launch (start us, length us, event | category | flops | bytes accessed | tf_op | source)
XLA Modules:
  0.0 29.2 jit_solution(5585927794259264681)
XLA Ops:
  0.0 4.0 %collective-permute-start.3 = (f32[64,512]{1,0:T(8,128)}, f32[64,512]{1,0:T(8,128)S(1)}, u32[]{:S(2)}, u32[]{:S(2)}) collective-permute-start(f32[64,512]{1,0:T(8,128)} %features_ref.1), channel_id=1, source_target_pairs={{0,8},{1,9},{2,10},{3,11},{4,12},{5,13},{6,14},{7,15},{8,0},{9,1},... | collective-permute-start | bytes 393224 | tf_op jit(solution)/shard_map/ppermute | solution.py:19
  4.0 1.7 %shard_map.37 = (f32[96,512]{1,0:T(8,128)}, f32[32,512]{1,0:T(8,128)}) custom-call(f32[64,512]{1,0:T(8,128)} %features_ref.1, f32[16,512]{1,0:T(8,128)} %solves_ref.1, f32[16,512]{1,0:T(8,128)} %probes_ref.1), custom_call_target="tpu_custom_call" | custom-call | tf_op jit(solution)/shard_map/pallas_call | solution.py:150
  5.7 0.0 collective-permute-start.4
  5.7 1.9 %collective-permute-start.2 = (f32[96,512]{1,0:T(8,128)}, f32[96,512]{1,0:T(8,128)S(1)}, u32[]{:S(2)}, u32[]{:S(2)}) collective-permute-start(f32[96,512]{1,0:T(8,128)} %get-tuple-element.19.refs_0_.refs_1_), channel_id=1, source_target_pairs={{0,2},{1,3},{2,0},{3,1},{4,6},{5,7},{6,4},{7,5},{8,10},{9,11},{10,... | collective-permute-start | bytes 589832 | tf_op jit(solution)/shard_map/ppermute | solution.py:19
  7.5 0.0 collective-permute-start.1
  7.5 1.6 %collective-permute-start = (f32[96,512]{1,0:T(8,128)}, f32[96,512]{1,0:T(8,128)S(1)}, u32[]{:S(2)}, u32[]{:S(2)}) collective-permute-start(f32[96,512]{1,0:T(8,128)} %get-tuple-element.19.refs_0_.refs_1_), channel_id=1, source_target_pairs={{0,4},{1,5},{2,6},{3,7},{4,0},{5,1},{6,2},{7,3},{8,12},{9,13},{10,... | collective-permute-start | bytes 589832 | tf_op jit(solution)/shard_map/ppermute | solution.py:19
  9.1 0.0 copy-start
  9.1 1.0 %copy-done = f32[96,512]{1,0:T(8,128)S(1)} copy-done((f32[96,512]{1,0:T(8,128)S(1)}, f32[96,512]{1,0:T(8,128)}, u32[]{:S(2)}) %copy-start) | copy-done | bytes 196632
  10.1 0.8 %shard_map.38.refs_2_ = f32[64,512]{1,0:T(8,128)S(1)} custom-call(f32[96,512]{1,0:T(8,128)S(1)} %copy-done), custom_call_target="tpu_custom_call" | custom-call | flops 33554432 | bytes 196608 | tf_op jit(solution)/shard_map/pallas_call | solution.py:125
  10.8 2.6 %collective-permute-done.4 = f32[32,512]{1,0:T(8,128)S(1)} collective-permute-done((f32[32,512]{1,0:T(8,128)}, f32[32,512]{1,0:T(8,128)S(1)}, u32[]{:S(2)}, u32[]{:S(2)}) %collective-permute-start.4) | collective-permute-done | bytes 65568 | tf_op jit(solution)/shard_map/ppermute | solution.py:19
  13.5 0.0 collective-permute-done.3
  13.5 1.5 %collective-permute-start.6 = (f32[64,512]{1,0:T(8,128)S(1)}, f32[64,512]{1,0:T(8,128)S(1)}, u32[]{:S(2)}, u32[]{:S(2)}) collective-permute-start(f32[64,512]{1,0:T(8,128)S(1)} %collective-permute-done.3), channel_id=1, source_target_pairs={{0,2},{1,3},{2,0},{3,1},{4,6},{5,7},{6,4},{7,5},{8,10},{9,11},{10,... | collective-permute-start | bytes 393224 | tf_op jit(solution)/shard_map/ppermute | solution.py:19
  15.0 0.6 %collective-permute-start.7 = (f32[32,512]{1,0:T(8,128)S(1)}, f32[32,512]{1,0:T(8,128)S(1)}, u32[]{:S(2)}, u32[]{:S(2)}) collective-permute-start(f32[32,512]{1,0:T(8,128)S(1)} %collective-permute-done.4), channel_id=1, source_target_pairs={{0,2},{1,3},{2,0},{3,1},{4,6},{5,7},{6,4},{7,5},{8,10},{9,11},{10,... | collective-permute-start | bytes 196616 | tf_op jit(solution)/shard_map/ppermute | solution.py:19
  15.6 0.8 %shard_map.39.refs_7_ = f32[64,512]{1,0:T(8,128)S(1)} custom-call(f32[96,512]{1,0:T(8,128)S(1)} %copy-done, f32[96,512]{1,0:T(8,128)S(1)} %constant_dynamic-update-slice_fusion.refs_1_.refs_3_, f32[64,512]{1,0:T(8,128)S(1)} %shard_map.38.refs_2_), custom_call_target="tpu_custom_call" | custom-call | flops 1073741824 | bytes 589824 | tf_op jit(solution)/shard_map/pallas_call | solution.py:125
  16.4 0.0 collective-permute-done.2.refs_4_.refs_2_
  16.4 0.0 collective-permute-done.1.refs_2_.refs_1_
  16.4 0.5 %collective-permute-done.refs_0_ = f32[96,512]{1,0:T(8,128)S(1)} collective-permute-done((f32[96,512]{1,0:T(8,128)}, f32[96,512]{1,0:T(8,128)S(1)}, u32[]{:S(2)}, u32[]{:S(2)}) %collective-permute-start) | collective-permute-done | bytes 196640 | tf_op jit(solution)/shard_map/ppermute | solution.py:19
  16.9 0.1 collective-permute-start.5
  17.0 2.0 %shard_map.40.refs_3_ = f32[64,512]{1,0:T(8,128)S(1)} custom-call(f32[96,512]{1,0:T(8,128)S(1)} %collective-permute-done.refs_0_, f32[96,512]{1,0:T(8,128)S(1)} %copy-done, f32[96,512]{1,0:T(8,128)S(1)} %collective-permute-done.1.refs_2_.refs_1_, f32[96,512]{1,0:T(8,128)S(1)} %constant_dynamic-update-slice_fusion.refs_1_.refs_3_, ...), custom_call_target="tpu_custom_call" | custom-call | flops 4294967296 | bytes 983040 | tf_op jit(solution)/shard_map/pallas_call | solution.py:125
  19.1 0.0 collective-permute-done.5
  19.1 1.1 %shard_map.41.refs_2_ = f32[64,512]{1,0:T(8,128)S(1)} custom-call(f32[96,512]{1,0:T(8,128)S(1)} %collective-permute-done.refs_0_, f32[96,512]{1,0:T(8,128)S(1)} %get-tuple-element.34.refs_1_.refs_3_, f32[96,512]{1,0:T(8,128)S(1)} %get-tuple-element.33.refs_2_.refs_4_, f32[64,512]{1,0:T(8,128)S(1)} %shard_map.40.refs_3_), custom_call_target="tpu_custom_call" | custom-call | flops 67108864 | bytes 786432 | tf_op jit(solution)/shard_map/pallas_call | solution.py:125
  20.2 0.0 collective-permute-done.7
  20.3 0.0 collective-permute-done.6
  20.3 0.5 %collective-permute-start.8 = (f32[96,512]{1,0:T(8,128)S(1)}, f32[96,512]{1,0:T(8,128)S(1)}, u32[]{:S(2)}, u32[]{:S(2)}) collective-permute-start(f32[96,512]{1,0:T(8,128)S(1)} %constant_dynamic-update-slice_fusion.2.refs_5_.refs_1_), channel_id=1, source_target_pairs={{0,1},{1,0},{2,3},{3,2},{4,5},{5,4},{6,7},{7,6},{8,9},{9,8},{10,11... | collective-permute-start | bytes 589832 | tf_op jit(solution)/shard_map/ppermute | solution.py:19
  20.8 0.8 %shard_map.43.refs_2_ = f32[64,512]{1,0:T(8,128)S(1)} custom-call(f32[96,512]{1,0:T(8,128)S(1)} %collective-permute-done.refs_0_, f32[96,512]{1,0:T(8,128)S(1)} %constant_dynamic-update-slice_fusion.2.refs_5_.refs_1_, f32[64,512]{1,0:T(8,128)S(1)} %shard_map.41.refs_2_), custom_call_target="tpu_custom_call" | custom-call | flops 33554432 | bytes 589824 | tf_op jit(solution)/shard_map/pallas_call | solution.py:125
  21.6 0.3 %collective-permute-done.8.refs_6_.refs_1_ = f32[96,512]{1,0:T(8,128)S(1)} collective-permute-done((f32[96,512]{1,0:T(8,128)S(1)}, f32[96,512]{1,0:T(8,128)S(1)}, u32[]{:S(2)}, u32[]{:S(2)}) %collective-permute-start.8) | collective-permute-done | bytes 196640 | tf_op jit(solution)/shard_map/ppermute | solution.py:19
  21.9 0.8 %shard_map.44 = (f32[32,512]{1,0:T(8,128)S(1)}, f32[32,512]{1,0:T(8,128)S(1)}) custom-call(f32[96,512]{1,0:T(8,128)S(1)} %collective-permute-done.refs_0_, f32[96,512]{1,0:T(8,128)S(1)} %collective-permute-done.8.refs_6_.refs_1_, f32[64,512]{1,0:T(8,128)S(1)} %shard_map.43.refs_2_), custom_call_target="tpu_custom_call" | custom-call | flops 33554432 | bytes 589824 | tf_op jit(solution)/shard_map/pallas_call | solution.py:125
  22.7 0.8 %collective-permute-start.9 = (f32[32,512]{1,0:T(8,128)S(1)}, f32[32,512]{1,0:T(8,128)S(1)}, u32[]{:S(2)}, u32[]{:S(2)}) collective-permute-start(f32[32,512]{1,0:T(8,128)S(1)} %get-tuple-element.31), channel_id=1, source_target_pairs={{0,4},{1,5},{2,6},{3,7},{4,0},{5,1},{6,2},{7,3},{8,12},{9,13},{10,... | collective-permute-start | bytes 196616 | tf_op jit(solution)/shard_map/ppermute | solution.py:19
  23.4 1.3 %collective-permute-start.10 = (f32[32,512]{1,0:T(8,128)S(1)}, f32[32,512]{1,0:T(8,128)S(1)}, u32[]{:S(2)}, u32[]{:S(2)}) collective-permute-start(f32[32,512]{1,0:T(8,128)S(1)} %get-tuple-element.32), channel_id=1, source_target_pairs={{0,4},{1,5},{2,6},{3,7},{4,0},{5,1},{6,2},{7,3},{8,12},{9,13},{10,... | collective-permute-start | bytes 196616 | tf_op jit(solution)/shard_map/ppermute | solution.py:19
  24.8 3.0 %shard_map.42 = f32[64,512]{1,0:T(8,128)S(1)} custom-call(f32[96,512]{1,0:T(8,128)S(1)} %copy-done, f32[96,512]{1,0:T(8,128)S(1)} %collective-permute-done.1.refs_2_.refs_1_, f32[96,512]{1,0:T(8,128)S(1)} %collective-permute-done.2.refs_4_.refs_2_, f32[96,512]{1,0:T(8,128)S(1)} %get-tuple-element.34.refs_1_.refs_3_, ...), custom_call_target="tpu_custom_call" | custom-call | flops 6442450944 | bytes 1572864 | tf_op jit(solution)/shard_map/pallas_call | solution.py:125
  27.8 0.0 collective-permute-done.9
  27.8 0.7 %collective-permute-done.10 = f32[32,512]{1,0:T(8,128)S(1)} collective-permute-done((f32[32,512]{1,0:T(8,128)S(1)}, f32[32,512]{1,0:T(8,128)S(1)}, u32[]{:S(2)}, u32[]{:S(2)}) %collective-permute-start.10) | collective-permute-done | bytes 65568 | tf_op jit(solution)/shard_map/ppermute | solution.py:19
  28.5 0.7 %maximum_add_fusion = f32[64,512]{1,0:T(8,128)} fusion(f32[64,512]{1,0:T(8,128)S(1)} %shard_map.42, f32[32,512]{1,0:T(8,128)S(1)} %collective-permute-done.10, f32[32,512]{1,0:T(8,128)S(1)} %collective-permute-done.9), kind=kLoop, calls=%fused_computation.1 | loop fusion | flops 65536 | bytes 393216 | tf_op jit(solution)/shard_map/add | solution.py:199
  (6 shorter events, 0.1 us)
Async XLA Ops:
  0.0 13.5 %collective-permute-start.3 = (f32[64,512]{1,0:T(8,128)}, f32[64,512]{1,0:T(8,128)S(1)}, u32[]{:S(2)}, u32[]{:S(2)}) collective-permute-start(f32[64,512]{1,0:T(8,128)} %features_ref.1), channel_id=1, source_target_pairs={{0,8},{1,9},{2,10},{3,11},{4,12},{5,13},{6,14},{7,15},{8,0},{9,1},... | collective-permute-start | bytes 393224 | tf_op jit(solution)/shard_map/ppermute | solution.py:19
  5.7 7.8 %collective-permute-start.4 = (f32[32,512]{1,0:T(8,128)}, f32[32,512]{1,0:T(8,128)S(1)}, u32[]{:S(2)}, u32[]{:S(2)}) collective-permute-start(f32[32,512]{1,0:T(8,128)} %get-tuple-element.20), channel_id=1, source_target_pairs={{0,8},{1,9},{2,10},{3,11},{4,12},{5,13},{6,14},{7,15},{8,0},{9,1},... | collective-permute-start | bytes 196616 | tf_op jit(solution)/shard_map/ppermute | solution.py:19
  5.7 10.7 %collective-permute-start.2 = (f32[96,512]{1,0:T(8,128)}, f32[96,512]{1,0:T(8,128)S(1)}, u32[]{:S(2)}, u32[]{:S(2)}) collective-permute-start(f32[96,512]{1,0:T(8,128)} %get-tuple-element.19.refs_0_.refs_1_), channel_id=1, source_target_pairs={{0,2},{1,3},{2,0},{3,1},{4,6},{5,7},{6,4},{7,5},{8,10},{9,11},{10,... | collective-permute-start | bytes 589832 | tf_op jit(solution)/shard_map/ppermute | solution.py:19
  7.5 8.8 %collective-permute-start.1 = (f32[96,512]{1,0:T(8,128)}, f32[96,512]{1,0:T(8,128)S(1)}, u32[]{:S(2)}, u32[]{:S(2)}) collective-permute-start(f32[96,512]{1,0:T(8,128)} %get-tuple-element.19.refs_0_.refs_1_), channel_id=1, source_target_pairs={{0,1},{1,0},{2,3},{3,2},{4,5},{5,4},{6,7},{7,6},{8,9},{9,8},{10,11... | collective-permute-start | bytes 589832 | tf_op jit(solution)/shard_map/ppermute | solution.py:19
  7.5 9.3 %collective-permute-start = (f32[96,512]{1,0:T(8,128)}, f32[96,512]{1,0:T(8,128)S(1)}, u32[]{:S(2)}, u32[]{:S(2)}) collective-permute-start(f32[96,512]{1,0:T(8,128)} %get-tuple-element.19.refs_0_.refs_1_), channel_id=1, source_target_pairs={{0,4},{1,5},{2,6},{3,7},{4,0},{5,1},{6,2},{7,3},{8,12},{9,13},{10,... | collective-permute-start | bytes 589832 | tf_op jit(solution)/shard_map/ppermute | solution.py:19
  9.1 1.0 %copy-start = (f32[96,512]{1,0:T(8,128)S(1)}, f32[96,512]{1,0:T(8,128)}, u32[]{:S(2)}) copy-start(f32[96,512]{1,0:T(8,128)} %get-tuple-element.19.refs_0_.refs_1_) | copy-start | bytes 589828
  13.5 6.8 %collective-permute-start.6 = (f32[64,512]{1,0:T(8,128)S(1)}, f32[64,512]{1,0:T(8,128)S(1)}, u32[]{:S(2)}, u32[]{:S(2)}) collective-permute-start(f32[64,512]{1,0:T(8,128)S(1)} %collective-permute-done.3), channel_id=1, source_target_pairs={{0,2},{1,3},{2,0},{3,1},{4,6},{5,7},{6,4},{7,5},{8,10},{9,11},{10,... | collective-permute-start | bytes 393224 | tf_op jit(solution)/shard_map/ppermute | solution.py:19
  15.0 5.2 %collective-permute-start.7 = (f32[32,512]{1,0:T(8,128)S(1)}, f32[32,512]{1,0:T(8,128)S(1)}, u32[]{:S(2)}, u32[]{:S(2)}) collective-permute-start(f32[32,512]{1,0:T(8,128)S(1)} %collective-permute-done.4), channel_id=1, source_target_pairs={{0,2},{1,3},{2,0},{3,1},{4,6},{5,7},{6,4},{7,5},{8,10},{9,11},{10,... | collective-permute-start | bytes 196616 | tf_op jit(solution)/shard_map/ppermute | solution.py:19
  16.9 2.2 %collective-permute-start.5 = (f32[192,512]{1,0:T(8,128)S(1)}, f32[192,512]{1,0:T(8,128)S(1)}, u32[]{:S(2)}, u32[]{:S(2)}) collective-permute-start(f32[192,512]{1,0:T(8,128)S(1)} %pad_maximum_fusion), channel_id=1, source_target_pairs={{0,1},{1,0},{2,3},{3,2},{4,5},{5,4},{6,7},{7,6},{8,9},{9,8},{10,11... | collective-permute-start | bytes 1179656 | tf_op jit(solution)/shard_map/ppermute | solution.py:19
  20.3 1.6 %collective-permute-start.8 = (f32[96,512]{1,0:T(8,128)S(1)}, f32[96,512]{1,0:T(8,128)S(1)}, u32[]{:S(2)}, u32[]{:S(2)}) collective-permute-start(f32[96,512]{1,0:T(8,128)S(1)} %constant_dynamic-update-slice_fusion.2.refs_5_.refs_1_), channel_id=1, source_target_pairs={{0,1},{1,0},{2,3},{3,2},{4,5},{5,4},{6,7},{7,6},{8,9},{9,8},{10,11... | collective-permute-start | bytes 589832 | tf_op jit(solution)/shard_map/ppermute | solution.py:19
  22.7 5.1 %collective-permute-start.9 = (f32[32,512]{1,0:T(8,128)S(1)}, f32[32,512]{1,0:T(8,128)S(1)}, u32[]{:S(2)}, u32[]{:S(2)}) collective-permute-start(f32[32,512]{1,0:T(8,128)S(1)} %get-tuple-element.31), channel_id=1, source_target_pairs={{0,4},{1,5},{2,6},{3,7},{4,0},{5,1},{6,2},{7,3},{8,12},{9,13},{10,... | collective-permute-start | bytes 196616 | tf_op jit(solution)/shard_map/ppermute | solution.py:19
  23.4 5.0 %collective-permute-start.10 = (f32[32,512]{1,0:T(8,128)S(1)}, f32[32,512]{1,0:T(8,128)S(1)}, u32[]{:S(2)}, u32[]{:S(2)}) collective-permute-start(f32[32,512]{1,0:T(8,128)S(1)} %get-tuple-element.32), channel_id=1, source_target_pairs={{0,4},{1,5},{2,6},{3,7},{4,0},{5,1},{6,2},{7,3},{8,12},{9,13},{10,... | collective-permute-start | bytes 196616 | tf_op jit(solution)/shard_map/ppermute | solution.py:19

commit v23 on v11

--- a/solution.py
+++ b/solution.py
@@ -10,7 +10,7 @@
 LOG2E = 1.4426950408889634
 NORM_ROWS = 16
 ONES_ROWS = 16
-STACK = 4
+STACK = 7
 VMEM_LIMIT = 24 << 20
 
 

time: 28.8 us -> 28.8 us (level)
  no operation moved by 1% of the time
where the time goes in v23:
time: 28.8 us; the launch traced here: 28.6 us
  starting transfers between devices  11.7 us (41%)
  Pallas kernels  10.6 us (37%)
  waiting for transfers between devices  4.46 us (15%)
  local copies, waits for them, and re-layouts  1.02 us (4%)
  other arithmetic  0.7 us (2%)
    ppermute x11, starting transfers between devices, swapped(): lax.ppermute(value, axis, [(source, source ^ bit) for source in range(cou...  11.7 us
    pallas_call x6, Pallas kernels, pair_terms(): pl.pallas_call(functools.partial(kernel, width, vectors, placed, len(bloc...  8.91 us
    ppermute x11, waiting for transfers between devices, swapped(): lax.ppermute(value, axis, [(source, source ^ bit) for source in range(cou...  4.46 us
    pallas_call x1, Pallas kernels, packed(): pl.pallas_call(body, out_shape=[jax.ShapeDtypeStruct((rows, points), jnp....  1.65 us
    unnamed x4, local copies, waits for them, and re-layouts  0.98 us
    add x1, other arithmetic, local(): return here + from_near  0.67 us
  transfers between devices with their start and end apart: 11, of which 4 were waited for; matrix products, arithmetic and copies ran while one was open for 0% of the time, Pallas kernels for 34%

profile of v23, /device:TPU:0, one launch (start us, length us, event | category | flops | bytes accessed | tf_op | source)
XLA Modules:
  0.0 28.6 jit_solution(15350447780829938867)
XLA Ops:
  0.0 4.0 %collective-permute-start.1 = (f32[64,512]{1,0:T(8,128)}, f32[64,512]{1,0:T(8,128)S(1)}, u32[]{:S(2)}, u32[]{:S(2)}) collective-permute-start(f32[64,512]{1,0:T(8,128)} %features_ref.1), channel_id=1, source_target_pairs={{0,8},{1,9},{2,10},{3,11},{4,12},{5,13},{6,14},{7,15},{8,0},{9,1},... | collective-permute-start | bytes 393224 | tf_op jit(solution)/shard_map/ppermute | solution.py:19
  4.0 1.7 %shard_map.37 = (f32[96,512]{1,0:T(8,128)}, f32[32,512]{1,0:T(8,128)}) custom-call(f32[64,512]{1,0:T(8,128)} %features_ref.1, f32[16,512]{1,0:T(8,128)} %solves_ref.1, f32[16,512]{1,0:T(8,128)} %probes_ref.1), custom_call_target="tpu_custom_call" | custom-call | tf_op jit(solution)/shard_map/pallas_call | solution.py:150
  5.7 0.0 collective-permute-start.2
  5.7 0.0 collective-permute-start
  5.7 1.9 %collective-permute-start.3 = (f32[96,512]{1,0:T(8,128)}, f32[96,512]{1,0:T(8,128)S(1)}, u32[]{:S(2)}, u32[]{:S(2)}) collective-permute-start(f32[96,512]{1,0:T(8,128)} %get-tuple-element.15.refs_0_.refs_1_), channel_id=1, source_target_pairs={{0,2},{1,3},{2,0},{3,1},{4,6},{5,7},{6,4},{7,5},{8,10},{9,11},{10,... | collective-permute-start | bytes 589832 | tf_op jit(solution)/shard_map/ppermute | solution.py:19
  7.5 1.6 %collective-permute-start.7 = (f32[96,512]{1,0:T(8,128)}, f32[96,512]{1,0:T(8,128)S(1)}, u32[]{:S(2)}, u32[]{:S(2)}) collective-permute-start(f32[96,512]{1,0:T(8,128)} %get-tuple-element.15.refs_0_.refs_1_), channel_id=1, source_target_pairs={{0,4},{1,5},{2,6},{3,7},{4,0},{5,1},{6,2},{7,3},{8,12},{9,13},{10,... | collective-permute-start | bytes 589832 | tf_op jit(solution)/shard_map/ppermute | solution.py:19
  9.1 0.0 copy-start
  9.1 1.0 %copy-done = f32[96,512]{1,0:T(8,128)S(1)} copy-done((f32[96,512]{1,0:T(8,128)S(1)}, f32[96,512]{1,0:T(8,128)}, u32[]{:S(2)}) %copy-start) | copy-done | bytes 196632
  10.1 0.8 %shard_map.38.refs_8_ = f32[64,512]{1,0:T(8,128)S(1)} custom-call(f32[96,512]{1,0:T(8,128)S(1)} %copy-done), custom_call_target="tpu_custom_call" | custom-call | flops 33554432 | bytes 196608 | tf_op jit(solution)/shard_map/pallas_call | solution.py:125
  10.8 2.6 %collective-permute-done.2 = f32[32,512]{1,0:T(8,128)S(1)} collective-permute-done((f32[32,512]{1,0:T(8,128)}, f32[32,512]{1,0:T(8,128)S(1)}, u32[]{:S(2)}, u32[]{:S(2)}) %collective-permute-start.2) | collective-permute-done | bytes 65568 | tf_op jit(solution)/shard_map/ppermute | solution.py:19
  13.5 0.0 collective-permute-done.1
  13.5 1.5 %collective-permute-start.5 = (f32[64,512]{1,0:T(8,128)S(1)}, f32[64,512]{1,0:T(8,128)S(1)}, u32[]{:S(2)}, u32[]{:S(2)}) collective-permute-start(f32[64,512]{1,0:T(8,128)S(1)} %collective-permute-done.1), channel_id=1, source_target_pairs={{0,2},{1,3},{2,0},{3,1},{4,6},{5,7},{6,4},{7,5},{8,10},{9,11},{10,... | collective-permute-start | bytes 393224 | tf_op jit(solution)/shard_map/ppermute | solution.py:19
  15.0 0.5 %collective-permute-start.6 = (f32[32,512]{1,0:T(8,128)S(1)}, f32[32,512]{1,0:T(8,128)S(1)}, u32[]{:S(2)}, u32[]{:S(2)}) collective-permute-start(f32[32,512]{1,0:T(8,128)S(1)} %collective-permute-done.2), channel_id=1, source_target_pairs={{0,2},{1,3},{2,0},{3,1},{4,6},{5,7},{6,4},{7,5},{8,10},{9,11},{10,... | collective-permute-start | bytes 196616 | tf_op jit(solution)/shard_map/ppermute | solution.py:19
  15.5 0.0 collective-permute-done.3.refs_4_.refs_3_
  15.6 0.1 collective-permute-start.4
  15.7 0.0 collective-permute-done.refs_2_.refs_1_
  15.7 1.0 %collective-permute-done.7.refs_0_ = f32[96,512]{1,0:T(8,128)S(1)} collective-permute-done((f32[96,512]{1,0:T(8,128)}, f32[96,512]{1,0:T(8,128)S(1)}, u32[]{:S(2)}, u32[]{:S(2)}) %collective-permute-start.7) | collective-permute-done | bytes 196640 | tf_op jit(solution)/shard_map/ppermute | solution.py:19
  16.7 2.0 %shard_map.39.refs_3_ = f32[64,512]{1,0:T(8,128)S(1)} custom-call(f32[96,512]{1,0:T(8,128)S(1)} %collective-permute-done.7.refs_0_, f32[96,512]{1,0:T(8,128)S(1)} %copy-done, f32[96,512]{1,0:T(8,128)S(1)} %collective-permute-done.refs_2_.refs_1_, f32[96,512]{1,0:T(8,128)S(1)} %constant_dynamic-update-slice_fusion.refs_3_.refs_2_, ...), custom_call_target="tpu_custom_call" | custom-call | flops 4294967296 | bytes 983040 | tf_op jit(solution)/shard_map/pallas_call | solution.py:125
  18.7 0.0 collective-permute-done.4
  18.8 1.1 %shard_map.40.refs_2_ = f32[64,512]{1,0:T(8,128)S(1)} custom-call(f32[96,512]{1,0:T(8,128)S(1)} %collective-permute-done.7.refs_0_, f32[96,512]{1,0:T(8,128)S(1)} %get-tuple-element.26.refs_1_.refs_4_, f32[96,512]{1,0:T(8,128)S(1)} %get-tuple-element.25.refs_2_.refs_5_, f32[64,512]{1,0:T(8,128)S(1)} %shard_map.39.refs_3_), custom_call_target="tpu_custom_call" | custom-call | flops 67108864 | bytes 786432 | tf_op jit(solution)/shard_map/pallas_call | solution.py:125
  19.9 0.0 collective-permute-done.6
  19.9 0.0 collective-permute-done.5
  20.0 0.1 collective-permute-start.8
  20.0 0.8 %shard_map.42.refs_2_ = f32[64,512]{1,0:T(8,128)S(1)} custom-call(f32[96,512]{1,0:T(8,128)S(1)} %collective-permute-done.7.refs_0_, f32[96,512]{1,0:T(8,128)S(1)} %constant_dynamic-update-slice_fusion.2.refs_6_.refs_1_, f32[64,512]{1,0:T(8,128)S(1)} %shard_map.40.refs_2_), custom_call_target="tpu_custom_call" | custom-call | flops 33554432 | bytes 589824 | tf_op jit(solution)/shard_map/pallas_call | solution.py:125
  20.8 0.7 %collective-permute-done.8.refs_7_.refs_1_ = f32[96,512]{1,0:T(8,128)S(1)} collective-permute-done((f32[96,512]{1,0:T(8,128)S(1)}, f32[96,512]{1,0:T(8,128)S(1)}, u32[]{:S(2)}, u32[]{:S(2)}) %collective-permute-start.8) | collective-permute-done | bytes 196640 | tf_op jit(solution)/shard_map/ppermute | solution.py:19
  21.5 0.8 %shard_map.43 = (f32[32,512]{1,0:T(8,128)S(1)}, f32[32,512]{1,0:T(8,128)S(1)}) custom-call(f32[96,512]{1,0:T(8,128)S(1)} %collective-permute-done.7.refs_0_, f32[96,512]{1,0:T(8,128)S(1)} %collective-permute-done.8.refs_7_.refs_1_, f32[64,512]{1,0:T(8,128)S(1)} %shard_map.42.refs_2_), custom_call_target="tpu_custom_call" | custom-call | flops 33554432 | bytes 589824 | tf_op jit(solution)/shard_map/pallas_call | solution.py:125
  22.2 1.2 %collective-permute-start.10 = (f32[32,512]{1,0:T(8,128)S(1)}, f32[32,512]{1,0:T(8,128)S(1)}, u32[]{:S(2)}, u32[]{:S(2)}) collective-permute-start(f32[32,512]{1,0:T(8,128)S(1)} %get-tuple-element.24), channel_id=1, source_target_pairs={{0,4},{1,5},{2,6},{3,7},{4,0},{5,1},{6,2},{7,3},{8,12},{9,13},{10,... | collective-permute-start | bytes 196616 | tf_op jit(solution)/shard_map/ppermute | solution.py:19
  23.4 0.9 %collective-permute-start.9 = (f32[32,512]{1,0:T(8,128)S(1)}, f32[32,512]{1,0:T(8,128)S(1)}, u32[]{:S(2)}, u32[]{:S(2)}) collective-permute-start(f32[32,512]{1,0:T(8,128)S(1)} %get-tuple-element.23), channel_id=1, source_target_pairs={{0,4},{1,5},{2,6},{3,7},{4,0},{5,1},{6,2},{7,3},{8,12},{9,13},{10,... | collective-permute-start | bytes 196616 | tf_op jit(solution)/shard_map/ppermute | solution.py:19
  24.3 3.5 %shard_map.41 = f32[64,512]{1,0:T(8,128)S(1)} custom-call(f32[96,512]{1,0:T(8,128)S(1)} %copy-done, f32[96,512]{1,0:T(8,128)S(1)} %collective-permute-done.refs_2_.refs_1_, f32[96,512]{1,0:T(8,128)S(1)} %constant_dynamic-update-slice_fusion.refs_3_.refs_2_, f32[96,512]{1,0:T(8,128)S(1)} %collective-permute-done.3.refs_4_.refs_3_, ...), custom_call_target="tpu_custom_call" | custom-call | flops 7516192768 | bytes 1769472 | tf_op jit(solution)/shard_map/pallas_call | solution.py:125
  27.8 0.0 collective-permute-done.10
  27.8 0.1 collective-permute-done.9
  28.0 0.7 %maximum_add_fusion = f32[64,512]{1,0:T(8,128)} fusion(f32[64,512]{1,0:T(8,128)S(1)} %shard_map.41, f32[32,512]{1,0:T(8,128)S(1)} %collective-permute-done.10, f32[32,512]{1,0:T(8,128)S(1)} %collective-permute-done.9), kind=kLoop, calls=%fused_computation.1 | loop fusion | flops 65536 | bytes 393216 | tf_op jit(solution)/shard_map/add | solution.py:197
  (6 shorter events, 0.1 us)
Async XLA Ops:
  0.0 13.5 %collective-permute-start.1 = (f32[64,512]{1,0:T(8,128)}, f32[64,512]{1,0:T(8,128)S(1)}, u32[]{:S(2)}, u32[]{:S(2)}) collective-permute-start(f32[64,512]{1,0:T(8,128)} %features_ref.1), channel_id=1, source_target_pairs={{0,8},{1,9},{2,10},{3,11},{4,12},{5,13},{6,14},{7,15},{8,0},{9,1},... | collective-permute-start | bytes 393224 | tf_op jit(solution)/shard_map/ppermute | solution.py:19
  5.7 7.8 %collective-permute-start.2 = (f32[32,512]{1,0:T(8,128)}, f32[32,512]{1,0:T(8,128)S(1)}, u32[]{:S(2)}, u32[]{:S(2)}) collective-permute-start(f32[32,512]{1,0:T(8,128)} %get-tuple-element.16), channel_id=1, source_target_pairs={{0,8},{1,9},{2,10},{3,11},{4,12},{5,13},{6,14},{7,15},{8,0},{9,1},... | collective-permute-start | bytes 196616 | tf_op jit(solution)/shard_map/ppermute | solution.py:19
  5.7 10.0 %collective-permute-start = (f32[96,512]{1,0:T(8,128)}, f32[96,512]{1,0:T(8,128)S(1)}, u32[]{:S(2)}, u32[]{:S(2)}) collective-permute-start(f32[96,512]{1,0:T(8,128)} %get-tuple-element.15.refs_0_.refs_1_), channel_id=1, source_target_pairs={{0,1},{1,0},{2,3},{3,2},{4,5},{5,4},{6,7},{7,6},{8,9},{9,8},{10,11... | collective-permute-start | bytes 589832 | tf_op jit(solution)/shard_map/ppermute | solution.py:19
  5.7 9.8 %collective-permute-start.3 = (f32[96,512]{1,0:T(8,128)}, f32[96,512]{1,0:T(8,128)S(1)}, u32[]{:S(2)}, u32[]{:S(2)}) collective-permute-start(f32[96,512]{1,0:T(8,128)} %get-tuple-element.15.refs_0_.refs_1_), channel_id=1, source_target_pairs={{0,2},{1,3},{2,0},{3,1},{4,6},{5,7},{6,4},{7,5},{8,10},{9,11},{10,... | collective-permute-start | bytes 589832 | tf_op jit(solution)/shard_map/ppermute | solution.py:19
  7.5 9.1 %collective-permute-start.7 = (f32[96,512]{1,0:T(8,128)}, f32[96,512]{1,0:T(8,128)S(1)}, u32[]{:S(2)}, u32[]{:S(2)}) collective-permute-start(f32[96,512]{1,0:T(8,128)} %get-tuple-element.15.refs_0_.refs_1_), channel_id=1, source_target_pairs={{0,4},{1,5},{2,6},{3,7},{4,0},{5,1},{6,2},{7,3},{8,12},{9,13},{10,... | collective-permute-start | bytes 589832 | tf_op jit(solution)/shard_map/ppermute | solution.py:19
  9.1 1.0 %copy-start = (f32[96,512]{1,0:T(8,128)S(1)}, f32[96,512]{1,0:T(8,128)}, u32[]{:S(2)}) copy-start(f32[96,512]{1,0:T(8,128)} %get-tuple-element.15.refs_0_.refs_1_) | copy-start | bytes 589828
  13.5 6.4 %collective-permute-start.5 = (f32[64,512]{1,0:T(8,128)S(1)}, f32[64,512]{1,0:T(8,128)S(1)}, u32[]{:S(2)}, u32[]{:S(2)}) collective-permute-start(f32[64,512]{1,0:T(8,128)S(1)} %collective-permute-done.1), channel_id=1, source_target_pairs={{0,2},{1,3},{2,0},{3,1},{4,6},{5,7},{6,4},{7,5},{8,10},{9,11},{10,... | collective-permute-start | bytes 393224 | tf_op jit(solution)/shard_map/ppermute | solution.py:19
  15.0 4.9 %collective-permute-start.6 = (f32[32,512]{1,0:T(8,128)S(1)}, f32[32,512]{1,0:T(8,128)S(1)}, u32[]{:S(2)}, u32[]{:S(2)}) collective-permute-start(f32[32,512]{1,0:T(8,128)S(1)} %collective-permute-done.2), channel_id=1, source_target_pairs={{0,2},{1,3},{2,0},{3,1},{4,6},{5,7},{6,4},{7,5},{8,10},{9,11},{10,... | collective-permute-start | bytes 196616 | tf_op jit(solution)/shard_map/ppermute | solution.py:19
  15.6 3.2 %collective-permute-start.4 = (f32[192,512]{1,0:T(8,128)S(1)}, f32[192,512]{1,0:T(8,128)S(1)}, u32[]{:S(2)}, u32[]{:S(2)}) collective-permute-start(f32[192,512]{1,0:T(8,128)S(1)} %pad_maximum_fusion), channel_id=1, source_target_pairs={{0,1},{1,0},{2,3},{3,2},{4,5},{5,4},{6,7},{7,6},{8,9},{9,8},{10,11... | collective-permute-start | bytes 1179656 | tf_op jit(solution)/shard_map/ppermute | solution.py:19
  20.0 1.5 %collective-permute-start.8 = (f32[96,512]{1,0:T(8,128)S(1)}, f32[96,512]{1,0:T(8,128)S(1)}, u32[]{:S(2)}, u32[]{:S(2)}) collective-permute-start(f32[96,512]{1,0:T(8,128)S(1)} %constant_dynamic-update-slice_fusion.2.refs_6_.refs_1_), channel_id=1, source_target_pairs={{0,1},{1,0},{2,3},{3,2},{4,5},{5,4},{6,7},{7,6},{8,9},{9,8},{10,11... | collective-permute-start | bytes 589832 | tf_op jit(solution)/shard_map/ppermute | solution.py:19
  22.2 5.6 %collective-permute-start.10 = (f32[32,512]{1,0:T(8,128)S(1)}, f32[32,512]{1,0:T(8,128)S(1)}, u32[]{:S(2)}, u32[]{:S(2)}) collective-permute-start(f32[32,512]{1,0:T(8,128)S(1)} %get-tuple-element.24), channel_id=1, source_target_pairs={{0,4},{1,5},{2,6},{3,7},{4,0},{5,1},{6,2},{7,3},{8,12},{9,13},{10,... | collective-permute-start | bytes 196616 | tf_op jit(solution)/shard_map/ppermute | solution.py:19
  23.4 4.5 %collective-permute-start.9 = (f32[32,512]{1,0:T(8,128)S(1)}, f32[32,512]{1,0:T(8,128)S(1)}, u32[]{:S(2)}, u32[]{:S(2)}) collective-permute-start(f32[32,512]{1,0:T(8,128)S(1)} %get-tuple-element.23), channel_id=1, source_target_pairs={{0,4},{1,5},{2,6},{3,7},{4,0},{5,1},{6,2},{7,3},{8,12},{9,13},{10,... | collective-permute-start | bytes 196616 | tf_op jit(solution)/shard_map/ppermute | solution.py:19

commit v24 on v11

--- a/solution.py
+++ b/solution.py
@@ -191,8 +191,8 @@
     last_siblings = [swap(block, 1) for block in last]
     (there,) = terms([(near, last)], before=[there], weight=64)
     rest = [sibling] + first + siblings + last + last_siblings
-    toward_near = terms([(near, last_siblings)], before=[there], weight=64, pieces=2)
-    from_near = jnp.concatenate([swap(piece, 4) for piece in toward_near], 0)
+    toward_near = terms([(near, last_siblings)], before=[there], weight=64)
+    from_near = swap(toward_near[0], 4)
     (here,) = terms([(mine, rest)], before=[here], weight=2048)
     return here + from_near
 

time: 28.8 us -> 28.7 us (level)
  starting transfers between devices: 11.7 us -> 10.8 us
  waiting for transfers between devices: 4.48 us -> 5.24 us
    ppermute x11 -> x10, starting transfers between devices: 11.7 us -> 10.8 us  [swapped(): lax.ppermute(value, axis, [(source, source ^ bit) for source in range(cou...]
    ppermute x11 -> x10, waiting for transfers between devices: 4.48 us -> 5.24 us  [swapped(): lax.ppermute(value, axis, [(source, source ^ bit) for source in range(cou...]
    unnamed x4 -> x6, local copies, waits for them, and re-layouts: 0.98 us -> 0.98 us
  transfers between devices with their start and end apart: 11 -> 10, of which waited for: 4 -> 4; matrix products, arithmetic and copies ran while one was open for 0% -> 0% of each run, Pallas kernels for 34% -> 34%
where the time goes in v24:
time: 28.7 us; the launch traced here: 28.5 us
  starting transfers between devices  10.8 us (38%)
  Pallas kernels  10.5 us (37%)
  waiting for transfers between devices  5.24 us (18%)
  local copies, waits for them, and re-layouts  1.03 us (4%)
  other arithmetic  0.7 us (2%)
    ppermute x10, starting transfers between devices, swapped(): lax.ppermute(value, axis, [(source, source ^ bit) for source in range(cou...  10.8 us
    pallas_call x6, Pallas kernels, pair_terms(): pl.pallas_call(functools.partial(kernel, width, vectors, placed, len(bloc...  8.89 us
    ppermute x10, waiting for transfers between devices, swapped(): lax.ppermute(value, axis, [(source, source ^ bit) for source in range(cou...  5.24 us
    pallas_call x1, Pallas kernels, packed(): pl.pallas_call(body, out_shape=[jax.ShapeDtypeStruct((rows, points), jnp....  1.65 us
    unnamed x6, local copies, waits for them, and re-layouts  0.98 us
    add x1, other arithmetic, local(): return here + from_near  0.67 us
  transfers between devices with their start and end apart: 10, of which 4 were waited for; matrix products, arithmetic and copies ran while one was open for 0% of the time, Pallas kernels for 34%

profile of v24, /device:TPU:0, one launch (start us, length us, event | category | flops | bytes accessed | tf_op | source)
XLA Modules:
  0.0 28.5 jit_solution(5410682388420642766)
XLA Ops:
  0.0 4.0 %collective-permute-start.1 = (f32[64,512]{1,0:T(8,128)}, f32[64,512]{1,0:T(8,128)S(1)}, u32[]{:S(2)}, u32[]{:S(2)}) collective-permute-start(f32[64,512]{1,0:T(8,128)} %features_ref.1), channel_id=1, source_target_pairs={{0,8},{1,9},{2,10},{3,11},{4,12},{5,13},{6,14},{7,15},{8,0},{9,1},... | collective-permute-start | bytes 393224 | tf_op jit(solution)/shard_map/ppermute | solution.py:19
  4.0 1.7 %shard_map.37 = (f32[96,512]{1,0:T(8,128)}, f32[32,512]{1,0:T(8,128)}) custom-call(f32[64,512]{1,0:T(8,128)} %features_ref.1, f32[16,512]{1,0:T(8,128)} %solves_ref.1, f32[16,512]{1,0:T(8,128)} %probes_ref.1), custom_call_target="tpu_custom_call" | custom-call | tf_op jit(solution)/shard_map/pallas_call | solution.py:150
  5.7 0.0 collective-permute-start.2
  5.7 0.0 collective-permute-start
  5.7 1.9 %collective-permute-start.3 = (f32[96,512]{1,0:T(8,128)}, f32[96,512]{1,0:T(8,128)S(1)}, u32[]{:S(2)}, u32[]{:S(2)}) collective-permute-start(f32[96,512]{1,0:T(8,128)} %get-tuple-element.13.refs_0_.refs_1_), channel_id=1, source_target_pairs={{0,2},{1,3},{2,0},{3,1},{4,6},{5,7},{6,4},{7,5},{8,10},{9,11},{10,... | collective-permute-start | bytes 589832 | tf_op jit(solution)/shard_map/ppermute | solution.py:19
  7.5 1.6 %collective-permute-start.7 = (f32[96,512]{1,0:T(8,128)}, f32[96,512]{1,0:T(8,128)S(1)}, u32[]{:S(2)}, u32[]{:S(2)}) collective-permute-start(f32[96,512]{1,0:T(8,128)} %get-tuple-element.13.refs_0_.refs_1_), channel_id=1, source_target_pairs={{0,4},{1,5},{2,6},{3,7},{4,0},{5,1},{6,2},{7,3},{8,12},{9,13},{10,... | collective-permute-start | bytes 589832 | tf_op jit(solution)/shard_map/ppermute | solution.py:19
  9.1 0.0 copy-start
  9.1 1.0 %copy-done = f32[96,512]{1,0:T(8,128)S(1)} copy-done((f32[96,512]{1,0:T(8,128)S(1)}, f32[96,512]{1,0:T(8,128)}, u32[]{:S(2)}) %copy-start) | copy-done | bytes 196632
  10.1 0.8 %shard_map.38.refs_8_ = f32[64,512]{1,0:T(8,128)S(1)} custom-call(f32[96,512]{1,0:T(8,128)S(1)} %copy-done), custom_call_target="tpu_custom_call" | custom-call | flops 33554432 | bytes 196608 | tf_op jit(solution)/shard_map/pallas_call | solution.py:125
  10.8 2.6 %collective-permute-done.2 = f32[32,512]{1,0:T(8,128)S(1)} collective-permute-done((f32[32,512]{1,0:T(8,128)}, f32[32,512]{1,0:T(8,128)S(1)}, u32[]{:S(2)}, u32[]{:S(2)}) %collective-permute-start.2) | collective-permute-done | bytes 65568 | tf_op jit(solution)/shard_map/ppermute | solution.py:19
  13.5 0.0 collective-permute-done.1
  13.5 1.5 %collective-permute-start.5 = (f32[64,512]{1,0:T(8,128)S(1)}, f32[64,512]{1,0:T(8,128)S(1)}, u32[]{:S(2)}, u32[]{:S(2)}) collective-permute-start(f32[64,512]{1,0:T(8,128)S(1)} %collective-permute-done.1), channel_id=1, source_target_pairs={{0,2},{1,3},{2,0},{3,1},{4,6},{5,7},{6,4},{7,5},{8,10},{9,11},{10,... | collective-permute-start | bytes 393224 | tf_op jit(solution)/shard_map/ppermute | solution.py:19
  15.0 0.5 %collective-permute-start.6 = (f32[32,512]{1,0:T(8,128)S(1)}, f32[32,512]{1,0:T(8,128)S(1)}, u32[]{:S(2)}, u32[]{:S(2)}) collective-permute-start(f32[32,512]{1,0:T(8,128)S(1)} %collective-permute-done.2), channel_id=1, source_target_pairs={{0,2},{1,3},{2,0},{3,1},{4,6},{5,7},{6,4},{7,5},{8,10},{9,11},{10,... | collective-permute-start | bytes 196616 | tf_op jit(solution)/shard_map/ppermute | solution.py:19
  15.5 0.0 collective-permute-done.3.refs_4_.refs_3_
  15.6 0.1 collective-permute-start.4
  15.7 0.0 collective-permute-done.refs_2_.refs_1_
  15.7 1.0 %collective-permute-done.7.refs_0_ = f32[96,512]{1,0:T(8,128)S(1)} collective-permute-done((f32[96,512]{1,0:T(8,128)}, f32[96,512]{1,0:T(8,128)S(1)}, u32[]{:S(2)}, u32[]{:S(2)}) %collective-permute-start.7) | collective-permute-done | bytes 196640 | tf_op jit(solution)/shard_map/ppermute | solution.py:19
  16.7 2.0 %shard_map.39.refs_3_ = f32[64,512]{1,0:T(8,128)S(1)} custom-call(f32[96,512]{1,0:T(8,128)S(1)} %collective-permute-done.7.refs_0_, f32[96,512]{1,0:T(8,128)S(1)} %copy-done, f32[96,512]{1,0:T(8,128)S(1)} %collective-permute-done.refs_2_.refs_1_, f32[96,512]{1,0:T(8,128)S(1)} %constant_dynamic-update-slice_fusion.refs_3_.refs_2_, ...), custom_call_target="tpu_custom_call" | custom-call | flops 4294967296 | bytes 983040 | tf_op jit(solution)/shard_map/pallas_call | solution.py:125
  18.7 0.0 collective-permute-done.4
  18.8 1.1 %shard_map.40.refs_2_ = f32[64,512]{1,0:T(8,128)S(1)} custom-call(f32[96,512]{1,0:T(8,128)S(1)} %collective-permute-done.7.refs_0_, f32[96,512]{1,0:T(8,128)S(1)} %get-tuple-element.22.refs_1_.refs_4_, f32[96,512]{1,0:T(8,128)S(1)} %get-tuple-element.21.refs_2_.refs_5_, f32[64,512]{1,0:T(8,128)S(1)} %shard_map.39.refs_3_), custom_call_target="tpu_custom_call" | custom-call | flops 67108864 | bytes 786432 | tf_op jit(solution)/shard_map/pallas_call | solution.py:125
  19.9 0.0 collective-permute-done.6
  19.9 0.0 collective-permute-done.5
  20.0 0.1 collective-permute-start.8
  20.0 0.8 %shard_map.42.refs_2_ = f32[64,512]{1,0:T(8,128)S(1)} custom-call(f32[96,512]{1,0:T(8,128)S(1)} %collective-permute-done.7.refs_0_, f32[96,512]{1,0:T(8,128)S(1)} %constant_dynamic-update-slice_fusion.2.refs_6_.refs_1_, f32[64,512]{1,0:T(8,128)S(1)} %shard_map.40.refs_2_), custom_call_target="tpu_custom_call" | custom-call | flops 33554432 | bytes 589824 | tf_op jit(solution)/shard_map/pallas_call | solution.py:125
  20.8 0.0 copy-start.1
  20.8 0.6 %collective-permute-done.8.refs_7_.refs_1_ = f32[96,512]{1,0:T(8,128)S(1)} collective-permute-done((f32[96,512]{1,0:T(8,128)S(1)}, f32[96,512]{1,0:T(8,128)S(1)}, u32[]{:S(2)}, u32[]{:S(2)}) %collective-permute-start.8) | collective-permute-done | bytes 196640 | tf_op jit(solution)/shard_map/ppermute | solution.py:19
  21.5 0.8 %shard_map.43 = f32[64,512]{1,0:T(8,128)S(1)} custom-call(f32[96,512]{1,0:T(8,128)S(1)} %collective-permute-done.7.refs_0_, f32[96,512]{1,0:T(8,128)S(1)} %collective-permute-done.8.refs_7_.refs_1_, f32[64,512]{1,0:T(8,128)S(1)} %shard_map.42.refs_2_), custom_call_target="tpu_custom_call" | custom-call | flops 33554432 | bytes 589824 | tf_op jit(solution)/shard_map/pallas_call | solution.py:125
  22.2 1.2 %collective-permute-start.9 = (f32[64,512]{1,0:T(8,128)S(1)}, f32[64,512]{1,0:T(8,128)S(1)}, u32[]{:S(2)}, u32[]{:S(2)}) collective-permute-start(f32[64,512]{1,0:T(8,128)S(1)} %shard_map.43), channel_id=1, source_target_pairs={{0,4},{1,5},{2,6},{3,7},{4,0},{5,1},{6,2},{7,3},{8,12},{9,13},{10,... | collective-permute-start | bytes 393224 | tf_op jit(solution)/shard_map/ppermute | solution.py:19
  23.4 0.0 copy-done.1
  23.4 3.5 %shard_map.41 = f32[64,512]{1,0:T(8,128)S(1)} custom-call(f32[96,512]{1,0:T(8,128)S(1)} %copy-done.1, f32[96,512]{1,0:T(8,128)S(1)} %collective-permute-done.refs_2_.refs_1_, f32[96,512]{1,0:T(8,128)S(1)} %constant_dynamic-update-slice_fusion.refs_3_.refs_2_, f32[96,512]{1,0:T(8,128)S(1)} %collective-permute-done.3.refs_4_.refs_3_, ...), custom_call_target="tpu_custom_call" | custom-call | flops 7516192768 | bytes 1769472 | tf_op jit(solution)/shard_map/pallas_call | solution.py:125
  26.9 0.9 %collective-permute-done.9 = f32[64,512]{1,0:T(8,128)S(1)} collective-permute-done((f32[64,512]{1,0:T(8,128)S(1)}, f32[64,512]{1,0:T(8,128)S(1)}, u32[]{:S(2)}, u32[]{:S(2)}) %collective-permute-start.9) | collective-permute-done | bytes 131104 | tf_op jit(solution)/shard_map/ppermute | solution.py:19
  27.8 0.7 %add.3 = f32[64,512]{1,0:T(8,128)} add(f32[64,512]{1,0:T(8,128)S(1)} %shard_map.41, f32[64,512]{1,0:T(8,128)S(1)} %collective-permute-done.9) | non-fusion elementwise | flops 32768 | bytes 393216 | tf_op jit(solution)/shard_map/add | solution.py:197
  (6 shorter events, 0.1 us)
Async XLA Ops:
  0.0 13.5 %collective-permute-start.1 = (f32[64,512]{1,0:T(8,128)}, f32[64,512]{1,0:T(8,128)S(1)}, u32[]{:S(2)}, u32[]{:S(2)}) collective-permute-start(f32[64,512]{1,0:T(8,128)} %features_ref.1), channel_id=1, source_target_pairs={{0,8},{1,9},{2,10},{3,11},{4,12},{5,13},{6,14},{7,15},{8,0},{9,1},... | collective-permute-start | bytes 393224 | tf_op jit(solution)/shard_map/ppermute | solution.py:19
  5.7 7.8 %collective-permute-start.2 = (f32[32,512]{1,0:T(8,128)}, f32[32,512]{1,0:T(8,128)S(1)}, u32[]{:S(2)}, u32[]{:S(2)}) collective-permute-start(f32[32,512]{1,0:T(8,128)} %get-tuple-element.14), channel_id=1, source_target_pairs={{0,8},{1,9},{2,10},{3,11},{4,12},{5,13},{6,14},{7,15},{8,0},{9,1},... | collective-permute-start | bytes 196616 | tf_op jit(solution)/shard_map/ppermute | solution.py:19
  5.7 10.0 %collective-permute-start = (f32[96,512]{1,0:T(8,128)}, f32[96,512]{1,0:T(8,128)S(1)}, u32[]{:S(2)}, u32[]{:S(2)}) collective-permute-start(f32[96,512]{1,0:T(8,128)} %get-tuple-element.13.refs_0_.refs_1_), channel_id=1, source_target_pairs={{0,1},{1,0},{2,3},{3,2},{4,5},{5,4},{6,7},{7,6},{8,9},{9,8},{10,11... | collective-permute-start | bytes 589832 | tf_op jit(solution)/shard_map/ppermute | solution.py:19
  5.7 9.8 %collective-permute-start.3 = (f32[96,512]{1,0:T(8,128)}, f32[96,512]{1,0:T(8,128)S(1)}, u32[]{:S(2)}, u32[]{:S(2)}) collective-permute-start(f32[96,512]{1,0:T(8,128)} %get-tuple-element.13.refs_0_.refs_1_), channel_id=1, source_target_pairs={{0,2},{1,3},{2,0},{3,1},{4,6},{5,7},{6,4},{7,5},{8,10},{9,11},{10,... | collective-permute-start | bytes 589832 | tf_op jit(solution)/shard_map/ppermute | solution.py:19
  7.5 9.1 %collective-permute-start.7 = (f32[96,512]{1,0:T(8,128)}, f32[96,512]{1,0:T(8,128)S(1)}, u32[]{:S(2)}, u32[]{:S(2)}) collective-permute-start(f32[96,512]{1,0:T(8,128)} %get-tuple-element.13.refs_0_.refs_1_), channel_id=1, source_target_pairs={{0,4},{1,5},{2,6},{3,7},{4,0},{5,1},{6,2},{7,3},{8,12},{9,13},{10,... | collective-permute-start | bytes 589832 | tf_op jit(solution)/shard_map/ppermute | solution.py:19
  9.1 1.0 %copy-start = (f32[96,512]{1,0:T(8,128)S(1)}, f32[96,512]{1,0:T(8,128)}, u32[]{:S(2)}) copy-start(f32[96,512]{1,0:T(8,128)} %get-tuple-element.13.refs_0_.refs_1_) | copy-start | bytes 589828
  13.5 6.4 %collective-permute-start.5 = (f32[64,512]{1,0:T(8,128)S(1)}, f32[64,512]{1,0:T(8,128)S(1)}, u32[]{:S(2)}, u32[]{:S(2)}) collective-permute-start(f32[64,512]{1,0:T(8,128)S(1)} %collective-permute-done.1), channel_id=1, source_target_pairs={{0,2},{1,3},{2,0},{3,1},{4,6},{5,7},{6,4},{7,5},{8,10},{9,11},{10,... | collective-permute-start | bytes 393224 | tf_op jit(solution)/shard_map/ppermute | solution.py:19
  15.0 4.9 %collective-permute-start.6 = (f32[32,512]{1,0:T(8,128)S(1)}, f32[32,512]{1,0:T(8,128)S(1)}, u32[]{:S(2)}, u32[]{:S(2)}) collective-permute-start(f32[32,512]{1,0:T(8,128)S(1)} %collective-permute-done.2), channel_id=1, source_target_pairs={{0,2},{1,3},{2,0},{3,1},{4,6},{5,7},{6,4},{7,5},{8,10},{9,11},{10,... | collective-permute-start | bytes 196616 | tf_op jit(solution)/shard_map/ppermute | solution.py:19
  15.6 3.2 %collective-permute-start.4 = (f32[192,512]{1,0:T(8,128)S(1)}, f32[192,512]{1,0:T(8,128)S(1)}, u32[]{:S(2)}, u32[]{:S(2)}) collective-permute-start(f32[192,512]{1,0:T(8,128)S(1)} %pad_maximum_fusion), channel_id=1, source_target_pairs={{0,1},{1,0},{2,3},{3,2},{4,5},{5,4},{6,7},{7,6},{8,9},{9,8},{10,11... | collective-permute-start | bytes 1179656 | tf_op jit(solution)/shard_map/ppermute | solution.py:19
  20.0 1.5 %collective-permute-start.8 = (f32[96,512]{1,0:T(8,128)S(1)}, f32[96,512]{1,0:T(8,128)S(1)}, u32[]{:S(2)}, u32[]{:S(2)}) collective-permute-start(f32[96,512]{1,0:T(8,128)S(1)} %constant_dynamic-update-slice_fusion.2.refs_6_.refs_1_), channel_id=1, source_target_pairs={{0,1},{1,0},{2,3},{3,2},{4,5},{5,4},{6,7},{7,6},{8,9},{9,8},{10,11... | collective-permute-start | bytes 589832 | tf_op jit(solution)/shard_map/ppermute | solution.py:19
  20.8 2.6 %copy-start.1 = (f32[96,512]{1,0:T(8,128)S(1)}, f32[96,512]{1,0:T(8,128)}, u32[]{:S(2)}) copy-start(f32[96,512]{1,0:T(8,128)} %get-tuple-element.13.refs_0_.refs_1_) | copy-start | bytes 589828
  22.2 5.6 %collective-permute-start.9 = (f32[64,512]{1,0:T(8,128)S(1)}, f32[64,512]{1,0:T(8,128)S(1)}, u32[]{:S(2)}, u32[]{:S(2)}) collective-permute-start(f32[64,512]{1,0:T(8,128)S(1)} %shard_map.43), channel_id=1, source_target_pairs={{0,4},{1,5},{2,6},{3,7},{4,0},{5,1},{6,2},{7,3},{8,12},{9,13},{10,... | collective-permute-start | bytes 393224 | tf_op jit(solution)/shard_map/ppermute | solution.py:19

commit v25 on v24

--- a/solution.py
+++ b/solution.py
@@ -10,7 +10,7 @@
 LOG2E = 1.4426950408889634
 NORM_ROWS = 16
 ONES_ROWS = 16
-STACK = 4
+STACK = 7
 VMEM_LIMIT = 24 << 20
 
 

time: 28.7 us -> 28.7 us (level)
  no operation moved by 1% of the time
where the time goes in v25:
time: 28.7 us; the launch traced here: 28.5 us
  starting transfers between devices  10.8 us (38%)
  Pallas kernels  10.6 us (37%)
  waiting for transfers between devices  5.22 us (18%)
  local copies, waits for them, and re-layouts  1.03 us (4%)
  other arithmetic  0.7 us (2%)
    ppermute x10, starting transfers between devices, swapped(): lax.ppermute(value, axis, [(source, source ^ bit) for source in range(cou...  10.8 us
    pallas_call x6, Pallas kernels, pair_terms(): pl.pallas_call(functools.partial(kernel, width, vectors, placed, len(bloc...  8.91 us
    ppermute x10, waiting for transfers between devices, swapped(): lax.ppermute(value, axis, [(source, source ^ bit) for source in range(cou...  5.22 us
    pallas_call x1, Pallas kernels, packed(): pl.pallas_call(body, out_shape=[jax.ShapeDtypeStruct((rows, points), jnp....  1.65 us
    unnamed x6, local copies, waits for them, and re-layouts  0.98 us
    add x1, other arithmetic, local(): return here + from_near  0.67 us
  transfers between devices with their start and end apart: 10, of which 4 were waited for; matrix products, arithmetic and copies ran while one was open for 0% of the time, Pallas kernels for 34%

profile of v25, /device:TPU:0, one launch (start us, length us, event | category | flops | bytes accessed | tf_op | source)
XLA Modules:
  0.0 28.5 jit_solution(7494885797630302016)
XLA Ops:
  0.0 4.0 %collective-permute-start.1 = (f32[64,512]{1,0:T(8,128)}, f32[64,512]{1,0:T(8,128)S(1)}, u32[]{:S(2)}, u32[]{:S(2)}) collective-permute-start(f32[64,512]{1,0:T(8,128)} %features_ref.1), channel_id=1, source_target_pairs={{0,8},{1,9},{2,10},{3,11},{4,12},{5,13},{6,14},{7,15},{8,0},{9,1},... | collective-permute-start | bytes 393224 | tf_op jit(solution)/shard_map/ppermute | solution.py:19
  4.0 1.7 %shard_map.37 = (f32[96,512]{1,0:T(8,128)}, f32[32,512]{1,0:T(8,128)}) custom-call(f32[64,512]{1,0:T(8,128)} %features_ref.1, f32[16,512]{1,0:T(8,128)} %solves_ref.1, f32[16,512]{1,0:T(8,128)} %probes_ref.1), custom_call_target="tpu_custom_call" | custom-call | tf_op jit(solution)/shard_map/pallas_call | solution.py:150
  5.7 0.0 collective-permute-start.2
  5.7 0.0 collective-permute-start
  5.7 1.9 %collective-permute-start.3 = (f32[96,512]{1,0:T(8,128)}, f32[96,512]{1,0:T(8,128)S(1)}, u32[]{:S(2)}, u32[]{:S(2)}) collective-permute-start(f32[96,512]{1,0:T(8,128)} %get-tuple-element.13.refs_0_.refs_1_), channel_id=1, source_target_pairs={{0,2},{1,3},{2,0},{3,1},{4,6},{5,7},{6,4},{7,5},{8,10},{9,11},{10,... | collective-permute-start | bytes 589832 | tf_op jit(solution)/shard_map/ppermute | solution.py:19
  7.5 1.6 %collective-permute-start.7 = (f32[96,512]{1,0:T(8,128)}, f32[96,512]{1,0:T(8,128)S(1)}, u32[]{:S(2)}, u32[]{:S(2)}) collective-permute-start(f32[96,512]{1,0:T(8,128)} %get-tuple-element.13.refs_0_.refs_1_), channel_id=1, source_target_pairs={{0,4},{1,5},{2,6},{3,7},{4,0},{5,1},{6,2},{7,3},{8,12},{9,13},{10,... | collective-permute-start | bytes 589832 | tf_op jit(solution)/shard_map/ppermute | solution.py:19
  9.1 0.0 copy-start
  9.1 1.0 %copy-done = f32[96,512]{1,0:T(8,128)S(1)} copy-done((f32[96,512]{1,0:T(8,128)S(1)}, f32[96,512]{1,0:T(8,128)}, u32[]{:S(2)}) %copy-start) | copy-done | bytes 196632
  10.1 0.8 %shard_map.38.refs_8_ = f32[64,512]{1,0:T(8,128)S(1)} custom-call(f32[96,512]{1,0:T(8,128)S(1)} %copy-done), custom_call_target="tpu_custom_call" | custom-call | flops 33554432 | bytes 196608 | tf_op jit(solution)/shard_map/pallas_call | solution.py:125
  10.8 2.6 %collective-permute-done.2 = f32[32,512]{1,0:T(8,128)S(1)} collective-permute-done((f32[32,512]{1,0:T(8,128)}, f32[32,512]{1,0:T(8,128)S(1)}, u32[]{:S(2)}, u32[]{:S(2)}) %collective-permute-start.2) | collective-permute-done | bytes 65568 | tf_op jit(solution)/shard_map/ppermute | solution.py:19
  13.5 0.0 collective-permute-done.1
  13.5 1.5 %collective-permute-start.5 = (f32[64,512]{1,0:T(8,128)S(1)}, f32[64,512]{1,0:T(8,128)S(1)}, u32[]{:S(2)}, u32[]{:S(2)}) collective-permute-start(f32[64,512]{1,0:T(8,128)S(1)} %collective-permute-done.1), channel_id=1, source_target_pairs={{0,2},{1,3},{2,0},{3,1},{4,6},{5,7},{6,4},{7,5},{8,10},{9,11},{10,... | collective-permute-start | bytes 393224 | tf_op jit(solution)/shard_map/ppermute | solution.py:19
  15.0 0.5 %collective-permute-start.6 = (f32[32,512]{1,0:T(8,128)S(1)}, f32[32,512]{1,0:T(8,128)S(1)}, u32[]{:S(2)}, u32[]{:S(2)}) collective-permute-start(f32[32,512]{1,0:T(8,128)S(1)} %collective-permute-done.2), channel_id=1, source_target_pairs={{0,2},{1,3},{2,0},{3,1},{4,6},{5,7},{6,4},{7,5},{8,10},{9,11},{10,... | collective-permute-start | bytes 196616 | tf_op jit(solution)/shard_map/ppermute | solution.py:19
  15.5 0.0 collective-permute-done.3.refs_4_.refs_3_
  15.6 0.1 collective-permute-start.4
  15.7 0.0 collective-permute-done.refs_2_.refs_1_
  15.7 1.0 %collective-permute-done.7.refs_0_ = f32[96,512]{1,0:T(8,128)S(1)} collective-permute-done((f32[96,512]{1,0:T(8,128)}, f32[96,512]{1,0:T(8,128)S(1)}, u32[]{:S(2)}, u32[]{:S(2)}) %collective-permute-start.7) | collective-permute-done | bytes 196640 | tf_op jit(solution)/shard_map/ppermute | solution.py:19
  16.7 2.0 %shard_map.39.refs_3_ = f32[64,512]{1,0:T(8,128)S(1)} custom-call(f32[96,512]{1,0:T(8,128)S(1)} %collective-permute-done.7.refs_0_, f32[96,512]{1,0:T(8,128)S(1)} %copy-done, f32[96,512]{1,0:T(8,128)S(1)} %collective-permute-done.refs_2_.refs_1_, f32[96,512]{1,0:T(8,128)S(1)} %constant_dynamic-update-slice_fusion.refs_3_.refs_2_, ...), custom_call_target="tpu_custom_call" | custom-call | flops 4294967296 | bytes 983040 | tf_op jit(solution)/shard_map/pallas_call | solution.py:125
  18.7 0.0 collective-permute-done.4
  18.8 1.1 %shard_map.40.refs_2_ = f32[64,512]{1,0:T(8,128)S(1)} custom-call(f32[96,512]{1,0:T(8,128)S(1)} %collective-permute-done.7.refs_0_, f32[96,512]{1,0:T(8,128)S(1)} %get-tuple-element.22.refs_1_.refs_4_, f32[96,512]{1,0:T(8,128)S(1)} %get-tuple-element.21.refs_2_.refs_5_, f32[64,512]{1,0:T(8,128)S(1)} %shard_map.39.refs_3_), custom_call_target="tpu_custom_call" | custom-call | flops 67108864 | bytes 786432 | tf_op jit(solution)/shard_map/pallas_call | solution.py:125
  19.9 0.0 collective-permute-done.6
  19.9 0.0 collective-permute-done.5
  20.0 0.1 collective-permute-start.8
  20.0 0.8 %shard_map.42.refs_2_ = f32[64,512]{1,0:T(8,128)S(1)} custom-call(f32[96,512]{1,0:T(8,128)S(1)} %collective-permute-done.7.refs_0_, f32[96,512]{1,0:T(8,128)S(1)} %constant_dynamic-update-slice_fusion.2.refs_6_.refs_1_, f32[64,512]{1,0:T(8,128)S(1)} %shard_map.40.refs_2_), custom_call_target="tpu_custom_call" | custom-call | flops 33554432 | bytes 589824 | tf_op jit(solution)/shard_map/pallas_call | solution.py:125
  20.8 0.0 copy-start.1
  20.8 0.6 %collective-permute-done.8.refs_7_.refs_1_ = f32[96,512]{1,0:T(8,128)S(1)} collective-permute-done((f32[96,512]{1,0:T(8,128)S(1)}, f32[96,512]{1,0:T(8,128)S(1)}, u32[]{:S(2)}, u32[]{:S(2)}) %collective-permute-start.8) | collective-permute-done | bytes 196640 | tf_op jit(solution)/shard_map/ppermute | solution.py:19
  21.5 0.8 %shard_map.43 = f32[64,512]{1,0:T(8,128)S(1)} custom-call(f32[96,512]{1,0:T(8,128)S(1)} %collective-permute-done.7.refs_0_, f32[96,512]{1,0:T(8,128)S(1)} %collective-permute-done.8.refs_7_.refs_1_, f32[64,512]{1,0:T(8,128)S(1)} %shard_map.42.refs_2_), custom_call_target="tpu_custom_call" | custom-call | flops 33554432 | bytes 589824 | tf_op jit(solution)/shard_map/pallas_call | solution.py:125
  22.2 1.2 %collective-permute-start.9 = (f32[64,512]{1,0:T(8,128)S(1)}, f32[64,512]{1,0:T(8,128)S(1)}, u32[]{:S(2)}, u32[]{:S(2)}) collective-permute-start(f32[64,512]{1,0:T(8,128)S(1)} %shard_map.43), channel_id=1, source_target_pairs={{0,4},{1,5},{2,6},{3,7},{4,0},{5,1},{6,2},{7,3},{8,12},{9,13},{10,... | collective-permute-start | bytes 393224 | tf_op jit(solution)/shard_map/ppermute | solution.py:19
  23.4 0.0 copy-done.1
  23.4 3.5 %shard_map.41 = f32[64,512]{1,0:T(8,128)S(1)} custom-call(f32[96,512]{1,0:T(8,128)S(1)} %copy-done.1, f32[96,512]{1,0:T(8,128)S(1)} %collective-permute-done.refs_2_.refs_1_, f32[96,512]{1,0:T(8,128)S(1)} %constant_dynamic-update-slice_fusion.refs_3_.refs_2_, f32[96,512]{1,0:T(8,128)S(1)} %collective-permute-done.3.refs_4_.refs_3_, ...), custom_call_target="tpu_custom_call" | custom-call | flops 7516192768 | bytes 1769472 | tf_op jit(solution)/shard_map/pallas_call | solution.py:125
  26.9 0.9 %collective-permute-done.9 = f32[64,512]{1,0:T(8,128)S(1)} collective-permute-done((f32[64,512]{1,0:T(8,128)S(1)}, f32[64,512]{1,0:T(8,128)S(1)}, u32[]{:S(2)}, u32[]{:S(2)}) %collective-permute-start.9) | collective-permute-done | bytes 131104 | tf_op jit(solution)/shard_map/ppermute | solution.py:19
  27.8 0.7 %add.3 = f32[64,512]{1,0:T(8,128)} add(f32[64,512]{1,0:T(8,128)S(1)} %shard_map.41, f32[64,512]{1,0:T(8,128)S(1)} %collective-permute-done.9) | non-fusion elementwise | flops 32768 | bytes 393216 | tf_op jit(solution)/shard_map/add | solution.py:197
  (6 shorter events, 0.1 us)
Async XLA Ops:
  0.0 13.5 %collective-permute-start.1 = (f32[64,512]{1,0:T(8,128)}, f32[64,512]{1,0:T(8,128)S(1)}, u32[]{:S(2)}, u32[]{:S(2)}) collective-permute-start(f32[64,512]{1,0:T(8,128)} %features_ref.1), channel_id=1, source_target_pairs={{0,8},{1,9},{2,10},{3,11},{4,12},{5,13},{6,14},{7,15},{8,0},{9,1},... | collective-permute-start | bytes 393224 | tf_op jit(solution)/shard_map/ppermute | solution.py:19
  5.7 7.8 %collective-permute-start.2 = (f32[32,512]{1,0:T(8,128)}, f32[32,512]{1,0:T(8,128)S(1)}, u32[]{:S(2)}, u32[]{:S(2)}) collective-permute-start(f32[32,512]{1,0:T(8,128)} %get-tuple-element.14), channel_id=1, source_target_pairs={{0,8},{1,9},{2,10},{3,11},{4,12},{5,13},{6,14},{7,15},{8,0},{9,1},... | collective-permute-start | bytes 196616 | tf_op jit(solution)/shard_map/ppermute | solution.py:19
  5.7 10.0 %collective-permute-start = (f32[96,512]{1,0:T(8,128)}, f32[96,512]{1,0:T(8,128)S(1)}, u32[]{:S(2)}, u32[]{:S(2)}) collective-permute-start(f32[96,512]{1,0:T(8,128)} %get-tuple-element.13.refs_0_.refs_1_), channel_id=1, source_target_pairs={{0,1},{1,0},{2,3},{3,2},{4,5},{5,4},{6,7},{7,6},{8,9},{9,8},{10,11... | collective-permute-start | bytes 589832 | tf_op jit(solution)/shard_map/ppermute | solution.py:19
  5.7 9.8 %collective-permute-start.3 = (f32[96,512]{1,0:T(8,128)}, f32[96,512]{1,0:T(8,128)S(1)}, u32[]{:S(2)}, u32[]{:S(2)}) collective-permute-start(f32[96,512]{1,0:T(8,128)} %get-tuple-element.13.refs_0_.refs_1_), channel_id=1, source_target_pairs={{0,2},{1,3},{2,0},{3,1},{4,6},{5,7},{6,4},{7,5},{8,10},{9,11},{10,... | collective-permute-start | bytes 589832 | tf_op jit(solution)/shard_map/ppermute | solution.py:19
  7.5 9.1 %collective-permute-start.7 = (f32[96,512]{1,0:T(8,128)}, f32[96,512]{1,0:T(8,128)S(1)}, u32[]{:S(2)}, u32[]{:S(2)}) collective-permute-start(f32[96,512]{1,0:T(8,128)} %get-tuple-element.13.refs_0_.refs_1_), channel_id=1, source_target_pairs={{0,4},{1,5},{2,6},{3,7},{4,0},{5,1},{6,2},{7,3},{8,12},{9,13},{10,... | collective-permute-start | bytes 589832 | tf_op jit(solution)/shard_map/ppermute | solution.py:19
  9.1 1.0 %copy-start = (f32[96,512]{1,0:T(8,128)S(1)}, f32[96,512]{1,0:T(8,128)}, u32[]{:S(2)}) copy-start(f32[96,512]{1,0:T(8,128)} %get-tuple-element.13.refs_0_.refs_1_) | copy-start | bytes 589828
  13.5 6.4 %collective-permute-start.5 = (f32[64,512]{1,0:T(8,128)S(1)}, f32[64,512]{1,0:T(8,128)S(1)}, u32[]{:S(2)}, u32[]{:S(2)}) collective-permute-start(f32[64,512]{1,0:T(8,128)S(1)} %collective-permute-done.1), channel_id=1, source_target_pairs={{0,2},{1,3},{2,0},{3,1},{4,6},{5,7},{6,4},{7,5},{8,10},{9,11},{10,... | collective-permute-start | bytes 393224 | tf_op jit(solution)/shard_map/ppermute | solution.py:19
  15.0 4.9 %collective-permute-start.6 = (f32[32,512]{1,0:T(8,128)S(1)}, f32[32,512]{1,0:T(8,128)S(1)}, u32[]{:S(2)}, u32[]{:S(2)}) collective-permute-start(f32[32,512]{1,0:T(8,128)S(1)} %collective-permute-done.2), channel_id=1, source_target_pairs={{0,2},{1,3},{2,0},{3,1},{4,6},{5,7},{6,4},{7,5},{8,10},{9,11},{10,... | collective-permute-start | bytes 196616 | tf_op jit(solution)/shard_map/ppermute | solution.py:19
  15.6 3.2 %collective-permute-start.4 = (f32[192,512]{1,0:T(8,128)S(1)}, f32[192,512]{1,0:T(8,128)S(1)}, u32[]{:S(2)}, u32[]{:S(2)}) collective-permute-start(f32[192,512]{1,0:T(8,128)S(1)} %pad_maximum_fusion), channel_id=1, source_target_pairs={{0,1},{1,0},{2,3},{3,2},{4,5},{5,4},{6,7},{7,6},{8,9},{9,8},{10,11... | collective-permute-start | bytes 1179656 | tf_op jit(solution)/shard_map/ppermute | solution.py:19
  20.0 1.5 %collective-permute-start.8 = (f32[96,512]{1,0:T(8,128)S(1)}, f32[96,512]{1,0:T(8,128)S(1)}, u32[]{:S(2)}, u32[]{:S(2)}) collective-permute-start(f32[96,512]{1,0:T(8,128)S(1)} %constant_dynamic-update-slice_fusion.2.refs_6_.refs_1_), channel_id=1, source_target_pairs={{0,1},{1,0},{2,3},{3,2},{4,5},{5,4},{6,7},{7,6},{8,9},{9,8},{10,11... | collective-permute-start | bytes 589832 | tf_op jit(solution)/shard_map/ppermute | solution.py:19
  20.8 2.6 %copy-start.1 = (f32[96,512]{1,0:T(8,128)S(1)}, f32[96,512]{1,0:T(8,128)}, u32[]{:S(2)}) copy-start(f32[96,512]{1,0:T(8,128)} %get-tuple-element.13.refs_0_.refs_1_) | copy-start | bytes 589828
  22.2 5.6 %collective-permute-start.9 = (f32[64,512]{1,0:T(8,128)S(1)}, f32[64,512]{1,0:T(8,128)S(1)}, u32[]{:S(2)}, u32[]{:S(2)}) collective-permute-start(f32[64,512]{1,0:T(8,128)S(1)} %shard_map.43), channel_id=1, source_target_pairs={{0,4},{1,5},{2,6},{3,7},{4,0},{5,1},{6,2},{7,3},{8,12},{9,13},{10,... | collective-permute-start | bytes 393224 | tf_op jit(solution)/shard_map/ppermute | solution.py:19
